TPU v7x, 32 devices: a whole 2x2x4 slice. The times are simulated.
32 devices in a mesh: groups: 1, ep: 32 (over z, y, x, core).
Axes of the slice: x: 2, y: 2, z: 4, core: 2. Of those that a mesh axis runs over, the one named last changes fastest.
Arguments:
- hidden: bfloat16 [2, 128, 7168], P(None, ('groups', 'ep')), may hold values from -6 to 6
- norm_gain: float32 [7168], replicated, may hold values from 0.25 to 1.75
- router: bfloat16 [7168, 6], replicated, may hold values from -0.25 to 0.25
- expert_ids: int32 [2, 128, 2], P(None, ('groups', 'ep')), may hold values from 0 to 5, all different within a row
- replica: int32 [2, 128, 2], P(None, ('groups', 'ep')), may hold values from 0 to 1
- copy_table: int32 [6, 2], replicated, may hold values from 0 to 7, as said below
- gate_w: bfloat16 [7168, 8192], P(None, 'ep'), may hold values from -0.0625 to 0.0625
- up_w: bfloat16 [7168, 8192], P(None, 'ep'), may hold values from -0.0625 to 0.0625
- down_w: bfloat16 [8192, 7168], P('ep'), may hold values from -0.1875 to 0.1875
- query: bfloat16 [2, 128, 64, 576], P(None, ('groups', 'ep')), may hold values from -96 to 96
- cache: bfloat16 [128, 64, 576], P(('groups', 'ep')), may hold values from -6 to 6
- lengths: int32 [128], P(('groups', 'ep')), may hold values from 2 to 62
- fresh_kv: bfloat16 [2, 128, 576], P(None, ('groups', 'ep')), may hold values from -6 to 6
Outputs:
- attended: bfloat16 [2, 128, 64, 512], P(None, ('groups', 'ep'))
- moe_out: bfloat16 [2, 128, 7168], P(None, ('groups', 'ep'))
Inputs may be any that keep to these rules, and one draw needn't show every extreme that they name: `copy_table`: column 0 names a different copy for every expert; column 1 equals column 0 except for 2 experts, whose column 1 names the remaining copies, so every copy appears.
All inputs are finite; a program needn't handle non-finite values.
Results may differ from a plain program's by a relative error of at most 0.012.
Values may be sent and summed in bfloat16 or wider, within the bound.
No kernel may reach another device: no remote copies, remote signals or barrier semaphores. Data moves between devices by JAX's collectives and lax.ppermute only.
A program may use at most 128 MiB of HBM per device.

v0:
```python
import jax
import jax.numpy as jnp
from jax import lax
from jax.sharding import PartitionSpec as P

D = 7168
KV = 512
SPAN_BITS = 2
SPAN = 4
DS = 1792


softmax_scale = 192.0 ** (-0.5)
routed_scale = 2.5
norm_eps = 1e-06
masked_score = -1e30


def swapped(value, axis, distance):
    mask = 2**distance
    pairs = [(source, source ^ mask) for source in range(lax.axis_size(axis))]
    return lax.ppermute(value, axis, pairs)


def attend(queries, cache, lengths, fresh):
    old_scores = (
        jnp.einsum("nhl,ncl->nhc", queries, cache, preferred_element_type=jnp.float32)
        * softmax_scale
    )
    new_scores = (
        jnp.einsum("nhl,nml->nhm", queries, fresh, preferred_element_type=jnp.float32)
        * softmax_scale
    )
    positions = lax.broadcasted_iota(jnp.int32, old_scores.shape, 2)
    valid = positions < lengths[:, None, None]
    old_scores = jnp.where(valid, old_scores, masked_score)
    highest = jnp.maximum(jnp.max(old_scores, axis=2), jnp.max(new_scores, axis=2))[:, :, None]
    old_terms = jnp.where(valid, jnp.exp(old_scores - highest), 0.0)
    new_terms = jnp.exp(new_scores - highest)
    total = jnp.sum(old_terms, axis=2, keepdims=True) + jnp.sum(new_terms, axis=2, keepdims=True)
    old_probs = (old_terms / total).astype(jnp.bfloat16)
    new_probs = (new_terms / total).astype(jnp.bfloat16)
    output = jnp.einsum(
        "nhc,ncv->nhv", old_probs, cache[:, :, :KV], preferred_element_type=jnp.float32
    )
    output = output + jnp.einsum(
        "nhm,nmv->nhv", new_probs, fresh[:, :, :KV], preferred_element_type=jnp.float32
    )
    return output.astype(jnp.bfloat16)


def expert_rows(received, gate_w, up_w, down_w):
    row_total = received.shape[0] * received.shape[1]
    flat_rows = received.reshape(row_total, received.shape[2])
    gate = jnp.dot(flat_rows, gate_w, preferred_element_type=jnp.float32)
    upper = jnp.dot(flat_rows, up_w, preferred_element_type=jnp.float32)
    inner = (jax.nn.silu(gate) * upper).astype(jnp.bfloat16)
    partial_out = jnp.dot(inner, down_w, preferred_element_type=jnp.float32).astype(jnp.bfloat16)
    return partial_out.reshape(received.shape[0], received.shape[1], partial_out.shape[1])


def split_halves(values, upper_bit):
    half_width = values.shape[2] // 2
    low_half = values[:, :, :half_width]
    high_half = values[:, :, half_width:]
    kept_half = jnp.where(upper_bit, high_half, low_half)
    given_half = jnp.where(upper_bit, low_half, high_half)
    return (kept_half, given_half)


def mixture(hidden, norm_gain, router, expert_ids, replica, copy_table, gate_w, up_w, down_w):
    axis_count = lax.axis_size("ep")
    phys_count = axis_count // SPAN
    row_count = hidden.shape[0]
    top_count = expert_ids.shape[1]
    slot_count = max(2, 2 * row_count * top_count // phys_count)
    member = lax.axis_index("ep") % SPAN
    hidden_f = hidden.astype(jnp.float32)
    mean_square = jnp.mean(hidden_f * hidden_f, axis=1, keepdims=True)
    normed = (hidden_f * lax.rsqrt(mean_square + norm_eps) * norm_gain).astype(jnp.bfloat16)
    scores = jax.nn.sigmoid(jnp.dot(normed, router, preferred_element_type=jnp.float32))
    expert_count = router.shape[1]
    chooser = expert_ids[:, :, None] == lax.broadcasted_iota(
        jnp.int32, (row_count, top_count, expert_count), 2
    )
    picked = jnp.sum(jnp.where(chooser, scores[:, None, :], 0.0), axis=2)
    weights = routed_scale * picked / jnp.sum(picked, axis=1, keepdims=True)
    copy_choice = jnp.where(
        replica[:, :, None] == 0, copy_table[None, None, :, 0], copy_table[None, None, :, 1]
    )
    copies = jnp.sum(jnp.where(chooser, copy_choice, 0), axis=2).reshape(-1)
    onehot = (
        copies[:, None] == lax.broadcasted_iota(jnp.int32, (copies.shape[0], phys_count), 1)
    ).astype(jnp.int32)
    slot_index = jnp.sum(jnp.cumsum(onehot, axis=0) * onehot, axis=1) - 1
    target = jnp.where(slot_index < slot_count, copies * slot_count + slot_index, -1)
    lanes = lax.broadcasted_iota(jnp.int32, (phys_count * slot_count, target.shape[0]), 0)
    placing = (lanes == target[None, :]).astype(jnp.bfloat16)
    assigned = jnp.repeat(normed, top_count, axis=0)
    packed = jnp.dot(placing, assigned, preferred_element_type=jnp.float32).astype(jnp.bfloat16)
    outgoing = (
        packed.reshape(phys_count, slot_count, SPAN, DS)
        .transpose(0, 2, 1, 3)
        .reshape(axis_count, slot_count, DS)
    )
    gathered_piece = lax.all_to_all(outgoing, "ep", split_axis=0, concat_axis=0, tiled=True)
    for bit_level in range(SPAN_BITS):
        partner = swapped(gathered_piece, "ep", bit_level)
        is_lower = member // 2**bit_level % 2 == 0
        gathered_piece = jnp.where(
            is_lower,
            jnp.concatenate([gathered_piece, partner], axis=2),
            jnp.concatenate([partner, gathered_piece], axis=2),
        )
    partial_out = expert_rows(gathered_piece, gate_w, up_w, down_w)
    top_level = SPAN_BITS - 1
    kept_half, given_half = split_halves(partial_out, member // 2**top_level % 2 == 1)
    summed = kept_half.astype(jnp.float32) + swapped(given_half, "ep", top_level).astype(
        jnp.float32
    )
    bit_level = 0
    kept_half, given_half = split_halves(summed, member // 2**bit_level % 2 == 1)
    summed = kept_half + swapped(given_half.astype(jnp.bfloat16), "ep", bit_level).astype(
        given_half.dtype
    )
    returned = lax.all_to_all(
        summed.astype(jnp.bfloat16), "ep", split_axis=0, concat_axis=0, tiled=True
    ).astype(summed.dtype)
    copy_out = (
        returned.reshape(phys_count, SPAN, slot_count, DS)
        .transpose(0, 2, 1, 3)
        .reshape(phys_count, slot_count, D)
    )
    columns = lax.broadcasted_iota(jnp.int32, (target.shape[0], phys_count * slot_count), 1)
    combining = jnp.where(columns == target[:, None], weights.reshape(-1)[:, None], 0.0)
    per_row = jnp.sum(combining.reshape(row_count, top_count, phys_count * slot_count), axis=1)
    result = jnp.dot(
        per_row,
        copy_out.reshape(phys_count * slot_count, D),
        precision=lax.Precision.HIGHEST,
        preferred_element_type=jnp.float32,
    )
    return result.astype(jnp.bfloat16)


def per_device(
    hidden,
    norm_gain,
    router,
    expert_ids,
    replica,
    copy_table,
    gate_w,
    up_w,
    down_w,
    query,
    cache,
    lengths,
    fresh_kv,
):
    attended = []
    moe_parts = []
    for decode_step in range(2):
        moe_parts.append(
            mixture(
                hidden[decode_step],
                norm_gain,
                router,
                expert_ids[decode_step],
                replica[decode_step],
                copy_table,
                gate_w,
                up_w,
                down_w,
            )
        )
        fresh = jnp.moveaxis(fresh_kv[: decode_step + 1], 0, 1)
        attended.append(attend(query[decode_step], cache, lengths, fresh))
    return (jnp.stack(attended), jnp.stack(moe_parts))


def solution(mesh):
    return jax.shard_map(
        per_device,
        mesh=mesh,
        in_specs=(
            P(None, ("groups", "ep"), None),
            P(),
            P(),
            P(None, ("groups", "ep"), None),
            P(None, ("groups", "ep"), None),
            P(),
            P(None, "ep"),
            P(None, "ep"),
            P("ep", None),
            P(None, ("groups", "ep"), None, None),
            P(("groups", "ep"), None, None),
            P(("groups", "ep")),
            P(None, ("groups", "ep"), None),
        ),
        out_specs=(P(None, ("groups", "ep"), None, None), P(None, ("groups", "ep"), None)),
        check_vma=False,
    )
```

profile of v0, /device:TPU:0, one launch (start us, length us, event | category | flops | bytes accessed | tf_op | source)
XLA Modules:
  0.0 114.0 jit_solution(12735398771006569943)
XLA Ops:
  0.7 0.8 slice_bitcast_fusion.4
  1.5 0.7 compare_bitcast_fusion
  2.2 0.8 slice_bitcast_fusion.6
  2.9 0.2 select_reduce_fusion.9
  3.4 0.2 select_reduce_fusion.8
  3.6 1.1 fusion.30
  4.7 1.0 fusion.32
  5.8 0.2 convolution_convert_fusion.3
  6.2 0.9 copy.50
  7.0 7.3 %all-to-all-start = ((bf16[32,2,1792]{2,1,0:T(2,128)(2,1)}), bf16[32,2,1792]{2,1,0:T(2,128)(2,1)S(1)}, u32[]{:S(2)}, u32[]{:S(2)}) async-start(bf16[32,2,1792]{2,1,0:T(2,128)(2,1)} %bitcast.18), calls=%async_computation | async-start | bytes 458752 | tf_op jit(solution)/shard_map/all_to_all | solution.py:106
  14.4 0.3 fusion.80
  14.7 0.3 fusion.81
  15.0 0.2 fusion.82
  15.7 0.2 select_reduce_fusion.5
  16.0 0.2 fusion.15
  16.2 0.2 select_reduce_fusion.2
  16.4 0.2 fusion.12
  16.8 0.2 convolution_convert_fusion.2
  17.1 0.9 copy.57
  18.0 0.2 select_reduce_fusion
  18.2 0.2 fusion.18
  18.6 0.6 fusion.69
  19.2 0.6 compare_select_fusion.1
  19.8 0.3 fusion.25
  20.1 4.0 %all-to-all-done = bf16[32,2,1792]{2,1,0:T(2,128)(2,1)S(1)} async-done(((bf16[32,2,1792]{2,1,0:T(2,128)(2,1)}), bf16[32,2,1792]{2,1,0:T(2,128)(2,1)S(1)}, u32[]{:S(2)}, u32[]{:S(2)}) %all-to-all-start) | async-done | bytes 229408 | tf_op jit(solution)/shard_map/all_to_all | solution.py:106
  24.2 2.8 %all-to-all-start.2 = ((bf16[32,2,1792]{2,1,0:T(2,128)(2,1)}), bf16[32,2,1792]{2,1,0:T(2,128)(2,1)S(1)}, u32[]{:S(2)}, u32[]{:S(2)}) async-start(bf16[32,2,1792]{2,1,0:T(2,128)(2,1)} %bitcast.27), calls=%async_computation.2 | async-start | bytes 458752 | tf_op jit(solution)/shard_map/all_to_all | solution.py:106
  26.9 0.6 multiply_divide_fusion
  27.6 0.6 fusion.60
  28.3 8.3 %all-to-all-done.2 = bf16[32,2,1792]{2,1,0:T(2,128)(2,1)S(1)} async-done(((bf16[32,2,1792]{2,1,0:T(2,128)(2,1)}), bf16[32,2,1792]{2,1,0:T(2,128)(2,1)S(1)}, u32[]{:S(2)}, u32[]{:S(2)}) %all-to-all-start.2) | async-done | bytes 229408 | tf_op jit(solution)/shard_map/all_to_all | solution.py:106
  36.6 0.2 collective-permute-start.4
  36.9 1.5 %broadcast_select_fusion.1 = bf16[32,2,3584]{2,1,0:T(2,128)(2,1)} fusion(pred[]{:T(512)S(6)} %eq.136, bf16[32,2,1792]{2,1,0:T(2,128)(2,1)S(1)} %collective-permute-done, bf16[32,2,1792]{2,1,0:T(2,128)(2,1)S(1)} %all-to-all-done), kind=kLoop, calls=%fused_computation.36 | loop fusion | flops 2064384 | bytes 917505 | tf_op jit(solution)/shard_map/jit(_where)/select_n | solution.py:110
  38.4 0.7 collective-permute-start.1
  39.1 1.5 %broadcast_select_fusion = bf16[32,2,3584]{2,1,0:T(2,128)(2,1)} fusion(pred[]{:T(512)S(6)} %eq.136, bf16[32,2,1792]{2,1,0:T(2,128)(2,1)S(1)} %collective-permute-done.4, bf16[32,2,1792]{2,1,0:T(2,128)(2,1)S(1)} %all-to-all-done.2), kind=kLoop, calls=%fused_computation.35 | loop fusion | flops 2064384 | bytes 917505 | tf_op jit(solution)/shard_map/jit(_where)/select_n | solution.py:110
  40.6 1.3 %collective-permute-start.5 = (bf16[32,2,3584]{2,1,0:T(2,128)(2,1)}, bf16[32,2,3584]{2,1,0:T(2,128)(2,1)}, u32[]{:S(2)}, u32[]{:S(2)}) collective-permute-start(bf16[32,2,3584]{2,1,0:T(2,128)(2,1)} %broadcast_select_fusion), channel_id=1, source_target_pairs={{0,2},{1,3},{2,0},{3,1},{4,6},{5,7},{6,4},{7,5},{8,10},{9,11},{10,... | collective-permute-start | bytes 1376264 | tf_op jit(solution)/shard_map/ppermute | solution.py:22
  42.3 9.7 %collective-permute-done.1 = bf16[32,2,3584]{2,1,0:T(2,128)(2,1)} collective-permute-done((bf16[32,2,3584]{2,1,0:T(2,128)(2,1)}, bf16[32,2,3584]{2,1,0:T(2,128)(2,1)}, u32[]{:S(2)}, u32[]{:S(2)}) %collective-permute-start.1) | collective-permute-done | bytes 458784 | tf_op jit(solution)/shard_map/ppermute | solution.py:22
  52.0 1.2 %concatenate.58 = bf16[64,3584]{1,0:T(8,128)(2,1)S(1)} reshape(bf16[32,2,3584]{2,1,0:T(2,128)(2,1)} %collective-permute-done.1) | data formatting | bytes 917504 | tf_op jit(solution)/shard_map/concatenate | solution.py:112
  53.2 2.7 %fusion.29 = f32[64,256]{1,0:T(8,128)S(1)} fusion(bf16[7168,256]{1,0:T(8,128)(2,1)} %param.19, bf16[64,3584]{1,0:T(8,128)(2,1)S(1)} %concatenate.58, bf16[64,3584]{1,0:T(8,128)(2,1)S(1)} %maximum_select_fusion.2, pred[]{:T(512)S(6)} %eq.135), kind=kOutput, calls=%fused_computation.61 | convolution fusion | flops 239009792 | bytes 4653057 | tf_op jit(solution)/shard_map/dot_general | solution.py:55
  55.9 5.5 %convolution_convert_fusion.1 = bf16[64,7168]{1,0:T(8,128)(2,1)S(1)} fusion(bf16[256,7168]{1,0:T(8,128)(2,1)} %param.21, bf16[7168,256]{1,0:T(8,128)(2,1)} %param.20, bf16[64,3584]{1,0:T(8,128)(2,1)S(1)} %concatenate.58, bf16[64,3584]{1,0:T(8,128)(2,1)S(1)} %maximum_select_fusion.2, pred[]{:T(512)S(6)} %eq.135, f32[64,256]{1,0:T(8,128)S(1)} %fusion.29), kind=kOutput, calls=%fused_computation.1 | convolution fusion | flops 474447872 | bytes 9240577 | tf_op jit(solution)/shard_map/dot_general | solution.py:58
  61.4 0.3 reshape.242
  61.7 1.3 %broadcast_select_fusion.4 = bf16[32,2,3584]{2,1,0:T(2,128)(2,1)} fusion(pred[]{:T(512)S(6)} %eq.134, bf16[32,2,7168]{2,1,0:T(2,128)(2,1)S(1)} %reshape.242), kind=kLoop, calls=%fused_computation.39 | loop fusion | flops 229376 | bytes 1376257 | tf_op jit(solution)/shard_map/jit(_where)/select_n | solution.py:67
  63.0 0.8 collective-permute-start.2
  63.8 1.2 %concatenate.67 = bf16[64,3584]{1,0:T(8,128)(2,1)S(1)} reshape(bf16[32,2,3584]{2,1,0:T(2,128)(2,1)} %collective-permute-done.5) | data formatting | bytes 917504 | tf_op jit(solution)/shard_map/concatenate | solution.py:112
  65.0 2.7 %fusion.28 = f32[64,256]{1,0:T(8,128)S(1)} fusion(bf16[7168,256]{1,0:T(8,128)(2,1)} %param.19, bf16[64,3584]{1,0:T(8,128)(2,1)S(1)} %concatenate.67, bf16[64,3584]{1,0:T(8,128)(2,1)S(1)} %maximum_select_fusion.3, pred[]{:T(512)S(6)} %eq.135), kind=kOutput, calls=%fused_computation.60 | convolution fusion | flops 239009792 | bytes 4653057 | tf_op jit(solution)/shard_map/dot_general | solution.py:55
  67.7 5.7 %convolution_convert_fusion = bf16[64,7168]{1,0:T(8,128)(2,1)S(1)} fusion(bf16[256,7168]{1,0:T(8,128)(2,1)} %param.21, bf16[7168,256]{1,0:T(8,128)(2,1)} %param.20, bf16[64,3584]{1,0:T(8,128)(2,1)S(1)} %concatenate.67, bf16[64,3584]{1,0:T(8,128)(2,1)} %copy-done.1, pred[]{:T(512)S(6)} %eq.135, f32[64,256]{1,0:T(8,128)S(1)} %fusion.28), kind=kOutput, calls=%fused_computation | convolution fusion | flops 474447872 | bytes 9240577 | tf_op jit(solution)/shard_map/dot_general | solution.py:58
  73.4 0.3 reshape.247
  73.8 0.5 broadcast_select_fusion.2
  74.3 1.3 %collective-permute-start.6 = (bf16[32,2,3584]{2,1,0:T(2,128)(2,1)S(1)}, bf16[32,2,3584]{2,1,0:T(2,128)(2,1)S(1)}, u32[]{:S(2)}, u32[]{:S(2)}) collective-permute-start(bf16[32,2,3584]{2,1,0:T(2,128)(2,1)S(1)} %broadcast_select_fusion.2), channel_id=1, source_target_pairs={{0,2},{1,3},{2,0},{3,1},{4,6},{5,7},{6,4},{7,5},{8,10},{9,11},{10,... | collective-permute-start | bytes 1376264 | tf_op jit(solution)/shard_map/ppermute | solution.py:22
  75.6 1.7 %convert_add_fusion.1 = f32[32,2,3584]{2,1,0:T(2,128)S(1)} fusion(bf16[32,2,3584]{2,1,0:T(2,128)(2,1)} %collective-permute-done.2, pred[]{:T(512)S(6)} %eq.134, bf16[32,2,7168]{2,1,0:T(2,128)(2,1)S(1)} %reshape.242), kind=kLoop, calls=%fused_computation.34 | loop fusion | flops 917504 | bytes 2293761 | tf_op jit(solution)/shard_map/add | solution.py:118
  77.2 0.2 select_convert_fusion.1
  77.5 7.4 %collective-permute-done.6 = bf16[32,2,3584]{2,1,0:T(2,128)(2,1)S(1)} collective-permute-done((bf16[32,2,3584]{2,1,0:T(2,128)(2,1)S(1)}, bf16[32,2,3584]{2,1,0:T(2,128)(2,1)S(1)}, u32[]{:S(2)}, u32[]{:S(2)}) %collective-permute-start.6) | collective-permute-done | bytes 458784 | tf_op jit(solution)/shard_map/ppermute | solution.py:22
  84.9 0.6 convert_add_fusion
  85.5 0.2 select_convert_fusion
  85.9 1.0 add_convert_fusion.1
  86.9 3.5 %all-to-all-start.1 = ((bf16[32,2,1792]{2,1,0:T(2,128)(2,1)}), bf16[32,2,1792]{2,1,0:T(2,128)(2,1)S(1)}, u32[]{:S(2)}, u32[]{:S(2)}) async-start(bf16[32,2,1792]{2,1,0:T(2,128)(2,1)} %add_convert_fusion.1), calls=%async_computation.1 | async-start | bytes 458752 | tf_op jit(solution)/shard_map/all_to_all | solution.py:126
  90.4 1.0 add_convert_fusion
  91.4 8.8 %all-to-all-done.1 = bf16[32,2,1792]{2,1,0:T(2,128)(2,1)S(1)} async-done(((bf16[32,2,1792]{2,1,0:T(2,128)(2,1)}), bf16[32,2,1792]{2,1,0:T(2,128)(2,1)S(1)}, u32[]{:S(2)}, u32[]{:S(2)}) %all-to-all-start.1) | async-done | bytes 229408 | tf_op jit(solution)/shard_map/all_to_all | solution.py:126
  100.2 2.6 %all-to-all-start.3 = ((bf16[32,2,1792]{2,1,0:T(2,128)(2,1)}), bf16[32,2,1792]{2,1,0:T(2,128)(2,1)S(1)}, u32[]{:S(2)}, u32[]{:S(2)}) async-start(bf16[32,2,1792]{2,1,0:T(2,128)(2,1)} %add_convert_fusion), calls=%async_computation.3 | async-start | bytes 458752 | tf_op jit(solution)/shard_map/all_to_all | solution.py:126
  102.9 0.3 fusion.5
  103.2 0.3 fusion.4
  103.6 0.8 pad_maximum_fusion
  104.6 8.1 %all-to-all-done.3 = bf16[32,2,1792]{2,1,0:T(2,128)(2,1)S(1)} async-done(((bf16[32,2,1792]{2,1,0:T(2,128)(2,1)}), bf16[32,2,1792]{2,1,0:T(2,128)(2,1)S(1)}, u32[]{:S(2)}, u32[]{:S(2)}) %all-to-all-start.3) | async-done | bytes 229408 | tf_op jit(solution)/shard_map/all_to_all | solution.py:126
  112.8 0.2 fusion
  113.0 0.2 fusion.1
  113.2 0.7 pad_maximum_fusion.1
  (76 shorter events, 2.9 us)
Async XLA Ops:
  0.6 15.4 %copy-start = (bf16[7168,6]{0,1:T(8,128)(2,1)S(1)}, bf16[7168,6]{0,1:T(8,128)(2,1)}, u32[]{:S(2)}) copy-start(bf16[7168,6]{0,1:T(8,128)(2,1)} %param.15) | copy-start | bytes 258052
  0.6 13.7 %copy-start.12 = (bf16[2,4,64,576]{3,2,1,0:T(8,128)(2,1)S(1)}, bf16[2,4,64,576]{3,2,1,0:T(8,128)(2,1)}, u32[]{:S(2)}) copy-start(bf16[2,4,64,576]{3,2,1,0:T(8,128)(2,1)} %param.22) | copy-start | bytes 1769476
  0.7 13.7 %copy-start.2 = (bf16[4,64,576]{2,1,0:T(8,128)(2,1)S(1)}, bf16[4,64,576]{2,1,0:T(8,128)(2,1)}, u32[]{:S(2)}) copy-start(bf16[4,64,576]{2,1,0:T(8,128)(2,1)} %param.23) | copy-start | bytes 884740
  0.7 13.7 %copy-start.8 = (s32[4]{0:T(128)S(1)}, s32[4]{0:T(128)}, u32[]{:S(2)}) copy-start(s32[4]{0:T(128)} %param.24) | copy-start | bytes 52
  5.8 9.1 %copy-start.4 = (bf16[2,4,576]{2,1,0:T(4,128)(2,1)S(1)}, bf16[2,4,576]{2,1,0:T(4,128)(2,1)}, u32[]{:S(2)}) copy-start(bf16[2,4,576]{2,1,0:T(4,128)(2,1)} %param.25) | copy-start | bytes 27652
  7.0 17.1 %all-to-all-start = ((bf16[32,2,1792]{2,1,0:T(2,128)(2,1)}), bf16[32,2,1792]{2,1,0:T(2,128)(2,1)S(1)}, u32[]{:S(2)}, u32[]{:S(2)}) async-start(bf16[32,2,1792]{2,1,0:T(2,128)(2,1)} %bitcast.18), calls=%async_computation | async-start | bytes 458752 | tf_op jit(solution)/shard_map/all_to_all | solution.py:106
  24.2 12.4 %all-to-all-start.2 = ((bf16[32,2,1792]{2,1,0:T(2,128)(2,1)}), bf16[32,2,1792]{2,1,0:T(2,128)(2,1)S(1)}, u32[]{:S(2)}, u32[]{:S(2)}) async-start(bf16[32,2,1792]{2,1,0:T(2,128)(2,1)} %bitcast.27), calls=%async_computation.2 | async-start | bytes 458752 | tf_op jit(solution)/shard_map/all_to_all | solution.py:106
  27.5 9.3 %collective-permute-start = (bf16[32,2,1792]{2,1,0:T(2,128)(2,1)S(1)}, bf16[32,2,1792]{2,1,0:T(2,128)(2,1)S(1)}, u32[]{:S(2)}, u32[]{:S(2)}) collective-permute-start(bf16[32,2,1792]{2,1,0:T(2,128)(2,1)S(1)} %all-to-all-done), channel_id=1, source_target_pairs={{0,1},{1,0},{2,3},{3,2},{4,5},{5,4},{6,7},{7,6},{8,9},{9,8},{10,11... | collective-permute-start | bytes 688136 | tf_op jit(solution)/shard_map/ppermute | solution.py:22
  36.6 2.5 %collective-permute-start.4 = (bf16[32,2,1792]{2,1,0:T(2,128)(2,1)S(1)}, bf16[32,2,1792]{2,1,0:T(2,128)(2,1)S(1)}, u32[]{:S(2)}, u32[]{:S(2)}) collective-permute-start(bf16[32,2,1792]{2,1,0:T(2,128)(2,1)S(1)} %all-to-all-done.2), channel_id=1, source_target_pairs={{0,1},{1,0},{2,3},{3,2},{4,5},{5,4},{6,7},{7,6},{8,9},{9,8},{10,11... | collective-permute-start | bytes 688136 | tf_op jit(solution)/shard_map/ppermute | solution.py:22
  38.4 13.7 %collective-permute-start.1 = (bf16[32,2,3584]{2,1,0:T(2,128)(2,1)}, bf16[32,2,3584]{2,1,0:T(2,128)(2,1)}, u32[]{:S(2)}, u32[]{:S(2)}) collective-permute-start(bf16[32,2,3584]{2,1,0:T(2,128)(2,1)} %broadcast_select_fusion.1), channel_id=1, source_target_pairs={{0,2},{1,3},{2,0},{3,1},{4,6},{5,7},{6,4},{7,5},{8,10},{9,11},{10,... | collective-permute-start | bytes 1376264 | tf_op jit(solution)/shard_map/ppermute | solution.py:22
  40.6 23.2 %collective-permute-start.5 = (bf16[32,2,3584]{2,1,0:T(2,128)(2,1)}, bf16[32,2,3584]{2,1,0:T(2,128)(2,1)}, u32[]{:S(2)}, u32[]{:S(2)}) collective-permute-start(bf16[32,2,3584]{2,1,0:T(2,128)(2,1)} %broadcast_select_fusion), channel_id=1, source_target_pairs={{0,2},{1,3},{2,0},{3,1},{4,6},{5,7},{6,4},{7,5},{8,10},{9,11},{10,... | collective-permute-start | bytes 1376264 | tf_op jit(solution)/shard_map/ppermute | solution.py:22
  42.3 22.7 %copy-start.1 = (bf16[64,3584]{1,0:T(8,128)(2,1)}, bf16[64,3584]{1,0:T(8,128)(2,1)S(1)}, u32[]{:S(2)}) copy-start(bf16[64,3584]{1,0:T(8,128)(2,1)S(1)} %maximum_select_fusion.3) | copy-start | bytes 1376260
  63.0 12.6 %collective-permute-start.2 = (bf16[32,2,3584]{2,1,0:T(2,128)(2,1)}, bf16[32,2,3584]{2,1,0:T(2,128)(2,1)}, u32[]{:S(2)}, u32[]{:S(2)}) collective-permute-start(bf16[32,2,3584]{2,1,0:T(2,128)(2,1)} %broadcast_select_fusion.4), channel_id=1, source_target_pairs={{0,2},{1,3},{2,0},{3,1},{4,6},{5,7},{6,4},{7,5},{8,10},{9,11},{10,... | collective-permute-start | bytes 1376264 | tf_op jit(solution)/shard_map/ppermute | solution.py:22
  74.3 10.6 %collective-permute-start.6 = (bf16[32,2,3584]{2,1,0:T(2,128)(2,1)S(1)}, bf16[32,2,3584]{2,1,0:T(2,128)(2,1)S(1)}, u32[]{:S(2)}, u32[]{:S(2)}) collective-permute-start(bf16[32,2,3584]{2,1,0:T(2,128)(2,1)S(1)} %broadcast_select_fusion.2), channel_id=1, source_target_pairs={{0,2},{1,3},{2,0},{3,1},{4,6},{5,7},{6,4},{7,5},{8,10},{9,11},{10,... | collective-permute-start | bytes 1376264 | tf_op jit(solution)/shard_map/ppermute | solution.py:22
  77.5 8.4 %collective-permute-start.3 = (bf16[32,2,1792]{2,1,0:T(2,128)(2,1)S(1)}, bf16[32,2,1792]{2,1,0:T(2,128)(2,1)S(1)}, u32[]{:S(2)}, u32[]{:S(2)}) collective-permute-start(bf16[32,2,1792]{2,1,0:T(2,128)(2,1)S(1)} %select_convert_fusion.1), channel_id=1, source_target_pairs={{0,1},{1,0},{2,3},{3,2},{4,5},{5,4},{6,7},{7,6},{8,9},{9,8},{10,11... | collective-permute-start | bytes 688136 | tf_op jit(solution)/shard_map/ppermute | solution.py:22
  85.8 17.0 %copy-start.6 = (f32[4,2]{0,1:T(2,128)S(1)}, f32[4,2]{0,1:T(2,128)}, u32[]{:S(2)}) copy-start(f32[4,2]{0,1:T(2,128)} %multiply_divide_fusion) | copy-start | bytes 100
  85.8 17.0 %copy-start.7 = (s32[4,2]{0,1:T(2,128)S(1)}, s32[4,2]{0,1:T(2,128)}, u32[]{:S(2)}) copy-start(s32[4,2]{0,1:T(2,128)} %get-tuple-element.36) | copy-start | bytes 100
  85.8 4.6 %collective-permute-start.7 = (bf16[32,2,1792]{2,1,0:T(2,128)(2,1)S(1)}, bf16[32,2,1792]{2,1,0:T(2,128)(2,1)S(1)}, u32[]{:S(2)}, u32[]{:S(2)}) collective-permute-start(bf16[32,2,1792]{2,1,0:T(2,128)(2,1)S(1)} %select_convert_fusion), channel_id=1, source_target_pairs={{0,1},{1,0},{2,3},{3,2},{4,5},{5,4},{6,7},{7,6},{8,9},{9,8},{10,11... | collective-permute-start | bytes 688136 | tf_op jit(solution)/shard_map/ppermute | solution.py:22
  86.9 16.3 %copy-start.3 = (bf16[4,64,576]{2,1,0:T(8,128)(2,1)S(1)}, bf16[4,64,576]{2,1,0:T(8,128)(2,1)}, u32[]{:S(2)}) copy-start(bf16[4,64,576]{2,1,0:T(8,128)(2,1)} %param.23) | copy-start | bytes 884740
  86.9 16.3 %copy-start.5 = (f32[4,512]{1,0:T(4,128)S(1)}, f32[4,512]{1,0:T(4,128)}, u32[]{:S(2)}) copy-start(f32[4,512]{1,0:T(4,128)} %fusion.60) | copy-start | bytes 24580
  86.9 16.3 %copy-start.9 = (s32[4]{0:T(128)S(1)}, s32[4]{0:T(128)}, u32[]{:S(2)}) copy-start(s32[4]{0:T(128)} %param.24) | copy-start | bytes 52
  86.9 16.3 %copy-start.10 = (f32[4,64]{1,0:T(4,128)S(1)}, f32[4,64]{1,0:T(4,128)}, u32[]{:S(2)}) copy-start(f32[4,64]{1,0:T(4,128)} %get-tuple-element.16) | copy-start | bytes 3076
  86.9 16.3 %copy-start.11 = (f32[4,64]{1,0:T(4,128)S(1)}, f32[4,64]{1,0:T(4,128)}, u32[]{:S(2)}) copy-start(f32[4,64]{1,0:T(4,128)} %get-tuple-element.17) | copy-start | bytes 3076
  86.9 13.3 %all-to-all-start.1 = ((bf16[32,2,1792]{2,1,0:T(2,128)(2,1)}), bf16[32,2,1792]{2,1,0:T(2,128)(2,1)S(1)}, u32[]{:S(2)}, u32[]{:S(2)}) async-start(bf16[32,2,1792]{2,1,0:T(2,128)(2,1)} %add_convert_fusion.1), calls=%async_computation.1 | async-start | bytes 458752 | tf_op jit(solution)/shard_map/all_to_all | solution.py:126
  100.2 12.4 %all-to-all-start.3 = ((bf16[32,2,1792]{2,1,0:T(2,128)(2,1)}), bf16[32,2,1792]{2,1,0:T(2,128)(2,1)S(1)}, u32[]{:S(2)}, u32[]{:S(2)}) async-start(bf16[32,2,1792]{2,1,0:T(2,128)(2,1)} %add_convert_fusion), calls=%async_computation.3 | async-start | bytes 458752 | tf_op jit(solution)/shard_map/all_to_all | solution.py:126
where the time goes:
time: 115 us; the launch traced here: 114 us
  waiting for transfers between devices  46.3 us (40%)
  starting transfers between devices  20.5 us (18%)
  matrix products  19.8 us (17%)
  other arithmetic  18 us (16%)
  local copies, waits for them, and re-layouts  8.27 us (7%)
    ppermute x8, waiting for transfers between devices, swapped(): return lax.ppermute(value, axis, pairs)  17.1 us
    all_to_all x2, waiting for transfers between devices, mixture(): lax.all_to_all(summed.astype(jnp.bfloat16), 'ep', split_axis=0, concat_ax...  16.9 us
    all_to_all x2, waiting for transfers between devices, mixture(): lax.all_to_all(outgoing, 'ep', split_axis=0, concat_axis=0, tiled=True)  12.3 us
    dot_general x2, matrix products, expert_rows(): jnp.dot(inner, down_w, preferred_element_type=jnp.float32)  11.2 us
    all_to_all x2, starting transfers between devices, mixture(): lax.all_to_all(outgoing, 'ep', split_axis=0, concat_axis=0, tiled=True)  10.1 us
    all_to_all x2, starting transfers between devices, mixture(): lax.all_to_all(summed.astype(jnp.bfloat16), 'ep', split_axis=0, concat_ax...  6.04 us
    dot_general x2, matrix products, expert_rows(): gate = jnp.dot(flat_rows, gate_w, preferred_element_type=jnp.float32)  5.37 us
    ppermute x8, starting transfers between devices, swapped(): return lax.ppermute(value, axis, pairs)  4.44 us
  transfers between devices with their start and end apart: 12, of which 6 were waited for; matrix products, arithmetic and copies ran while one was open for 34% of the time, Pallas kernels for 0%

commit v1 on v0

v1 whole, which is shorter than its diff:
```python
import jax
import jax.numpy as jnp
from jax import lax
from jax.experimental import pallas as pl
from jax.experimental.pallas import tpu as pltpu
from jax.sharding import PartitionSpec as P

KV = 512
SPAN = 4

softmax_scale = 192.0 ** (-0.5)
routed_scale = 2.5
norm_eps = 1e-06
masked_score = -1e30


def flipped(value, low_core, high_core):
    pairs = [(e, e ^ (high_core if e % 2 else low_core)) for e in range(lax.axis_size("ep"))]
    return lax.ppermute(value, "ep", pairs)


def attend(queries, cache, lengths, fresh):
    old_scores = (
        jnp.einsum("nhl,ncl->nhc", queries, cache, preferred_element_type=jnp.float32)
        * softmax_scale
    )
    new_scores = (
        jnp.einsum("nhl,nml->nhm", queries, fresh, preferred_element_type=jnp.float32)
        * softmax_scale
    )
    positions = lax.broadcasted_iota(jnp.int32, old_scores.shape, 2)
    valid = positions < lengths[:, None, None]
    old_scores = jnp.where(valid, old_scores, masked_score)
    highest = jnp.maximum(jnp.max(old_scores, axis=2), jnp.max(new_scores, axis=2))[:, :, None]
    old_terms = jnp.where(valid, jnp.exp(old_scores - highest), 0.0)
    new_terms = jnp.exp(new_scores - highest)
    total = jnp.sum(old_terms, axis=2, keepdims=True) + jnp.sum(new_terms, axis=2, keepdims=True)
    old_probs = (old_terms / total).astype(jnp.bfloat16)
    new_probs = (new_terms / total).astype(jnp.bfloat16)
    output = jnp.einsum(
        "nhc,ncv->nhv", old_probs, cache[:, :, :KV], preferred_element_type=jnp.float32
    )
    output = output + jnp.einsum(
        "nhm,nmv->nhv", new_probs, fresh[:, :, :KV], preferred_element_type=jnp.float32
    )
    return output.astype(jnp.bfloat16)


def expert_kernel(*refs):
    rows_refs = refs[:-9]
    gate_ref, up_ref, down_ref, out_ref, gate_v, up_v, down_v, rows_v, sems = refs[-9:]
    depth, hidden_units = gate_ref.shape
    parts = gate_v.shape[0]
    step = depth // parts
    copies = []
    for i in range(parts):
        ds = pl.ds(i * step, step)
        copies.append(
            (
                pltpu.make_async_copy(gate_ref.at[ds, :], gate_v.at[i], sems.at[0, i]),
                pltpu.make_async_copy(up_ref.at[ds, :], up_v.at[i], sems.at[1, i]),
            )
        )
    downs = [
        pltpu.make_async_copy(down_ref.at[:, pl.ds(i * step, step)], down_v.at[i], sems.at[2, i])
        for i in range(parts)
    ]
    for pair in copies:
        pair[0].start()
        pair[1].start()
    for copy in downs:
        copy.start()
    at = 0
    for ref in rows_refs:
        rows_v[pl.ds(at, ref.shape[0]), :] = ref[...]
        at += ref.shape[0]
    gate = jnp.zeros((at, hidden_units), jnp.float32)
    upper = jnp.zeros((at, hidden_units), jnp.float32)
    for i in range(parts):
        copies[i][0].wait()
        copies[i][1].wait()
        x = rows_v[:, pl.ds(i * step, step)]
        gate += jnp.dot(x, gate_v[i], preferred_element_type=jnp.float32)
        upper += jnp.dot(x, up_v[i], preferred_element_type=jnp.float32)
    inner = (gate / (1.0 + jnp.exp(-gate)) * upper).astype(jnp.bfloat16)
    for i in range(parts):
        downs[i].wait()
        out_ref[:, pl.ds(i * step, step)] = jnp.dot(
            inner, down_v[i], preferred_element_type=jnp.float32
        ).astype(jnp.bfloat16)


def experts(row_parts, gate_w, up_w, down_w):
    rows = sum(part.shape[0] for part in row_parts)
    depth, hidden_units = gate_w.shape
    parts = 7
    step = depth // parts
    vmem = pl.BlockSpec(memory_space=pltpu.VMEM)
    hbm = pl.BlockSpec(memory_space=pl.ANY)
    return pl.pallas_call(
        expert_kernel,
        out_shape=jax.ShapeDtypeStruct((rows, depth), jnp.bfloat16),
        in_specs=[vmem] * len(row_parts) + [hbm] * 3,
        out_specs=vmem,
        scratch_shapes=[
            pltpu.VMEM((parts, step, hidden_units), jnp.bfloat16),
            pltpu.VMEM((parts, step, hidden_units), jnp.bfloat16),
            pltpu.VMEM((parts, hidden_units, step), jnp.bfloat16),
            pltpu.VMEM((rows, depth), jnp.bfloat16),
            pltpu.SemaphoreType.DMA((3, parts)),
        ],
        compiler_params=pltpu.CompilerParams(vmem_limit_bytes=(16 << 20) + rows * depth * 12),
        cost_estimate=pl.CostEstimate(
            flops=6 * rows * depth * hidden_units,
            bytes_accessed=6 * depth * hidden_units + 4 * rows * depth,
            transcendentals=rows * hidden_units,
        ),
        name="experts",
    )(*row_parts, gate_w, up_w, down_w)


def routing(chosen, scores, copy_table, targets, slots):
    ids, replica = chosen[0], chosen[1]
    expert_count = scores.shape[-1]
    sources, steps, rows, top = ids.shape
    chooser = ids[..., None] == lax.broadcasted_iota(jnp.int32, (*ids.shape, expert_count), 4)
    picked = jnp.sum(jnp.where(chooser, scores[:, :, :, None, :], 0.0), axis=4)
    weights = routed_scale * picked / jnp.sum(picked, axis=3, keepdims=True)
    table = jnp.where(replica[..., None] == 0, copy_table[:, 0], copy_table[:, 1])
    copies = jnp.sum(jnp.where(chooser, table, 0), axis=4)
    flat = copies.reshape(sources, steps, rows * top)
    same = flat[..., :, None] == flat[..., None, :]
    earlier = lax.broadcasted_iota(jnp.int32, same.shape, 3) < lax.broadcasted_iota(
        jnp.int32, same.shape, 2
    )
    slot = jnp.sum((same & earlier).astype(jnp.int32), axis=3).reshape(copies.shape)
    shape = (targets.shape[0], slots, sources, steps, rows, top)
    hit = (copies == targets[:, None, None, None, None, None]) & (
        slot == lax.broadcasted_iota(jnp.int32, shape, 1)
    )
    place = jnp.sum(hit.astype(jnp.float32), axis=5)
    weigh = jnp.sum(jnp.where(hit, weights, 0.0), axis=5)
    blocks = sources * steps
    own = jnp.eye(blocks, dtype=jnp.float32)

    def spread(values):
        values = values.reshape(targets.shape[0], slots, blocks, rows)
        wide = values.transpose(0, 2, 1, 3)[:, :, :, None, :] * own[None, :, None, :, None]
        return wide.reshape(targets.shape[0] * blocks * slots, blocks * rows)

    return spread(place), spread(weigh)


def mixture(hidden, norm_gain, router, expert_ids, replica, copy_table, gate_w, up_w, down_w):
    axis_count = lax.axis_size("ep")
    groups = axis_count // SPAN
    messages = groups // 2
    steps, row_count, depth = hidden.shape
    top_count = expert_ids.shape[2]
    slots = max(2, 2 * row_count * top_count // groups)
    index = lax.axis_index("ep")
    core = index % 2
    group = index // SPAN
    deltas = [(groups - 1 - 2 * m, groups - 2 - 2 * m) for m in range(messages)]

    raw = hidden.reshape(steps * row_count, depth)
    chosen = jnp.stack([expert_ids, replica])
    other_raw = flipped(raw, 1, 1)
    other_chosen = flipped(chosen, 1, 1)
    both_chosen = jnp.stack([chosen, other_chosen], axis=1)
    hidden_f = jnp.concatenate([raw, other_raw], axis=0).astype(jnp.float32)
    mean_square = jnp.mean(hidden_f * hidden_f, axis=1, keepdims=True)
    normed = (hidden_f * lax.rsqrt(mean_square + norm_eps) * norm_gain).astype(jnp.bfloat16)
    scores = jax.nn.sigmoid(jnp.dot(normed, router, preferred_element_type=jnp.float32))
    targets = group ^ jnp.where(
        core == 0, jnp.array([d[0] for d in deltas]), jnp.array([d[1] for d in deltas])
    )
    place, weigh = routing(
        both_chosen, scores.reshape(2, steps, row_count, -1), copy_table, targets, slots
    )
    packed = jnp.dot(
        place.astype(jnp.bfloat16), normed, preferred_element_type=jnp.float32
    ).astype(jnp.bfloat16)
    size = packed.shape[0] // messages

    def rounds(values):
        parts = [
            flipped(values[m * size : (m + 1) * size], SPAN * low, SPAN * high)
            for m, (low, high) in enumerate(deltas)
        ]
        return jnp.concatenate(parts, axis=0)

    near = rounds(packed)
    far = flipped(near, 2, 2)
    near_other = flipped(near, 1, 1)
    far_other = flipped(far, 1, 1)
    lane = near.shape[0]
    partial = experts([near, far, near_other, far_other], gate_w, up_w, down_w)
    summed = partial[: 2 * lane].astype(jnp.float32) + flipped(partial[2 * lane :], 1, 1).astype(
        jnp.float32
    )
    total = summed[:lane] + flipped(summed[lane:].astype(jnp.bfloat16), 2, 2).astype(jnp.float32)
    returned = rounds(total.astype(jnp.bfloat16))
    result = jnp.dot(
        weigh.T,
        returned.astype(jnp.float32),
        precision=lax.Precision.HIGHEST,
        preferred_element_type=jnp.float32,
    )
    half = steps * row_count
    result = result[:half] + flipped(result[half:].astype(jnp.bfloat16), 1, 1).astype(jnp.float32)
    return result.astype(jnp.bfloat16).reshape(steps, row_count, depth)


def per_device(
    hidden,
    norm_gain,
    router,
    expert_ids,
    replica,
    copy_table,
    gate_w,
    up_w,
    down_w,
    query,
    cache,
    lengths,
    fresh_kv,
):
    moe_out = mixture(
        hidden, norm_gain, router, expert_ids, replica, copy_table, gate_w, up_w, down_w
    )
    attended = []
    for decode_step in range(2):
        fresh = jnp.moveaxis(fresh_kv[: decode_step + 1], 0, 1)
        attended.append(attend(query[decode_step], cache, lengths, fresh))
    return (jnp.stack(attended), moe_out)


def solution(mesh):
    return jax.shard_map(
        per_device,
        mesh=mesh,
        in_specs=(
            P(None, ("groups", "ep"), None),
            P(),
            P(),
            P(None, ("groups", "ep"), None),
            P(None, ("groups", "ep"), None),
            P(),
            P(None, "ep"),
            P(None, "ep"),
            P("ep", None),
            P(None, ("groups", "ep"), None, None),
            P(("groups", "ep"), None, None),
            P(("groups", "ep")),
            P(None, ("groups", "ep"), None),
        ),
        out_specs=(P(None, ("groups", "ep"), None, None), P(None, ("groups", "ep"), None)),
        check_vma=False,
    )
```

time: 115 us -> 77.1 us (0.67)
  matrix products: 19.8 us -> 4.48 us
  other arithmetic: 18 us -> 3.84 us
  waiting for transfers between devices: 46.3 us -> 33 us
  Pallas kernels: 0 us -> 4.23 us
  starting transfers between devices: 20.5 us -> 22.8 us
    all_to_all x4 -> x0, waiting for transfers between devices: 29.2 us -> none  [the longest x2 16.9 us: mixture(): lax.all_to_all(summed.astype(jnp.bfloat16), 'ep', split_axis=0, concat_ax...]
    ppermute x8 -> x16, starting transfers between devices: 4.44 us -> 22.8 us  [flipped(): return lax.ppermute(value, 'ep', pairs)]
    all_to_all x4 -> x0, starting transfers between devices: 16.1 us -> none  [the longest x2 10.1 us: mixture(): lax.all_to_all(outgoing, 'ep', split_axis=0, concat_axis=0, tiled=True)]
    dot_general x8 -> x2, matrix products: 17.5 us -> 1.46 us  [the longest x1 1.07 us: mixture(): jnp.dot(place.astype(jnp.bfloat16), normed, preferred_element_type=jnp.fl...]
    ppermute x8 -> x16, waiting for transfers between devices: 17.1 us -> 33 us  [flipped(): return lax.ppermute(value, 'ep', pairs)]
    select_n x9 -> x0, other arithmetic: 5.52 us -> none  [the longest x4 3.18 us: mixture(): jnp.where(is_lower, jnp.concatenate([gathered_piece, partner], axis=2), j...]
    pallas_call x0 -> x1, Pallas kernels: none -> 4.23 us  [experts(): pl.pallas_call(expert_kernel, out_shape=jax.ShapeDtypeStruct((rows, depth...]
    unnamed x29 -> x20, local copies, waits for them, and re-layouts: 0.13 us -> 4.15 us
  transfers between devices with their start and end apart: 12 -> 16, of which waited for: 6 -> 8; matrix products, arithmetic and copies ran while one was open for 34% -> 8% of each run, Pallas kernels for 0% -> 0%
where the time goes in v1:
time: 77.1 us; the launch traced here: 76.8 us
  waiting for transfers between devices  33 us (43%)
  starting transfers between devices  22.8 us (30%)
  local copies, waits for them, and re-layouts  7.44 us (10%)
  matrix products  4.48 us (6%)
  Pallas kernels  4.23 us (5%)
  other arithmetic  3.84 us (5%)
  between operations  1 us (1%)
    ppermute x16, waiting for transfers between devices, flipped(): return lax.ppermute(value, 'ep', pairs)  33 us
    ppermute x16, starting transfers between devices, flipped(): return lax.ppermute(value, 'ep', pairs)  22.8 us
    pallas_call x1, Pallas kernels, experts(): pl.pallas_call(expert_kernel, out_shape=jax.ShapeDtypeStruct((rows, depth...  4.23 us
    unnamed x20, local copies, waits for them, and re-layouts  4.15 us
  transfers between devices with their start and end apart: 16, of which 8 were waited for; matrix products, arithmetic and copies ran while one was open for 8% of the time, Pallas kernels for 0%

profile of v1, /device:TPU:0, one launch (start us, length us, event | category | flops | bytes accessed | tf_op | source)
XLA Modules:
  0.0 76.8 jit_solution(17119041167899002315)
XLA Ops:
  0.6 0.0 copy-start
  0.7 0.7 pad_add_fusion.1
  1.4 0.5 collective-permute-start
  1.8 0.9 %reshape.111 = bf16[8,7168]{1,0:T(8,128)(2,1)S(1)} reshape(bf16[2,4,7168]{2,1,0:T(4,128)(2,1)} %param.15) | data formatting | bytes 229376 | tf_op jit(solution)/shard_map/reshape | solution.py:166
  2.8 0.1 collective-permute-start.1
  2.9 0.8 slice_bitcast_fusion.4
  3.7 0.7 fusion.56
  4.3 0.0 collective-permute-done
  4.4 0.3 select_reduce_fusion.3
  4.7 0.1 copy.38
  4.8 0.1 eq.91
  4.9 0.2 convert_reduce_fusion.1
  5.1 0.1 eq.95
  5.2 0.1 copy.39
  5.3 0.1 broadcast_compare_fusion
  5.4 0.0 collective-permute-done.1
  5.4 0.2 fusion.10
  5.6 0.0 copy-start.7
  5.6 1.1 %fusion.8 = f32[16,6]{0,1:T(8,128)S(1)} fusion(bf16[7168,6]{0,1:T(8,128)(2,1)S(1)} %copy-done, f32[7168]{0:T(1024)} %param.16, f32[16]{0:T(128)S(1)} %add_rsqrt_fusion, bf16[8,7168]{1,0:T(8,128)(2,1)S(1)} %collective-permute-done.1, bf16[8,7168]{1,0:T(8,128)(2,1)S(1)} %reshape.111), kind=kOutput, calls=%fused_computation.15 | convolution fusion | flops 2179360 | bytes 344512 | tf_op jit(solution)/shard_map/dot_general | solution.py:174
  6.7 0.1 copy.40
  6.7 0.2 select_reduce_fusion.1
  7.1 0.1 multiply_convert_fusion
  7.2 0.1 convert_element_type.82
  7.2 1.1 %convolution_convert_fusion = bf16[32,7168]{1,0:T(8,128)(2,1)S(1)} fusion(bf16[32,16]{1,0:T(8,128)(2,1)S(1)} %convert_element_type.82, f32[7168]{0:T(1024)} %param.16, f32[16]{0:T(128)S(1)} %add_rsqrt_fusion, bf16[8,7168]{1,0:T(8,128)(2,1)S(1)} %collective-permute-done.1, bf16[8,7168]{1,0:T(8,128)(2,1)S(1)} %reshape.111), kind=kOutput, calls=%fused_computation | convolution fusion | flops 8372224 | bytes 717888 | tf_op jit(solution)/shard_map/dot_general | solution.py:181
  8.3 0.0 copy-start.1
  8.4 6.1 %collective-permute-start.2 = (bf16[8,7168]{1,0:T(8,128)(2,1)S(1)}, bf16[8,7168]{1,0:T(8,128)(2,1)S(1)}, u32[]{:S(2)}, u32[]{:S(2)}) collective-permute-start(bf16[8,7168]{1,0:T(8,128)(2,1)S(1)} %get-tuple-element.15), channel_id=1, source_target_pairs={{0,28},{1,25},{2,30},{3,27},{4,24},{5,29},{6,26},{7,31},{8,20},{9,... | collective-permute-start | bytes 344072 | tf_op jit(solution)/shard_map/ppermute | solution.py:19
  14.5 0.1 collective-permute-start.3
  14.5 1.7 %collective-permute-start.4 = (bf16[8,7168]{1,0:T(8,128)(2,1)S(1)}, bf16[8,7168]{1,0:T(8,128)(2,1)S(1)}, u32[]{:S(2)}, u32[]{:S(2)}) collective-permute-start(bf16[8,7168]{1,0:T(8,128)(2,1)S(1)} %get-tuple-element.13), channel_id=1, source_target_pairs={{0,12},{1,9},{2,14},{3,11},{4,8},{5,13},{6,10},{7,15},{8,4},{9,1},... | collective-permute-start | bytes 344072 | tf_op jit(solution)/shard_map/ppermute | solution.py:19
  16.2 2.3 %collective-permute-start.5 = (bf16[8,7168]{1,0:T(8,128)(2,1)S(1)}, bf16[8,7168]{1,0:T(8,128)(2,1)S(1)}, u32[]{:S(2)}, u32[]{:S(2)}) collective-permute-start(bf16[8,7168]{1,0:T(8,128)(2,1)S(1)} %get-tuple-element.12), channel_id=1, source_target_pairs={{0,4},{1,1},{2,6},{3,3},{4,0},{5,5},{6,2},{7,7},{8,12},{9,9},{10,1... | collective-permute-start | bytes 344072 | tf_op jit(solution)/shard_map/ppermute | solution.py:19
  18.5 0.0 collective-permute-done.2
  18.5 5.8 %collective-permute-done.3 = bf16[8,7168]{1,0:T(8,128)(2,1)S(1)} collective-permute-done((bf16[8,7168]{1,0:T(8,128)(2,1)S(1)}, bf16[8,7168]{1,0:T(8,128)(2,1)S(1)}, u32[]{:S(2)}, u32[]{:S(2)}) %collective-permute-start.3) | collective-permute-done | bytes 114720 | tf_op jit(solution)/shard_map/ppermute | solution.py:19
  24.4 1.5 %collective-permute-start.6 = (bf16[32,7168]{1,0:T(8,128)(2,1)S(1)}, bf16[32,7168]{1,0:T(8,128)(2,1)S(1)}, u32[]{:S(2)}, u32[]{:S(2)}) collective-permute-start(bf16[32,7168]{1,0:T(8,128)(2,1)S(1)} %constant_dynamic-update-slice_fusion.refs_0_), channel_id=1, source_target_pairs={{0,2},{1,3},{2,0},{3,1},{4,6},{5,7},{6,4},{7,5},{8,10},{9,11},{10,... | collective-permute-start | bytes 1376264 | tf_op jit(solution)/shard_map/ppermute | solution.py:19
  25.9 0.2 fusion.68
  26.2 0.3 fusion.67
  26.5 0.1 collective-permute-start.7
  26.6 8.2 %collective-permute-done.6.refs_1_ = bf16[32,7168]{1,0:T(8,128)(2,1)S(1)} collective-permute-done((bf16[32,7168]{1,0:T(8,128)(2,1)S(1)}, bf16[32,7168]{1,0:T(8,128)(2,1)S(1)}, u32[]{:S(2)}, u32[]{:S(2)}) %collective-permute-start.6) | collective-permute-done | bytes 458784 | tf_op jit(solution)/shard_map/ppermute | solution.py:19
  34.8 0.3 fusion.66
  35.0 1.5 %collective-permute-done.8.refs_3_ = bf16[32,7168]{1,0:T(8,128)(2,1)S(1)} collective-permute-done((bf16[32,7168]{1,0:T(8,128)(2,1)S(1)}, bf16[32,7168]{1,0:T(8,128)(2,1)S(1)}, u32[]{:S(2)}, u32[]{:S(2)}) %collective-permute-start.8) | collective-permute-done | bytes 458784 | tf_op jit(solution)/shard_map/ppermute | solution.py:19
  36.6 2.0 %copy-done.2 = bf16[7168,256]{1,0:T(8,128)(2,1)S(1)} copy-done((bf16[7168,256]{1,0:T(8,128)(2,1)S(1)}, bf16[7168,256]{1,0:T(8,128)(2,1)}, u32[]{:S(2)}) %copy-start.2) | copy-done | bytes 3670040
  38.6 2.0 %copy-done.3 = bf16[256,7168]{1,0:T(8,128)(2,1)S(1)} copy-done((bf16[256,7168]{1,0:T(8,128)(2,1)S(1)}, bf16[256,7168]{1,0:T(8,128)(2,1)}, u32[]{:S(2)}) %copy-start.3) | copy-done | bytes 3670040
  40.6 4.2 %experts.1 = bf16[128,7168]{1,0:T(8,128)(2,1)S(1)} custom-call(bf16[32,7168]{1,0:T(8,128)(2,1)S(1)} %constant_dynamic-update-slice_fusion.refs_0_, bf16[32,7168]{1,0:T(8,128)(2,1)S(1)} %collective-permute-done.6.refs_1_, bf16[32,7168]{1,0:T(8,128)(2,1)S(1)} %collective-permute-done.7.refs_2_, bf16[32,7168]{1,0:T(8,128)(2,1)S(1)} %collective-permute-done.8.refs_3_, ...), custom_call_target="tpu_custom_call" | custom-call | flops 1409286144 | bytes 14680064 | tf_op jit(solution)/shard_map/experts/pallas_call | solution.py:100
  44.9 0.1 slice.108
  45.0 0.2 collective-permute-start.9
  45.2 0.2 fusion.23
  45.4 0.1 fusion.34
  45.5 2.0 %collective-permute-done.9 = bf16[64,7168]{1,0:T(8,128)(2,1)S(1)} collective-permute-done((bf16[64,7168]{1,0:T(8,128)(2,1)S(1)}, bf16[64,7168]{1,0:T(8,128)(2,1)S(1)}, u32[]{:S(2)}, u32[]{:S(2)}) %collective-permute-start.9) | collective-permute-done | bytes 917536 | tf_op jit(solution)/shard_map/ppermute | solution.py:19
  47.5 0.2 convert_add_fusion
  47.7 1.5 %collective-permute-start.10 = (bf16[32,7168]{1,0:T(8,128)(2,1)S(1)}, bf16[32,7168]{1,0:T(8,128)(2,1)S(1)}, u32[]{:S(2)}, u32[]{:S(2)}) collective-permute-start(bf16[32,7168]{1,0:T(8,128)(2,1)S(1)} %slice.163), channel_id=1, source_target_pairs={{0,2},{1,3},{2,0},{3,1},{4,6},{5,7},{6,4},{7,5},{8,10},{9,11},{10,... | collective-permute-start | bytes 1376264 | tf_op jit(solution)/shard_map/ppermute | solution.py:19
  49.3 0.3 fusion.2
  49.6 0.3 fusion.30
  50.0 10.4 %collective-permute-done.10 = bf16[32,7168]{1,0:T(8,128)(2,1)S(1)} collective-permute-done((bf16[32,7168]{1,0:T(8,128)(2,1)S(1)}, bf16[32,7168]{1,0:T(8,128)(2,1)S(1)}, u32[]{:S(2)}, u32[]{:S(2)}) %collective-permute-start.10) | collective-permute-done | bytes 458784 | tf_op jit(solution)/shard_map/ppermute | solution.py:19
  60.4 0.1 fusion.9
  60.5 3.6 %collective-permute-start.11 = (bf16[8,7168]{1,0:T(8,128)(2,1)S(1)}, bf16[8,7168]{1,0:T(8,128)(2,1)S(1)}, u32[]{:S(2)}, u32[]{:S(2)}) collective-permute-start(bf16[8,7168]{1,0:T(8,128)(2,1)S(1)} %get-tuple-element.8), channel_id=1, source_target_pairs={{0,28},{1,25},{2,30},{3,27},{4,24},{5,29},{6,26},{7,31},{8,20},{9,... | collective-permute-start | bytes 344072 | tf_op jit(solution)/shard_map/ppermute | solution.py:19
  64.1 3.1 %collective-permute-start.13 = (bf16[8,7168]{1,0:T(8,128)(2,1)S(1)}, bf16[8,7168]{1,0:T(8,128)(2,1)S(1)}, u32[]{:S(2)}, u32[]{:S(2)}) collective-permute-start(bf16[8,7168]{1,0:T(8,128)(2,1)S(1)} %get-tuple-element.10), channel_id=1, source_target_pairs={{0,12},{1,9},{2,14},{3,11},{4,8},{5,13},{6,10},{7,15},{8,4},{9,1},... | collective-permute-start | bytes 344072 | tf_op jit(solution)/shard_map/ppermute | solution.py:19
  67.2 1.9 %collective-permute-start.14 = (bf16[8,7168]{1,0:T(8,128)(2,1)S(1)}, bf16[8,7168]{1,0:T(8,128)(2,1)S(1)}, u32[]{:S(2)}, u32[]{:S(2)}) collective-permute-start(bf16[8,7168]{1,0:T(8,128)(2,1)S(1)} %get-tuple-element.9), channel_id=1, source_target_pairs={{0,4},{1,1},{2,6},{3,3},{4,0},{5,5},{6,2},{7,7},{8,12},{9,9},{10,1... | collective-permute-start | bytes 344072 | tf_op jit(solution)/shard_map/ppermute | solution.py:19
  69.2 0.3 fusion.3
  69.5 0.1 mul.92
  69.6 3.7 %collective-permute-done.12 = bf16[8,7168]{1,0:T(8,128)(2,1)S(1)} collective-permute-done((bf16[8,7168]{1,0:T(8,128)(2,1)S(1)}, bf16[8,7168]{1,0:T(8,128)(2,1)S(1)}, u32[]{:S(2)}, u32[]{:S(2)}) %collective-permute-start.12) | collective-permute-done | bytes 114720 | tf_op jit(solution)/shard_map/ppermute | solution.py:19
  73.4 0.9 %collective-permute-done.14 = bf16[8,7168]{1,0:T(8,128)(2,1)S(1)} collective-permute-done((bf16[8,7168]{1,0:T(8,128)(2,1)S(1)}, bf16[8,7168]{1,0:T(8,128)(2,1)S(1)}, u32[]{:S(2)}, u32[]{:S(2)}) %collective-permute-start.14) | collective-permute-done | bytes 114720 | tf_op jit(solution)/shard_map/ppermute | solution.py:19
  74.2 0.4 fusion.13
  74.7 0.1 collective-permute-start.15
  74.7 0.8 %pad_maximum_fusion = bf16[2,4,64,512]{3,2,1,0:T(8,128)(2,1)} fusion(bf16[1,4,64,512]{3,2,1,0:T(8,128)(2,1)S(1)} %fusion.3, bf16[1,4,64,512]{3,2,1,0:T(8,128)(2,1)S(1)} %fusion.2), kind=kLoop, calls=%fused_computation.22 | loop fusion | flops 262144 | bytes 1048576 | tf_op jit(solution)/shard_map/stack | solution.py:237
  75.6 0.5 collective-permute-done.15
  76.1 0.7 reshape.114
  (45 shorter events, 0.4 us)
Async XLA Ops:
  0.6 4.9 %copy-start = (bf16[7168,6]{0,1:T(8,128)(2,1)S(1)}, bf16[7168,6]{0,1:T(8,128)(2,1)}, u32[]{:S(2)}) copy-start(bf16[7168,6]{0,1:T(8,128)(2,1)} %param.17) | copy-start | bytes 258052
  0.6 13.8 %copy-start.5 = (bf16[2,4,576]{2,1,0:T(4,128)(2,1)S(1)}, bf16[2,4,576]{2,1,0:T(4,128)(2,1)}, u32[]{:S(2)}) copy-start(bf16[2,4,576]{2,1,0:T(4,128)(2,1)} %param.27) | copy-start | bytes 27652
  1.4 2.9 %collective-permute-start = (s32[2,2,4,2]{2,3,1,0:T(2,128)S(1)}, s32[2,2,4,2]{2,3,1,0:T(2,128)S(1)}, u32[]{:S(2)}, u32[]{:S(2)}) collective-permute-start(s32[2,2,4,2]{2,3,1,0:T(2,128)S(1)} %get-tuple-element.20), channel_id=1, source_target_pairs={{0,1},{1,0},{2,3},{3,2},{4,5},{5,4},{6,7},{7,6},{8,9},{9,8},{10,11... | collective-permute-start | bytes 392 | tf_op jit(solution)/shard_map/ppermute | solution.py:19
  2.8 2.6 %collective-permute-start.1 = (bf16[8,7168]{1,0:T(8,128)(2,1)S(1)}, bf16[8,7168]{1,0:T(8,128)(2,1)S(1)}, u32[]{:S(2)}, u32[]{:S(2)}) collective-permute-start(bf16[8,7168]{1,0:T(8,128)(2,1)S(1)} %reshape.111), channel_id=1, source_target_pairs={{0,1},{1,0},{2,3},{3,2},{4,5},{5,4},{6,7},{7,6},{8,9},{9,8},{10,11... | collective-permute-start | bytes 344072 | tf_op jit(solution)/shard_map/ppermute | solution.py:19
  5.6 20.4 %copy-start.7 = (bf16[2,4,64,576]{3,2,1,0:T(8,128)(2,1)S(1)}, bf16[2,4,64,576]{3,2,1,0:T(8,128)(2,1)}, u32[]{:S(2)}) copy-start(bf16[2,4,64,576]{3,2,1,0:T(8,128)(2,1)} %param.24) | copy-start | bytes 1769476
  6.6 19.5 %copy-start.4 = (bf16[4,64,576]{2,1,0:T(8,128)(2,1)S(1)}, bf16[4,64,576]{2,1,0:T(8,128)(2,1)}, u32[]{:S(2)}) copy-start(bf16[4,64,576]{2,1,0:T(8,128)(2,1)} %param.25) | copy-start | bytes 884740
  6.7 19.5 %copy-start.6 = (s32[4]{0:T(128)S(1)}, s32[4]{0:T(128)}, u32[]{:S(2)}) copy-start(s32[4]{0:T(128)} %param.26) | copy-start | bytes 52
  8.3 28.2 %copy-start.1 = (bf16[7168,256]{1,0:T(8,128)(2,1)S(1)}, bf16[7168,256]{1,0:T(8,128)(2,1)}, u32[]{:S(2)}) copy-start(bf16[7168,256]{1,0:T(8,128)(2,1)} %refs_4_.1) | copy-start | bytes 11010052
  8.4 10.1 %collective-permute-start.2 = (bf16[8,7168]{1,0:T(8,128)(2,1)S(1)}, bf16[8,7168]{1,0:T(8,128)(2,1)S(1)}, u32[]{:S(2)}, u32[]{:S(2)}) collective-permute-start(bf16[8,7168]{1,0:T(8,128)(2,1)S(1)} %get-tuple-element.15), channel_id=1, source_target_pairs={{0,28},{1,25},{2,30},{3,27},{4,24},{5,29},{6,26},{7,31},{8,20},{9,... | collective-permute-start | bytes 344072 | tf_op jit(solution)/shard_map/ppermute | solution.py:19
  14.5 9.9 %collective-permute-start.3 = (bf16[8,7168]{1,0:T(8,128)(2,1)S(1)}, bf16[8,7168]{1,0:T(8,128)(2,1)S(1)}, u32[]{:S(2)}, u32[]{:S(2)}) collective-permute-start(bf16[8,7168]{1,0:T(8,128)(2,1)S(1)} %get-tuple-element.14), channel_id=1, source_target_pairs={{0,20},{1,17},{2,22},{3,19},{4,16},{5,21},{6,18},{7,23},{8,28},{9,... | collective-permute-start | bytes 344072 | tf_op jit(solution)/shard_map/ppermute | solution.py:19
  14.5 9.8 %collective-permute-start.4 = (bf16[8,7168]{1,0:T(8,128)(2,1)S(1)}, bf16[8,7168]{1,0:T(8,128)(2,1)S(1)}, u32[]{:S(2)}, u32[]{:S(2)}) collective-permute-start(bf16[8,7168]{1,0:T(8,128)(2,1)S(1)} %get-tuple-element.13), channel_id=1, source_target_pairs={{0,12},{1,9},{2,14},{3,11},{4,8},{5,13},{6,10},{7,15},{8,4},{9,1},... | collective-permute-start | bytes 344072 | tf_op jit(solution)/shard_map/ppermute | solution.py:19
  16.2 8.2 %collective-permute-start.5 = (bf16[8,7168]{1,0:T(8,128)(2,1)S(1)}, bf16[8,7168]{1,0:T(8,128)(2,1)S(1)}, u32[]{:S(2)}, u32[]{:S(2)}) collective-permute-start(bf16[8,7168]{1,0:T(8,128)(2,1)S(1)} %get-tuple-element.12), channel_id=1, source_target_pairs={{0,4},{1,1},{2,6},{3,3},{4,0},{5,5},{6,2},{7,7},{8,12},{9,9},{10,1... | collective-permute-start | bytes 344072 | tf_op jit(solution)/shard_map/ppermute | solution.py:19
  24.4 10.4 %collective-permute-start.6 = (bf16[32,7168]{1,0:T(8,128)(2,1)S(1)}, bf16[32,7168]{1,0:T(8,128)(2,1)S(1)}, u32[]{:S(2)}, u32[]{:S(2)}) collective-permute-start(bf16[32,7168]{1,0:T(8,128)(2,1)S(1)} %constant_dynamic-update-slice_fusion.refs_0_), channel_id=1, source_target_pairs={{0,2},{1,3},{2,0},{3,1},{4,6},{5,7},{6,4},{7,5},{8,10},{9,11},{10,... | collective-permute-start | bytes 1376264 | tf_op jit(solution)/shard_map/ppermute | solution.py:19
  26.5 8.6 %collective-permute-start.7 = (bf16[32,7168]{1,0:T(8,128)(2,1)S(1)}, bf16[32,7168]{1,0:T(8,128)(2,1)S(1)}, u32[]{:S(2)}, u32[]{:S(2)}) collective-permute-start(bf16[32,7168]{1,0:T(8,128)(2,1)S(1)} %constant_dynamic-update-slice_fusion.refs_0_), channel_id=1, source_target_pairs={{0,1},{1,0},{2,3},{3,2},{4,5},{5,4},{6,7},{7,6},{8,9},{9,8},{10,11... | collective-permute-start | bytes 1376264 | tf_op jit(solution)/shard_map/ppermute | solution.py:19
  34.8 1.8 %collective-permute-start.8 = (bf16[32,7168]{1,0:T(8,128)(2,1)S(1)}, bf16[32,7168]{1,0:T(8,128)(2,1)S(1)}, u32[]{:S(2)}, u32[]{:S(2)}) collective-permute-start(bf16[32,7168]{1,0:T(8,128)(2,1)S(1)} %collective-permute-done.6.refs_1_), channel_id=1, source_target_pairs={{0,1},{1,0},{2,3},{3,2},{4,5},{5,4},{6,7},{7,6},{8,9},{9,8},{10,11... | collective-permute-start | bytes 1376264 | tf_op jit(solution)/shard_map/ppermute | solution.py:19
  36.6 2.0 %copy-start.2 = (bf16[7168,256]{1,0:T(8,128)(2,1)S(1)}, bf16[7168,256]{1,0:T(8,128)(2,1)}, u32[]{:S(2)}) copy-start(bf16[7168,256]{1,0:T(8,128)(2,1)} %refs_5_.1) | copy-start | bytes 11010052
  38.6 2.0 %copy-start.3 = (bf16[256,7168]{1,0:T(8,128)(2,1)S(1)}, bf16[256,7168]{1,0:T(8,128)(2,1)}, u32[]{:S(2)}) copy-start(bf16[256,7168]{1,0:T(8,128)(2,1)} %refs_6_.1) | copy-start | bytes 11010052
  45.0 2.5 %collective-permute-start.9 = (bf16[64,7168]{1,0:T(8,128)(2,1)S(1)}, bf16[64,7168]{1,0:T(8,128)(2,1)S(1)}, u32[]{:S(2)}, u32[]{:S(2)}) collective-permute-start(bf16[64,7168]{1,0:T(8,128)(2,1)S(1)} %slice.108), channel_id=1, source_target_pairs={{0,1},{1,0},{2,3},{3,2},{4,5},{5,4},{6,7},{7,6},{8,9},{9,8},{10,11... | collective-permute-start | bytes 2752520 | tf_op jit(solution)/shard_map/ppermute | solution.py:19
  47.7 12.6 %collective-permute-start.10 = (bf16[32,7168]{1,0:T(8,128)(2,1)S(1)}, bf16[32,7168]{1,0:T(8,128)(2,1)S(1)}, u32[]{:S(2)}, u32[]{:S(2)}) collective-permute-start(bf16[32,7168]{1,0:T(8,128)(2,1)S(1)} %slice.163), channel_id=1, source_target_pairs={{0,2},{1,3},{2,0},{3,1},{4,6},{5,7},{6,4},{7,5},{8,10},{9,11},{10,... | collective-permute-start | bytes 1376264 | tf_op jit(solution)/shard_map/ppermute | solution.py:19
  60.5 9.1 %collective-permute-start.11 = (bf16[8,7168]{1,0:T(8,128)(2,1)S(1)}, bf16[8,7168]{1,0:T(8,128)(2,1)S(1)}, u32[]{:S(2)}, u32[]{:S(2)}) collective-permute-start(bf16[8,7168]{1,0:T(8,128)(2,1)S(1)} %get-tuple-element.8), channel_id=1, source_target_pairs={{0,28},{1,25},{2,30},{3,27},{4,24},{5,29},{6,26},{7,31},{8,20},{9,... | collective-permute-start | bytes 344072 | tf_op jit(solution)/shard_map/ppermute | solution.py:19
  64.1 9.2 %collective-permute-start.12 = (bf16[8,7168]{1,0:T(8,128)(2,1)S(1)}, bf16[8,7168]{1,0:T(8,128)(2,1)S(1)}, u32[]{:S(2)}, u32[]{:S(2)}) collective-permute-start(bf16[8,7168]{1,0:T(8,128)(2,1)S(1)} %get-tuple-element.11), channel_id=1, source_target_pairs={{0,20},{1,17},{2,22},{3,19},{4,16},{5,21},{6,18},{7,23},{8,28},{9,... | collective-permute-start | bytes 344072 | tf_op jit(solution)/shard_map/ppermute | solution.py:19
  64.1 9.2 %collective-permute-start.13 = (bf16[8,7168]{1,0:T(8,128)(2,1)S(1)}, bf16[8,7168]{1,0:T(8,128)(2,1)S(1)}, u32[]{:S(2)}, u32[]{:S(2)}) collective-permute-start(bf16[8,7168]{1,0:T(8,128)(2,1)S(1)} %get-tuple-element.10), channel_id=1, source_target_pairs={{0,12},{1,9},{2,14},{3,11},{4,8},{5,13},{6,10},{7,15},{8,4},{9,1},... | collective-permute-start | bytes 344072 | tf_op jit(solution)/shard_map/ppermute | solution.py:19
  67.2 7.0 %collective-permute-start.14 = (bf16[8,7168]{1,0:T(8,128)(2,1)S(1)}, bf16[8,7168]{1,0:T(8,128)(2,1)S(1)}, u32[]{:S(2)}, u32[]{:S(2)}) collective-permute-start(bf16[8,7168]{1,0:T(8,128)(2,1)S(1)} %get-tuple-element.9), channel_id=1, source_target_pairs={{0,4},{1,1},{2,6},{3,3},{4,0},{5,5},{6,2},{7,7},{8,12},{9,9},{10,1... | collective-permute-start | bytes 344072 | tf_op jit(solution)/shard_map/ppermute | solution.py:19
  74.7 1.4 %collective-permute-start.15 = (bf16[8,7168]{1,0:T(8,128)(2,1)S(1)}, bf16[8,7168]{1,0:T(8,128)(2,1)S(1)}, u32[]{:S(2)}, u32[]{:S(2)}) collective-permute-start(bf16[8,7168]{1,0:T(8,128)(2,1)S(1)} %slice.164), channel_id=1, source_target_pairs={{0,1},{1,0},{2,3},{3,2},{4,5},{5,4},{6,7},{7,6},{8,9},{9,8},{10,11... | collective-permute-start | bytes 344072 | tf_op jit(solution)/shard_map/ppermute | solution.py:19

commit v2 on v0

v2 whole, which is shorter than its diff:
```python
import functools

import jax
import jax.numpy as jnp
from jax import lax
from jax.experimental import pallas as pl
from jax.experimental.pallas import tpu as pltpu
from jax.sharding import PartitionSpec as P

KV = 512
SPAN = 4

softmax_scale = 192.0 ** (-0.5)
routed_scale = 2.5
norm_eps = 1e-06
masked_score = -1e30


def flipped(value, low_core, high_core):
    pairs = [(e, e ^ (high_core if e % 2 else low_core)) for e in range(lax.axis_size("ep"))]
    return lax.ppermute(value, "ep", pairs)


def attend_kernel(lengths_ref, query_ref, cache_ref, fresh_ref, out_ref):
    steps, tokens, heads, _ = query_ref.shape
    slots = cache_ref.shape[1]
    pad = 128 - slots
    for n in range(tokens):
        row = lax.broadcasted_iota(jnp.int32, (pad, 1), 0)
        extra = jnp.zeros((pad, fresh_ref.shape[2]), jnp.float32)
        for s in range(steps):
            block = fresh_ref[s].astype(jnp.float32)
            which = lax.broadcasted_iota(jnp.int32, block.shape, 0) == n
            one = jnp.sum(jnp.where(which, block, 0.0), axis=0, keepdims=True)
            extra = jnp.where(row == s, one, extra)
        keys = jnp.concatenate([cache_ref[n], extra.astype(jnp.bfloat16)], axis=0)
        queries = jnp.concatenate([query_ref[s, n] for s in range(steps)], axis=0)
        scores = (
            lax.dot_general(
                queries, keys, (((1,), (1,)), ((), ())), preferred_element_type=jnp.float32
            )
            * softmax_scale
        )
        position = lax.broadcasted_iota(jnp.int32, scores.shape, 1)
        step = lax.broadcasted_iota(jnp.int32, scores.shape, 0) // heads
        valid = (position < lengths_ref[n]) | (
            (position >= slots) & (position - slots <= step)
        )
        scores = jnp.where(valid, scores, masked_score)
        terms = jnp.exp(scores - jnp.max(scores, axis=1, keepdims=True))
        terms = jnp.where(valid, terms, 0.0)
        probs = (terms / jnp.sum(terms, axis=1, keepdims=True)).astype(jnp.bfloat16)
        mixed = jnp.dot(probs, keys[:, :KV], preferred_element_type=jnp.float32)
        for s in range(steps):
            out_ref[s, n] = mixed[s * heads : (s + 1) * heads].astype(jnp.bfloat16)


def attend(query, cache, lengths, fresh):
    steps, tokens, heads, width = query.shape
    vmem = pl.BlockSpec(memory_space=pltpu.VMEM)
    return pl.pallas_call(
        attend_kernel,
        out_shape=jax.ShapeDtypeStruct((steps, tokens, heads, KV), jnp.bfloat16),
        in_specs=[pl.BlockSpec(memory_space=pltpu.SMEM)] + [vmem] * 3,
        out_specs=vmem,
        compiler_params=pltpu.CompilerParams(vmem_limit_bytes=12 << 20),
        cost_estimate=pl.CostEstimate(
            flops=4 * steps * tokens * heads * 128 * width,
            bytes_accessed=2 * (2 * query.size + cache.size),
            transcendentals=steps * tokens * heads * 128,
        ),
        name="attention",
    )(lengths, query, cache, fresh)


def expert_kernel(mine_ref, other_ref, gate_ref, up_ref, down_ref, out_ref, send_ref, rows_v):
    rows = mine_ref.shape[0]
    depth, hidden_units = gate_ref.shape
    rows_v[:rows, :] = mine_ref[...]
    rows_v[rows:, :] = other_ref[...]
    parts = 7
    step = depth // parts
    gate = jnp.zeros((2 * rows, hidden_units), jnp.float32)
    upper = jnp.zeros((2 * rows, hidden_units), jnp.float32)
    for i in range(parts):
        ds = pl.ds(i * step, step)
        x = rows_v[:, ds]
        gate += jnp.dot(x, gate_ref[ds, :], preferred_element_type=jnp.float32)
        upper += jnp.dot(x, up_ref[ds, :], preferred_element_type=jnp.float32)
    inner = (gate / (1.0 + jnp.exp(-gate)) * upper).astype(jnp.bfloat16)
    for i in range(parts):
        ds = pl.ds(i * step, step)
        partial = jnp.dot(inner, down_ref[:, ds], preferred_element_type=jnp.float32)
        out_ref[:, ds] = partial[:rows].astype(jnp.bfloat16)
        send_ref[:, ds] = partial[rows:].astype(jnp.bfloat16)


def experts(mine, other, gate_w, up_w, down_w):
    rows, depth = mine.shape
    hidden_units = gate_w.shape[1]
    vmem = pl.BlockSpec(memory_space=pltpu.VMEM)
    return pl.pallas_call(
        expert_kernel,
        out_shape=[jax.ShapeDtypeStruct((rows, depth), jnp.bfloat16)] * 2,
        in_specs=[vmem] * 5,
        out_specs=[vmem] * 2,
        scratch_shapes=[pltpu.VMEM((2 * rows, depth), jnp.bfloat16)],
        compiler_params=pltpu.CompilerParams(vmem_limit_bytes=(16 << 20) + rows * depth * 24),
        cost_estimate=pl.CostEstimate(
            flops=12 * rows * depth * hidden_units,
            bytes_accessed=6 * depth * hidden_units + 8 * rows * depth,
            transcendentals=2 * rows * hidden_units,
        ),
        name="experts",
    )(mine, other, gate_w, up_w, down_w)


def pack_kernel(
    slots,
    groups,
    table_ref,
    ids_ref,
    replica_ref,
    other_ids_ref,
    other_replica_ref,
    raw_ref,
    other_ref,
    gain_ref,
    normed_ref,
    place_ref,
    choose_ref,
    *refs,
):
    message_refs, raw_v = refs[:-1], refs[-1]
    steps, tokens, depth = raw_ref.shape
    top = ids_ref.shape[2]
    index = lax.axis_index("ep")
    core = lax.rem(index, 2)
    group = lax.div(index, SPAN)
    message_rows = 2 * steps * slots
    for b, ref in enumerate((raw_ref, other_ref)):
        for s in range(steps):
            at = (b * steps + s) * tokens
            raw_v[at : at + tokens, :] = ref[s].astype(jnp.float32)
    raw = raw_v[...]
    mean_square = jnp.mean(raw * raw, axis=1, keepdims=True)
    normed = (raw * lax.rsqrt(mean_square + norm_eps) * gain_ref[...]).astype(jnp.bfloat16)
    normed_ref[...] = normed

    row = lax.broadcasted_iota(jnp.int32, place_ref.shape[1:], 0)
    column = lax.broadcasted_iota(jnp.int32, place_ref.shape[1:], 1)
    expert = lax.broadcasted_iota(jnp.int32, choose_ref.shape[1:], 0)
    token = lax.broadcasted_iota(jnp.int32, choose_ref.shape[1:], 1)
    place_row = [jnp.full(place_ref.shape[1:], -1, jnp.int32) for _ in range(top)]
    choice = [jnp.full(choose_ref.shape[1:], -1, jnp.int32) for _ in range(top)]
    for b, (ids, replicas) in enumerate(
        ((ids_ref, replica_ref), (other_ids_ref, other_replica_ref))
    ):
        for s in range(steps):
            block = b * steps + s
            earlier = []
            for t in range(tokens):
                for k in range(top):
                    copy = table_ref[ids[s, t, k], replicas[s, t, k]]
                    slot = sum([(copy == c).astype(jnp.int32) for c in earlier], jnp.int32(0))
                    earlier.append(copy)
                    delta = copy ^ group
                    kept = ((delta & 1) != core) & (slot < slots)
                    at = ((groups - 1 - delta) >> 1) * message_rows + block * slots + slot
                    at = jnp.where(kept, at, -1)
                    here = block * tokens + t
                    place_row[k] = jnp.where(column == here, at, place_row[k])
                    choice[k] = jnp.where(token == here, ids[s, t, k], choice[k])
    total = jnp.zeros(place_ref.shape[1:], jnp.float32)
    for k in range(top):
        hit = (place_row[k] == row).astype(jnp.float32)
        place_ref[k] = hit
        choose_ref[k] = (choice[k] == expert).astype(jnp.float32)
        total = total + hit
    packed = jnp.dot(total.astype(jnp.bfloat16), normed, preferred_element_type=jnp.float32)
    for m, ref in enumerate(message_refs):
        ref[...] = packed[m * message_rows : (m + 1) * message_rows].astype(jnp.bfloat16)


def pack(slots, groups, hidden, other, gain, copy_table, own_choice, other_choice, experts_total):
    steps, tokens, depth = hidden.shape
    top = own_choice[0].shape[2]
    messages = groups // 2
    message_rows = 2 * steps * slots
    columns = 2 * steps * tokens
    vmem = pl.BlockSpec(memory_space=pltpu.VMEM)
    smem = pl.BlockSpec(memory_space=pltpu.SMEM)
    shape = jax.ShapeDtypeStruct
    out = pl.pallas_call(
        functools.partial(pack_kernel, slots, groups),
        out_shape=[
            shape((columns, depth), jnp.bfloat16),
            shape((top, messages * message_rows, columns), jnp.float32),
            shape((top, experts_total, columns), jnp.float32),
        ]
        + [shape((message_rows, depth), jnp.bfloat16)] * messages,
        in_specs=[smem] * 5 + [vmem] * 3,
        out_specs=[vmem] * (3 + messages),
        scratch_shapes=[pltpu.VMEM((columns, depth), jnp.float32)],
        compiler_params=pltpu.CompilerParams(
            vmem_limit_bytes=(8 << 20) + 4 * messages * message_rows * depth * 2
        ),
        name="pack",
    )(copy_table, *own_choice, *other_choice, hidden, other, gain)
    return out[0], out[1], out[2], out[3:]


def weigh_kernel(normed_ref, router_ref, place_ref, choose_ref, weigh_ref):
    scores = jax.nn.sigmoid(
        lax.dot_general(
            router_ref[...],
            normed_ref[...],
            (((1,), (1,)), ((), ())),
            preferred_element_type=jnp.float32,
        )
    )
    top = place_ref.shape[0]
    picked = [jnp.sum(choose_ref[k] * scores, axis=0, keepdims=True) for k in range(top)]
    total = sum(picked[1:], picked[0])
    weigh = jnp.zeros(weigh_ref.shape, jnp.float32)
    for k in range(top):
        weigh = weigh + place_ref[k] * (routed_scale * picked[k] / total)
    weigh_ref[...] = weigh


def weigh(normed, router_t, place, choose):
    vmem = pl.BlockSpec(memory_space=pltpu.VMEM)
    return pl.pallas_call(
        weigh_kernel,
        out_shape=jax.ShapeDtypeStruct(place.shape[1:], jnp.float32),
        in_specs=[vmem] * 4,
        out_specs=vmem,
        cost_estimate=pl.CostEstimate(
            flops=2 * normed.size * 256, bytes_accessed=2 * normed.size, transcendentals=256
        ),
        name="weigh",
    )(normed, router_t, place, choose)


def combine_kernel(weigh_ref, *refs):
    part_refs, own_ref, send_ref = refs[:-2], refs[-2], refs[-1]
    weights = weigh_ref[...]
    high = weights.astype(jnp.bfloat16)
    left = weights - high.astype(jnp.float32)
    middle = left.astype(jnp.bfloat16)
    low = (left - middle.astype(jnp.float32)).astype(jnp.bfloat16)
    rows = jnp.concatenate([ref[...].astype(jnp.float32) for ref in part_refs], axis=0)
    rows = rows.astype(jnp.bfloat16)
    pieces = [
        lax.dot_general(w, rows, (((0,), (0,)), ((), ())), preferred_element_type=jnp.float32)
        for w in (high, middle, low)
    ]
    result = pieces[0] + (pieces[1] + pieces[2])
    half = own_ref.shape[0]
    own_ref[...] = result[:half]
    send_ref[...] = result[half:].astype(jnp.bfloat16)


def combine(weights, parts):
    depth = parts[0].shape[1]
    half = weights.shape[1] // 2
    vmem = pl.BlockSpec(memory_space=pltpu.VMEM)
    return pl.pallas_call(
        combine_kernel,
        out_shape=[
            jax.ShapeDtypeStruct((half, depth), jnp.float32),
            jax.ShapeDtypeStruct((half, depth), jnp.bfloat16),
        ],
        in_specs=[vmem] * (1 + len(parts)),
        out_specs=[vmem] * 2,
        compiler_params=pltpu.CompilerParams(
            vmem_limit_bytes=(8 << 20) + 8 * weights.shape[0] * depth
        ),
        name="combine",
    )(weights, *parts)


def finish_kernel(own_ref, received_ref, out_ref):
    result = own_ref[...] + received_ref[...].astype(jnp.float32)
    steps, tokens, _ = out_ref.shape
    for s in range(steps):
        out_ref[s] = result[s * tokens : (s + 1) * tokens].astype(jnp.bfloat16)


def finish(own, received, shape):
    vmem = pl.BlockSpec(memory_space=pltpu.VMEM)
    return pl.pallas_call(
        finish_kernel,
        out_shape=jax.ShapeDtypeStruct(shape, jnp.bfloat16),
        in_specs=[vmem] * 2,
        out_specs=vmem,
        name="finish",
    )(own, received)


def mixture(hidden, norm_gain, router, expert_ids, replica, copy_table, gate_w, up_w, down_w):
    groups = lax.axis_size("ep") // SPAN
    messages = groups // 2
    tokens = hidden.shape[1]
    slots = max(2, 2 * tokens * expert_ids.shape[2] // groups)
    deltas = [(groups - 1 - 2 * m, groups - 2 - 2 * m) for m in range(messages)]

    def swapped(value):
        return flipped(value, 1, 1)

    other_choice = (swapped(expert_ids), swapped(replica))
    normed, place, choose, packed = pack(
        slots,
        groups,
        hidden,
        swapped(hidden),
        norm_gain[None, :],
        copy_table,
        (expert_ids, replica),
        other_choice,
        router.shape[1],
    )

    def rounds(parts):
        return [
            flipped(part, SPAN * low, SPAN * high) for part, (low, high) in zip(parts, deltas)
        ]

    near = jnp.concatenate(rounds(packed), axis=0)
    weights = weigh(normed, router.T, place, choose)
    far = flipped(near, 2, 2)
    near_own, near_send = experts(near, swapped(near), gate_w, up_w, down_w)
    near_sum = near_own.astype(jnp.float32) + swapped(near_send).astype(jnp.float32)
    far_own, far_send = experts(far, swapped(far), gate_w, up_w, down_w)
    far_sum = far_own.astype(jnp.float32) + swapped(far_send).astype(jnp.float32)
    total = near_sum + flipped(far_sum.astype(jnp.bfloat16), 2, 2).astype(jnp.float32)
    total = total.astype(jnp.bfloat16)
    size = total.shape[0] // messages
    returned = rounds([total[m * size : (m + 1) * size] for m in range(messages)])
    own, send = combine(weights, returned)
    return finish(own, swapped(send), hidden.shape)


def per_device(
    hidden,
    norm_gain,
    router,
    expert_ids,
    replica,
    copy_table,
    gate_w,
    up_w,
    down_w,
    query,
    cache,
    lengths,
    fresh_kv,
):
    moe_out = mixture(
        hidden, norm_gain, router, expert_ids, replica, copy_table, gate_w, up_w, down_w
    )
    attended = attend(query, cache, lengths, fresh_kv)
    return (attended, moe_out)


def solution(mesh):
    return jax.shard_map(
        per_device,
        mesh=mesh,
        in_specs=(
            P(None, ("groups", "ep"), None),
            P(),
            P(),
            P(None, ("groups", "ep"), None),
            P(None, ("groups", "ep"), None),
            P(),
            P(None, "ep"),
            P(None, "ep"),
            P("ep", None),
            P(None, ("groups", "ep"), None, None),
            P(("groups", "ep"), None, None),
            P(("groups", "ep")),
            P(None, ("groups", "ep"), None),
        ),
        out_specs=(P(None, ("groups", "ep"), None, None), P(None, ("groups", "ep"), None)),
        check_vma=False,
    )
```

time: 115 us -> 84.8 us (0.74)
  matrix products: 19.8 us -> 0 us
  other arithmetic: 18 us -> 0.27 us
  waiting for transfers between devices: 46.3 us -> 30.9 us
  Pallas kernels: 0 us -> 12.5 us
  local copies, waits for them, and re-layouts: 8.27 us -> 16 us
  starting transfers between devices: 20.5 us -> 23.7 us
    all_to_all x4 -> x0, waiting for transfers between devices: 29.2 us -> none  [the longest x2 16.9 us: mixture(): lax.all_to_all(summed.astype(jnp.bfloat16), 'ep', split_axis=0, concat_ax...]
    dot_general x17 -> x0, matrix products: 19.8 us -> none  [the longest x2 11.2 us: expert_rows(): jnp.dot(inner, down_w, preferred_element_type=jnp.float32)]
    ppermute x8 -> x18, starting transfers between devices: 4.44 us -> 23.7 us  [flipped(): return lax.ppermute(value, 'ep', pairs)]
    all_to_all x4 -> x0, starting transfers between devices: 16.1 us -> none  [the longest x2 10.1 us: mixture(): lax.all_to_all(outgoing, 'ep', split_axis=0, concat_axis=0, tiled=True)]
    unnamed x29 -> x42, local copies, waits for them, and re-layouts: 0.13 us -> 15.9 us
    ppermute x8 -> x18, waiting for transfers between devices: 17.1 us -> 30.9 us  [flipped(): return lax.ppermute(value, 'ep', pairs)]
    pallas_call x0 -> x7, Pallas kernels: none -> 12.5 us  [the longest x2 4.21 us: experts(): pl.pallas_call(expert_kernel, out_shape=[jax.ShapeDtypeStruct((rows, dept...]
    select_n x9 -> x0, other arithmetic: 5.52 us -> none  [the longest x4 3.18 us: mixture(): jnp.where(is_lower, jnp.concatenate([gathered_piece, partner], axis=2), j...]
  transfers between devices with their start and end apart: 12 -> 18, of which waited for: 6 -> 8; matrix products, arithmetic and copies ran while one was open for 34% -> 3% of each run, Pallas kernels for 0% -> 11%
where the time goes in v2:
time: 84.8 us; the launch traced here: 84.2 us
  waiting for transfers between devices  30.9 us (36%)
  starting transfers between devices  23.7 us (28%)
  local copies, waits for them, and re-layouts  16 us (19%)
  Pallas kernels  12.5 us (15%)
    ppermute x18, waiting for transfers between devices, flipped(): return lax.ppermute(value, 'ep', pairs)  30.9 us
    ppermute x18, starting transfers between devices, flipped(): return lax.ppermute(value, 'ep', pairs)  23.7 us
    unnamed x42, local copies, waits for them, and re-layouts  15.9 us
    pallas_call x2, Pallas kernels, experts(): pl.pallas_call(expert_kernel, out_shape=[jax.ShapeDtypeStruct((rows, dept...  4.21 us
    pallas_call x1, Pallas kernels, attend(): pl.pallas_call(attend_kernel, out_shape=jax.ShapeDtypeStruct((steps, toke...  2.97 us
    pallas_call x1, Pallas kernels, weigh(): pl.pallas_call(weigh_kernel, out_shape=jax.ShapeDtypeStruct(place.shape[1...  1.83 us
  transfers between devices with their start and end apart: 18, of which 8 were waited for; matrix products, arithmetic and copies ran while one was open for 3% of the time, Pallas kernels for 11%

profile of v2, /device:TPU:0, one launch (start us, length us, event | category | flops | bytes accessed | tf_op | source)
XLA Modules:
  0.0 84.2 jit_solution(14195868175249544389)
XLA Ops:
  0.6 0.5 collective-permute-start.2
  1.1 0.8 copy.18.ids_ref
  1.9 0.1 collective-permute-start
  2.0 0.8 copy.19.replica_ref
  2.8 0.5 collective-permute-start.1
  3.2 0.8 copy.17.table_ref
  4.0 0.0 collective-permute-done.other_ids_ref
  4.0 0.1 collective-permute-done.1.other_replica_ref
  4.0 0.0 collective-permute-done.2.other_ref
  4.0 0.9 %copy-done.10 = bf16[2,4,7168]{2,1,0:T(4,128)(2,1)S(1)} copy-done((bf16[2,4,7168]{2,1,0:T(4,128)(2,1)S(1)}, bf16[2,4,7168]{2,1,0:T(4,128)(2,1)}, u32[]{:S(2)}) %copy-start.10) | copy-done | bytes 114712
  4.9 0.7 copy-done.13
  5.7 1.5 %pack.1 = (bf16[16,7168]{1,0:T(8,128)(2,1)S(1)}, f32[2,32,16]{2,1,0:T(8,128)S(1)}, f32[2,6,16]{2,1,0:T(8,128)S(1)}, bf16[8,7168]{1,0:T(8,128)(2,1)S(1)}, bf16[8,...) custom-call(s32[6,2]{1,0:T(8,128)S(1)} %copy.17.table_ref, ...), custom_call_target="tpu_custom_call" | custom-call | tf_op jit(solution)/shard_map/pack/pallas_call | solution.py:194
  7.2 0.0 copy-start.8
  7.2 0.7 copy-done.8
  7.9 0.6 copy-done.12
  8.5 0.6 copy-done.15
  9.1 5.9 %collective-permute-start.3 = (bf16[8,7168]{1,0:T(8,128)(2,1)S(1)}, bf16[8,7168]{1,0:T(8,128)(2,1)S(1)}, u32[]{:S(2)}, u32[]{:S(2)}) collective-permute-start(bf16[8,7168]{1,0:T(8,128)(2,1)S(1)} %get-tuple-element.18), channel_id=1, source_target_pairs={{0,28},{1,25},{2,30},{3,27},{4,24},{5,29},{6,26},{7,31},{8,20},{9,... | collective-permute-start | bytes 344072 | tf_op jit(solution)/shard_map/ppermute | solution.py:21
  15.0 0.0 collective-permute-start.4
  15.0 1.7 %collective-permute-start.5 = (bf16[8,7168]{1,0:T(8,128)(2,1)S(1)}, bf16[8,7168]{1,0:T(8,128)(2,1)S(1)}, u32[]{:S(2)}, u32[]{:S(2)}) collective-permute-start(bf16[8,7168]{1,0:T(8,128)(2,1)S(1)} %get-tuple-element.20), channel_id=1, source_target_pairs={{0,12},{1,9},{2,14},{3,11},{4,8},{5,13},{6,10},{7,15},{8,4},{9,1},... | collective-permute-start | bytes 344072 | tf_op jit(solution)/shard_map/ppermute | solution.py:21
  16.6 2.2 %collective-permute-start.6 = (bf16[8,7168]{1,0:T(8,128)(2,1)S(1)}, bf16[8,7168]{1,0:T(8,128)(2,1)S(1)}, u32[]{:S(2)}, u32[]{:S(2)}) collective-permute-start(bf16[8,7168]{1,0:T(8,128)(2,1)S(1)} %get-tuple-element.21), channel_id=1, source_target_pairs={{0,4},{1,1},{2,6},{3,3},{4,0},{5,5},{6,2},{7,7},{8,12},{9,9},{10,1... | collective-permute-start | bytes 344072 | tf_op jit(solution)/shard_map/ppermute | solution.py:21
  18.9 0.1 collective-permute-done.3
  19.0 6.0 %collective-permute-done.4 = bf16[8,7168]{1,0:T(8,128)(2,1)S(1)} collective-permute-done((bf16[8,7168]{1,0:T(8,128)(2,1)S(1)}, bf16[8,7168]{1,0:T(8,128)(2,1)S(1)}, u32[]{:S(2)}, u32[]{:S(2)}) %collective-permute-start.4) | collective-permute-done | bytes 114720 | tf_op jit(solution)/shard_map/ppermute | solution.py:21
  25.0 0.0 collective-permute-done.5
  25.0 0.0 collective-permute-done.6
  25.0 1.6 %collective-permute-start.9 = (bf16[32,7168]{1,0:T(8,128)(2,1)S(1)}, bf16[32,7168]{1,0:T(8,128)(2,1)S(1)}, u32[]{:S(2)}, u32[]{:S(2)}) collective-permute-start(bf16[32,7168]{1,0:T(8,128)(2,1)S(1)} %constant_dynamic-update-slice_fusion.mine_ref), channel_id=1, source_target_pairs={{0,2},{1,3},{2,0},{3,1},{4,6},{5,7},{6,4},{7,5},{8,10},{9,11},{10,... | collective-permute-start | bytes 1376264 | tf_op jit(solution)/shard_map/ppermute | solution.py:21
  26.6 8.8 %collective-permute-done.9.mine_ref = bf16[32,7168]{1,0:T(8,128)(2,1)S(1)} collective-permute-done((bf16[32,7168]{1,0:T(8,128)(2,1)S(1)}, bf16[32,7168]{1,0:T(8,128)(2,1)S(1)}, u32[]{:S(2)}, u32[]{:S(2)}) %collective-permute-start.9) | collective-permute-done | bytes 458784 | tf_op jit(solution)/shard_map/ppermute | solution.py:21
  35.4 0.0 collective-permute-start.10
  35.4 0.5 collective-permute-start.7
  35.9 1.3 %collective-permute-done.10.other_ref = bf16[32,7168]{1,0:T(8,128)(2,1)S(1)} collective-permute-done((bf16[32,7168]{1,0:T(8,128)(2,1)S(1)}, bf16[32,7168]{1,0:T(8,128)(2,1)S(1)}, u32[]{:S(2)}, u32[]{:S(2)}) %collective-permute-start.10) | collective-permute-done | bytes 458784 | tf_op jit(solution)/shard_map/ppermute | solution.py:21
  37.2 2.0 %copy-done = bf16[7168,256]{1,0:T(8,128)(2,1)S(1)} copy-done((bf16[7168,256]{1,0:T(8,128)(2,1)S(1)}, bf16[7168,256]{1,0:T(8,128)(2,1)}, u32[]{:S(2)}) %copy-start) | copy-done | bytes 3670040
  39.2 2.0 %copy-done.2 = bf16[7168,256]{1,0:T(8,128)(2,1)S(1)} copy-done((bf16[7168,256]{1,0:T(8,128)(2,1)S(1)}, bf16[7168,256]{1,0:T(8,128)(2,1)}, u32[]{:S(2)}) %copy-start.2) | copy-done | bytes 3670040
  41.3 2.0 %copy-done.4 = bf16[256,7168]{1,0:T(8,128)(2,1)S(1)} copy-done((bf16[256,7168]{1,0:T(8,128)(2,1)S(1)}, bf16[256,7168]{1,0:T(8,128)(2,1)}, u32[]{:S(2)}) %copy-start.4) | copy-done | bytes 3670040
  43.3 2.1 %experts.3 = (bf16[32,7168]{1,0:T(8,128)(2,1)S(1)}, bf16[32,7168]{1,0:T(8,128)(2,1)S(1)}) custom-call(bf16[32,7168]{1,0:T(8,128)(2,1)S(1)} %collective-permute-done.9.mine_ref, bf16[32,7168]{1,0:T(8,128)(2,1)S(1)} %collective-permute-done.10.other_ref, bf16[7168,256]{1,0:T(8,128)(2,1)S(1)} %copy-done, bf16[7168,256]{1,0:T(8,128)(2,1)S(1)} %copy-done.2, ...), custom_call_target="tpu_custom_call" | custom-call | flops 704643072 | bytes 12845056 | tf_op jit(solution)/shard_map/experts/pallas_call | solution.py:102
  45.4 0.2 collective-permute-start.11
  45.6 0.0 collective-permute-done.7.other_ref
  45.6 0.8 copy-done.3
  46.5 1.0 %copy-done.5 = bf16[256,7168]{1,0:T(8,128)(2,1)S(1)} copy-done((bf16[256,7168]{1,0:T(8,128)(2,1)S(1)}, bf16[256,7168]{1,0:T(8,128)(2,1)}, u32[]{:S(2)}) %copy-start.5) | copy-done | bytes 3670040
  47.5 2.1 %experts.2 = (bf16[32,7168]{1,0:T(8,128)(2,1)S(1)}, bf16[32,7168]{1,0:T(8,128)(2,1)S(1)}) custom-call(bf16[32,7168]{1,0:T(8,128)(2,1)S(1)} %constant_dynamic-update-slice_fusion.mine_ref, bf16[32,7168]{1,0:T(8,128)(2,1)S(1)} %collective-permute-done.7.other_ref, bf16[7168,256]{1,0:T(8,128)(2,1)S(1)} %copy-done.1, bf16[7168,256]{1,0:T(8,128)(2,1)S(1)} %copy-done.3, ...), custom_call_target="tpu_custom_call" | custom-call | flops 704643072 | bytes 12845056 | tf_op jit(solution)/shard_map/experts/pallas_call | solution.py:102
  49.6 0.0 copy-start.6
  49.6 0.0 copy-start.7
  49.6 0.0 copy-start.14
  49.7 0.0 copy-start.16
  49.7 0.2 collective-permute-start.8
  49.9 0.0 collective-permute-done.11
  49.9 0.1 add_convert_fusion.1
  50.0 1.6 %collective-permute-start.12 = (bf16[32,7168]{1,0:T(8,128)(2,1)S(1)}, bf16[32,7168]{1,0:T(8,128)(2,1)S(1)}, u32[]{:S(2)}, u32[]{:S(2)}) collective-permute-start(bf16[32,7168]{1,0:T(8,128)(2,1)S(1)} %add_convert_fusion.1), channel_id=1, source_target_pairs={{0,2},{1,3},{2,0},{3,1},{4,6},{5,7},{6,4},{7,5},{8,10},{9,11},{10,... | collective-permute-start | bytes 1376264 | tf_op jit(solution)/shard_map/ppermute | solution.py:21
  51.6 0.0 collective-permute-done.8
  51.6 11.3 %collective-permute-done.12 = bf16[32,7168]{1,0:T(8,128)(2,1)S(1)} collective-permute-done((bf16[32,7168]{1,0:T(8,128)(2,1)S(1)}, bf16[32,7168]{1,0:T(8,128)(2,1)S(1)}, u32[]{:S(2)}, u32[]{:S(2)}) %collective-permute-start.12) | collective-permute-done | bytes 458784 | tf_op jit(solution)/shard_map/ppermute | solution.py:21
  62.8 0.2 add_convert_fusion
  63.1 3.8 %collective-permute-start.13 = (bf16[8,7168]{1,0:T(8,128)(2,1)S(1)}, bf16[8,7168]{1,0:T(8,128)(2,1)S(1)}, u32[]{:S(2)}, u32[]{:S(2)}) collective-permute-start(bf16[8,7168]{1,0:T(8,128)(2,1)S(1)} %get-tuple-element.31), channel_id=1, source_target_pairs={{0,28},{1,25},{2,30},{3,27},{4,24},{5,29},{6,26},{7,31},{8,20},{9,... | collective-permute-start | bytes 344072 | tf_op jit(solution)/shard_map/ppermute | solution.py:21
  66.9 0.0 collective-permute-start.14
  66.9 3.1 %collective-permute-start.15 = (bf16[8,7168]{1,0:T(8,128)(2,1)S(1)}, bf16[8,7168]{1,0:T(8,128)(2,1)S(1)}, u32[]{:S(2)}, u32[]{:S(2)}) collective-permute-start(bf16[8,7168]{1,0:T(8,128)(2,1)S(1)} %get-tuple-element.29), channel_id=1, source_target_pairs={{0,12},{1,9},{2,14},{3,11},{4,8},{5,13},{6,10},{7,15},{8,4},{9,1},... | collective-permute-start | bytes 344072 | tf_op jit(solution)/shard_map/ppermute | solution.py:21
  70.0 1.9 %collective-permute-start.16 = (bf16[8,7168]{1,0:T(8,128)(2,1)S(1)}, bf16[8,7168]{1,0:T(8,128)(2,1)S(1)}, u32[]{:S(2)}, u32[]{:S(2)}) collective-permute-start(bf16[8,7168]{1,0:T(8,128)(2,1)S(1)} %get-tuple-element.28), channel_id=1, source_target_pairs={{0,4},{1,1},{2,6},{3,3},{4,0},{5,5},{6,2},{7,7},{8,12},{9,9},{10,1... | collective-permute-start | bytes 344072 | tf_op jit(solution)/shard_map/ppermute | solution.py:21
  71.9 1.8 %weigh.1.weigh_ref = f32[32,16]{1,0:T(8,128)} custom-call(bf16[16,7168]{1,0:T(8,128)(2,1)} %copy-done.8, bf16[6,7168]{1,0:T(8,128)(2,1)} %bitcast.3, f32[2,32,16]{2,1,0:T(8,128)} %copy-done.12, f32[2,6,16]{2,1,0:T(8,128)} %copy-done.15), custom_call_target="tpu_custom_call" | custom-call | flops 58720256 | bytes 229376 | tf_op jit(solution)/shard_map/weigh/pallas_call | solution.py:233
  73.7 0.0 collective-permute-done.13.refs_0_
  73.7 2.6 %collective-permute-done.14.refs_1_ = bf16[8,7168]{1,0:T(8,128)(2,1)S(1)} collective-permute-done((bf16[8,7168]{1,0:T(8,128)(2,1)S(1)}, bf16[8,7168]{1,0:T(8,128)(2,1)S(1)}, u32[]{:S(2)}, u32[]{:S(2)}) %collective-permute-start.14) | collective-permute-done | bytes 114720 | tf_op jit(solution)/shard_map/ppermute | solution.py:21
  76.3 0.0 collective-permute-done.15.refs_2_
  76.4 0.7 collective-permute-done.16.refs_3_
  77.1 0.7 copy-done.11
  77.8 0.4 combine.1
  78.2 0.7 copy-done.9
  78.9 3.0 %attention.1 = bf16[2,4,64,512]{3,2,1,0:T(8,128)(2,1)} custom-call(s32[4]{0:T(128)S(1)} %copy-done.16, bf16[2,4,64,576]{3,2,1,0:T(8,128)(2,1)S(1)} %copy-done.6, bf16[4,64,576]{2,1,0:T(8,128)(2,1)S(1)} %copy-done.7, bf16[2,4,576]{2,1,0:T(4,128)(2,1)S(1)} %copy-done.14), custom_call_target="tpu_custom_call" | custom-call | flops 150994944 | bytes 1474560 | tf_op jit(solution)/shard_map/attention/pallas_call | solution.py:61
  81.9 0.6 copy-done.17
  82.5 1.7 %finish.1 = bf16[2,4,7168]{2,1,0:T(4,128)(2,1)} custom-call(f32[8,7168]{1,0:T(8,128)} %copy-done.9, bf16[8,7168]{1,0:T(8,128)(2,1)} %copy-done.17), custom_call_target="tpu_custom_call" | custom-call | tf_op jit(solution)/shard_map/finish/pallas_call | solution.py:292
  (25 shorter events, 0.1 us)
Async XLA Ops:
  0.6 3.4 %collective-permute-start.2 = (bf16[2,4,7168]{2,1,0:T(4,128)(2,1)}, bf16[2,4,7168]{2,1,0:T(4,128)(2,1)S(1)}, u32[]{:S(2)}, u32[]{:S(2)}) collective-permute-start(bf16[2,4,7168]{2,1,0:T(4,128)(2,1)} %raw_ref.1), channel_id=1, source_target_pairs={{0,1},{1,0},{2,3},{3,2},{4,5},{5,4},{6,7},{7,6},{8,9},{9,8},{10,11... | collective-permute-start | bytes 344072 | tf_op jit(solution)/shard_map/ppermute | solution.py:21
  1.9 2.1 %collective-permute-start = (s32[2,4,2]{2,1,0:T(4,128)S(1)}, s32[2,4,2]{2,1,0:T(4,128)S(1)}, u32[]{:S(2)}, u32[]{:S(2)}) collective-permute-start(s32[2,4,2]{2,1,0:T(4,128)S(1)} %copy.18.ids_ref), channel_id=1, source_target_pairs={{0,1},{1,0},{2,3},{3,2},{4,5},{5,4},{6,7},{7,6},{8,9},{9,8},{10,11... | collective-permute-start | bytes 200 | tf_op jit(solution)/shard_map/ppermute | solution.py:21
  2.8 1.3 %collective-permute-start.1 = (s32[2,4,2]{2,1,0:T(4,128)S(1)}, s32[2,4,2]{2,1,0:T(4,128)S(1)}, u32[]{:S(2)}, u32[]{:S(2)}) collective-permute-start(s32[2,4,2]{2,1,0:T(4,128)S(1)} %copy.19.replica_ref), channel_id=1, source_target_pairs={{0,1},{1,0},{2,3},{3,2},{4,5},{5,4},{6,7},{7,6},{8,9},{9,8},{10,11... | collective-permute-start | bytes 200 | tf_op jit(solution)/shard_map/ppermute | solution.py:21
  4.0 0.9 %copy-start.10 = (bf16[2,4,7168]{2,1,0:T(4,128)(2,1)S(1)}, bf16[2,4,7168]{2,1,0:T(4,128)(2,1)}, u32[]{:S(2)}) copy-start(bf16[2,4,7168]{2,1,0:T(4,128)(2,1)} %raw_ref.1) | copy-start | bytes 344068
  4.9 0.7 copy-start.13
  7.2 0.7 copy-start.8
  7.9 0.6 copy-start.12
  8.5 0.6 copy-start.15
  9.1 9.9 %collective-permute-start.3 = (bf16[8,7168]{1,0:T(8,128)(2,1)S(1)}, bf16[8,7168]{1,0:T(8,128)(2,1)S(1)}, u32[]{:S(2)}, u32[]{:S(2)}) collective-permute-start(bf16[8,7168]{1,0:T(8,128)(2,1)S(1)} %get-tuple-element.18), channel_id=1, source_target_pairs={{0,28},{1,25},{2,30},{3,27},{4,24},{5,29},{6,26},{7,31},{8,20},{9,... | collective-permute-start | bytes 344072 | tf_op jit(solution)/shard_map/ppermute | solution.py:21
  15.0 10.0 %collective-permute-start.4 = (bf16[8,7168]{1,0:T(8,128)(2,1)S(1)}, bf16[8,7168]{1,0:T(8,128)(2,1)S(1)}, u32[]{:S(2)}, u32[]{:S(2)}) collective-permute-start(bf16[8,7168]{1,0:T(8,128)(2,1)S(1)} %get-tuple-element.19), channel_id=1, source_target_pairs={{0,20},{1,17},{2,22},{3,19},{4,16},{5,21},{6,18},{7,23},{8,28},{9,... | collective-permute-start | bytes 344072 | tf_op jit(solution)/shard_map/ppermute | solution.py:21
  15.0 10.0 %collective-permute-start.5 = (bf16[8,7168]{1,0:T(8,128)(2,1)S(1)}, bf16[8,7168]{1,0:T(8,128)(2,1)S(1)}, u32[]{:S(2)}, u32[]{:S(2)}) collective-permute-start(bf16[8,7168]{1,0:T(8,128)(2,1)S(1)} %get-tuple-element.20), channel_id=1, source_target_pairs={{0,12},{1,9},{2,14},{3,11},{4,8},{5,13},{6,10},{7,15},{8,4},{9,1},... | collective-permute-start | bytes 344072 | tf_op jit(solution)/shard_map/ppermute | solution.py:21
  16.6 8.4 %collective-permute-start.6 = (bf16[8,7168]{1,0:T(8,128)(2,1)S(1)}, bf16[8,7168]{1,0:T(8,128)(2,1)S(1)}, u32[]{:S(2)}, u32[]{:S(2)}) collective-permute-start(bf16[8,7168]{1,0:T(8,128)(2,1)S(1)} %get-tuple-element.21), channel_id=1, source_target_pairs={{0,4},{1,1},{2,6},{3,3},{4,0},{5,5},{6,2},{7,7},{8,12},{9,9},{10,1... | collective-permute-start | bytes 344072 | tf_op jit(solution)/shard_map/ppermute | solution.py:21
  25.0 10.3 %collective-permute-start.9 = (bf16[32,7168]{1,0:T(8,128)(2,1)S(1)}, bf16[32,7168]{1,0:T(8,128)(2,1)S(1)}, u32[]{:S(2)}, u32[]{:S(2)}) collective-permute-start(bf16[32,7168]{1,0:T(8,128)(2,1)S(1)} %constant_dynamic-update-slice_fusion.mine_ref), channel_id=1, source_target_pairs={{0,2},{1,3},{2,0},{3,1},{4,6},{5,7},{6,4},{7,5},{8,10},{9,11},{10,... | collective-permute-start | bytes 1376264 | tf_op jit(solution)/shard_map/ppermute | solution.py:21
  35.4 1.8 %collective-permute-start.10 = (bf16[32,7168]{1,0:T(8,128)(2,1)S(1)}, bf16[32,7168]{1,0:T(8,128)(2,1)S(1)}, u32[]{:S(2)}, u32[]{:S(2)}) collective-permute-start(bf16[32,7168]{1,0:T(8,128)(2,1)S(1)} %collective-permute-done.9.mine_ref), channel_id=1, source_target_pairs={{0,1},{1,0},{2,3},{3,2},{4,5},{5,4},{6,7},{7,6},{8,9},{9,8},{10,11... | collective-permute-start | bytes 1376264 | tf_op jit(solution)/shard_map/ppermute | solution.py:21
  35.4 10.3 %collective-permute-start.7 = (bf16[32,7168]{1,0:T(8,128)(2,1)S(1)}, bf16[32,7168]{1,0:T(8,128)(2,1)S(1)}, u32[]{:S(2)}, u32[]{:S(2)}) collective-permute-start(bf16[32,7168]{1,0:T(8,128)(2,1)S(1)} %constant_dynamic-update-slice_fusion.mine_ref), channel_id=1, source_target_pairs={{0,1},{1,0},{2,3},{3,2},{4,5},{5,4},{6,7},{7,6},{8,9},{9,8},{10,11... | collective-permute-start | bytes 1376264 | tf_op jit(solution)/shard_map/ppermute | solution.py:21
  37.2 2.0 %copy-start = (bf16[7168,256]{1,0:T(8,128)(2,1)S(1)}, bf16[7168,256]{1,0:T(8,128)(2,1)}, u32[]{:S(2)}) copy-start(bf16[7168,256]{1,0:T(8,128)(2,1)} %gate_ref.3) | copy-start | bytes 11010052
  39.2 2.0 %copy-start.2 = (bf16[7168,256]{1,0:T(8,128)(2,1)S(1)}, bf16[7168,256]{1,0:T(8,128)(2,1)}, u32[]{:S(2)}) copy-start(bf16[7168,256]{1,0:T(8,128)(2,1)} %up_ref.3) | copy-start | bytes 11010052
  41.3 2.0 %copy-start.4 = (bf16[256,7168]{1,0:T(8,128)(2,1)S(1)}, bf16[256,7168]{1,0:T(8,128)(2,1)}, u32[]{:S(2)}) copy-start(bf16[256,7168]{1,0:T(8,128)(2,1)} %down_ref.3) | copy-start | bytes 11010052
  43.3 2.3 %copy-start.1 = (bf16[7168,256]{1,0:T(8,128)(2,1)S(1)}, bf16[7168,256]{1,0:T(8,128)(2,1)}, u32[]{:S(2)}) copy-start(bf16[7168,256]{1,0:T(8,128)(2,1)} %gate_ref.3) | copy-start | bytes 11010052
  43.3 3.2 %copy-start.3 = (bf16[7168,256]{1,0:T(8,128)(2,1)S(1)}, bf16[7168,256]{1,0:T(8,128)(2,1)}, u32[]{:S(2)}) copy-start(bf16[7168,256]{1,0:T(8,128)(2,1)} %up_ref.3) | copy-start | bytes 11010052
  43.3 4.2 %copy-start.5 = (bf16[256,7168]{1,0:T(8,128)(2,1)S(1)}, bf16[256,7168]{1,0:T(8,128)(2,1)}, u32[]{:S(2)}) copy-start(bf16[256,7168]{1,0:T(8,128)(2,1)} %down_ref.3) | copy-start | bytes 11010052
  45.4 4.4 %collective-permute-start.11 = (bf16[32,7168]{1,0:T(8,128)(2,1)S(1)}, bf16[32,7168]{1,0:T(8,128)(2,1)S(1)}, u32[]{:S(2)}, u32[]{:S(2)}) collective-permute-start(bf16[32,7168]{1,0:T(8,128)(2,1)S(1)} %get-tuple-element.25), channel_id=1, source_target_pairs={{0,1},{1,0},{2,3},{3,2},{4,5},{5,4},{6,7},{7,6},{8,9},{9,8},{10,11... | collective-permute-start | bytes 1376264 | tf_op jit(solution)/shard_map/ppermute | solution.py:21
  49.6 29.3 %copy-start.6 = (bf16[2,4,64,576]{3,2,1,0:T(8,128)(2,1)S(1)}, bf16[2,4,64,576]{3,2,1,0:T(8,128)(2,1)}, u32[]{:S(2)}) copy-start(bf16[2,4,64,576]{3,2,1,0:T(8,128)(2,1)} %query_ref.1) | copy-start | bytes 1769476
  49.6 29.3 %copy-start.7 = (bf16[4,64,576]{2,1,0:T(8,128)(2,1)S(1)}, bf16[4,64,576]{2,1,0:T(8,128)(2,1)}, u32[]{:S(2)}) copy-start(bf16[4,64,576]{2,1,0:T(8,128)(2,1)} %cache_ref.1) | copy-start | bytes 884740
  49.6 29.3 %copy-start.14 = (bf16[2,4,576]{2,1,0:T(4,128)(2,1)S(1)}, bf16[2,4,576]{2,1,0:T(4,128)(2,1)}, u32[]{:S(2)}) copy-start(bf16[2,4,576]{2,1,0:T(4,128)(2,1)} %fresh_ref.1) | copy-start | bytes 27652
  49.7 29.3 %copy-start.16 = (s32[4]{0:T(128)S(1)}, s32[4]{0:T(128)}, u32[]{:S(2)}) copy-start(s32[4]{0:T(128)} %lengths_ref.1) | copy-start | bytes 52
  49.7 1.9 %collective-permute-start.8 = (bf16[32,7168]{1,0:T(8,128)(2,1)S(1)}, bf16[32,7168]{1,0:T(8,128)(2,1)S(1)}, u32[]{:S(2)}, u32[]{:S(2)}) collective-permute-start(bf16[32,7168]{1,0:T(8,128)(2,1)S(1)} %get-tuple-element.23), channel_id=1, source_target_pairs={{0,1},{1,0},{2,3},{3,2},{4,5},{5,4},{6,7},{7,6},{8,9},{9,8},{10,11... | collective-permute-start | bytes 1376264 | tf_op jit(solution)/shard_map/ppermute | solution.py:21
  50.0 12.9 %collective-permute-start.12 = (bf16[32,7168]{1,0:T(8,128)(2,1)S(1)}, bf16[32,7168]{1,0:T(8,128)(2,1)S(1)}, u32[]{:S(2)}, u32[]{:S(2)}) collective-permute-start(bf16[32,7168]{1,0:T(8,128)(2,1)S(1)} %add_convert_fusion.1), channel_id=1, source_target_pairs={{0,2},{1,3},{2,0},{3,1},{4,6},{5,7},{6,4},{7,5},{8,10},{9,11},{10,... | collective-permute-start | bytes 1376264 | tf_op jit(solution)/shard_map/ppermute | solution.py:21
  63.1 10.7 %collective-permute-start.13 = (bf16[8,7168]{1,0:T(8,128)(2,1)S(1)}, bf16[8,7168]{1,0:T(8,128)(2,1)S(1)}, u32[]{:S(2)}, u32[]{:S(2)}) collective-permute-start(bf16[8,7168]{1,0:T(8,128)(2,1)S(1)} %get-tuple-element.31), channel_id=1, source_target_pairs={{0,28},{1,25},{2,30},{3,27},{4,24},{5,29},{6,26},{7,31},{8,20},{9,... | collective-permute-start | bytes 344072 | tf_op jit(solution)/shard_map/ppermute | solution.py:21
  66.9 9.5 %collective-permute-start.14 = (bf16[8,7168]{1,0:T(8,128)(2,1)S(1)}, bf16[8,7168]{1,0:T(8,128)(2,1)S(1)}, u32[]{:S(2)}, u32[]{:S(2)}) collective-permute-start(bf16[8,7168]{1,0:T(8,128)(2,1)S(1)} %get-tuple-element.30), channel_id=1, source_target_pairs={{0,20},{1,17},{2,22},{3,19},{4,16},{5,21},{6,18},{7,23},{8,28},{9,... | collective-permute-start | bytes 344072 | tf_op jit(solution)/shard_map/ppermute | solution.py:21
  66.9 9.5 %collective-permute-start.15 = (bf16[8,7168]{1,0:T(8,128)(2,1)S(1)}, bf16[8,7168]{1,0:T(8,128)(2,1)S(1)}, u32[]{:S(2)}, u32[]{:S(2)}) collective-permute-start(bf16[8,7168]{1,0:T(8,128)(2,1)S(1)} %get-tuple-element.29), channel_id=1, source_target_pairs={{0,12},{1,9},{2,14},{3,11},{4,8},{5,13},{6,10},{7,15},{8,4},{9,1},... | collective-permute-start | bytes 344072 | tf_op jit(solution)/shard_map/ppermute | solution.py:21
  70.0 7.1 %collective-permute-start.16 = (bf16[8,7168]{1,0:T(8,128)(2,1)S(1)}, bf16[8,7168]{1,0:T(8,128)(2,1)S(1)}, u32[]{:S(2)}, u32[]{:S(2)}) collective-permute-start(bf16[8,7168]{1,0:T(8,128)(2,1)S(1)} %get-tuple-element.28), channel_id=1, source_target_pairs={{0,4},{1,1},{2,6},{3,3},{4,0},{5,5},{6,2},{7,7},{8,12},{9,9},{10,1... | collective-permute-start | bytes 344072 | tf_op jit(solution)/shard_map/ppermute | solution.py:21
  77.1 0.7 copy-start.11
  78.2 0.7 copy-start.9
  78.9 3.0 %collective-permute-start.17 = (bf16[8,7168]{1,0:T(8,128)(2,1)S(1)}, bf16[8,7168]{1,0:T(8,128)(2,1)S(1)}, u32[]{:S(2)}, u32[]{:S(2)}) collective-permute-start(bf16[8,7168]{1,0:T(8,128)(2,1)S(1)} %get-tuple-element.27), channel_id=1, source_target_pairs={{0,1},{1,0},{2,3},{3,2},{4,5},{5,4},{6,7},{7,6},{8,9},{9,8},{10,11... | collective-permute-start | bytes 344072 | tf_op jit(solution)/shard_map/ppermute | solution.py:21
  81.9 0.6 copy-start.17

commit v3 on v2

--- a/solution.py
+++ b/solution.py
@@ -14,6 +14,8 @@
 routed_scale = 2.5
 norm_eps = 1e-06
 masked_score = -1e30
+EXPERT_PARTS = 7
+MARK = jax.ShapeDtypeStruct((8, 128), jnp.float32)
 
 
 def flipped(value, low_core, high_core):
@@ -21,7 +23,8 @@
     return lax.ppermute(value, "ep", pairs)
 
 
-def attend_kernel(lengths_ref, query_ref, cache_ref, fresh_ref, out_ref):
+def attend_kernel(lengths_ref, query_ref, cache_ref, fresh_ref, out_ref, mark_ref):
+    mark_ref[...] = jnp.zeros(mark_ref.shape, mark_ref.dtype)
     steps, tokens, heads, _ = query_ref.shape
     slots = cache_ref.shape[1]
     pad = 128 - slots
@@ -60,9 +63,9 @@
     vmem = pl.BlockSpec(memory_space=pltpu.VMEM)
     return pl.pallas_call(
         attend_kernel,
-        out_shape=jax.ShapeDtypeStruct((steps, tokens, heads, KV), jnp.bfloat16),
+        out_shape=[jax.ShapeDtypeStruct((steps, tokens, heads, KV), jnp.bfloat16), MARK],
         in_specs=[pl.BlockSpec(memory_space=pltpu.SMEM)] + [vmem] * 3,
-        out_specs=vmem,
+        out_specs=[vmem] * 2,
         compiler_params=pltpu.CompilerParams(vmem_limit_bytes=12 << 20),
         cost_estimate=pl.CostEstimate(
             flops=4 * steps * tokens * heads * 128 * width,
@@ -73,46 +76,142 @@
     )(lengths, query, cache, fresh)
 
 
-def expert_kernel(mine_ref, other_ref, gate_ref, up_ref, down_ref, out_ref, send_ref, rows_v):
-    rows = mine_ref.shape[0]
-    depth, hidden_units = gate_ref.shape
-    rows_v[:rows, :] = mine_ref[...]
-    rows_v[rows:, :] = other_ref[...]
-    parts = 7
-    step = depth // parts
-    gate = jnp.zeros((2 * rows, hidden_units), jnp.float32)
-    upper = jnp.zeros((2 * rows, hidden_units), jnp.float32)
-    for i in range(parts):
+def load_kernel(gate_ref, up_ref, down_ref, _, gate_v, up_v, down_v, mark_ref, sems):
+    copies = [
+        pltpu.make_async_copy(source, target, sems.at[i])
+        for i, (source, target) in enumerate(
+            ((gate_ref, gate_v), (up_ref, up_v), (down_ref, down_v))
+        )
+    ]
+    for copy in copies:
+        copy.start()
+    mark_ref[...] = jnp.zeros(mark_ref.shape, mark_ref.dtype)
+    for copy in copies:
+        copy.wait()
+
+
+def load(weights, earlier):
+    vmem = pl.BlockSpec(memory_space=pltpu.VMEM)
+    anywhere = pl.BlockSpec(memory_space=pl.ANY)
+    *held, mark = pl.pallas_call(
+        load_kernel,
+        out_shape=[jax.ShapeDtypeStruct(w.shape, w.dtype) for w in weights] + [MARK],
+        in_specs=[anywhere] * 4,
+        out_specs=[vmem] * 4,
+        scratch_shapes=[pltpu.SemaphoreType.DMA((3,))],
+        compiler_params=pltpu.CompilerParams(vmem_limit_bytes=40 << 20),
+        name="load",
+    )(*weights, earlier)
+    return held, mark
+
+
+def expert_kernel(count, *refs):
+    part_refs, refs = refs[:count], refs[count:]
+    gate_ref, up_ref, down_ref, _, *out_refs, mark_ref, rows_v = refs
+    size = out_refs[0].shape[0]
+    step = rows_v.shape[1] // EXPERT_PARTS
+    rows = part_refs[0].shape[0]
+    for i, ref in enumerate(part_refs):
+        rows_v[i * rows : (i + 1) * rows, :] = ref[...]
+    mark_ref[...] = jnp.zeros(mark_ref.shape, mark_ref.dtype)
+    gate, upper = 0.0, 0.0
+    for i in range(EXPERT_PARTS):
         ds = pl.ds(i * step, step)
         x = rows_v[:, ds]
-        gate += jnp.dot(x, gate_ref[ds, :], preferred_element_type=jnp.float32)
-        upper += jnp.dot(x, up_ref[ds, :], preferred_element_type=jnp.float32)
+        gate = gate + jnp.dot(x, gate_ref[ds, :], preferred_element_type=jnp.float32)
+        upper = upper + jnp.dot(x, up_ref[ds, :], preferred_element_type=jnp.float32)
     inner = (gate / (1.0 + jnp.exp(-gate)) * upper).astype(jnp.bfloat16)
-    for i in range(parts):
+    for i in range(EXPERT_PARTS):
         ds = pl.ds(i * step, step)
         partial = jnp.dot(inner, down_ref[:, ds], preferred_element_type=jnp.float32)
-        out_ref[:, ds] = partial[:rows].astype(jnp.bfloat16)
-        send_ref[:, ds] = partial[rows:].astype(jnp.bfloat16)
-
-
-def experts(mine, other, gate_w, up_w, down_w):
-    rows, depth = mine.shape
-    hidden_units = gate_w.shape[1]
-    vmem = pl.BlockSpec(memory_space=pltpu.VMEM)
-    return pl.pallas_call(
-        expert_kernel,
-        out_shape=[jax.ShapeDtypeStruct((rows, depth), jnp.bfloat16)] * 2,
-        in_specs=[vmem] * 5,
-        out_specs=[vmem] * 2,
-        scratch_shapes=[pltpu.VMEM((2 * rows, depth), jnp.bfloat16)],
-        compiler_params=pltpu.CompilerParams(vmem_limit_bytes=(16 << 20) + rows * depth * 24),
-        cost_estimate=pl.CostEstimate(
-            flops=12 * rows * depth * hidden_units,
-            bytes_accessed=6 * depth * hidden_units + 8 * rows * depth,
-            transcendentals=2 * rows * hidden_units,
+        for j, ref in enumerate(out_refs):
+            ref[:, ds] = partial[j * size : (j + 1) * size].astype(jnp.bfloat16)
+
+
+def experts(parts, weights, earlier, size):
+    rows, depth = parts[0].shape
+    count = len(parts)
+    outs = count * rows // size
+    vmem = pl.BlockSpec(memory_space=pltpu.VMEM)
+    out = pl.pallas_call(
+        functools.partial(expert_kernel, count),
+        out_shape=[jax.ShapeDtypeStruct((size, depth), jnp.bfloat16)] * outs + [MARK],
+        in_specs=[vmem] * (count + 3) + [pl.BlockSpec(memory_space=pl.ANY)],
+        out_specs=[vmem] * (outs + 1),
+        scratch_shapes=[pltpu.VMEM((count * rows, depth), jnp.bfloat16)],
+        compiler_params=pltpu.CompilerParams(
+            vmem_limit_bytes=(16 << 20) + count * rows * depth * 8
         ),
         name="experts",
-    )(mine, other, gate_w, up_w, down_w)
+    )(*parts, *weights, earlier)
+    return out[:outs], out[outs]
+
+
+def join_kernel(count, *refs):
+    out_ref = refs[-1]
+    rows, depth = out_ref.shape
+    step = depth // EXPERT_PARTS
+    for i in range(EXPERT_PARTS):
+        ds = pl.ds(i * step, step)
+        joined = jnp.concatenate([ref[:, ds].astype(jnp.float32) for ref in refs[:count]], axis=0)
+        out_ref[:, ds] = joined.astype(jnp.bfloat16)
+
+
+def join(parts, earlier):
+    depth = parts[0].shape[1]
+    rows = sum(part.shape[0] for part in parts)
+    vmem = pl.BlockSpec(memory_space=pltpu.VMEM)
+    return pl.pallas_call(
+        functools.partial(join_kernel, len(parts)),
+        out_shape=jax.ShapeDtypeStruct((rows, depth), jnp.bfloat16),
+        in_specs=[vmem] * len(parts) + [pl.BlockSpec(memory_space=pl.ANY)] * len(earlier),
+        out_specs=vmem,
+        compiler_params=pltpu.CompilerParams(vmem_limit_bytes=(2 << 20) + 8 * rows * depth),
+        name="join",
+    )(*parts, *earlier)
+
+
+def after_kernel(value_ref, earlier_ref, out_ref):
+    out_ref[...] = value_ref[...]
+
+
+def after(value, earlier):
+    vmem = pl.BlockSpec(memory_space=pltpu.VMEM)
+    return pl.pallas_call(
+        after_kernel,
+        out_shape=jax.ShapeDtypeStruct(value.shape, value.dtype),
+        in_specs=[vmem, pl.BlockSpec(memory_space=pl.ANY)],
+        out_specs=vmem,
+        compiler_params=pltpu.CompilerParams(vmem_limit_bytes=(2 << 20) + 6 * value.size),
+        name="after",
+    )(value, earlier)
+
+
+def add_kernel(count, messages, *refs):
+    terms, part_refs = refs[:count], refs[-messages:]
+    depth = terms[0].shape[1]
+    size = part_refs[0].shape[0]
+    step = depth // EXPERT_PARTS
+    for i in range(EXPERT_PARTS):
+        ds = pl.ds(i * step, step)
+        total = terms[0][:, ds].astype(jnp.float32)
+        for ref in terms[1:]:
+            total = total + ref[:, ds].astype(jnp.float32)
+        for m, ref in enumerate(part_refs):
+            ref[:, ds] = total[m * size : (m + 1) * size].astype(jnp.bfloat16)
+
+
+def add(terms, messages, earlier):
+    rows, depth = terms[0].shape
+    vmem = pl.BlockSpec(memory_space=pltpu.VMEM)
+    return pl.pallas_call(
+        functools.partial(add_kernel, len(terms), messages),
+        out_shape=[jax.ShapeDtypeStruct((rows // messages, depth), jnp.bfloat16)] * messages,
+        in_specs=[vmem] * len(terms) + [pl.BlockSpec(memory_space=pl.ANY)] * len(earlier),
+        out_specs=[vmem] * messages,
+        compiler_params=pltpu.CompilerParams(vmem_limit_bytes=(4 << 20) + 16 * rows * depth),
+        name="add",
+    )(*terms, *earlier)
 
 
 def pack_kernel(
@@ -133,7 +232,7 @@
 ):
     message_refs, raw_v = refs[:-1], refs[-1]
     steps, tokens, depth = raw_ref.shape
-    top = ids_ref.shape[2]
+    top = ids_ref.shape[1]
     index = lax.axis_index("ep")
     core = lax.rem(index, 2)
     group = lax.div(index, SPAN)
@@ -161,7 +260,7 @@
             earlier = []
             for t in range(tokens):
                 for k in range(top):
-                    copy = table_ref[ids[s, t, k], replicas[s, t, k]]
+                    copy = table_ref[replicas[s, k, t], ids[s, k, t]]
                     slot = sum([(copy == c).astype(jnp.int32) for c in earlier], jnp.int32(0))
                     earlier.append(copy)
                     delta = copy ^ group
@@ -170,7 +269,7 @@
                     at = jnp.where(kept, at, -1)
                     here = block * tokens + t
                     place_row[k] = jnp.where(column == here, at, place_row[k])
-                    choice[k] = jnp.where(token == here, ids[s, t, k], choice[k])
+                    choice[k] = jnp.where(token == here, ids[s, k, t], choice[k])
     total = jnp.zeros(place_ref.shape[1:], jnp.float32)
     for k in range(top):
         hit = (place_row[k] == row).astype(jnp.float32)
@@ -184,7 +283,7 @@
 
 def pack(slots, groups, hidden, other, gain, copy_table, own_choice, other_choice, experts_total):
     steps, tokens, depth = hidden.shape
-    top = own_choice[0].shape[2]
+    top = own_choice[0].shape[1]
     messages = groups // 2
     message_rows = 2 * steps * slots
     columns = 2 * steps * tokens
@@ -203,7 +302,7 @@
         out_specs=[vmem] * (3 + messages),
         scratch_shapes=[pltpu.VMEM((columns, depth), jnp.float32)],
         compiler_params=pltpu.CompilerParams(
-            vmem_limit_bytes=(8 << 20) + 4 * messages * message_rows * depth * 2
+            vmem_limit_bytes=62 << 20
         ),
         name="pack",
     )(copy_table, *own_choice, *other_choice, hidden, other, gain)
@@ -238,6 +337,7 @@
         cost_estimate=pl.CostEstimate(
             flops=2 * normed.size * 256, bytes_accessed=2 * normed.size, transcendentals=256
         ),
+        compiler_params=pltpu.CompilerParams(vmem_limit_bytes=4 << 20),
         name="weigh",
     )(normed, router_t, place, choose)
 
@@ -294,11 +394,14 @@
         out_shape=jax.ShapeDtypeStruct(shape, jnp.bfloat16),
         in_specs=[vmem] * 2,
         out_specs=vmem,
+        compiler_params=pltpu.CompilerParams(vmem_limit_bytes=4 << 20),
         name="finish",
     )(own, received)
 
 
-def mixture(hidden, norm_gain, router, expert_ids, replica, copy_table, gate_w, up_w, down_w):
+def mixture(
+    hidden, norm_gain, router, expert_ids, replica, copy_table, gate_w, up_w, down_w, attended_mark
+):
     groups = lax.axis_size("ep") // SPAN
     messages = groups // 2
     tokens = hidden.shape[1]
@@ -308,15 +411,16 @@
     def swapped(value):
         return flipped(value, 1, 1)
 
-    other_choice = (swapped(expert_ids), swapped(replica))
+    own_choice = (expert_ids.transpose(0, 2, 1), replica.transpose(0, 2, 1))
+    other_choice = (swapped(own_choice[0]), swapped(own_choice[1]))
     normed, place, choose, packed = pack(
         slots,
         groups,
         hidden,
         swapped(hidden),
         norm_gain[None, :],
-        copy_table,
-        (expert_ids, replica),
+        copy_table.T,
+        own_choice,
         other_choice,
         router.shape[1],
     )
@@ -326,17 +430,25 @@
             flipped(part, SPAN * low, SPAN * high) for part, (low, high) in zip(parts, deltas)
         ]
 
-    near = jnp.concatenate(rounds(packed), axis=0)
     weights = weigh(normed, router.T, place, choose)
+    expert_weights = (gate_w, up_w, down_w)
+    half = messages // 2
+    size = packed[0].shape[0]
+    received = rounds(packed)
+    held, mark = load(expert_weights, place)
+    near = join(received, [mark])
     far = flipped(near, 2, 2)
-    near_own, near_send = experts(near, swapped(near), gate_w, up_w, down_w)
-    near_sum = near_own.astype(jnp.float32) + swapped(near_send).astype(jnp.float32)
-    far_own, far_send = experts(far, swapped(far), gate_w, up_w, down_w)
-    far_sum = far_own.astype(jnp.float32) + swapped(far_send).astype(jnp.float32)
-    total = near_sum + flipped(far_sum.astype(jnp.bfloat16), 2, 2).astype(jnp.float32)
-    total = total.astype(jnp.bfloat16)
-    size = total.shape[0] // messages
-    returned = rounds([total[m * size : (m + 1) * size] for m in range(messages)])
+    near_out, mark = experts([near, swapped(near)], held, mark, half * size)
+    far_out, mark = experts([far, swapped(after(far, mark))], held, mark, half * size)
+    (far_sum_a,) = add([far_out[0], swapped(far_out[2])], 1, [])
+    (far_sum_b,) = add([far_out[1], swapped(far_out[3])], 1, [])
+    total_a = add(
+        [near_out[0], swapped(near_out[2]), flipped(far_sum_a, 2, 2)],
+        half,
+        [mark, weights, attended_mark],
+    )
+    total_b = add([near_out[1], swapped(near_out[3]), flipped(far_sum_b, 2, 2)], half, [total_a[0]])
+    returned = rounds([*total_a, *total_b])
     own, send = combine(weights, returned)
     return finish(own, swapped(send), hidden.shape)
 
@@ -356,10 +468,19 @@
     lengths,
     fresh_kv,
 ):
+    attended, attended_mark = attend(query, cache, lengths, fresh_kv)
     moe_out = mixture(
-        hidden, norm_gain, router, expert_ids, replica, copy_table, gate_w, up_w, down_w
+        hidden,
+        norm_gain,
+        router,
+        expert_ids,
+        replica,
+        copy_table,
+        gate_w,
+        up_w,
+        down_w,
+        attended_mark,
     )
-    attended = attend(query, cache, lengths, fresh_kv)
     return (attended, moe_out)
 
 

time: 84.8 us -> 68.1 us (0.80)
  local copies, waits for them, and re-layouts: 16 us -> 1.44 us
  waiting for transfers between devices: 30.9 us -> 23.6 us
  starting transfers between devices: 23.7 us -> 26.6 us
  Pallas kernels: 12.5 us -> 15.4 us
    unnamed x42 -> x22, local copies, waits for them, and re-layouts: 15.9 us -> 1.44 us
    ppermute x18 -> x21, waiting for transfers between devices: 30.9 us -> 23.6 us  [flipped(): return lax.ppermute(value, 'ep', pairs)]
    pallas_call x3 -> x10, Pallas kernels: 7.18 us -> 11.8 us  [the longest x2 4.26 us: experts(): pl.pallas_call(functools.partial(expert_kernel, count), out_shape=[jax.Sh...]
    ppermute x18 -> x21, starting transfers between devices: 23.7 us -> 26.6 us  [flipped(): return lax.ppermute(value, 'ep', pairs)]
    pallas_call x1, Pallas kernels: 1.83 us -> 0.22 us  [weigh(): pl.pallas_call(weigh_kernel, out_shape=jax.ShapeDtypeStruct(place.shape[1...]
    pallas_call x1, Pallas kernels: 1.69 us -> 0.68 us  [finish(): pl.pallas_call(finish_kernel, out_shape=jax.ShapeDtypeStruct(shape, jnp.b...]
  transfers between devices with their start and end apart: 18 -> 21, of which waited for: 8 -> 12; matrix products, arithmetic and copies ran while one was open for 3% -> 0% of each run, Pallas kernels for 11% -> 15%
where the time goes in v3:
time: 68.1 us; the launch traced here: 67.8 us
  starting transfers between devices  26.6 us (39%)
  waiting for transfers between devices  23.6 us (35%)
  Pallas kernels  15.4 us (23%)
  local copies, waits for them, and re-layouts  1.44 us (2%)
  between operations  0.84 us (1%)
    ppermute x21, starting transfers between devices, flipped(): return lax.ppermute(value, 'ep', pairs)  26.6 us
    ppermute x21, waiting for transfers between devices, flipped(): return lax.ppermute(value, 'ep', pairs)  23.6 us
    pallas_call x2, Pallas kernels, experts(): pl.pallas_call(functools.partial(expert_kernel, count), out_shape=[jax.Sh...  4.26 us
    pallas_call x1, Pallas kernels, load(): pl.pallas_call(load_kernel, out_shape=[jax.ShapeDtypeStruct(w.shape, w.dt...  4.23 us
    pallas_call x1, Pallas kernels, attend(): pl.pallas_call(attend_kernel, out_shape=[jax.ShapeDtypeStruct((steps, tok...  2.97 us
    pallas_call x1, Pallas kernels, pack(): pl.pallas_call(functools.partial(pack_kernel, slots, groups), out_shape=[...  2.29 us
    unnamed x22, local copies, waits for them, and re-layouts  1.44 us
  transfers between devices with their start and end apart: 21, of which 12 were waited for; matrix products, arithmetic and copies ran while one was open for 0% of the time, Pallas kernels for 15%

profile of v3, /device:TPU:0, one launch (start us, length us, event | category | flops | bytes accessed | tf_op | source)
XLA Modules:
  0.0 67.8 jit_solution(11353763530565114818)
XLA Ops:
  0.6 0.5 collective-permute-start.2
  1.1 0.1 collective-permute-start
  1.2 0.4 collective-permute-start.1
  1.7 0.9 %collective-permute-done.other_ids_ref = s32[2,2,4]{2,1,0:T(2,128)S(1)} collective-permute-done((s32[2,2,4]{2,1,0:T(2,128)}, s32[2,2,4]{2,1,0:T(2,128)S(1)}, u32[]{:S(2)}, u32[]{:S(2)}) %collective-permute-start) | collective-permute-done | bytes 96 | tf_op jit(solution)/shard_map/ppermute | solution.py:23
  2.5 0.2 collective-permute-done.1.other_replica_ref
  2.7 0.0 collective-permute-done.2.other_ref
  2.7 0.4 copy-done.9
  3.1 0.2 copy-done.10
  3.3 0.1 copy-done.8
  3.3 2.3 %pack.1 = (bf16[16,7168]{1,0:T(8,128)(2,1)}, f32[2,32,16]{2,1,0:T(8,128)}, f32[2,6,16]{2,1,0:T(8,128)}, bf16[8,7168]{1,0:T(8,128)(2,1)}, bf16[8,7168]{1,0:T(8,12...) custom-call(s32[2,6]{1,0:T(2,128)} %bitcast.11, s32[2,2,4]{2,1,0:T(2,128)} %bitcast.8, s32[2,2,4]{2,1,0:T(2,128)} %bitcast.10, ...), custom_call_target="tpu_custom_call" | custom-call | tf_op jit(solution)/shard_map/pack/pallas_call | solution.py:293
  5.6 5.9 %collective-permute-start.3 = (bf16[8,7168]{1,0:T(8,128)(2,1)}, bf16[8,7168]{1,0:T(8,128)(2,1)S(1)}, u32[]{:S(2)}, u32[]{:S(2)}) collective-permute-start(bf16[8,7168]{1,0:T(8,128)(2,1)} %get-tuple-element.35), channel_id=1, source_target_pairs={{0,28},{1,25},{2,30},{3,27},{4,24},{5,29},{6,26},{7,31},{8,20},{9,... | collective-permute-start | bytes 344072 | tf_op jit(solution)/shard_map/ppermute | solution.py:23
  11.5 0.0 collective-permute-start.4
  11.5 1.7 %collective-permute-start.5 = (bf16[8,7168]{1,0:T(8,128)(2,1)}, bf16[8,7168]{1,0:T(8,128)(2,1)S(1)}, u32[]{:S(2)}, u32[]{:S(2)}) collective-permute-start(bf16[8,7168]{1,0:T(8,128)(2,1)} %get-tuple-element.37), channel_id=1, source_target_pairs={{0,12},{1,9},{2,14},{3,11},{4,8},{5,13},{6,10},{7,15},{8,4},{9,1},... | collective-permute-start | bytes 344072 | tf_op jit(solution)/shard_map/ppermute | solution.py:23
  13.2 2.3 %collective-permute-start.6 = (bf16[8,7168]{1,0:T(8,128)(2,1)}, bf16[8,7168]{1,0:T(8,128)(2,1)S(1)}, u32[]{:S(2)}, u32[]{:S(2)}) collective-permute-start(bf16[8,7168]{1,0:T(8,128)(2,1)} %get-tuple-element.38), channel_id=1, source_target_pairs={{0,4},{1,1},{2,6},{3,3},{4,0},{5,5},{6,2},{7,7},{8,12},{9,9},{10,1... | collective-permute-start | bytes 344072 | tf_op jit(solution)/shard_map/ppermute | solution.py:23
  15.5 0.7 %copy-done.3 = f32[2,32,16]{2,1,0:T(8,128)S(1)} copy-done((f32[2,32,16]{2,1,0:T(8,128)S(1)}, f32[2,32,16]{2,1,0:T(8,128)}, u32[]{:S(2)}) %copy-start.3) | copy-done | bytes 4120
  16.3 4.2 %load.1 = (bf16[7168,256]{1,0:T(8,128)(2,1)S(1)}, bf16[7168,256]{1,0:T(8,128)(2,1)S(1)}, bf16[256,7168]{1,0:T(8,128)(2,1)S(1)}, f32[8,128]{1,0:T(8,128)S(1)}) custom-call(bf16[7168,256]{1,0:T(8,128)(2,1)} %gate_ref.1, bf16[7168,256]{1,0:T(8,128)(2,1)} %up_ref.1, bf16[256,7168]{1,0:T(8,128)(2,1)} %down_ref.1, f32[2,32,16]{2,1,0:T(8,128)S(1)} %copy-done.3), custom_call_target="tpu_custom_call" | custom-call | tf_op jit(solution)/shard_map/load/pallas_call | solution.py:96
  20.5 0.0 collective-permute-done.3.refs_0_
  20.5 1.2 %collective-permute-done.4.refs_1_ = bf16[8,7168]{1,0:T(8,128)(2,1)S(1)} collective-permute-done((bf16[8,7168]{1,0:T(8,128)(2,1)}, bf16[8,7168]{1,0:T(8,128)(2,1)S(1)}, u32[]{:S(2)}, u32[]{:S(2)}) %collective-permute-start.4) | collective-permute-done | bytes 114720 | tf_op jit(solution)/shard_map/ppermute | solution.py:23
  21.8 0.0 collective-permute-done.5.refs_2_
  21.8 0.0 collective-permute-done.6.refs_3_
  21.8 0.1 collective-permute-start.7
  21.9 1.6 %collective-permute-start.9 = (bf16[32,7168]{1,0:T(8,128)(2,1)S(1)}, bf16[32,7168]{1,0:T(8,128)(2,1)S(1)}, u32[]{:S(2)}, u32[]{:S(2)}) collective-permute-start(bf16[32,7168]{1,0:T(8,128)(2,1)S(1)} %join.1.refs_0_), channel_id=1, source_target_pairs={{0,2},{1,3},{2,0},{3,1},{4,6},{5,7},{6,4},{7,5},{8,10},{9,11},{10,... | collective-permute-start | bytes 1376264 | tf_op jit(solution)/shard_map/ppermute | solution.py:23
  23.4 0.2 collective-permute-done.7.refs_1_
  23.7 2.1 %experts.2 = (bf16[16,7168]{1,0:T(8,128)(2,1)S(1)}, bf16[16,7168]{1,0:T(8,128)(2,1)S(1)}, bf16[16,7168]{1,0:T(8,128)(2,1)S(1)}, bf16[16,7168]{1,0:T(8,128)(2,1)S(1)}, f32[8,128]{1,0:T(8,128)S(1)}) custom-call(bf16[32,7168]{1,0:T(8,128)(2,1)S(1)} %join.1.refs_0_, bf16[32,7168]{1,0:T(8,128)(2,1)S(1)} %collective-permute-done.7.refs_1_, ...), custom_call_target="tpu_custom_call" | custom-call | tf_op jit(solution)/shard_map/experts/pallas_call | solution.py:136
  25.8 9.0 %collective-permute-done.9.value_ref.refs_0_ = bf16[32,7168]{1,0:T(8,128)(2,1)S(1)} collective-permute-done((bf16[32,7168]{1,0:T(8,128)(2,1)S(1)}, bf16[32,7168]{1,0:T(8,128)(2,1)S(1)}, u32[]{:S(2)}, u32[]{:S(2)}) %collective-permute-start.9) | collective-permute-done | bytes 458784 | tf_op jit(solution)/shard_map/ppermute | solution.py:23
  34.8 0.0 copy-start
  34.9 0.0 copy-start.1
  34.9 0.0 copy-start.5
  34.9 0.0 copy-start.7
  34.9 0.0 copy-start.2
  34.9 0.0 copy-start.4
  34.9 0.1 collective-permute-start.10
  35.0 1.8 %collective-permute-done.10.refs_1_ = bf16[32,7168]{1,0:T(8,128)(2,1)S(1)} collective-permute-done((bf16[32,7168]{1,0:T(8,128)(2,1)S(1)}, bf16[32,7168]{1,0:T(8,128)(2,1)S(1)}, u32[]{:S(2)}, u32[]{:S(2)}) %collective-permute-start.10) | collective-permute-done | bytes 458784 | tf_op jit(solution)/shard_map/ppermute | solution.py:23
  36.8 2.1 %experts.3 = (bf16[16,7168]{1,0:T(8,128)(2,1)S(1)}, bf16[16,7168]{1,0:T(8,128)(2,1)S(1)}, bf16[16,7168]{1,0:T(8,128)(2,1)S(1)}, bf16[16,7168]{1,0:T(8,128)(2,1)S(1)}, f32[8,128]{1,0:T(8,128)S(1)}) custom-call(bf16[32,7168]{1,0:T(8,128)(2,1)S(1)} %collective-permute-done.9.value_ref.refs_0_, bf16[32,7168]{1,0:T(8,128)(2,1)S(1)} %collective-permute-done.10.refs_1_, ...), custom_call_target="tpu_custom_call" | custom-call | tf_op jit(solution)/shard_map/experts/pallas_call | solution.py:136
  38.9 0.2 collective-permute-start.11
  39.1 0.4 collective-permute-start.16
  39.5 0.1 collective-permute-start.8
  39.7 0.8 %collective-permute-done.11.refs_1_ = bf16[16,7168]{1,0:T(8,128)(2,1)S(1)} collective-permute-done((bf16[16,7168]{1,0:T(8,128)(2,1)S(1)}, bf16[16,7168]{1,0:T(8,128)(2,1)S(1)}, u32[]{:S(2)}, u32[]{:S(2)}) %collective-permute-start.11) | collective-permute-done | bytes 229408 | tf_op jit(solution)/shard_map/ppermute | solution.py:23
  40.5 0.1 add.4
  40.6 1.6 %collective-permute-start.12 = (bf16[16,7168]{1,0:T(8,128)(2,1)S(1)}, bf16[16,7168]{1,0:T(8,128)(2,1)S(1)}, u32[]{:S(2)}, u32[]{:S(2)}) collective-permute-start(bf16[16,7168]{1,0:T(8,128)(2,1)S(1)} %add.4), channel_id=1, source_target_pairs={{0,2},{1,3},{2,0},{3,1},{4,6},{5,7},{6,4},{7,5},{8,10},{9,11},{10,... | collective-permute-start | bytes 688136 | tf_op jit(solution)/shard_map/ppermute | solution.py:23
  42.1 0.0 collective-permute-start.15
  42.1 0.0 collective-permute-done.16.refs_1_
  42.1 0.1 add.6
  42.2 0.6 collective-permute-start.17
  42.8 3.0 %attention.1 = (bf16[2,4,64,512]{3,2,1,0:T(8,128)(2,1)}, f32[8,128]{1,0:T(8,128)S(1)}) custom-call(s32[4]{0:T(128)S(1)} %copy-done.7, bf16[2,4,64,576]{3,2,1,0:T(8,128)(2,1)S(1)} %copy-done, bf16[4,64,576]{2,1,0:T(8,128)(2,1)S(1)} %copy-done.1, bf16[2,4,576]{2,1,0:T(4,128)(2,1)S(1)} %copy-done.5), custom_call_target="tpu_custom_call" | custom-call | flops 150994944 | bytes 1474560 | tf_op jit(solution)/shard_map/attention/pallas_call | solution.py:64
  45.8 0.2 weigh.1.refs_4_.weigh_ref
  46.0 0.0 collective-permute-done.8.refs_1_
  46.0 3.1 %collective-permute-done.12.refs_2_ = bf16[16,7168]{1,0:T(8,128)(2,1)S(1)} collective-permute-done((bf16[16,7168]{1,0:T(8,128)(2,1)S(1)}, bf16[16,7168]{1,0:T(8,128)(2,1)S(1)}, u32[]{:S(2)}, u32[]{:S(2)}) %collective-permute-start.12) | collective-permute-done | bytes 229408 | tf_op jit(solution)/shard_map/ppermute | solution.py:23
  49.1 0.1 add.5
  49.2 3.5 %collective-permute-start.13 = (bf16[8,7168]{1,0:T(8,128)(2,1)S(1)}, bf16[8,7168]{1,0:T(8,128)(2,1)S(1)}, u32[]{:S(2)}, u32[]{:S(2)}) collective-permute-start(bf16[8,7168]{1,0:T(8,128)(2,1)S(1)} %get-tuple-element.50.refs_3_), channel_id=1, source_target_pairs={{0,28},{1,25},{2,30},{3,27},{4,24},{5,29},{6,26},{7,31},{8,20},{9,... | collective-permute-start | bytes 344072 | tf_op jit(solution)/shard_map/ppermute | solution.py:23
  52.7 0.0 collective-permute-done.15.refs_1_
  52.7 0.5 collective-permute-done.17.refs_2_
  53.2 0.1 add.7
  53.3 1.2 %collective-permute-start.18 = (bf16[8,7168]{1,0:T(8,128)(2,1)S(1)}, bf16[8,7168]{1,0:T(8,128)(2,1)S(1)}, u32[]{:S(2)}, u32[]{:S(2)}) collective-permute-start(bf16[8,7168]{1,0:T(8,128)(2,1)S(1)} %get-tuple-element.56), channel_id=1, source_target_pairs={{0,12},{1,9},{2,14},{3,11},{4,8},{5,13},{6,10},{7,15},{8,4},{9,1},... | collective-permute-start | bytes 344072 | tf_op jit(solution)/shard_map/ppermute | solution.py:23
  54.5 3.0 %collective-permute-start.19 = (bf16[8,7168]{1,0:T(8,128)(2,1)S(1)}, bf16[8,7168]{1,0:T(8,128)(2,1)S(1)}, u32[]{:S(2)}, u32[]{:S(2)}) collective-permute-start(bf16[8,7168]{1,0:T(8,128)(2,1)S(1)} %get-tuple-element.57), channel_id=1, source_target_pairs={{0,4},{1,1},{2,6},{3,3},{4,0},{5,5},{6,2},{7,7},{8,12},{9,9},{10,1... | collective-permute-start | bytes 344072 | tf_op jit(solution)/shard_map/ppermute | solution.py:23
  57.5 3.3 %collective-permute-start.14 = (bf16[8,7168]{1,0:T(8,128)(2,1)S(1)}, bf16[8,7168]{1,0:T(8,128)(2,1)S(1)}, u32[]{:S(2)}, u32[]{:S(2)}) collective-permute-start(bf16[8,7168]{1,0:T(8,128)(2,1)S(1)} %get-tuple-element.51), channel_id=1, source_target_pairs={{0,20},{1,17},{2,22},{3,19},{4,16},{5,21},{6,18},{7,23},{8,28},{9,... | collective-permute-start | bytes 344072 | tf_op jit(solution)/shard_map/ppermute | solution.py:23
  60.8 0.0 collective-permute-done.18.refs_2_
  60.8 0.5 collective-permute-done.19.refs_3_
  61.3 0.0 collective-permute-done.13.refs_0_
  61.3 4.0 %collective-permute-done.14.refs_1_ = bf16[8,7168]{1,0:T(8,128)(2,1)S(1)} collective-permute-done((bf16[8,7168]{1,0:T(8,128)(2,1)S(1)}, bf16[8,7168]{1,0:T(8,128)(2,1)S(1)}, u32[]{:S(2)}, u32[]{:S(2)}) %collective-permute-start.14) | collective-permute-done | bytes 114720 | tf_op jit(solution)/shard_map/ppermute | solution.py:23
  65.3 0.4 combine.1
  65.7 0.1 collective-permute-start.20
  65.8 1.3 %collective-permute-done.20.received_ref = bf16[8,7168]{1,0:T(8,128)(2,1)S(1)} collective-permute-done((bf16[8,7168]{1,0:T(8,128)(2,1)S(1)}, bf16[8,7168]{1,0:T(8,128)(2,1)S(1)}, u32[]{:S(2)}, u32[]{:S(2)}) %collective-permute-start.20) | collective-permute-done | bytes 114720 | tf_op jit(solution)/shard_map/ppermute | solution.py:23
  67.1 0.7 finish.1
  (14 shorter events, 0.1 us)
Async XLA Ops:
  0.6 2.1 %collective-permute-start.2 = (bf16[2,4,7168]{2,1,0:T(4,128)(2,1)}, bf16[2,4,7168]{2,1,0:T(4,128)(2,1)S(1)}, u32[]{:S(2)}, u32[]{:S(2)}) collective-permute-start(bf16[2,4,7168]{2,1,0:T(4,128)(2,1)} %raw_ref.1), channel_id=1, source_target_pairs={{0,1},{1,0},{2,3},{3,2},{4,5},{5,4},{6,7},{7,6},{8,9},{9,8},{10,11... | collective-permute-start | bytes 344072 | tf_op jit(solution)/shard_map/ppermute | solution.py:23
  1.1 1.4 %collective-permute-start = (s32[2,2,4]{2,1,0:T(2,128)}, s32[2,2,4]{2,1,0:T(2,128)S(1)}, u32[]{:S(2)}, u32[]{:S(2)}) collective-permute-start(s32[2,2,4]{2,1,0:T(2,128)} %bitcast.7), channel_id=1, source_target_pairs={{0,1},{1,0},{2,3},{3,2},{4,5},{5,4},{6,7},{7,6},{8,9},{9,8},{10,11... | collective-permute-start | bytes 200 | tf_op jit(solution)/shard_map/ppermute | solution.py:23
  1.2 1.5 %collective-permute-start.1 = (s32[2,2,4]{2,1,0:T(2,128)}, s32[2,2,4]{2,1,0:T(2,128)S(1)}, u32[]{:S(2)}, u32[]{:S(2)}) collective-permute-start(s32[2,2,4]{2,1,0:T(2,128)} %bitcast.9), channel_id=1, source_target_pairs={{0,1},{1,0},{2,3},{3,2},{4,5},{5,4},{6,7},{7,6},{8,9},{9,8},{10,11... | collective-permute-start | bytes 200 | tf_op jit(solution)/shard_map/ppermute | solution.py:23
  2.5 0.6 copy-start.9
  2.7 0.6 copy-start.10
  2.7 0.6 copy-start.8
  5.6 14.9 %collective-permute-start.3 = (bf16[8,7168]{1,0:T(8,128)(2,1)}, bf16[8,7168]{1,0:T(8,128)(2,1)S(1)}, u32[]{:S(2)}, u32[]{:S(2)}) collective-permute-start(bf16[8,7168]{1,0:T(8,128)(2,1)} %get-tuple-element.35), channel_id=1, source_target_pairs={{0,28},{1,25},{2,30},{3,27},{4,24},{5,29},{6,26},{7,31},{8,20},{9,... | collective-permute-start | bytes 344072 | tf_op jit(solution)/shard_map/ppermute | solution.py:23
  11.5 10.2 %collective-permute-start.4 = (bf16[8,7168]{1,0:T(8,128)(2,1)}, bf16[8,7168]{1,0:T(8,128)(2,1)S(1)}, u32[]{:S(2)}, u32[]{:S(2)}) collective-permute-start(bf16[8,7168]{1,0:T(8,128)(2,1)} %get-tuple-element.36), channel_id=1, source_target_pairs={{0,20},{1,17},{2,22},{3,19},{4,16},{5,21},{6,18},{7,23},{8,28},{9,... | collective-permute-start | bytes 344072 | tf_op jit(solution)/shard_map/ppermute | solution.py:23
  11.5 10.2 %collective-permute-start.5 = (bf16[8,7168]{1,0:T(8,128)(2,1)}, bf16[8,7168]{1,0:T(8,128)(2,1)S(1)}, u32[]{:S(2)}, u32[]{:S(2)}) collective-permute-start(bf16[8,7168]{1,0:T(8,128)(2,1)} %get-tuple-element.37), channel_id=1, source_target_pairs={{0,12},{1,9},{2,14},{3,11},{4,8},{5,13},{6,10},{7,15},{8,4},{9,1},... | collective-permute-start | bytes 344072 | tf_op jit(solution)/shard_map/ppermute | solution.py:23
  13.2 8.5 %collective-permute-start.6 = (bf16[8,7168]{1,0:T(8,128)(2,1)}, bf16[8,7168]{1,0:T(8,128)(2,1)S(1)}, u32[]{:S(2)}, u32[]{:S(2)}) collective-permute-start(bf16[8,7168]{1,0:T(8,128)(2,1)} %get-tuple-element.38), channel_id=1, source_target_pairs={{0,4},{1,1},{2,6},{3,3},{4,0},{5,5},{6,2},{7,7},{8,12},{9,9},{10,1... | collective-permute-start | bytes 344072 | tf_op jit(solution)/shard_map/ppermute | solution.py:23
  15.5 0.8 %copy-start.3 = (f32[2,32,16]{2,1,0:T(8,128)S(1)}, f32[2,32,16]{2,1,0:T(8,128)}, u32[]{:S(2)}) copy-start(f32[2,32,16]{2,1,0:T(8,128)} %get-tuple-element.33.place_ref._) | copy-start | bytes 12292
  21.8 1.9 %collective-permute-start.7 = (bf16[32,7168]{1,0:T(8,128)(2,1)S(1)}, bf16[32,7168]{1,0:T(8,128)(2,1)S(1)}, u32[]{:S(2)}, u32[]{:S(2)}) collective-permute-start(bf16[32,7168]{1,0:T(8,128)(2,1)S(1)} %join.1.refs_0_), channel_id=1, source_target_pairs={{0,1},{1,0},{2,3},{3,2},{4,5},{5,4},{6,7},{7,6},{8,9},{9,8},{10,11... | collective-permute-start | bytes 1376264 | tf_op jit(solution)/shard_map/ppermute | solution.py:23
  21.9 12.9 %collective-permute-start.9 = (bf16[32,7168]{1,0:T(8,128)(2,1)S(1)}, bf16[32,7168]{1,0:T(8,128)(2,1)S(1)}, u32[]{:S(2)}, u32[]{:S(2)}) collective-permute-start(bf16[32,7168]{1,0:T(8,128)(2,1)S(1)} %join.1.refs_0_), channel_id=1, source_target_pairs={{0,2},{1,3},{2,0},{3,1},{4,6},{5,7},{6,4},{7,5},{8,10},{9,11},{10,... | collective-permute-start | bytes 1376264 | tf_op jit(solution)/shard_map/ppermute | solution.py:23
  34.8 7.9 %copy-start = (bf16[2,4,64,576]{3,2,1,0:T(8,128)(2,1)S(1)}, bf16[2,4,64,576]{3,2,1,0:T(8,128)(2,1)}, u32[]{:S(2)}) copy-start(bf16[2,4,64,576]{3,2,1,0:T(8,128)(2,1)} %query_ref.1) | copy-start | bytes 1769476
  34.9 7.9 %copy-start.1 = (bf16[4,64,576]{2,1,0:T(8,128)(2,1)S(1)}, bf16[4,64,576]{2,1,0:T(8,128)(2,1)}, u32[]{:S(2)}) copy-start(bf16[4,64,576]{2,1,0:T(8,128)(2,1)} %cache_ref.1) | copy-start | bytes 884740
  34.9 7.9 %copy-start.5 = (bf16[2,4,576]{2,1,0:T(4,128)(2,1)S(1)}, bf16[2,4,576]{2,1,0:T(4,128)(2,1)}, u32[]{:S(2)}) copy-start(bf16[2,4,576]{2,1,0:T(4,128)(2,1)} %fresh_ref.1) | copy-start | bytes 27652
  34.9 7.9 %copy-start.7 = (s32[4]{0:T(128)S(1)}, s32[4]{0:T(128)}, u32[]{:S(2)}) copy-start(s32[4]{0:T(128)} %lengths_ref.1) | copy-start | bytes 52
  34.9 10.9 %copy-start.2 = (bf16[16,7168]{1,0:T(8,128)(2,1)S(1)}, bf16[16,7168]{1,0:T(8,128)(2,1)}, u32[]{:S(2)}) copy-start(bf16[16,7168]{1,0:T(8,128)(2,1)} %get-tuple-element.32.normed_ref) | copy-start | bytes 688132
  34.9 10.9 %copy-start.4 = (bf16[7168,6]{0,1:T(8,128)(2,1)S(1)}, bf16[7168,6]{0,1:T(8,128)(2,1)}, u32[]{:S(2)}) copy-start(bf16[7168,6]{0,1:T(8,128)(2,1)} %param.15) | copy-start | bytes 258052
  34.9 10.9 %copy-start.6 = (f32[2,6,16]{2,1,0:T(8,128)S(1)}, f32[2,6,16]{2,1,0:T(8,128)}, u32[]{:S(2)}) copy-start(f32[2,6,16]{2,1,0:T(8,128)} %get-tuple-element.34.choose_ref) | copy-start | bytes 2308
  34.9 1.9 %collective-permute-start.10 = (bf16[32,7168]{1,0:T(8,128)(2,1)S(1)}, bf16[32,7168]{1,0:T(8,128)(2,1)S(1)}, u32[]{:S(2)}, u32[]{:S(2)}) collective-permute-start(bf16[32,7168]{1,0:T(8,128)(2,1)S(1)} %after.1), channel_id=1, source_target_pairs={{0,1},{1,0},{2,3},{3,2},{4,5},{5,4},{6,7},{7,6},{8,9},{9,8},{10,11... | collective-permute-start | bytes 1376264 | tf_op jit(solution)/shard_map/ppermute | solution.py:23
  38.9 1.6 %collective-permute-start.11 = (bf16[16,7168]{1,0:T(8,128)(2,1)S(1)}, bf16[16,7168]{1,0:T(8,128)(2,1)S(1)}, u32[]{:S(2)}, u32[]{:S(2)}) collective-permute-start(bf16[16,7168]{1,0:T(8,128)(2,1)S(1)} %get-tuple-element.47), channel_id=1, source_target_pairs={{0,1},{1,0},{2,3},{3,2},{4,5},{5,4},{6,7},{7,6},{8,9},{9,8},{10,11... | collective-permute-start | bytes 688136 | tf_op jit(solution)/shard_map/ppermute | solution.py:23
  39.1 3.0 %collective-permute-start.16 = (bf16[16,7168]{1,0:T(8,128)(2,1)S(1)}, bf16[16,7168]{1,0:T(8,128)(2,1)S(1)}, u32[]{:S(2)}, u32[]{:S(2)}) collective-permute-start(bf16[16,7168]{1,0:T(8,128)(2,1)S(1)} %get-tuple-element.55), channel_id=1, source_target_pairs={{0,1},{1,0},{2,3},{3,2},{4,5},{5,4},{6,7},{7,6},{8,9},{9,8},{10,11... | collective-permute-start | bytes 688136 | tf_op jit(solution)/shard_map/ppermute | solution.py:23
  39.5 6.5 %collective-permute-start.8 = (bf16[16,7168]{1,0:T(8,128)(2,1)S(1)}, bf16[16,7168]{1,0:T(8,128)(2,1)S(1)}, u32[]{:S(2)}, u32[]{:S(2)}) collective-permute-start(bf16[16,7168]{1,0:T(8,128)(2,1)S(1)} %get-tuple-element.44), channel_id=1, source_target_pairs={{0,1},{1,0},{2,3},{3,2},{4,5},{5,4},{6,7},{7,6},{8,9},{9,8},{10,11... | collective-permute-start | bytes 688136 | tf_op jit(solution)/shard_map/ppermute | solution.py:23
  40.6 8.5 %collective-permute-start.12 = (bf16[16,7168]{1,0:T(8,128)(2,1)S(1)}, bf16[16,7168]{1,0:T(8,128)(2,1)S(1)}, u32[]{:S(2)}, u32[]{:S(2)}) collective-permute-start(bf16[16,7168]{1,0:T(8,128)(2,1)S(1)} %add.4), channel_id=1, source_target_pairs={{0,2},{1,3},{2,0},{3,1},{4,6},{5,7},{6,4},{7,5},{8,10},{9,11},{10,... | collective-permute-start | bytes 688136 | tf_op jit(solution)/shard_map/ppermute | solution.py:23
  42.1 10.6 %collective-permute-start.15 = (bf16[16,7168]{1,0:T(8,128)(2,1)S(1)}, bf16[16,7168]{1,0:T(8,128)(2,1)S(1)}, u32[]{:S(2)}, u32[]{:S(2)}) collective-permute-start(bf16[16,7168]{1,0:T(8,128)(2,1)S(1)} %get-tuple-element.53), channel_id=1, source_target_pairs={{0,1},{1,0},{2,3},{3,2},{4,5},{5,4},{6,7},{7,6},{8,9},{9,8},{10,11... | collective-permute-start | bytes 688136 | tf_op jit(solution)/shard_map/ppermute | solution.py:23
  42.2 11.0 %collective-permute-start.17 = (bf16[16,7168]{1,0:T(8,128)(2,1)S(1)}, bf16[16,7168]{1,0:T(8,128)(2,1)S(1)}, u32[]{:S(2)}, u32[]{:S(2)}) collective-permute-start(bf16[16,7168]{1,0:T(8,128)(2,1)S(1)} %add.6), channel_id=1, source_target_pairs={{0,2},{1,3},{2,0},{3,1},{4,6},{5,7},{6,4},{7,5},{8,10},{9,11},{10,... | collective-permute-start | bytes 688136 | tf_op jit(solution)/shard_map/ppermute | solution.py:23
  49.2 12.2 %collective-permute-start.13 = (bf16[8,7168]{1,0:T(8,128)(2,1)S(1)}, bf16[8,7168]{1,0:T(8,128)(2,1)S(1)}, u32[]{:S(2)}, u32[]{:S(2)}) collective-permute-start(bf16[8,7168]{1,0:T(8,128)(2,1)S(1)} %get-tuple-element.50.refs_3_), channel_id=1, source_target_pairs={{0,28},{1,25},{2,30},{3,27},{4,24},{5,29},{6,26},{7,31},{8,20},{9,... | collective-permute-start | bytes 344072 | tf_op jit(solution)/shard_map/ppermute | solution.py:23
  53.3 7.5 %collective-permute-start.18 = (bf16[8,7168]{1,0:T(8,128)(2,1)S(1)}, bf16[8,7168]{1,0:T(8,128)(2,1)S(1)}, u32[]{:S(2)}, u32[]{:S(2)}) collective-permute-start(bf16[8,7168]{1,0:T(8,128)(2,1)S(1)} %get-tuple-element.56), channel_id=1, source_target_pairs={{0,12},{1,9},{2,14},{3,11},{4,8},{5,13},{6,10},{7,15},{8,4},{9,1},... | collective-permute-start | bytes 344072 | tf_op jit(solution)/shard_map/ppermute | solution.py:23
  54.5 6.8 %collective-permute-start.19 = (bf16[8,7168]{1,0:T(8,128)(2,1)S(1)}, bf16[8,7168]{1,0:T(8,128)(2,1)S(1)}, u32[]{:S(2)}, u32[]{:S(2)}) collective-permute-start(bf16[8,7168]{1,0:T(8,128)(2,1)S(1)} %get-tuple-element.57), channel_id=1, source_target_pairs={{0,4},{1,1},{2,6},{3,3},{4,0},{5,5},{6,2},{7,7},{8,12},{9,9},{10,1... | collective-permute-start | bytes 344072 | tf_op jit(solution)/shard_map/ppermute | solution.py:23
  57.5 7.9 %collective-permute-start.14 = (bf16[8,7168]{1,0:T(8,128)(2,1)S(1)}, bf16[8,7168]{1,0:T(8,128)(2,1)S(1)}, u32[]{:S(2)}, u32[]{:S(2)}) collective-permute-start(bf16[8,7168]{1,0:T(8,128)(2,1)S(1)} %get-tuple-element.51), channel_id=1, source_target_pairs={{0,20},{1,17},{2,22},{3,19},{4,16},{5,21},{6,18},{7,23},{8,28},{9,... | collective-permute-start | bytes 344072 | tf_op jit(solution)/shard_map/ppermute | solution.py:23
  65.7 1.4 %collective-permute-start.20 = (bf16[8,7168]{1,0:T(8,128)(2,1)S(1)}, bf16[8,7168]{1,0:T(8,128)(2,1)S(1)}, u32[]{:S(2)}, u32[]{:S(2)}) collective-permute-start(bf16[8,7168]{1,0:T(8,128)(2,1)S(1)} %get-tuple-element.59), channel_id=1, source_target_pairs={{0,1},{1,0},{2,3},{3,2},{4,5},{5,4},{6,7},{7,6},{8,9},{9,8},{10,11... | collective-permute-start | bytes 344072 | tf_op jit(solution)/shard_map/ppermute | solution.py:23

commit v4 on v3

--- a/solution.py
+++ b/solution.py
@@ -21,6 +21,18 @@
 def flipped(value, low_core, high_core):
     pairs = [(e, e ^ (high_core if e % 2 else low_core)) for e in range(lax.axis_size("ep"))]
     return lax.ppermute(value, "ep", pairs)
+
+
+def lanes(groups):
+    hops = [(d & 1) + (d >> 1) for d in range(groups)]
+    chosen = ([], [])
+    for d in sorted(range(groups), key=lambda d: (-hops[d], -d)):
+        sums = [sum(hops[e] for e in lane) for lane in chosen]
+        lane = 0 if sums[0] <= sums[1] else 1
+        if 2 * len(chosen[lane]) == groups:
+            lane = 1 - lane
+        chosen[lane].append(d)
+    return list(zip(*chosen))
 
 
 def attend_kernel(lengths_ref, query_ref, cache_ref, fresh_ref, out_ref, mark_ref):
@@ -216,7 +228,7 @@
 
 def pack_kernel(
     slots,
-    groups,
+    deltas,
     table_ref,
     ids_ref,
     replica_ref,
@@ -250,6 +262,15 @@
     column = lax.broadcasted_iota(jnp.int32, place_ref.shape[1:], 1)
     expert = lax.broadcasted_iota(jnp.int32, choose_ref.shape[1:], 0)
     token = lax.broadcasted_iota(jnp.int32, choose_ref.shape[1:], 1)
+    message = row // message_rows
+    target = sum(
+        [
+            jnp.where(message == m, jnp.where(core == 0, low, high) - m, 0)
+            for m, (low, high) in enumerate(deltas)
+        ],
+        message,
+    )
+    row = target * message_rows + row % message_rows
     place_row = [jnp.full(place_ref.shape[1:], -1, jnp.int32) for _ in range(top)]
     choice = [jnp.full(choose_ref.shape[1:], -1, jnp.int32) for _ in range(top)]
     for b, (ids, replicas) in enumerate(
@@ -264,9 +285,8 @@
                     slot = sum([(copy == c).astype(jnp.int32) for c in earlier], jnp.int32(0))
                     earlier.append(copy)
                     delta = copy ^ group
-                    kept = ((delta & 1) != core) & (slot < slots)
-                    at = ((groups - 1 - delta) >> 1) * message_rows + block * slots + slot
-                    at = jnp.where(kept, at, -1)
+                    at = delta * message_rows + block * slots + slot
+                    at = jnp.where(slot < slots, at, -1)
                     here = block * tokens + t
                     place_row[k] = jnp.where(column == here, at, place_row[k])
                     choice[k] = jnp.where(token == here, ids[s, k, t], choice[k])
@@ -281,17 +301,17 @@
         ref[...] = packed[m * message_rows : (m + 1) * message_rows].astype(jnp.bfloat16)
 
 
-def pack(slots, groups, hidden, other, gain, copy_table, own_choice, other_choice, experts_total):
+def pack(slots, deltas, hidden, other, gain, copy_table, own_choice, other_choice, experts_total):
     steps, tokens, depth = hidden.shape
     top = own_choice[0].shape[1]
-    messages = groups // 2
+    messages = len(deltas)
     message_rows = 2 * steps * slots
     columns = 2 * steps * tokens
     vmem = pl.BlockSpec(memory_space=pltpu.VMEM)
     smem = pl.BlockSpec(memory_space=pltpu.SMEM)
     shape = jax.ShapeDtypeStruct
     out = pl.pallas_call(
-        functools.partial(pack_kernel, slots, groups),
+        functools.partial(pack_kernel, slots, deltas),
         out_shape=[
             shape((columns, depth), jnp.bfloat16),
             shape((top, messages * message_rows, columns), jnp.float32),
@@ -342,9 +362,7 @@
     )(normed, router_t, place, choose)
 
 
-def combine_kernel(weigh_ref, *refs):
-    part_refs, own_ref, send_ref = refs[:-2], refs[-2], refs[-1]
-    weights = weigh_ref[...]
+def weighted(weights, part_refs):
     high = weights.astype(jnp.bfloat16)
     left = weights - high.astype(jnp.float32)
     middle = left.astype(jnp.bfloat16)
@@ -355,7 +373,17 @@
         lax.dot_general(w, rows, (((0,), (0,)), ((), ())), preferred_element_type=jnp.float32)
         for w in (high, middle, low)
     ]
-    result = pieces[0] + (pieces[1] + pieces[2])
+    return pieces[0] + (pieces[1] + pieces[2])
+
+
+def first_half_kernel(weigh_ref, *refs):
+    part_refs, out_ref = refs[:-1], refs[-1]
+    out_ref[...] = weighted(weigh_ref[: weigh_ref.shape[0] // 2, :], part_refs)
+
+
+def second_half_kernel(weigh_ref, first_ref, *refs):
+    part_refs, own_ref, send_ref = refs[:-2], refs[-2], refs[-1]
+    result = first_ref[...] + weighted(weigh_ref[weigh_ref.shape[0] // 2 :, :], part_refs)
     half = own_ref.shape[0]
     own_ref[...] = result[:half]
     send_ref[...] = result[half:].astype(jnp.bfloat16)
@@ -363,21 +391,29 @@
 
 def combine(weights, parts):
     depth = parts[0].shape[1]
-    half = weights.shape[1] // 2
-    vmem = pl.BlockSpec(memory_space=pltpu.VMEM)
-    return pl.pallas_call(
-        combine_kernel,
+    tokens = weights.shape[1]
+    vmem = pl.BlockSpec(memory_space=pltpu.VMEM)
+    params = pltpu.CompilerParams(vmem_limit_bytes=(8 << 20) + 8 * weights.shape[0] * depth)
+    middle = len(parts) // 2
+    first = pl.pallas_call(
+        first_half_kernel,
+        out_shape=jax.ShapeDtypeStruct((tokens, depth), jnp.float32),
+        in_specs=[vmem] * (1 + middle),
+        out_specs=vmem,
+        compiler_params=params,
+        name="combine",
+    )(weights, *parts[:middle])
+    return pl.pallas_call(
+        second_half_kernel,
         out_shape=[
-            jax.ShapeDtypeStruct((half, depth), jnp.float32),
-            jax.ShapeDtypeStruct((half, depth), jnp.bfloat16),
+            jax.ShapeDtypeStruct((tokens // 2, depth), jnp.float32),
+            jax.ShapeDtypeStruct((tokens // 2, depth), jnp.bfloat16),
         ],
-        in_specs=[vmem] * (1 + len(parts)),
+        in_specs=[vmem] * (2 + len(parts) - middle),
         out_specs=[vmem] * 2,
-        compiler_params=pltpu.CompilerParams(
-            vmem_limit_bytes=(8 << 20) + 8 * weights.shape[0] * depth
-        ),
+        compiler_params=params,
         name="combine",
-    )(weights, *parts)
+    )(weights, first, *parts[middle:])
 
 
 def finish_kernel(own_ref, received_ref, out_ref):
@@ -406,7 +442,7 @@
     messages = groups // 2
     tokens = hidden.shape[1]
     slots = max(2, 2 * tokens * expert_ids.shape[2] // groups)
-    deltas = [(groups - 1 - 2 * m, groups - 2 - 2 * m) for m in range(messages)]
+    deltas = lanes(groups)
 
     def swapped(value):
         return flipped(value, 1, 1)
@@ -415,7 +451,7 @@
     other_choice = (swapped(own_choice[0]), swapped(own_choice[1]))
     normed, place, choose, packed = pack(
         slots,
-        groups,
+        deltas,
         hidden,
         swapped(hidden),
         norm_gain[None, :],

time: 68.1 us -> 63.4 us (0.931)
  starting transfers between devices: 26.6 us -> 19.3 us
  waiting for transfers between devices: 23.6 us -> 26 us
    ppermute x21, starting transfers between devices: 26.6 us -> 19.3 us  [flipped(): return lax.ppermute(value, 'ep', pairs)]
    ppermute x21, waiting for transfers between devices: 23.6 us -> 26 us  [flipped(): return lax.ppermute(value, 'ep', pairs)]
    pallas_call x2 -> x3, Pallas kernels: 2.67 us -> 2.97 us  [the longest x1 2.25 us: pack(): pl.pallas_call(functools.partial(pack_kernel, slots, deltas), out_shape=[...]
  transfers between devices with their start and end apart: 21 -> 21, of which waited for: 12 -> 13; matrix products, arithmetic and copies ran while one was open for 0% -> 0% of each run, Pallas kernels for 15% -> 16%
where the time goes in v4:
time: 63.4 us; the launch traced here: 63.2 us
  waiting for transfers between devices  26 us (41%)
  starting transfers between devices  19.3 us (30%)
  Pallas kernels  15.7 us (25%)
  local copies, waits for them, and re-layouts  1.45 us (2%)
  between operations  0.83 us (1%)
    ppermute x21, waiting for transfers between devices, flipped(): return lax.ppermute(value, 'ep', pairs)  26 us
    ppermute x21, starting transfers between devices, flipped(): return lax.ppermute(value, 'ep', pairs)  19.3 us
    pallas_call x2, Pallas kernels, experts(): pl.pallas_call(functools.partial(expert_kernel, count), out_shape=[jax.Sh...  4.26 us
    pallas_call x1, Pallas kernels, load(): pl.pallas_call(load_kernel, out_shape=[jax.ShapeDtypeStruct(w.shape, w.dt...  4.23 us
    pallas_call x1, Pallas kernels, attend(): pl.pallas_call(attend_kernel, out_shape=[jax.ShapeDtypeStruct((steps, tok...  2.97 us
    pallas_call x1, Pallas kernels, pack(): pl.pallas_call(functools.partial(pack_kernel, slots, deltas), out_shape=[...  2.25 us
    unnamed x22, local copies, waits for them, and re-layouts  1.45 us
  transfers between devices with their start and end apart: 21, of which 13 were waited for; matrix products, arithmetic and copies ran while one was open for 0% of the time, Pallas kernels for 16%

profile of v4, /device:TPU:0, one launch (start us, length us, event | category | flops | bytes accessed | tf_op | source)
XLA Modules:
  0.0 63.2 jit_solution(15437673072781710138)
XLA Ops:
  0.6 0.5 collective-permute-start.2
  1.1 0.1 collective-permute-start
  1.2 0.4 collective-permute-start.1
  1.7 0.9 %collective-permute-done.other_ids_ref = s32[2,2,4]{2,1,0:T(2,128)S(1)} collective-permute-done((s32[2,2,4]{2,1,0:T(2,128)}, s32[2,2,4]{2,1,0:T(2,128)S(1)}, u32[]{:S(2)}, u32[]{:S(2)}) %collective-permute-start) | collective-permute-done | bytes 96 | tf_op jit(solution)/shard_map/ppermute | solution.py:23
  2.5 0.2 collective-permute-done.1.other_replica_ref
  2.7 0.0 collective-permute-done.2.other_ref
  2.7 0.4 copy-done.9
  3.1 0.2 copy-done.10
  3.3 0.1 copy-done.8
  3.3 2.3 %pack.1 = (bf16[16,7168]{1,0:T(8,128)(2,1)}, f32[2,32,16]{2,1,0:T(8,128)}, f32[2,6,16]{2,1,0:T(8,128)}, bf16[8,7168]{1,0:T(8,128)(2,1)}, bf16[8,7168]{1,0:T(8,12...) custom-call(s32[2,6]{1,0:T(2,128)} %bitcast.11, s32[2,2,4]{2,1,0:T(2,128)} %bitcast.8, s32[2,2,4]{2,1,0:T(2,128)} %bitcast.10, ...), custom_call_target="tpu_custom_call" | custom-call | tf_op jit(solution)/shard_map/pack/pallas_call | solution.py:313
  5.6 5.9 %collective-permute-start.3 = (bf16[8,7168]{1,0:T(8,128)(2,1)}, bf16[8,7168]{1,0:T(8,128)(2,1)S(1)}, u32[]{:S(2)}, u32[]{:S(2)}) collective-permute-start(bf16[8,7168]{1,0:T(8,128)(2,1)} %get-tuple-element.35), channel_id=1, source_target_pairs={{0,28},{1,25},{2,30},{3,27},{4,24},{5,29},{6,26},{7,31},{8,20},{9,... | collective-permute-start | bytes 344072 | tf_op jit(solution)/shard_map/ppermute | solution.py:23
  11.5 0.0 collective-permute-start.4
  11.5 0.6 collective-permute-start.5
  12.1 1.5 %collective-permute-start.6 = (bf16[8,7168]{1,0:T(8,128)(2,1)}, bf16[8,7168]{1,0:T(8,128)(2,1)S(1)}, u32[]{:S(2)}, u32[]{:S(2)}) collective-permute-start(bf16[8,7168]{1,0:T(8,128)(2,1)} %get-tuple-element.38), channel_id=1, source_target_pairs={{0,0},{1,5},{2,2},{3,7},{4,4},{5,1},{6,6},{7,3},{8,8},{9,13},{10,1... | collective-permute-start | bytes 344072 | tf_op jit(solution)/shard_map/ppermute | solution.py:23
  13.6 0.8 %copy-done.3 = f32[2,32,16]{2,1,0:T(8,128)S(1)} copy-done((f32[2,32,16]{2,1,0:T(8,128)S(1)}, f32[2,32,16]{2,1,0:T(8,128)}, u32[]{:S(2)}) %copy-start.3) | copy-done | bytes 4120
  14.4 4.2 %load.1 = (bf16[7168,256]{1,0:T(8,128)(2,1)S(1)}, bf16[7168,256]{1,0:T(8,128)(2,1)S(1)}, bf16[256,7168]{1,0:T(8,128)(2,1)S(1)}, f32[8,128]{1,0:T(8,128)S(1)}) custom-call(bf16[7168,256]{1,0:T(8,128)(2,1)} %gate_ref.1, bf16[7168,256]{1,0:T(8,128)(2,1)} %up_ref.1, bf16[256,7168]{1,0:T(8,128)(2,1)} %down_ref.1, f32[2,32,16]{2,1,0:T(8,128)S(1)} %copy-done.3), custom_call_target="tpu_custom_call" | custom-call | tf_op jit(solution)/shard_map/load/pallas_call | solution.py:108
  18.6 0.0 collective-permute-done.3.refs_0_
  18.6 2.1 %collective-permute-done.4.refs_1_ = bf16[8,7168]{1,0:T(8,128)(2,1)S(1)} collective-permute-done((bf16[8,7168]{1,0:T(8,128)(2,1)}, bf16[8,7168]{1,0:T(8,128)(2,1)S(1)}, u32[]{:S(2)}, u32[]{:S(2)}) %collective-permute-start.4) | collective-permute-done | bytes 114720 | tf_op jit(solution)/shard_map/ppermute | solution.py:23
  20.7 0.0 collective-permute-done.5.refs_2_
  20.8 0.0 collective-permute-done.6.refs_3_
  20.8 0.1 collective-permute-start.7
  20.9 1.5 %collective-permute-start.9 = (bf16[32,7168]{1,0:T(8,128)(2,1)S(1)}, bf16[32,7168]{1,0:T(8,128)(2,1)S(1)}, u32[]{:S(2)}, u32[]{:S(2)}) collective-permute-start(bf16[32,7168]{1,0:T(8,128)(2,1)S(1)} %join.1.refs_0_), channel_id=1, source_target_pairs={{0,2},{1,3},{2,0},{3,1},{4,6},{5,7},{6,4},{7,5},{8,10},{9,11},{10,... | collective-permute-start | bytes 1376264 | tf_op jit(solution)/shard_map/ppermute | solution.py:23
  22.4 0.2 collective-permute-done.7.refs_1_
  22.7 2.1 %experts.2 = (bf16[16,7168]{1,0:T(8,128)(2,1)S(1)}, bf16[16,7168]{1,0:T(8,128)(2,1)S(1)}, bf16[16,7168]{1,0:T(8,128)(2,1)S(1)}, bf16[16,7168]{1,0:T(8,128)(2,1)S(1)}, f32[8,128]{1,0:T(8,128)S(1)}) custom-call(bf16[32,7168]{1,0:T(8,128)(2,1)S(1)} %join.1.refs_0_, bf16[32,7168]{1,0:T(8,128)(2,1)S(1)} %collective-permute-done.7.refs_1_, ...), custom_call_target="tpu_custom_call" | custom-call | tf_op jit(solution)/shard_map/experts/pallas_call | solution.py:148
  24.8 9.0 %collective-permute-done.9.value_ref.refs_0_ = bf16[32,7168]{1,0:T(8,128)(2,1)S(1)} collective-permute-done((bf16[32,7168]{1,0:T(8,128)(2,1)S(1)}, bf16[32,7168]{1,0:T(8,128)(2,1)S(1)}, u32[]{:S(2)}, u32[]{:S(2)}) %collective-permute-start.9) | collective-permute-done | bytes 458784 | tf_op jit(solution)/shard_map/ppermute | solution.py:23
  33.8 0.0 copy-start
  33.9 0.0 copy-start.1
  33.9 0.0 copy-start.5
  33.9 0.0 copy-start.7
  33.9 0.0 copy-start.4
  33.9 0.1 collective-permute-start.10
  34.0 1.8 %collective-permute-done.10.refs_1_ = bf16[32,7168]{1,0:T(8,128)(2,1)S(1)} collective-permute-done((bf16[32,7168]{1,0:T(8,128)(2,1)S(1)}, bf16[32,7168]{1,0:T(8,128)(2,1)S(1)}, u32[]{:S(2)}, u32[]{:S(2)}) %collective-permute-start.10) | collective-permute-done | bytes 458784 | tf_op jit(solution)/shard_map/ppermute | solution.py:23
  35.8 2.1 %experts.3 = (bf16[16,7168]{1,0:T(8,128)(2,1)S(1)}, bf16[16,7168]{1,0:T(8,128)(2,1)S(1)}, bf16[16,7168]{1,0:T(8,128)(2,1)S(1)}, bf16[16,7168]{1,0:T(8,128)(2,1)S(1)}, f32[8,128]{1,0:T(8,128)S(1)}) custom-call(bf16[32,7168]{1,0:T(8,128)(2,1)S(1)} %collective-permute-done.9.value_ref.refs_0_, bf16[32,7168]{1,0:T(8,128)(2,1)S(1)} %collective-permute-done.10.refs_1_, ...), custom_call_target="tpu_custom_call" | custom-call | tf_op jit(solution)/shard_map/experts/pallas_call | solution.py:148
  37.9 0.2 collective-permute-start.11
  38.1 0.4 collective-permute-start.16
  38.5 0.1 collective-permute-start.8
  38.7 0.8 %collective-permute-done.11.refs_1_ = bf16[16,7168]{1,0:T(8,128)(2,1)S(1)} collective-permute-done((bf16[16,7168]{1,0:T(8,128)(2,1)S(1)}, bf16[16,7168]{1,0:T(8,128)(2,1)S(1)}, u32[]{:S(2)}, u32[]{:S(2)}) %collective-permute-start.11) | collective-permute-done | bytes 229408 | tf_op jit(solution)/shard_map/ppermute | solution.py:23
  39.5 0.1 add.4
  39.6 1.6 %collective-permute-start.12 = (bf16[16,7168]{1,0:T(8,128)(2,1)S(1)}, bf16[16,7168]{1,0:T(8,128)(2,1)S(1)}, u32[]{:S(2)}, u32[]{:S(2)}) collective-permute-start(bf16[16,7168]{1,0:T(8,128)(2,1)S(1)} %add.4), channel_id=1, source_target_pairs={{0,2},{1,3},{2,0},{3,1},{4,6},{5,7},{6,4},{7,5},{8,10},{9,11},{10,... | collective-permute-start | bytes 688136 | tf_op jit(solution)/shard_map/ppermute | solution.py:23
  41.1 0.0 collective-permute-start.15
  41.1 0.0 collective-permute-done.16.refs_1_
  41.1 0.1 add.6
  41.2 0.6 collective-permute-start.17
  41.8 3.0 %attention.1 = (bf16[2,4,64,512]{3,2,1,0:T(8,128)(2,1)}, f32[8,128]{1,0:T(8,128)S(1)}) custom-call(s32[4]{0:T(128)S(1)} %copy-done.7, bf16[2,4,64,576]{3,2,1,0:T(8,128)(2,1)S(1)} %copy-done, bf16[4,64,576]{2,1,0:T(8,128)(2,1)S(1)} %copy-done.1, bf16[2,4,576]{2,1,0:T(4,128)(2,1)S(1)} %copy-done.5), custom_call_target="tpu_custom_call" | custom-call | flops 150994944 | bytes 1474560 | tf_op jit(solution)/shard_map/attention/pallas_call | solution.py:76
  44.8 0.2 weigh.1.refs_4_.weigh_ref
  45.0 0.0 collective-permute-done.8.refs_1_
  45.0 3.1 %collective-permute-done.12.refs_2_ = bf16[16,7168]{1,0:T(8,128)(2,1)S(1)} collective-permute-done((bf16[16,7168]{1,0:T(8,128)(2,1)S(1)}, bf16[16,7168]{1,0:T(8,128)(2,1)S(1)}, u32[]{:S(2)}, u32[]{:S(2)}) %collective-permute-start.12) | collective-permute-done | bytes 229408 | tf_op jit(solution)/shard_map/ppermute | solution.py:23
  48.1 0.1 add.5
  48.2 3.5 %collective-permute-start.13 = (bf16[8,7168]{1,0:T(8,128)(2,1)S(1)}, bf16[8,7168]{1,0:T(8,128)(2,1)S(1)}, u32[]{:S(2)}, u32[]{:S(2)}) collective-permute-start(bf16[8,7168]{1,0:T(8,128)(2,1)S(1)} %get-tuple-element.50.refs_3_), channel_id=1, source_target_pairs={{0,28},{1,25},{2,30},{3,27},{4,24},{5,29},{6,26},{7,31},{8,20},{9,... | collective-permute-start | bytes 344072 | tf_op jit(solution)/shard_map/ppermute | solution.py:23
  51.7 0.0 collective-permute-start.14
  51.7 0.0 collective-permute-done.15.refs_1_
  51.7 0.5 collective-permute-done.17.refs_2_
  52.2 0.1 add.7
  52.3 1.4 %collective-permute-start.18 = (bf16[8,7168]{1,0:T(8,128)(2,1)S(1)}, bf16[8,7168]{1,0:T(8,128)(2,1)S(1)}, u32[]{:S(2)}, u32[]{:S(2)}) collective-permute-start(bf16[8,7168]{1,0:T(8,128)(2,1)S(1)} %get-tuple-element.56), channel_id=1, source_target_pairs={{0,12},{1,9},{2,14},{3,11},{4,8},{5,13},{6,10},{7,15},{8,4},{9,1},... | collective-permute-start | bytes 344072 | tf_op jit(solution)/shard_map/ppermute | solution.py:23
  53.7 0.7 %collective-permute-start.19 = (bf16[8,7168]{1,0:T(8,128)(2,1)S(1)}, bf16[8,7168]{1,0:T(8,128)(2,1)S(1)}, u32[]{:S(2)}, u32[]{:S(2)}) collective-permute-start(bf16[8,7168]{1,0:T(8,128)(2,1)S(1)} %get-tuple-element.57), channel_id=1, source_target_pairs={{0,0},{1,5},{2,2},{3,7},{4,4},{5,1},{6,6},{7,3},{8,8},{9,13},{10,1... | collective-permute-start | bytes 344072 | tf_op jit(solution)/shard_map/ppermute | solution.py:23
  54.3 1.6 %collective-permute-done.13.refs_0_ = bf16[8,7168]{1,0:T(8,128)(2,1)S(1)} collective-permute-done((bf16[8,7168]{1,0:T(8,128)(2,1)S(1)}, bf16[8,7168]{1,0:T(8,128)(2,1)S(1)}, u32[]{:S(2)}, u32[]{:S(2)}) %collective-permute-start.13) | collective-permute-done | bytes 114720 | tf_op jit(solution)/shard_map/ppermute | solution.py:23
  55.9 3.8 %collective-permute-done.14.refs_1_ = bf16[8,7168]{1,0:T(8,128)(2,1)S(1)} collective-permute-done((bf16[8,7168]{1,0:T(8,128)(2,1)S(1)}, bf16[8,7168]{1,0:T(8,128)(2,1)S(1)}, u32[]{:S(2)}, u32[]{:S(2)}) %collective-permute-start.14) | collective-permute-done | bytes 114720 | tf_op jit(solution)/shard_map/ppermute | solution.py:23
  59.7 0.4 combine.2.first_ref
  60.1 0.6 %collective-permute-done.18.refs_0_ = bf16[8,7168]{1,0:T(8,128)(2,1)S(1)} collective-permute-done((bf16[8,7168]{1,0:T(8,128)(2,1)S(1)}, bf16[8,7168]{1,0:T(8,128)(2,1)S(1)}, u32[]{:S(2)}, u32[]{:S(2)}) %collective-permute-start.18) | collective-permute-done | bytes 114720 | tf_op jit(solution)/shard_map/ppermute | solution.py:23
  60.8 0.0 collective-permute-done.19.refs_1_
  60.8 0.4 combine.3
  61.1 0.1 collective-permute-start.20
  61.2 1.3 %collective-permute-done.20.received_ref = bf16[8,7168]{1,0:T(8,128)(2,1)S(1)} collective-permute-done((bf16[8,7168]{1,0:T(8,128)(2,1)S(1)}, bf16[8,7168]{1,0:T(8,128)(2,1)S(1)}, u32[]{:S(2)}, u32[]{:S(2)}) %collective-permute-start.20) | collective-permute-done | bytes 114720 | tf_op jit(solution)/shard_map/ppermute | solution.py:23
  62.5 0.7 %finish.1 = bf16[2,4,7168]{2,1,0:T(4,128)(2,1)} custom-call(f32[8,7168]{1,0:T(8,128)S(1)} %get-tuple-element.58.own_ref, bf16[8,7168]{1,0:T(8,128)(2,1)S(1)} %collective-permute-done.20.received_ref), custom_call_target="tpu_custom_call" | custom-call | tf_op jit(solution)/shard_map/finish/pallas_call | solution.py:428
  (15 shorter events, 0.1 us)
Async XLA Ops:
  0.6 2.1 %collective-permute-start.2 = (bf16[2,4,7168]{2,1,0:T(4,128)(2,1)}, bf16[2,4,7168]{2,1,0:T(4,128)(2,1)S(1)}, u32[]{:S(2)}, u32[]{:S(2)}) collective-permute-start(bf16[2,4,7168]{2,1,0:T(4,128)(2,1)} %raw_ref.1), channel_id=1, source_target_pairs={{0,1},{1,0},{2,3},{3,2},{4,5},{5,4},{6,7},{7,6},{8,9},{9,8},{10,11... | collective-permute-start | bytes 344072 | tf_op jit(solution)/shard_map/ppermute | solution.py:23
  1.1 1.4 %collective-permute-start = (s32[2,2,4]{2,1,0:T(2,128)}, s32[2,2,4]{2,1,0:T(2,128)S(1)}, u32[]{:S(2)}, u32[]{:S(2)}) collective-permute-start(s32[2,2,4]{2,1,0:T(2,128)} %bitcast.7), channel_id=1, source_target_pairs={{0,1},{1,0},{2,3},{3,2},{4,5},{5,4},{6,7},{7,6},{8,9},{9,8},{10,11... | collective-permute-start | bytes 200 | tf_op jit(solution)/shard_map/ppermute | solution.py:23
  1.2 1.5 %collective-permute-start.1 = (s32[2,2,4]{2,1,0:T(2,128)}, s32[2,2,4]{2,1,0:T(2,128)S(1)}, u32[]{:S(2)}, u32[]{:S(2)}) collective-permute-start(s32[2,2,4]{2,1,0:T(2,128)} %bitcast.9), channel_id=1, source_target_pairs={{0,1},{1,0},{2,3},{3,2},{4,5},{5,4},{6,7},{7,6},{8,9},{9,8},{10,11... | collective-permute-start | bytes 200 | tf_op jit(solution)/shard_map/ppermute | solution.py:23
  2.5 0.6 copy-start.9
  2.7 0.6 copy-start.10
  2.7 0.6 %copy-start.8 = (bf16[2,4,7168]{2,1,0:T(4,128)(2,1)}, bf16[2,4,7168]{2,1,0:T(4,128)(2,1)S(1)}, u32[]{:S(2)}) copy-start(bf16[2,4,7168]{2,1,0:T(4,128)(2,1)S(1)} %collective-permute-done.2.other_ref) | copy-start | bytes 344068
  5.6 13.0 %collective-permute-start.3 = (bf16[8,7168]{1,0:T(8,128)(2,1)}, bf16[8,7168]{1,0:T(8,128)(2,1)S(1)}, u32[]{:S(2)}, u32[]{:S(2)}) collective-permute-start(bf16[8,7168]{1,0:T(8,128)(2,1)} %get-tuple-element.35), channel_id=1, source_target_pairs={{0,28},{1,25},{2,30},{3,27},{4,24},{5,29},{6,26},{7,31},{8,20},{9,... | collective-permute-start | bytes 344072 | tf_op jit(solution)/shard_map/ppermute | solution.py:23
  11.5 9.3 %collective-permute-start.4 = (bf16[8,7168]{1,0:T(8,128)(2,1)}, bf16[8,7168]{1,0:T(8,128)(2,1)S(1)}, u32[]{:S(2)}, u32[]{:S(2)}) collective-permute-start(bf16[8,7168]{1,0:T(8,128)(2,1)} %get-tuple-element.36), channel_id=1, source_target_pairs={{0,16},{1,21},{2,18},{3,23},{4,20},{5,17},{6,22},{7,19},{8,24},{9,... | collective-permute-start | bytes 344072 | tf_op jit(solution)/shard_map/ppermute | solution.py:23
  11.5 9.3 %collective-permute-start.5 = (bf16[8,7168]{1,0:T(8,128)(2,1)}, bf16[8,7168]{1,0:T(8,128)(2,1)S(1)}, u32[]{:S(2)}, u32[]{:S(2)}) collective-permute-start(bf16[8,7168]{1,0:T(8,128)(2,1)} %get-tuple-element.37), channel_id=1, source_target_pairs={{0,12},{1,9},{2,14},{3,11},{4,8},{5,13},{6,10},{7,15},{8,4},{9,1},... | collective-permute-start | bytes 344072 | tf_op jit(solution)/shard_map/ppermute | solution.py:23
  12.1 8.7 %collective-permute-start.6 = (bf16[8,7168]{1,0:T(8,128)(2,1)}, bf16[8,7168]{1,0:T(8,128)(2,1)S(1)}, u32[]{:S(2)}, u32[]{:S(2)}) collective-permute-start(bf16[8,7168]{1,0:T(8,128)(2,1)} %get-tuple-element.38), channel_id=1, source_target_pairs={{0,0},{1,5},{2,2},{3,7},{4,4},{5,1},{6,6},{7,3},{8,8},{9,13},{10,1... | collective-permute-start | bytes 344072 | tf_op jit(solution)/shard_map/ppermute | solution.py:23
  13.6 0.8 %copy-start.3 = (f32[2,32,16]{2,1,0:T(8,128)S(1)}, f32[2,32,16]{2,1,0:T(8,128)}, u32[]{:S(2)}) copy-start(f32[2,32,16]{2,1,0:T(8,128)} %get-tuple-element.33.place_ref._) | copy-start | bytes 12292
  20.8 1.9 %collective-permute-start.7 = (bf16[32,7168]{1,0:T(8,128)(2,1)S(1)}, bf16[32,7168]{1,0:T(8,128)(2,1)S(1)}, u32[]{:S(2)}, u32[]{:S(2)}) collective-permute-start(bf16[32,7168]{1,0:T(8,128)(2,1)S(1)} %join.1.refs_0_), channel_id=1, source_target_pairs={{0,1},{1,0},{2,3},{3,2},{4,5},{5,4},{6,7},{7,6},{8,9},{9,8},{10,11... | collective-permute-start | bytes 1376264 | tf_op jit(solution)/shard_map/ppermute | solution.py:23
  20.9 12.9 %collective-permute-start.9 = (bf16[32,7168]{1,0:T(8,128)(2,1)S(1)}, bf16[32,7168]{1,0:T(8,128)(2,1)S(1)}, u32[]{:S(2)}, u32[]{:S(2)}) collective-permute-start(bf16[32,7168]{1,0:T(8,128)(2,1)S(1)} %join.1.refs_0_), channel_id=1, source_target_pairs={{0,2},{1,3},{2,0},{3,1},{4,6},{5,7},{6,4},{7,5},{8,10},{9,11},{10,... | collective-permute-start | bytes 1376264 | tf_op jit(solution)/shard_map/ppermute | solution.py:23
  33.8 7.9 %copy-start = (bf16[2,4,64,576]{3,2,1,0:T(8,128)(2,1)S(1)}, bf16[2,4,64,576]{3,2,1,0:T(8,128)(2,1)}, u32[]{:S(2)}) copy-start(bf16[2,4,64,576]{3,2,1,0:T(8,128)(2,1)} %query_ref.1) | copy-start | bytes 1769476
  33.9 7.9 %copy-start.1 = (bf16[4,64,576]{2,1,0:T(8,128)(2,1)S(1)}, bf16[4,64,576]{2,1,0:T(8,128)(2,1)}, u32[]{:S(2)}) copy-start(bf16[4,64,576]{2,1,0:T(8,128)(2,1)} %cache_ref.1) | copy-start | bytes 884740
  33.9 7.9 %copy-start.5 = (bf16[2,4,576]{2,1,0:T(4,128)(2,1)S(1)}, bf16[2,4,576]{2,1,0:T(4,128)(2,1)}, u32[]{:S(2)}) copy-start(bf16[2,4,576]{2,1,0:T(4,128)(2,1)} %fresh_ref.1) | copy-start | bytes 27652
  33.9 7.9 %copy-start.7 = (s32[4]{0:T(128)S(1)}, s32[4]{0:T(128)}, u32[]{:S(2)}) copy-start(s32[4]{0:T(128)} %lengths_ref.1) | copy-start | bytes 52
  33.9 10.9 %copy-start.2 = (bf16[16,7168]{1,0:T(8,128)(2,1)S(1)}, bf16[16,7168]{1,0:T(8,128)(2,1)}, u32[]{:S(2)}) copy-start(bf16[16,7168]{1,0:T(8,128)(2,1)} %get-tuple-element.32.normed_ref) | copy-start | bytes 688132
  33.9 10.9 %copy-start.4 = (bf16[7168,6]{0,1:T(8,128)(2,1)S(1)}, bf16[7168,6]{0,1:T(8,128)(2,1)}, u32[]{:S(2)}) copy-start(bf16[7168,6]{0,1:T(8,128)(2,1)} %param.15) | copy-start | bytes 258052
  33.9 10.9 %copy-start.6 = (f32[2,6,16]{2,1,0:T(8,128)S(1)}, f32[2,6,16]{2,1,0:T(8,128)}, u32[]{:S(2)}) copy-start(f32[2,6,16]{2,1,0:T(8,128)} %get-tuple-element.34.choose_ref) | copy-start | bytes 2308
  33.9 1.9 %collective-permute-start.10 = (bf16[32,7168]{1,0:T(8,128)(2,1)S(1)}, bf16[32,7168]{1,0:T(8,128)(2,1)S(1)}, u32[]{:S(2)}, u32[]{:S(2)}) collective-permute-start(bf16[32,7168]{1,0:T(8,128)(2,1)S(1)} %after.1), channel_id=1, source_target_pairs={{0,1},{1,0},{2,3},{3,2},{4,5},{5,4},{6,7},{7,6},{8,9},{9,8},{10,11... | collective-permute-start | bytes 1376264 | tf_op jit(solution)/shard_map/ppermute | solution.py:23
  37.9 1.6 %collective-permute-start.11 = (bf16[16,7168]{1,0:T(8,128)(2,1)S(1)}, bf16[16,7168]{1,0:T(8,128)(2,1)S(1)}, u32[]{:S(2)}, u32[]{:S(2)}) collective-permute-start(bf16[16,7168]{1,0:T(8,128)(2,1)S(1)} %get-tuple-element.47), channel_id=1, source_target_pairs={{0,1},{1,0},{2,3},{3,2},{4,5},{5,4},{6,7},{7,6},{8,9},{9,8},{10,11... | collective-permute-start | bytes 688136 | tf_op jit(solution)/shard_map/ppermute | solution.py:23
  38.1 3.0 %collective-permute-start.16 = (bf16[16,7168]{1,0:T(8,128)(2,1)S(1)}, bf16[16,7168]{1,0:T(8,128)(2,1)S(1)}, u32[]{:S(2)}, u32[]{:S(2)}) collective-permute-start(bf16[16,7168]{1,0:T(8,128)(2,1)S(1)} %get-tuple-element.55), channel_id=1, source_target_pairs={{0,1},{1,0},{2,3},{3,2},{4,5},{5,4},{6,7},{7,6},{8,9},{9,8},{10,11... | collective-permute-start | bytes 688136 | tf_op jit(solution)/shard_map/ppermute | solution.py:23
  38.5 6.5 %collective-permute-start.8 = (bf16[16,7168]{1,0:T(8,128)(2,1)S(1)}, bf16[16,7168]{1,0:T(8,128)(2,1)S(1)}, u32[]{:S(2)}, u32[]{:S(2)}) collective-permute-start(bf16[16,7168]{1,0:T(8,128)(2,1)S(1)} %get-tuple-element.44), channel_id=1, source_target_pairs={{0,1},{1,0},{2,3},{3,2},{4,5},{5,4},{6,7},{7,6},{8,9},{9,8},{10,11... | collective-permute-start | bytes 688136 | tf_op jit(solution)/shard_map/ppermute | solution.py:23
  39.6 8.5 %collective-permute-start.12 = (bf16[16,7168]{1,0:T(8,128)(2,1)S(1)}, bf16[16,7168]{1,0:T(8,128)(2,1)S(1)}, u32[]{:S(2)}, u32[]{:S(2)}) collective-permute-start(bf16[16,7168]{1,0:T(8,128)(2,1)S(1)} %add.4), channel_id=1, source_target_pairs={{0,2},{1,3},{2,0},{3,1},{4,6},{5,7},{6,4},{7,5},{8,10},{9,11},{10,... | collective-permute-start | bytes 688136 | tf_op jit(solution)/shard_map/ppermute | solution.py:23
  41.1 10.6 %collective-permute-start.15 = (bf16[16,7168]{1,0:T(8,128)(2,1)S(1)}, bf16[16,7168]{1,0:T(8,128)(2,1)S(1)}, u32[]{:S(2)}, u32[]{:S(2)}) collective-permute-start(bf16[16,7168]{1,0:T(8,128)(2,1)S(1)} %get-tuple-element.53), channel_id=1, source_target_pairs={{0,1},{1,0},{2,3},{3,2},{4,5},{5,4},{6,7},{7,6},{8,9},{9,8},{10,11... | collective-permute-start | bytes 688136 | tf_op jit(solution)/shard_map/ppermute | solution.py:23
  41.2 11.0 %collective-permute-start.17 = (bf16[16,7168]{1,0:T(8,128)(2,1)S(1)}, bf16[16,7168]{1,0:T(8,128)(2,1)S(1)}, u32[]{:S(2)}, u32[]{:S(2)}) collective-permute-start(bf16[16,7168]{1,0:T(8,128)(2,1)S(1)} %add.6), channel_id=1, source_target_pairs={{0,2},{1,3},{2,0},{3,1},{4,6},{5,7},{6,4},{7,5},{8,10},{9,11},{10,... | collective-permute-start | bytes 688136 | tf_op jit(solution)/shard_map/ppermute | solution.py:23
  48.2 7.8 %collective-permute-start.13 = (bf16[8,7168]{1,0:T(8,128)(2,1)S(1)}, bf16[8,7168]{1,0:T(8,128)(2,1)S(1)}, u32[]{:S(2)}, u32[]{:S(2)}) collective-permute-start(bf16[8,7168]{1,0:T(8,128)(2,1)S(1)} %get-tuple-element.50.refs_3_), channel_id=1, source_target_pairs={{0,28},{1,25},{2,30},{3,27},{4,24},{5,29},{6,26},{7,31},{8,20},{9,... | collective-permute-start | bytes 344072 | tf_op jit(solution)/shard_map/ppermute | solution.py:23
  51.7 8.1 %collective-permute-start.14 = (bf16[8,7168]{1,0:T(8,128)(2,1)S(1)}, bf16[8,7168]{1,0:T(8,128)(2,1)S(1)}, u32[]{:S(2)}, u32[]{:S(2)}) collective-permute-start(bf16[8,7168]{1,0:T(8,128)(2,1)S(1)} %get-tuple-element.51), channel_id=1, source_target_pairs={{0,16},{1,21},{2,18},{3,23},{4,20},{5,17},{6,22},{7,19},{8,24},{9,... | collective-permute-start | bytes 344072 | tf_op jit(solution)/shard_map/ppermute | solution.py:23
  52.3 8.5 %collective-permute-start.18 = (bf16[8,7168]{1,0:T(8,128)(2,1)S(1)}, bf16[8,7168]{1,0:T(8,128)(2,1)S(1)}, u32[]{:S(2)}, u32[]{:S(2)}) collective-permute-start(bf16[8,7168]{1,0:T(8,128)(2,1)S(1)} %get-tuple-element.56), channel_id=1, source_target_pairs={{0,12},{1,9},{2,14},{3,11},{4,8},{5,13},{6,10},{7,15},{8,4},{9,1},... | collective-permute-start | bytes 344072 | tf_op jit(solution)/shard_map/ppermute | solution.py:23
  53.7 7.1 %collective-permute-start.19 = (bf16[8,7168]{1,0:T(8,128)(2,1)S(1)}, bf16[8,7168]{1,0:T(8,128)(2,1)S(1)}, u32[]{:S(2)}, u32[]{:S(2)}) collective-permute-start(bf16[8,7168]{1,0:T(8,128)(2,1)S(1)} %get-tuple-element.57), channel_id=1, source_target_pairs={{0,0},{1,5},{2,2},{3,7},{4,4},{5,1},{6,6},{7,3},{8,8},{9,13},{10,1... | collective-permute-start | bytes 344072 | tf_op jit(solution)/shard_map/ppermute | solution.py:23
  61.1 1.4 %collective-permute-start.20 = (bf16[8,7168]{1,0:T(8,128)(2,1)S(1)}, bf16[8,7168]{1,0:T(8,128)(2,1)S(1)}, u32[]{:S(2)}, u32[]{:S(2)}) collective-permute-start(bf16[8,7168]{1,0:T(8,128)(2,1)S(1)} %get-tuple-element.59), channel_id=1, source_target_pairs={{0,1},{1,0},{2,3},{3,2},{4,5},{5,4},{6,7},{7,6},{8,9},{9,8},{10,11... | collective-permute-start | bytes 344072 | tf_op jit(solution)/shard_map/ppermute | solution.py:23

commit v5 on v4

--- a/solution.py
+++ b/solution.py
@@ -183,20 +183,24 @@
     )(*parts, *earlier)
 
 
-def after_kernel(value_ref, earlier_ref, out_ref):
-    out_ref[...] = value_ref[...]
-
-
-def after(value, earlier):
-    vmem = pl.BlockSpec(memory_space=pltpu.VMEM)
-    return pl.pallas_call(
-        after_kernel,
-        out_shape=jax.ShapeDtypeStruct(value.shape, value.dtype),
-        in_specs=[vmem, pl.BlockSpec(memory_space=pl.ANY)],
-        out_specs=vmem,
+def after_kernel(pieces, value_ref, *refs):
+    out_refs = refs[-pieces:]
+    rows = out_refs[0].shape[0]
+    for i, ref in enumerate(out_refs):
+        ref[...] = value_ref[i * rows : (i + 1) * rows, :]
+
+
+def after(value, earlier, pieces):
+    rows, depth = value.shape
+    vmem = pl.BlockSpec(memory_space=pltpu.VMEM)
+    return pl.pallas_call(
+        functools.partial(after_kernel, pieces),
+        out_shape=[jax.ShapeDtypeStruct((rows // pieces, depth), value.dtype)] * pieces,
+        in_specs=[vmem] + [pl.BlockSpec(memory_space=pl.ANY)] * len(earlier),
+        out_specs=[vmem] * pieces,
         compiler_params=pltpu.CompilerParams(vmem_limit_bytes=(2 << 20) + 6 * value.size),
         name="after",
-    )(value, earlier)
+    )(value, *earlier)
 
 
 def add_kernel(count, messages, *refs):
@@ -210,15 +214,15 @@
         for ref in terms[1:]:
             total = total + ref[:, ds].astype(jnp.float32)
         for m, ref in enumerate(part_refs):
-            ref[:, ds] = total[m * size : (m + 1) * size].astype(jnp.bfloat16)
-
-
-def add(terms, messages, earlier):
+            ref[:, ds] = total[m * size : (m + 1) * size].astype(ref.dtype)
+
+
+def add(terms, messages, earlier, kind=jnp.bfloat16):
     rows, depth = terms[0].shape
     vmem = pl.BlockSpec(memory_space=pltpu.VMEM)
     return pl.pallas_call(
         functools.partial(add_kernel, len(terms), messages),
-        out_shape=[jax.ShapeDtypeStruct((rows // messages, depth), jnp.bfloat16)] * messages,
+        out_shape=[jax.ShapeDtypeStruct((rows // messages, depth), kind)] * messages,
         in_specs=[vmem] * len(terms) + [pl.BlockSpec(memory_space=pl.ANY)] * len(earlier),
         out_specs=[vmem] * messages,
         compiler_params=pltpu.CompilerParams(vmem_limit_bytes=(4 << 20) + 16 * rows * depth),
@@ -475,16 +479,19 @@
     near = join(received, [mark])
     far = flipped(near, 2, 2)
     near_out, mark = experts([near, swapped(near)], held, mark, half * size)
-    far_out, mark = experts([far, swapped(after(far, mark))], held, mark, half * size)
-    (far_sum_a,) = add([far_out[0], swapped(far_out[2])], 1, [])
-    (far_sum_b,) = add([far_out[1], swapped(far_out[3])], 1, [])
-    total_a = add(
-        [near_out[0], swapped(near_out[2]), flipped(far_sum_a, 2, 2)],
-        half,
-        [mark, weights, attended_mark],
-    )
-    total_b = add([near_out[1], swapped(near_out[3]), flipped(far_sum_b, 2, 2)], half, [total_a[0]])
-    returned = rounds([*total_a, *total_b])
+    (far_next,) = after(far, [mark, weights, attended_mark], 1)
+    far_out, mark = experts([far, swapped(far_next)], held, mark, half * size)
+    far_a_out, far_b_out = far_out[::2], far_out[1::2]
+    far_sums = add([far_a_out[0], swapped(far_a_out[1])], half, [])
+    far_sums += add([far_b_out[0], swapped(far_b_out[1])], half, [])
+    near_sums = add([near_out[0], swapped(near_out[2])], half, [], jnp.float32)
+    near_sums += add([near_out[1], swapped(near_out[3])], half, [], jnp.float32)
+    totals = []
+    earlier = [mark]
+    for near_sum, far_sum in zip(near_sums, far_sums):
+        totals += add([near_sum, flipped(far_sum, 2, 2)], messages // len(far_sums), earlier)
+        earlier = totals[-1:]
+    returned = rounds(totals)
     own, send = combine(weights, returned)
     return finish(own, swapped(send), hidden.shape)
 

time: 63.4 us -> 61 us (0.962)
  waiting for transfers between devices: 26 us -> 20.6 us
  starting transfers between devices: 19.3 us -> 22.1 us
    ppermute x21 -> x23, waiting for transfers between devices: 26 us -> 20.6 us  [flipped(): return lax.ppermute(value, 'ep', pairs)]
    ppermute x21 -> x23, starting transfers between devices: 19.3 us -> 22.1 us  [flipped(): return lax.ppermute(value, 'ep', pairs)]
  transfers between devices with their start and end apart: 21 -> 23, of which waited for: 13 -> 12; matrix products, arithmetic and copies ran while one was open for 0% -> 0% of each run, Pallas kernels for 16% -> 17%
where the time goes in v5:
time: 61 us; the launch traced here: 60.7 us
  starting transfers between devices  22.1 us (36%)
  waiting for transfers between devices  20.6 us (34%)
  Pallas kernels  15.8 us (26%)
  local copies, waits for them, and re-layouts  1.43 us (2%)
  between operations  0.84 us (1%)
    ppermute x23, starting transfers between devices, flipped(): return lax.ppermute(value, 'ep', pairs)  22.1 us
    ppermute x23, waiting for transfers between devices, flipped(): return lax.ppermute(value, 'ep', pairs)  20.6 us
    pallas_call x1, Pallas kernels, load(): pl.pallas_call(load_kernel, out_shape=[jax.ShapeDtypeStruct(w.shape, w.dt...  4.31 us
    pallas_call x2, Pallas kernels, experts(): pl.pallas_call(functools.partial(expert_kernel, count), out_shape=[jax.Sh...  4.26 us
    pallas_call x1, Pallas kernels, attend(): pl.pallas_call(attend_kernel, out_shape=[jax.ShapeDtypeStruct((steps, tok...  2.97 us
    pallas_call x1, Pallas kernels, pack(): pl.pallas_call(functools.partial(pack_kernel, slots, deltas), out_shape=[...  2.25 us
    unnamed x22, local copies, waits for them, and re-layouts  1.43 us
  transfers between devices with their start and end apart: 23, of which 12 were waited for; matrix products, arithmetic and copies ran while one was open for 0% of the time, Pallas kernels for 17%

profile of v5, /device:TPU:0, one launch (start us, length us, event | category | flops | bytes accessed | tf_op | source)
XLA Modules:
  0.0 60.7 jit_solution(18015684097592606822)
XLA Ops:
  0.6 0.5 collective-permute-start.2
  1.1 0.1 collective-permute-start
  1.2 0.4 collective-permute-start.1
  1.7 0.9 %collective-permute-done.other_ids_ref = s32[2,2,4]{2,1,0:T(2,128)S(1)} collective-permute-done((s32[2,2,4]{2,1,0:T(2,128)}, s32[2,2,4]{2,1,0:T(2,128)S(1)}, u32[]{:S(2)}, u32[]{:S(2)}) %collective-permute-start) | collective-permute-done | bytes 96 | tf_op jit(solution)/shard_map/ppermute | solution.py:23
  2.5 0.2 collective-permute-done.1.other_replica_ref
  2.7 0.0 collective-permute-done.2.other_ref
  2.7 0.4 copy-done.9
  3.1 0.2 copy-done.10
  3.3 0.1 copy-done.8
  3.3 2.3 %pack.1 = (bf16[16,7168]{1,0:T(8,128)(2,1)}, f32[2,32,16]{2,1,0:T(8,128)}, f32[2,6,16]{2,1,0:T(8,128)}, bf16[8,7168]{1,0:T(8,128)(2,1)}, bf16[8,7168]{1,0:T(8,12...) custom-call(s32[2,6]{1,0:T(2,128)} %bitcast.11, s32[2,2,4]{2,1,0:T(2,128)} %bitcast.8, s32[2,2,4]{2,1,0:T(2,128)} %bitcast.10, ...), custom_call_target="tpu_custom_call" | custom-call | tf_op jit(solution)/shard_map/pack/pallas_call | solution.py:317
  5.6 5.9 %collective-permute-start.3 = (bf16[8,7168]{1,0:T(8,128)(2,1)}, bf16[8,7168]{1,0:T(8,128)(2,1)S(1)}, u32[]{:S(2)}, u32[]{:S(2)}) collective-permute-start(bf16[8,7168]{1,0:T(8,128)(2,1)} %get-tuple-element.39), channel_id=1, source_target_pairs={{0,28},{1,25},{2,30},{3,27},{4,24},{5,29},{6,26},{7,31},{8,20},{9,... | collective-permute-start | bytes 344072 | tf_op jit(solution)/shard_map/ppermute | solution.py:23
  11.5 0.0 collective-permute-start.4
  11.5 0.6 collective-permute-start.5
  12.1 1.5 %collective-permute-start.6 = (bf16[8,7168]{1,0:T(8,128)(2,1)}, bf16[8,7168]{1,0:T(8,128)(2,1)S(1)}, u32[]{:S(2)}, u32[]{:S(2)}) collective-permute-start(bf16[8,7168]{1,0:T(8,128)(2,1)} %get-tuple-element.42), channel_id=1, source_target_pairs={{0,0},{1,5},{2,2},{3,7},{4,4},{5,1},{6,6},{7,3},{8,8},{9,13},{10,1... | collective-permute-start | bytes 344072 | tf_op jit(solution)/shard_map/ppermute | solution.py:23
  13.6 0.8 %copy-done.3 = f32[2,32,16]{2,1,0:T(8,128)S(1)} copy-done((f32[2,32,16]{2,1,0:T(8,128)S(1)}, f32[2,32,16]{2,1,0:T(8,128)}, u32[]{:S(2)}) %copy-start.3) | copy-done | bytes 4120
  14.4 0.0 copy-start.2
  14.4 0.0 copy-start.4
  14.4 4.3 %load.1 = (bf16[7168,256]{1,0:T(8,128)(2,1)S(1)}, bf16[7168,256]{1,0:T(8,128)(2,1)S(1)}, bf16[256,7168]{1,0:T(8,128)(2,1)S(1)}, f32[8,128]{1,0:T(8,128)S(1)}) custom-call(bf16[7168,256]{1,0:T(8,128)(2,1)} %gate_ref.1, bf16[7168,256]{1,0:T(8,128)(2,1)} %up_ref.1, bf16[256,7168]{1,0:T(8,128)(2,1)} %down_ref.1, f32[2,32,16]{2,1,0:T(8,128)S(1)} %copy-done.3), custom_call_target="tpu_custom_call" | custom-call | tf_op jit(solution)/shard_map/load/pallas_call | solution.py:108
  18.8 0.0 collective-permute-done.3.refs_0_
  18.8 2.0 %collective-permute-done.4.refs_1_ = bf16[8,7168]{1,0:T(8,128)(2,1)S(1)} collective-permute-done((bf16[8,7168]{1,0:T(8,128)(2,1)}, bf16[8,7168]{1,0:T(8,128)(2,1)S(1)}, u32[]{:S(2)}, u32[]{:S(2)}) %collective-permute-start.4) | collective-permute-done | bytes 114720 | tf_op jit(solution)/shard_map/ppermute | solution.py:23
  20.8 0.0 collective-permute-done.5.refs_2_
  20.8 0.0 collective-permute-done.6.refs_3_
  20.8 0.1 collective-permute-start.7
  20.9 1.5 %collective-permute-start.9 = (bf16[32,7168]{1,0:T(8,128)(2,1)S(1)}, bf16[32,7168]{1,0:T(8,128)(2,1)S(1)}, u32[]{:S(2)}, u32[]{:S(2)}) collective-permute-start(bf16[32,7168]{1,0:T(8,128)(2,1)S(1)} %join.1.refs_0_), channel_id=1, source_target_pairs={{0,2},{1,3},{2,0},{3,1},{4,6},{5,7},{6,4},{7,5},{8,10},{9,11},{10,... | collective-permute-start | bytes 1376264 | tf_op jit(solution)/shard_map/ppermute | solution.py:23
  22.4 0.0 copy-done
  22.5 3.0 %attention.1 = (bf16[2,4,64,512]{3,2,1,0:T(8,128)(2,1)}, f32[8,128]{1,0:T(8,128)S(1)}) custom-call(s32[4]{0:T(128)S(1)} %copy-done.7, bf16[2,4,64,576]{3,2,1,0:T(8,128)(2,1)S(1)} %copy-done, bf16[4,64,576]{2,1,0:T(8,128)(2,1)S(1)} %copy-done.1, bf16[2,4,576]{2,1,0:T(4,128)(2,1)S(1)} %copy-done.5), custom_call_target="tpu_custom_call" | custom-call | flops 150994944 | bytes 1474560 | tf_op jit(solution)/shard_map/attention/pallas_call | solution.py:76
  25.4 0.2 weigh.1.refs_1_.weigh_ref
  25.7 0.0 collective-permute-done.7.refs_1_
  25.7 2.1 %experts.2 = (bf16[16,7168]{1,0:T(8,128)(2,1)S(1)}, bf16[16,7168]{1,0:T(8,128)(2,1)S(1)}, bf16[16,7168]{1,0:T(8,128)(2,1)S(1)}, bf16[16,7168]{1,0:T(8,128)(2,1)S(1)}, f32[8,128]{1,0:T(8,128)S(1)}) custom-call(bf16[32,7168]{1,0:T(8,128)(2,1)S(1)} %join.1.refs_0_, bf16[32,7168]{1,0:T(8,128)(2,1)S(1)} %collective-permute-done.7.refs_1_, ...), custom_call_target="tpu_custom_call" | custom-call | tf_op jit(solution)/shard_map/experts/pallas_call | solution.py:148
  27.8 6.0 %collective-permute-done.9.value_ref.refs_0_ = bf16[32,7168]{1,0:T(8,128)(2,1)S(1)} collective-permute-done((bf16[32,7168]{1,0:T(8,128)(2,1)S(1)}, bf16[32,7168]{1,0:T(8,128)(2,1)S(1)}, u32[]{:S(2)}, u32[]{:S(2)}) %collective-permute-start.9) | collective-permute-done | bytes 458784 | tf_op jit(solution)/shard_map/ppermute | solution.py:23
  33.8 0.1 collective-permute-start.10
  33.9 1.8 %collective-permute-done.10.refs_1_ = bf16[32,7168]{1,0:T(8,128)(2,1)S(1)} collective-permute-done((bf16[32,7168]{1,0:T(8,128)(2,1)S(1)}, bf16[32,7168]{1,0:T(8,128)(2,1)S(1)}, u32[]{:S(2)}, u32[]{:S(2)}) %collective-permute-start.10) | collective-permute-done | bytes 458784 | tf_op jit(solution)/shard_map/ppermute | solution.py:23
  35.7 2.1 %experts.3 = (bf16[16,7168]{1,0:T(8,128)(2,1)S(1)}, bf16[16,7168]{1,0:T(8,128)(2,1)S(1)}, bf16[16,7168]{1,0:T(8,128)(2,1)S(1)}, bf16[16,7168]{1,0:T(8,128)(2,1)S(1)}, f32[8,128]{1,0:T(8,128)S(1)}) custom-call(bf16[32,7168]{1,0:T(8,128)(2,1)S(1)} %collective-permute-done.9.value_ref.refs_0_, bf16[32,7168]{1,0:T(8,128)(2,1)S(1)} %collective-permute-done.10.refs_1_, ...), custom_call_target="tpu_custom_call" | custom-call | tf_op jit(solution)/shard_map/experts/pallas_call | solution.py:148
  37.9 0.2 collective-permute-start.11
  38.1 0.4 collective-permute-start.17
  38.4 0.1 collective-permute-start.8
  38.6 0.4 collective-permute-start.16
  39.0 0.5 collective-permute-done.11.refs_1_
  39.4 0.1 add.9
  39.5 1.6 %collective-permute-start.12 = (bf16[8,7168]{1,0:T(8,128)(2,1)S(1)}, bf16[8,7168]{1,0:T(8,128)(2,1)S(1)}, u32[]{:S(2)}, u32[]{:S(2)}) collective-permute-start(bf16[8,7168]{1,0:T(8,128)(2,1)S(1)} %get-tuple-element.54), channel_id=1, source_target_pairs={{0,2},{1,3},{2,0},{3,1},{4,6},{5,7},{6,4},{7,5},{8,10},{9,11},{10,... | collective-permute-start | bytes 344072 | tf_op jit(solution)/shard_map/ppermute | solution.py:23
  41.1 0.5 collective-permute-start.14
  41.6 0.0 collective-permute-done.17.refs_1_
  41.6 0.1 add.13
  41.6 1.6 %collective-permute-start.18 = (bf16[8,7168]{1,0:T(8,128)(2,1)S(1)}, bf16[8,7168]{1,0:T(8,128)(2,1)S(1)}, u32[]{:S(2)}, u32[]{:S(2)}) collective-permute-start(bf16[8,7168]{1,0:T(8,128)(2,1)S(1)} %get-tuple-element.63), channel_id=1, source_target_pairs={{0,2},{1,3},{2,0},{3,1},{4,6},{5,7},{6,4},{7,5},{8,10},{9,11},{10,... | collective-permute-start | bytes 344072 | tf_op jit(solution)/shard_map/ppermute | solution.py:23
  43.2 0.0 collective-permute-done.8.refs_1_
  43.2 0.5 collective-permute-start.20
  43.8 0.0 collective-permute-done.16.refs_1_
  43.8 1.7 %collective-permute-done.12.refs_1_ = bf16[8,7168]{1,0:T(8,128)(2,1)S(1)} collective-permute-done((bf16[8,7168]{1,0:T(8,128)(2,1)S(1)}, bf16[8,7168]{1,0:T(8,128)(2,1)S(1)}, u32[]{:S(2)}, u32[]{:S(2)}) %collective-permute-start.12) | collective-permute-done | bytes 114720 | tf_op jit(solution)/shard_map/ppermute | solution.py:23
  45.6 3.5 %collective-permute-start.13 = (bf16[8,7168]{1,0:T(8,128)(2,1)S(1)}, bf16[8,7168]{1,0:T(8,128)(2,1)S(1)}, u32[]{:S(2)}, u32[]{:S(2)}) collective-permute-start(bf16[8,7168]{1,0:T(8,128)(2,1)S(1)} %add.10.refs_2_), channel_id=1, source_target_pairs={{0,28},{1,25},{2,30},{3,27},{4,24},{5,29},{6,26},{7,31},{8,20},{9,... | collective-permute-start | bytes 344072 | tf_op jit(solution)/shard_map/ppermute | solution.py:23
  49.1 0.0 collective-permute-done.14.refs_1_
  49.1 0.1 collective-permute-start.15
  49.2 1.3 %collective-permute-done.18.refs_1_ = bf16[8,7168]{1,0:T(8,128)(2,1)S(1)} collective-permute-done((bf16[8,7168]{1,0:T(8,128)(2,1)S(1)}, bf16[8,7168]{1,0:T(8,128)(2,1)S(1)}, u32[]{:S(2)}, u32[]{:S(2)}) %collective-permute-start.18) | collective-permute-done | bytes 114720 | tf_op jit(solution)/shard_map/ppermute | solution.py:23
  50.5 1.7 %collective-permute-start.19 = (bf16[8,7168]{1,0:T(8,128)(2,1)S(1)}, bf16[8,7168]{1,0:T(8,128)(2,1)S(1)}, u32[]{:S(2)}, u32[]{:S(2)}) collective-permute-start(bf16[8,7168]{1,0:T(8,128)(2,1)S(1)} %add.14.refs_2_), channel_id=1, source_target_pairs={{0,12},{1,9},{2,14},{3,11},{4,8},{5,13},{6,10},{7,15},{8,4},{9,1},... | collective-permute-start | bytes 344072 | tf_op jit(solution)/shard_map/ppermute | solution.py:23
  52.2 0.0 collective-permute-done.20.refs_1_
  52.2 0.7 %collective-permute-start.21 = (bf16[8,7168]{1,0:T(8,128)(2,1)S(1)}, bf16[8,7168]{1,0:T(8,128)(2,1)S(1)}, u32[]{:S(2)}, u32[]{:S(2)}) collective-permute-start(bf16[8,7168]{1,0:T(8,128)(2,1)S(1)} %add.15), channel_id=1, source_target_pairs={{0,0},{1,5},{2,2},{3,7},{4,4},{5,1},{6,6},{7,3},{8,8},{9,13},{10,1... | collective-permute-start | bytes 344072 | tf_op jit(solution)/shard_map/ppermute | solution.py:23
  52.9 1.5 %collective-permute-done.13.refs_0_ = bf16[8,7168]{1,0:T(8,128)(2,1)S(1)} collective-permute-done((bf16[8,7168]{1,0:T(8,128)(2,1)S(1)}, bf16[8,7168]{1,0:T(8,128)(2,1)S(1)}, u32[]{:S(2)}, u32[]{:S(2)}) %collective-permute-start.13) | collective-permute-done | bytes 114720 | tf_op jit(solution)/shard_map/ppermute | solution.py:23
  54.4 2.8 %collective-permute-done.15.refs_1_ = bf16[8,7168]{1,0:T(8,128)(2,1)S(1)} collective-permute-done((bf16[8,7168]{1,0:T(8,128)(2,1)S(1)}, bf16[8,7168]{1,0:T(8,128)(2,1)S(1)}, u32[]{:S(2)}, u32[]{:S(2)}) %collective-permute-start.15) | collective-permute-done | bytes 114720 | tf_op jit(solution)/shard_map/ppermute | solution.py:23
  57.2 0.4 combine.2.first_ref
  57.5 0.8 %collective-permute-done.19.refs_0_ = bf16[8,7168]{1,0:T(8,128)(2,1)S(1)} collective-permute-done((bf16[8,7168]{1,0:T(8,128)(2,1)S(1)}, bf16[8,7168]{1,0:T(8,128)(2,1)S(1)}, u32[]{:S(2)}, u32[]{:S(2)}) %collective-permute-start.19) | collective-permute-done | bytes 114720 | tf_op jit(solution)/shard_map/ppermute | solution.py:23
  58.3 0.0 collective-permute-done.21.refs_1_
  58.3 0.4 combine.3
  58.7 0.1 collective-permute-start.22
  58.8 1.3 %collective-permute-done.22.received_ref = bf16[8,7168]{1,0:T(8,128)(2,1)S(1)} collective-permute-done((bf16[8,7168]{1,0:T(8,128)(2,1)S(1)}, bf16[8,7168]{1,0:T(8,128)(2,1)S(1)}, u32[]{:S(2)}, u32[]{:S(2)}) %collective-permute-start.22) | collective-permute-done | bytes 114720 | tf_op jit(solution)/shard_map/ppermute | solution.py:23
  60.1 0.7 %finish.1 = bf16[2,4,7168]{2,1,0:T(4,128)(2,1)} custom-call(f32[8,7168]{1,0:T(8,128)S(1)} %get-tuple-element.66.own_ref, bf16[8,7168]{1,0:T(8,128)(2,1)S(1)} %collective-permute-done.22.received_ref), custom_call_target="tpu_custom_call" | custom-call | tf_op jit(solution)/shard_map/finish/pallas_call | solution.py:432
  (23 shorter events, 0.3 us)
Async XLA Ops:
  0.6 2.1 %collective-permute-start.2 = (bf16[2,4,7168]{2,1,0:T(4,128)(2,1)}, bf16[2,4,7168]{2,1,0:T(4,128)(2,1)S(1)}, u32[]{:S(2)}, u32[]{:S(2)}) collective-permute-start(bf16[2,4,7168]{2,1,0:T(4,128)(2,1)} %raw_ref.1), channel_id=1, source_target_pairs={{0,1},{1,0},{2,3},{3,2},{4,5},{5,4},{6,7},{7,6},{8,9},{9,8},{10,11... | collective-permute-start | bytes 344072 | tf_op jit(solution)/shard_map/ppermute | solution.py:23
  1.1 1.4 %collective-permute-start = (s32[2,2,4]{2,1,0:T(2,128)}, s32[2,2,4]{2,1,0:T(2,128)S(1)}, u32[]{:S(2)}, u32[]{:S(2)}) collective-permute-start(s32[2,2,4]{2,1,0:T(2,128)} %bitcast.7), channel_id=1, source_target_pairs={{0,1},{1,0},{2,3},{3,2},{4,5},{5,4},{6,7},{7,6},{8,9},{9,8},{10,11... | collective-permute-start | bytes 200 | tf_op jit(solution)/shard_map/ppermute | solution.py:23
  1.2 1.5 %collective-permute-start.1 = (s32[2,2,4]{2,1,0:T(2,128)}, s32[2,2,4]{2,1,0:T(2,128)S(1)}, u32[]{:S(2)}, u32[]{:S(2)}) collective-permute-start(s32[2,2,4]{2,1,0:T(2,128)} %bitcast.9), channel_id=1, source_target_pairs={{0,1},{1,0},{2,3},{3,2},{4,5},{5,4},{6,7},{7,6},{8,9},{9,8},{10,11... | collective-permute-start | bytes 200 | tf_op jit(solution)/shard_map/ppermute | solution.py:23
  2.5 0.6 copy-start.9
  2.7 0.6 copy-start.10
  2.7 0.6 %copy-start.8 = (bf16[2,4,7168]{2,1,0:T(4,128)(2,1)}, bf16[2,4,7168]{2,1,0:T(4,128)(2,1)S(1)}, u32[]{:S(2)}) copy-start(bf16[2,4,7168]{2,1,0:T(4,128)(2,1)S(1)} %collective-permute-done.2.other_ref) | copy-start | bytes 344068
  5.6 13.2 %collective-permute-start.3 = (bf16[8,7168]{1,0:T(8,128)(2,1)}, bf16[8,7168]{1,0:T(8,128)(2,1)S(1)}, u32[]{:S(2)}, u32[]{:S(2)}) collective-permute-start(bf16[8,7168]{1,0:T(8,128)(2,1)} %get-tuple-element.39), channel_id=1, source_target_pairs={{0,28},{1,25},{2,30},{3,27},{4,24},{5,29},{6,26},{7,31},{8,20},{9,... | collective-permute-start | bytes 344072 | tf_op jit(solution)/shard_map/ppermute | solution.py:23
  11.5 9.3 %collective-permute-start.4 = (bf16[8,7168]{1,0:T(8,128)(2,1)}, bf16[8,7168]{1,0:T(8,128)(2,1)S(1)}, u32[]{:S(2)}, u32[]{:S(2)}) collective-permute-start(bf16[8,7168]{1,0:T(8,128)(2,1)} %get-tuple-element.40), channel_id=1, source_target_pairs={{0,16},{1,21},{2,18},{3,23},{4,20},{5,17},{6,22},{7,19},{8,24},{9,... | collective-permute-start | bytes 344072 | tf_op jit(solution)/shard_map/ppermute | solution.py:23
  11.5 9.3 %collective-permute-start.5 = (bf16[8,7168]{1,0:T(8,128)(2,1)}, bf16[8,7168]{1,0:T(8,128)(2,1)S(1)}, u32[]{:S(2)}, u32[]{:S(2)}) collective-permute-start(bf16[8,7168]{1,0:T(8,128)(2,1)} %get-tuple-element.41), channel_id=1, source_target_pairs={{0,12},{1,9},{2,14},{3,11},{4,8},{5,13},{6,10},{7,15},{8,4},{9,1},... | collective-permute-start | bytes 344072 | tf_op jit(solution)/shard_map/ppermute | solution.py:23
  12.1 8.7 %collective-permute-start.6 = (bf16[8,7168]{1,0:T(8,128)(2,1)}, bf16[8,7168]{1,0:T(8,128)(2,1)S(1)}, u32[]{:S(2)}, u32[]{:S(2)}) collective-permute-start(bf16[8,7168]{1,0:T(8,128)(2,1)} %get-tuple-element.42), channel_id=1, source_target_pairs={{0,0},{1,5},{2,2},{3,7},{4,4},{5,1},{6,6},{7,3},{8,8},{9,13},{10,1... | collective-permute-start | bytes 344072 | tf_op jit(solution)/shard_map/ppermute | solution.py:23
  13.6 0.8 %copy-start.3 = (f32[2,32,16]{2,1,0:T(8,128)S(1)}, f32[2,32,16]{2,1,0:T(8,128)}, u32[]{:S(2)}) copy-start(f32[2,32,16]{2,1,0:T(8,128)} %get-tuple-element.37.place_ref._) | copy-start | bytes 12292
  14.4 8.0 %copy-start = (bf16[2,4,64,576]{3,2,1,0:T(8,128)(2,1)S(1)}, bf16[2,4,64,576]{3,2,1,0:T(8,128)(2,1)}, u32[]{:S(2)}) copy-start(bf16[2,4,64,576]{3,2,1,0:T(8,128)(2,1)} %query_ref.1) | copy-start | bytes 1769476
  14.4 8.0 %copy-start.1 = (bf16[4,64,576]{2,1,0:T(8,128)(2,1)S(1)}, bf16[4,64,576]{2,1,0:T(8,128)(2,1)}, u32[]{:S(2)}) copy-start(bf16[4,64,576]{2,1,0:T(8,128)(2,1)} %cache_ref.1) | copy-start | bytes 884740
  14.4 8.0 %copy-start.5 = (bf16[2,4,576]{2,1,0:T(4,128)(2,1)S(1)}, bf16[2,4,576]{2,1,0:T(4,128)(2,1)}, u32[]{:S(2)}) copy-start(bf16[2,4,576]{2,1,0:T(4,128)(2,1)} %fresh_ref.1) | copy-start | bytes 27652
  14.4 8.0 %copy-start.7 = (s32[4]{0:T(128)S(1)}, s32[4]{0:T(128)}, u32[]{:S(2)}) copy-start(s32[4]{0:T(128)} %lengths_ref.1) | copy-start | bytes 52
  14.4 11.0 %copy-start.2 = (bf16[16,7168]{1,0:T(8,128)(2,1)S(1)}, bf16[16,7168]{1,0:T(8,128)(2,1)}, u32[]{:S(2)}) copy-start(bf16[16,7168]{1,0:T(8,128)(2,1)} %get-tuple-element.36.normed_ref) | copy-start | bytes 688132
  14.4 11.0 %copy-start.4 = (bf16[7168,6]{0,1:T(8,128)(2,1)S(1)}, bf16[7168,6]{0,1:T(8,128)(2,1)}, u32[]{:S(2)}) copy-start(bf16[7168,6]{0,1:T(8,128)(2,1)} %param.15) | copy-start | bytes 258052
  14.4 11.0 %copy-start.6 = (f32[2,6,16]{2,1,0:T(8,128)S(1)}, f32[2,6,16]{2,1,0:T(8,128)}, u32[]{:S(2)}) copy-start(f32[2,6,16]{2,1,0:T(8,128)} %get-tuple-element.38.choose_ref) | copy-start | bytes 2308
  20.8 4.9 %collective-permute-start.7 = (bf16[32,7168]{1,0:T(8,128)(2,1)S(1)}, bf16[32,7168]{1,0:T(8,128)(2,1)S(1)}, u32[]{:S(2)}, u32[]{:S(2)}) collective-permute-start(bf16[32,7168]{1,0:T(8,128)(2,1)S(1)} %join.1.refs_0_), channel_id=1, source_target_pairs={{0,1},{1,0},{2,3},{3,2},{4,5},{5,4},{6,7},{7,6},{8,9},{9,8},{10,11... | collective-permute-start | bytes 1376264 | tf_op jit(solution)/shard_map/ppermute | solution.py:23
  20.9 12.9 %collective-permute-start.9 = (bf16[32,7168]{1,0:T(8,128)(2,1)S(1)}, bf16[32,7168]{1,0:T(8,128)(2,1)S(1)}, u32[]{:S(2)}, u32[]{:S(2)}) collective-permute-start(bf16[32,7168]{1,0:T(8,128)(2,1)S(1)} %join.1.refs_0_), channel_id=1, source_target_pairs={{0,2},{1,3},{2,0},{3,1},{4,6},{5,7},{6,4},{7,5},{8,10},{9,11},{10,... | collective-permute-start | bytes 1376264 | tf_op jit(solution)/shard_map/ppermute | solution.py:23
  33.8 1.9 %collective-permute-start.10 = (bf16[32,7168]{1,0:T(8,128)(2,1)S(1)}, bf16[32,7168]{1,0:T(8,128)(2,1)S(1)}, u32[]{:S(2)}, u32[]{:S(2)}) collective-permute-start(bf16[32,7168]{1,0:T(8,128)(2,1)S(1)} %after.1), channel_id=1, source_target_pairs={{0,1},{1,0},{2,3},{3,2},{4,5},{5,4},{6,7},{7,6},{8,9},{9,8},{10,11... | collective-permute-start | bytes 1376264 | tf_op jit(solution)/shard_map/ppermute | solution.py:23
  37.9 1.6 %collective-permute-start.11 = (bf16[16,7168]{1,0:T(8,128)(2,1)S(1)}, bf16[16,7168]{1,0:T(8,128)(2,1)S(1)}, u32[]{:S(2)}, u32[]{:S(2)}) collective-permute-start(bf16[16,7168]{1,0:T(8,128)(2,1)S(1)} %get-tuple-element.53), channel_id=1, source_target_pairs={{0,1},{1,0},{2,3},{3,2},{4,5},{5,4},{6,7},{7,6},{8,9},{9,8},{10,11... | collective-permute-start | bytes 688136 | tf_op jit(solution)/shard_map/ppermute | solution.py:23
  38.1 3.5 %collective-permute-start.17 = (bf16[16,7168]{1,0:T(8,128)(2,1)S(1)}, bf16[16,7168]{1,0:T(8,128)(2,1)S(1)}, u32[]{:S(2)}, u32[]{:S(2)}) collective-permute-start(bf16[16,7168]{1,0:T(8,128)(2,1)S(1)} %get-tuple-element.62), channel_id=1, source_target_pairs={{0,1},{1,0},{2,3},{3,2},{4,5},{5,4},{6,7},{7,6},{8,9},{9,8},{10,11... | collective-permute-start | bytes 688136 | tf_op jit(solution)/shard_map/ppermute | solution.py:23
  38.4 4.8 %collective-permute-start.8 = (bf16[16,7168]{1,0:T(8,128)(2,1)S(1)}, bf16[16,7168]{1,0:T(8,128)(2,1)S(1)}, u32[]{:S(2)}, u32[]{:S(2)}) collective-permute-start(bf16[16,7168]{1,0:T(8,128)(2,1)S(1)} %get-tuple-element.48), channel_id=1, source_target_pairs={{0,1},{1,0},{2,3},{3,2},{4,5},{5,4},{6,7},{7,6},{8,9},{9,8},{10,11... | collective-permute-start | bytes 688136 | tf_op jit(solution)/shard_map/ppermute | solution.py:23
  38.6 5.2 %collective-permute-start.16 = (bf16[16,7168]{1,0:T(8,128)(2,1)S(1)}, bf16[16,7168]{1,0:T(8,128)(2,1)S(1)}, u32[]{:S(2)}, u32[]{:S(2)}) collective-permute-start(bf16[16,7168]{1,0:T(8,128)(2,1)S(1)} %get-tuple-element.59), channel_id=1, source_target_pairs={{0,1},{1,0},{2,3},{3,2},{4,5},{5,4},{6,7},{7,6},{8,9},{9,8},{10,11... | collective-permute-start | bytes 688136 | tf_op jit(solution)/shard_map/ppermute | solution.py:23
  39.5 6.1 %collective-permute-start.12 = (bf16[8,7168]{1,0:T(8,128)(2,1)S(1)}, bf16[8,7168]{1,0:T(8,128)(2,1)S(1)}, u32[]{:S(2)}, u32[]{:S(2)}) collective-permute-start(bf16[8,7168]{1,0:T(8,128)(2,1)S(1)} %get-tuple-element.54), channel_id=1, source_target_pairs={{0,2},{1,3},{2,0},{3,1},{4,6},{5,7},{6,4},{7,5},{8,10},{9,11},{10,... | collective-permute-start | bytes 344072 | tf_op jit(solution)/shard_map/ppermute | solution.py:23
  41.1 8.0 %collective-permute-start.14 = (bf16[8,7168]{1,0:T(8,128)(2,1)S(1)}, bf16[8,7168]{1,0:T(8,128)(2,1)S(1)}, u32[]{:S(2)}, u32[]{:S(2)}) collective-permute-start(bf16[8,7168]{1,0:T(8,128)(2,1)S(1)} %get-tuple-element.57), channel_id=1, source_target_pairs={{0,2},{1,3},{2,0},{3,1},{4,6},{5,7},{6,4},{7,5},{8,10},{9,11},{10,... | collective-permute-start | bytes 344072 | tf_op jit(solution)/shard_map/ppermute | solution.py:23
  41.6 8.8 %collective-permute-start.18 = (bf16[8,7168]{1,0:T(8,128)(2,1)S(1)}, bf16[8,7168]{1,0:T(8,128)(2,1)S(1)}, u32[]{:S(2)}, u32[]{:S(2)}) collective-permute-start(bf16[8,7168]{1,0:T(8,128)(2,1)S(1)} %get-tuple-element.63), channel_id=1, source_target_pairs={{0,2},{1,3},{2,0},{3,1},{4,6},{5,7},{6,4},{7,5},{8,10},{9,11},{10,... | collective-permute-start | bytes 344072 | tf_op jit(solution)/shard_map/ppermute | solution.py:23
  43.2 9.0 %collective-permute-start.20 = (bf16[8,7168]{1,0:T(8,128)(2,1)S(1)}, bf16[8,7168]{1,0:T(8,128)(2,1)S(1)}, u32[]{:S(2)}, u32[]{:S(2)}) collective-permute-start(bf16[8,7168]{1,0:T(8,128)(2,1)S(1)} %get-tuple-element.65), channel_id=1, source_target_pairs={{0,2},{1,3},{2,0},{3,1},{4,6},{5,7},{6,4},{7,5},{8,10},{9,11},{10,... | collective-permute-start | bytes 344072 | tf_op jit(solution)/shard_map/ppermute | solution.py:23
  45.6 8.8 %collective-permute-start.13 = (bf16[8,7168]{1,0:T(8,128)(2,1)S(1)}, bf16[8,7168]{1,0:T(8,128)(2,1)S(1)}, u32[]{:S(2)}, u32[]{:S(2)}) collective-permute-start(bf16[8,7168]{1,0:T(8,128)(2,1)S(1)} %add.10.refs_2_), channel_id=1, source_target_pairs={{0,28},{1,25},{2,30},{3,27},{4,24},{5,29},{6,26},{7,31},{8,20},{9,... | collective-permute-start | bytes 344072 | tf_op jit(solution)/shard_map/ppermute | solution.py:23
  49.1 8.1 %collective-permute-start.15 = (bf16[8,7168]{1,0:T(8,128)(2,1)S(1)}, bf16[8,7168]{1,0:T(8,128)(2,1)S(1)}, u32[]{:S(2)}, u32[]{:S(2)}) collective-permute-start(bf16[8,7168]{1,0:T(8,128)(2,1)S(1)} %add.11.refs_2_), channel_id=1, source_target_pairs={{0,16},{1,21},{2,18},{3,23},{4,20},{5,17},{6,22},{7,19},{8,24},{9,... | collective-permute-start | bytes 344072 | tf_op jit(solution)/shard_map/ppermute | solution.py:23
  50.5 7.8 %collective-permute-start.19 = (bf16[8,7168]{1,0:T(8,128)(2,1)S(1)}, bf16[8,7168]{1,0:T(8,128)(2,1)S(1)}, u32[]{:S(2)}, u32[]{:S(2)}) collective-permute-start(bf16[8,7168]{1,0:T(8,128)(2,1)S(1)} %add.14.refs_2_), channel_id=1, source_target_pairs={{0,12},{1,9},{2,14},{3,11},{4,8},{5,13},{6,10},{7,15},{8,4},{9,1},... | collective-permute-start | bytes 344072 | tf_op jit(solution)/shard_map/ppermute | solution.py:23
  52.2 6.1 %collective-permute-start.21 = (bf16[8,7168]{1,0:T(8,128)(2,1)S(1)}, bf16[8,7168]{1,0:T(8,128)(2,1)S(1)}, u32[]{:S(2)}, u32[]{:S(2)}) collective-permute-start(bf16[8,7168]{1,0:T(8,128)(2,1)S(1)} %add.15), channel_id=1, source_target_pairs={{0,0},{1,5},{2,2},{3,7},{4,4},{5,1},{6,6},{7,3},{8,8},{9,13},{10,1... | collective-permute-start | bytes 344072 | tf_op jit(solution)/shard_map/ppermute | solution.py:23
  58.7 1.4 %collective-permute-start.22 = (bf16[8,7168]{1,0:T(8,128)(2,1)S(1)}, bf16[8,7168]{1,0:T(8,128)(2,1)S(1)}, u32[]{:S(2)}, u32[]{:S(2)}) collective-permute-start(bf16[8,7168]{1,0:T(8,128)(2,1)S(1)} %get-tuple-element.67), channel_id=1, source_target_pairs={{0,1},{1,0},{2,3},{3,2},{4,5},{5,4},{6,7},{7,6},{8,9},{9,8},{10,11... | collective-permute-start | bytes 344072 | tf_op jit(solution)/shard_map/ppermute | solution.py:23

commit v6 on v5

--- a/solution.py
+++ b/solution.py
@@ -26,13 +26,13 @@
 def lanes(groups):
     hops = [(d & 1) + (d >> 1) for d in range(groups)]
     chosen = ([], [])
-    for d in sorted(range(groups), key=lambda d: (-hops[d], -d)):
+    for d in sorted(range(2, groups), key=lambda d: (-hops[d], -d)):
         sums = [sum(hops[e] for e in lane) for lane in chosen]
         lane = 0 if sums[0] <= sums[1] else 1
-        if 2 * len(chosen[lane]) == groups:
+        if 2 * len(chosen[lane]) == groups - 2:
             lane = 1 - lane
         chosen[lane].append(d)
-    return list(zip(*chosen))
+    return [*zip(*chosen), (0, 1)]
 
 
 def attend_kernel(lengths_ref, query_ref, cache_ref, fresh_ref, out_ref, mark_ref):
@@ -181,26 +181,6 @@
         compiler_params=pltpu.CompilerParams(vmem_limit_bytes=(2 << 20) + 8 * rows * depth),
         name="join",
     )(*parts, *earlier)
-
-
-def after_kernel(pieces, value_ref, *refs):
-    out_refs = refs[-pieces:]
-    rows = out_refs[0].shape[0]
-    for i, ref in enumerate(out_refs):
-        ref[...] = value_ref[i * rows : (i + 1) * rows, :]
-
-
-def after(value, earlier, pieces):
-    rows, depth = value.shape
-    vmem = pl.BlockSpec(memory_space=pltpu.VMEM)
-    return pl.pallas_call(
-        functools.partial(after_kernel, pieces),
-        out_shape=[jax.ShapeDtypeStruct((rows // pieces, depth), value.dtype)] * pieces,
-        in_specs=[vmem] + [pl.BlockSpec(memory_space=pl.ANY)] * len(earlier),
-        out_specs=[vmem] * pieces,
-        compiler_params=pltpu.CompilerParams(vmem_limit_bytes=(2 << 20) + 6 * value.size),
-        name="after",
-    )(value, *earlier)
 
 
 def add_kernel(count, messages, *refs):
@@ -387,7 +367,10 @@
 
 def second_half_kernel(weigh_ref, first_ref, *refs):
     part_refs, own_ref, send_ref = refs[:-2], refs[-2], refs[-1]
-    result = first_ref[...] + weighted(weigh_ref[weigh_ref.shape[0] // 2 :, :], part_refs)
+    size = part_refs[0].shape[0]
+    weights = weigh_ref[weigh_ref.shape[0] // 2 :, :]
+    weights = jnp.concatenate([weights, weights[-size:]], axis=0)
+    result = first_ref[...] + weighted(weights, part_refs)
     half = own_ref.shape[0]
     own_ref[...] = result[:half]
     send_ref[...] = result[half:].astype(jnp.bfloat16)
@@ -398,7 +381,7 @@
     tokens = weights.shape[1]
     vmem = pl.BlockSpec(memory_space=pltpu.VMEM)
     params = pltpu.CompilerParams(vmem_limit_bytes=(8 << 20) + 8 * weights.shape[0] * depth)
-    middle = len(parts) // 2
+    middle = (len(parts) - 1) // 2
     first = pl.pallas_call(
         first_half_kernel,
         out_shape=jax.ShapeDtypeStruct((tokens, depth), jnp.float32),
@@ -470,28 +453,39 @@
             flipped(part, SPAN * low, SPAN * high) for part, (low, high) in zip(parts, deltas)
         ]
 
+    def to_near(part):
+        return flipped(part, 0, SPAN)
+
+    def to_far(part):
+        return flipped(part, 2, SPAN + 2)
+
     weights = weigh(normed, router.T, place, choose)
     expert_weights = (gate_w, up_w, down_w)
     half = messages // 2
     size = packed[0].shape[0]
-    received = rounds(packed)
+    received = rounds(packed[:-1])
+    near_last, far_last = to_near(packed[-1]), to_far(packed[-1])
     held, mark = load(expert_weights, place)
-    near = join(received, [mark])
-    far = flipped(near, 2, 2)
+    near = join([*received, near_last], [mark, far_last])
+    far = flipped(join(received, [mark, far_last]), 2, 2)
     near_out, mark = experts([near, swapped(near)], held, mark, half * size)
-    (far_next,) = after(far, [mark, weights, attended_mark], 1)
-    far_out, mark = experts([far, swapped(far_next)], held, mark, half * size)
-    far_a_out, far_b_out = far_out[::2], far_out[1::2]
-    far_sums = add([far_a_out[0], swapped(far_a_out[1])], half, [])
-    far_sums += add([far_b_out[0], swapped(far_b_out[1])], half, [])
-    near_sums = add([near_out[0], swapped(near_out[2])], half, [], jnp.float32)
-    near_sums += add([near_out[1], swapped(near_out[3])], half, [], jnp.float32)
+    near_sums = [
+        *add([near_out[0], swapped(near_out[2])], half, [], jnp.float32),
+        *add([near_out[1], swapped(near_out[3])], half, [], jnp.float32),
+    ]
+    returned_near = to_near(near_sums[-1].astype(jnp.bfloat16))
+    far = join([far, far_last], [mark, weights, attended_mark])
+    far_out, mark = experts([far, swapped(far)], held, mark, half * size)
+    far_sums = [
+        *add([far_out[0], swapped(far_out[2])], half, []),
+        *add([far_out[1], swapped(far_out[3])], half, []),
+    ]
     totals = []
     earlier = [mark]
-    for near_sum, far_sum in zip(near_sums, far_sums):
-        totals += add([near_sum, flipped(far_sum, 2, 2)], messages // len(far_sums), earlier)
+    for near_sum, far_sum in zip(near_sums[:-1], far_sums[:-1]):
+        totals += add([near_sum, flipped(far_sum, 2, 2)], 1, earlier)
         earlier = totals[-1:]
-    returned = rounds(totals)
+    returned = [*rounds(totals), returned_near, to_far(far_sums[-1])]
     own, send = combine(weights, returned)
     return finish(own, swapped(send), hidden.shape)
 

time: 61 us -> 59.9 us (0.982)
  waiting for transfers between devices: 20.6 us -> 15.8 us
  starting transfers between devices: 22.1 us -> 25.8 us
    ppermute x23 -> x24, waiting for transfers between devices: 20.6 us -> 15.8 us  [flipped(): return lax.ppermute(value, 'ep', pairs)]
    ppermute x23 -> x24, starting transfers between devices: 22.1 us -> 25.8 us  [flipped(): return lax.ppermute(value, 'ep', pairs)]
  transfers between devices with their start and end apart: 23 -> 24, of which waited for: 12 -> 11; matrix products, arithmetic and copies ran while one was open for 0% -> 0% of each run, Pallas kernels for 17% -> 17%
where the time goes in v6:
time: 59.9 us; the launch traced here: 59.7 us
  starting transfers between devices  25.8 us (43%)
  waiting for transfers between devices  15.8 us (26%)
  Pallas kernels  15.8 us (26%)
  local copies, waits for them, and re-layouts  1.43 us (2%)
  between operations  0.86 us (1%)
    ppermute x24, starting transfers between devices, flipped(): return lax.ppermute(value, 'ep', pairs)  25.8 us
    ppermute x24, waiting for transfers between devices, flipped(): return lax.ppermute(value, 'ep', pairs)  15.8 us
    pallas_call x1, Pallas kernels, load(): pl.pallas_call(load_kernel, out_shape=[jax.ShapeDtypeStruct(w.shape, w.dt...  4.31 us
    pallas_call x2, Pallas kernels, experts(): pl.pallas_call(functools.partial(expert_kernel, count), out_shape=[jax.Sh...  4.26 us
    pallas_call x1, Pallas kernels, attend(): pl.pallas_call(attend_kernel, out_shape=[jax.ShapeDtypeStruct((steps, tok...  2.96 us
    pallas_call x1, Pallas kernels, pack(): pl.pallas_call(functools.partial(pack_kernel, slots, deltas), out_shape=[...  2.25 us
    unnamed x22, local copies, waits for them, and re-layouts  1.43 us
  transfers between devices with their start and end apart: 24, of which 11 were waited for; matrix products, arithmetic and copies ran while one was open for 0% of the time, Pallas kernels for 17%

profile of v6, /device:TPU:0, one launch (start us, length us, event | category | flops | bytes accessed | tf_op | source)
XLA Modules:
  0.0 59.7 jit_solution(8378315096951581017)
XLA Ops:
  0.6 0.5 collective-permute-start.2
  1.1 0.1 collective-permute-start
  1.2 0.4 collective-permute-start.1
  1.7 0.9 %collective-permute-done.other_ids_ref = s32[2,2,4]{2,1,0:T(2,128)S(1)} collective-permute-done((s32[2,2,4]{2,1,0:T(2,128)}, s32[2,2,4]{2,1,0:T(2,128)S(1)}, u32[]{:S(2)}, u32[]{:S(2)}) %collective-permute-start) | collective-permute-done | bytes 96 | tf_op jit(solution)/shard_map/ppermute | solution.py:23
  2.5 0.2 collective-permute-done.1.other_replica_ref
  2.7 0.0 collective-permute-done.2.other_ref
  2.7 0.4 copy-done.9
  3.1 0.2 copy-done.10
  3.3 0.1 copy-done.8
  3.3 2.2 %pack.1 = (bf16[16,7168]{1,0:T(8,128)(2,1)}, f32[2,32,16]{2,1,0:T(8,128)}, f32[2,6,16]{2,1,0:T(8,128)}, bf16[8,7168]{1,0:T(8,128)(2,1)}, bf16[8,7168]{1,0:T(8,12...) custom-call(s32[2,6]{1,0:T(2,128)} %bitcast.11, s32[2,2,4]{2,1,0:T(2,128)} %bitcast.8, s32[2,2,4]{2,1,0:T(2,128)} %bitcast.10, ...), custom_call_target="tpu_custom_call" | custom-call | tf_op jit(solution)/shard_map/pack/pallas_call | solution.py:297
  5.6 5.9 %collective-permute-start.3 = (bf16[8,7168]{1,0:T(8,128)(2,1)}, bf16[8,7168]{1,0:T(8,128)(2,1)S(1)}, u32[]{:S(2)}, u32[]{:S(2)}) collective-permute-start(bf16[8,7168]{1,0:T(8,128)(2,1)} %get-tuple-element.39), channel_id=1, source_target_pairs={{0,28},{1,25},{2,30},{3,27},{4,24},{5,29},{6,26},{7,31},{8,20},{9,... | collective-permute-start | bytes 344072 | tf_op jit(solution)/shard_map/ppermute | solution.py:23
  11.5 0.0 collective-permute-start.4
  11.5 0.6 %collective-permute-start.5 = (bf16[8,7168]{1,0:T(8,128)(2,1)}, bf16[8,7168]{1,0:T(8,128)(2,1)S(1)}, u32[]{:S(2)}, u32[]{:S(2)}) collective-permute-start(bf16[8,7168]{1,0:T(8,128)(2,1)} %get-tuple-element.41), channel_id=1, source_target_pairs={{0,12},{1,9},{2,14},{3,11},{4,8},{5,13},{6,10},{7,15},{8,4},{9,1},... | collective-permute-start | bytes 344072 | tf_op jit(solution)/shard_map/ppermute | solution.py:23
  12.1 1.6 %collective-permute-start.7 = (bf16[8,7168]{1,0:T(8,128)(2,1)}, bf16[8,7168]{1,0:T(8,128)(2,1)S(1)}, u32[]{:S(2)}, u32[]{:S(2)}) collective-permute-start(bf16[8,7168]{1,0:T(8,128)(2,1)} %get-tuple-element.42), channel_id=1, source_target_pairs={{0,2},{1,7},{2,0},{3,5},{4,6},{5,3},{6,4},{7,1},{8,10},{9,15},{10,... | collective-permute-start | bytes 344072 | tf_op jit(solution)/shard_map/ppermute | solution.py:23
  13.7 1.5 %collective-permute-start.6 = (bf16[8,7168]{1,0:T(8,128)(2,1)}, bf16[8,7168]{1,0:T(8,128)(2,1)S(1)}, u32[]{:S(2)}, u32[]{:S(2)}) collective-permute-start(bf16[8,7168]{1,0:T(8,128)(2,1)} %get-tuple-element.42), channel_id=1, source_target_pairs={{0,0},{1,5},{2,2},{3,7},{4,4},{5,1},{6,6},{7,3},{8,8},{9,13},{10,1... | collective-permute-start | bytes 344072 | tf_op jit(solution)/shard_map/ppermute | solution.py:23
  15.3 0.8 %copy-done.3 = f32[2,32,16]{2,1,0:T(8,128)S(1)} copy-done((f32[2,32,16]{2,1,0:T(8,128)S(1)}, f32[2,32,16]{2,1,0:T(8,128)}, u32[]{:S(2)}) %copy-start.3) | copy-done | bytes 4120
  16.0 0.0 copy-start.4
  16.1 4.3 %load.1 = (bf16[7168,256]{1,0:T(8,128)(2,1)S(1)}, bf16[7168,256]{1,0:T(8,128)(2,1)S(1)}, bf16[256,7168]{1,0:T(8,128)(2,1)S(1)}, f32[8,128]{1,0:T(8,128)S(1)}) custom-call(bf16[7168,256]{1,0:T(8,128)(2,1)} %gate_ref.1, bf16[7168,256]{1,0:T(8,128)(2,1)} %up_ref.1, bf16[256,7168]{1,0:T(8,128)(2,1)} %down_ref.1, f32[2,32,16]{2,1,0:T(8,128)S(1)} %copy-done.3), custom_call_target="tpu_custom_call" | custom-call | tf_op jit(solution)/shard_map/load/pallas_call | solution.py:108
  20.4 0.0 collective-permute-done.3.refs_0_
  20.4 0.4 collective-permute-done.4.refs_1_
  20.7 0.0 collective-permute-done.5.refs_2_
  20.7 0.0 collective-permute-done.7.refs_5_.refs_4_.refs_1_
  20.8 0.0 collective-permute-done.6.refs_3_
  20.8 0.5 collective-permute-start.8
  21.3 1.2 %collective-permute-start.10 = (bf16[24,7168]{1,0:T(8,128)(2,1)S(1)}, bf16[24,7168]{1,0:T(8,128)(2,1)S(1)}, u32[]{:S(2)}, u32[]{:S(2)}) collective-permute-start(bf16[24,7168]{1,0:T(8,128)(2,1)S(1)} %join.4), channel_id=1, source_target_pairs={{0,2},{1,3},{2,0},{3,1},{4,6},{5,7},{6,4},{7,5},{8,10},{9,11},{10,... | collective-permute-start | bytes 1032200 | tf_op jit(solution)/shard_map/ppermute | solution.py:23
  22.6 3.0 %attention.1 = (bf16[2,4,64,512]{3,2,1,0:T(8,128)(2,1)}, f32[8,128]{1,0:T(8,128)S(1)}) custom-call(s32[4]{0:T(128)S(1)} %copy-done.7, bf16[2,4,64,576]{3,2,1,0:T(8,128)(2,1)S(1)} %copy-done, bf16[4,64,576]{2,1,0:T(8,128)(2,1)S(1)} %copy-done.1, bf16[2,4,576]{2,1,0:T(4,128)(2,1)S(1)} %copy-done.5), custom_call_target="tpu_custom_call" | custom-call | flops 150994944 | bytes 1474560 | tf_op jit(solution)/shard_map/attention/pallas_call | solution.py:76
  25.5 0.2 weigh.1.refs_3_.weigh_ref
  25.8 0.0 collective-permute-done.8.refs_1_
  25.8 2.1 %experts.2 = (bf16[16,7168]{1,0:T(8,128)(2,1)S(1)}, bf16[16,7168]{1,0:T(8,128)(2,1)S(1)}, bf16[16,7168]{1,0:T(8,128)(2,1)S(1)}, bf16[16,7168]{1,0:T(8,128)(2,1)S(1)}, f32[8,128]{1,0:T(8,128)S(1)}) custom-call(bf16[32,7168]{1,0:T(8,128)(2,1)S(1)} %join.3.refs_0_, bf16[32,7168]{1,0:T(8,128)(2,1)S(1)} %collective-permute-done.8.refs_1_, ...), custom_call_target="tpu_custom_call" | custom-call | tf_op jit(solution)/shard_map/experts/pallas_call | solution.py:148
  27.9 3.5 %collective-permute-done.10.refs_0_ = bf16[24,7168]{1,0:T(8,128)(2,1)S(1)} collective-permute-done((bf16[24,7168]{1,0:T(8,128)(2,1)S(1)}, bf16[24,7168]{1,0:T(8,128)(2,1)S(1)}, u32[]{:S(2)}, u32[]{:S(2)}) %collective-permute-start.10) | collective-permute-done | bytes 344096 | tf_op jit(solution)/shard_map/ppermute | solution.py:23
  31.5 0.1 collective-permute-start.11
  31.5 1.8 %collective-permute-done.11.refs_1_ = bf16[32,7168]{1,0:T(8,128)(2,1)S(1)} collective-permute-done((bf16[32,7168]{1,0:T(8,128)(2,1)S(1)}, bf16[32,7168]{1,0:T(8,128)(2,1)S(1)}, u32[]{:S(2)}, u32[]{:S(2)}) %collective-permute-start.11) | collective-permute-done | bytes 458784 | tf_op jit(solution)/shard_map/ppermute | solution.py:23
  33.4 2.1 %experts.3 = (bf16[16,7168]{1,0:T(8,128)(2,1)S(1)}, bf16[16,7168]{1,0:T(8,128)(2,1)S(1)}, bf16[16,7168]{1,0:T(8,128)(2,1)S(1)}, bf16[16,7168]{1,0:T(8,128)(2,1)S(1)}, f32[8,128]{1,0:T(8,128)S(1)}) custom-call(bf16[32,7168]{1,0:T(8,128)(2,1)S(1)} %join.5.refs_0_, bf16[32,7168]{1,0:T(8,128)(2,1)S(1)} %collective-permute-done.11.refs_1_, ...), custom_call_target="tpu_custom_call" | custom-call | tf_op jit(solution)/shard_map/experts/pallas_call | solution.py:148
  35.5 0.2 collective-permute-start.12
  35.7 0.4 collective-permute-start.18
  36.1 0.1 collective-permute-start.17
  36.2 0.4 collective-permute-start.9
  36.6 0.5 collective-permute-done.12.refs_1_
  37.0 0.1 add.8
  37.1 1.6 %collective-permute-start.13 = (bf16[8,7168]{1,0:T(8,128)(2,1)S(1)}, bf16[8,7168]{1,0:T(8,128)(2,1)S(1)}, u32[]{:S(2)}, u32[]{:S(2)}) collective-permute-start(bf16[8,7168]{1,0:T(8,128)(2,1)S(1)} %get-tuple-element.54), channel_id=1, source_target_pairs={{0,2},{1,3},{2,0},{3,1},{4,6},{5,7},{6,4},{7,5},{8,10},{9,11},{10,... | collective-permute-start | bytes 344072 | tf_op jit(solution)/shard_map/ppermute | solution.py:23
  38.7 0.5 collective-permute-start.15
  39.2 0.0 collective-permute-done.18.refs_1_
  39.2 0.1 add.12
  39.3 1.6 %collective-permute-start.19 = (bf16[8,7168]{1,0:T(8,128)(2,1)S(1)}, bf16[8,7168]{1,0:T(8,128)(2,1)S(1)}, u32[]{:S(2)}, u32[]{:S(2)}) collective-permute-start(bf16[8,7168]{1,0:T(8,128)(2,1)S(1)} %get-tuple-element.63), channel_id=1, source_target_pairs={{0,2},{1,3},{2,0},{3,1},{4,6},{5,7},{6,4},{7,5},{8,10},{9,11},{10,... | collective-permute-start | bytes 344072 | tf_op jit(solution)/shard_map/ppermute | solution.py:23
  40.8 0.0 collective-permute-done.17.refs_1_
  40.9 0.7 %collective-permute-start.21 = (bf16[8,7168]{1,0:T(8,128)(2,1)S(1)}, bf16[8,7168]{1,0:T(8,128)(2,1)S(1)}, u32[]{:S(2)}, u32[]{:S(2)}) collective-permute-start(bf16[8,7168]{1,0:T(8,128)(2,1)S(1)} %convert_element_type.3), channel_id=1, source_target_pairs={{0,0},{1,5},{2,2},{3,7},{4,4},{5,1},{6,6},{7,3},{8,8},{9,13},{10,1... | collective-permute-start | bytes 344072 | tf_op jit(solution)/shard_map/ppermute | solution.py:23
  41.6 0.0 collective-permute-done.9.refs_1_
  41.7 0.6 collective-permute-start.22
  42.2 0.9 %collective-permute-done.13.refs_1_ = bf16[8,7168]{1,0:T(8,128)(2,1)S(1)} collective-permute-done((bf16[8,7168]{1,0:T(8,128)(2,1)S(1)}, bf16[8,7168]{1,0:T(8,128)(2,1)S(1)}, u32[]{:S(2)}, u32[]{:S(2)}) %collective-permute-start.13) | collective-permute-done | bytes 114720 | tf_op jit(solution)/shard_map/ppermute | solution.py:23
  43.2 4.3 %collective-permute-start.14 = (bf16[8,7168]{1,0:T(8,128)(2,1)S(1)}, bf16[8,7168]{1,0:T(8,128)(2,1)S(1)}, u32[]{:S(2)}, u32[]{:S(2)}) collective-permute-start(bf16[8,7168]{1,0:T(8,128)(2,1)S(1)} %add.9.refs_2_), channel_id=1, source_target_pairs={{0,28},{1,25},{2,30},{3,27},{4,24},{5,29},{6,26},{7,31},{8,20},{9,... | collective-permute-start | bytes 344072 | tf_op jit(solution)/shard_map/ppermute | solution.py:23
  47.5 0.0 collective-permute-done.15.refs_1_
  47.5 0.5 collective-permute-start.16
  48.0 0.1 collective-permute-done.19.refs_1_
  48.1 2.5 %collective-permute-start.20 = (bf16[8,7168]{1,0:T(8,128)(2,1)S(1)}, bf16[8,7168]{1,0:T(8,128)(2,1)S(1)}, u32[]{:S(2)}, u32[]{:S(2)}) collective-permute-start(bf16[8,7168]{1,0:T(8,128)(2,1)S(1)} %add.13), channel_id=1, source_target_pairs={{0,12},{1,9},{2,14},{3,11},{4,8},{5,13},{6,10},{7,15},{8,4},{9,1},... | collective-permute-start | bytes 344072 | tf_op jit(solution)/shard_map/ppermute | solution.py:23
  50.6 1.4 %collective-permute-done.14.refs_0_ = bf16[8,7168]{1,0:T(8,128)(2,1)S(1)} collective-permute-done((bf16[8,7168]{1,0:T(8,128)(2,1)S(1)}, bf16[8,7168]{1,0:T(8,128)(2,1)S(1)}, u32[]{:S(2)}, u32[]{:S(2)}) %collective-permute-start.14) | collective-permute-done | bytes 114720 | tf_op jit(solution)/shard_map/ppermute | solution.py:23
  52.0 4.9 %collective-permute-done.16.refs_1_ = bf16[8,7168]{1,0:T(8,128)(2,1)S(1)} collective-permute-done((bf16[8,7168]{1,0:T(8,128)(2,1)S(1)}, bf16[8,7168]{1,0:T(8,128)(2,1)S(1)}, u32[]{:S(2)}, u32[]{:S(2)}) %collective-permute-start.16) | collective-permute-done | bytes 114720 | tf_op jit(solution)/shard_map/ppermute | solution.py:23
  56.8 0.4 combine.2.first_ref
  57.2 0.0 collective-permute-done.21.refs_1_
  57.2 0.0 collective-permute-done.22.refs_2_
  57.2 0.0 collective-permute-done.20.refs_0_
  57.2 0.4 combine.3
  57.6 0.1 collective-permute-start.23
  57.7 1.3 %collective-permute-done.23.received_ref = bf16[8,7168]{1,0:T(8,128)(2,1)S(1)} collective-permute-done((bf16[8,7168]{1,0:T(8,128)(2,1)S(1)}, bf16[8,7168]{1,0:T(8,128)(2,1)S(1)}, u32[]{:S(2)}, u32[]{:S(2)}) %collective-permute-start.23) | collective-permute-done | bytes 114720 | tf_op jit(solution)/shard_map/ppermute | solution.py:23
  59.0 0.7 %finish.1 = bf16[2,4,7168]{2,1,0:T(4,128)(2,1)} custom-call(f32[8,7168]{1,0:T(8,128)S(1)} %get-tuple-element.66.own_ref, bf16[8,7168]{1,0:T(8,128)(2,1)S(1)} %collective-permute-done.23.received_ref), custom_call_target="tpu_custom_call" | custom-call | tf_op jit(solution)/shard_map/finish/pallas_call | solution.py:415
  (26 shorter events, 0.3 us)
Async XLA Ops:
  0.6 2.1 %collective-permute-start.2 = (bf16[2,4,7168]{2,1,0:T(4,128)(2,1)}, bf16[2,4,7168]{2,1,0:T(4,128)(2,1)S(1)}, u32[]{:S(2)}, u32[]{:S(2)}) collective-permute-start(bf16[2,4,7168]{2,1,0:T(4,128)(2,1)} %raw_ref.1), channel_id=1, source_target_pairs={{0,1},{1,0},{2,3},{3,2},{4,5},{5,4},{6,7},{7,6},{8,9},{9,8},{10,11... | collective-permute-start | bytes 344072 | tf_op jit(solution)/shard_map/ppermute | solution.py:23
  1.1 1.4 %collective-permute-start = (s32[2,2,4]{2,1,0:T(2,128)}, s32[2,2,4]{2,1,0:T(2,128)S(1)}, u32[]{:S(2)}, u32[]{:S(2)}) collective-permute-start(s32[2,2,4]{2,1,0:T(2,128)} %bitcast.7), channel_id=1, source_target_pairs={{0,1},{1,0},{2,3},{3,2},{4,5},{5,4},{6,7},{7,6},{8,9},{9,8},{10,11... | collective-permute-start | bytes 200 | tf_op jit(solution)/shard_map/ppermute | solution.py:23
  1.2 1.5 %collective-permute-start.1 = (s32[2,2,4]{2,1,0:T(2,128)}, s32[2,2,4]{2,1,0:T(2,128)S(1)}, u32[]{:S(2)}, u32[]{:S(2)}) collective-permute-start(s32[2,2,4]{2,1,0:T(2,128)} %bitcast.9), channel_id=1, source_target_pairs={{0,1},{1,0},{2,3},{3,2},{4,5},{5,4},{6,7},{7,6},{8,9},{9,8},{10,11... | collective-permute-start | bytes 200 | tf_op jit(solution)/shard_map/ppermute | solution.py:23
  2.5 0.6 copy-start.9
  2.7 0.6 copy-start.10
  2.7 0.6 %copy-start.8 = (bf16[2,4,7168]{2,1,0:T(4,128)(2,1)}, bf16[2,4,7168]{2,1,0:T(4,128)(2,1)S(1)}, u32[]{:S(2)}) copy-start(bf16[2,4,7168]{2,1,0:T(4,128)(2,1)S(1)} %collective-permute-done.2.other_ref) | copy-start | bytes 344068
  5.6 14.8 %collective-permute-start.3 = (bf16[8,7168]{1,0:T(8,128)(2,1)}, bf16[8,7168]{1,0:T(8,128)(2,1)S(1)}, u32[]{:S(2)}, u32[]{:S(2)}) collective-permute-start(bf16[8,7168]{1,0:T(8,128)(2,1)} %get-tuple-element.39), channel_id=1, source_target_pairs={{0,28},{1,25},{2,30},{3,27},{4,24},{5,29},{6,26},{7,31},{8,20},{9,... | collective-permute-start | bytes 344072 | tf_op jit(solution)/shard_map/ppermute | solution.py:23
  11.5 9.3 %collective-permute-start.4 = (bf16[8,7168]{1,0:T(8,128)(2,1)}, bf16[8,7168]{1,0:T(8,128)(2,1)S(1)}, u32[]{:S(2)}, u32[]{:S(2)}) collective-permute-start(bf16[8,7168]{1,0:T(8,128)(2,1)} %get-tuple-element.40), channel_id=1, source_target_pairs={{0,16},{1,21},{2,18},{3,23},{4,20},{5,17},{6,22},{7,19},{8,24},{9,... | collective-permute-start | bytes 344072 | tf_op jit(solution)/shard_map/ppermute | solution.py:23
  11.5 9.3 %collective-permute-start.5 = (bf16[8,7168]{1,0:T(8,128)(2,1)}, bf16[8,7168]{1,0:T(8,128)(2,1)S(1)}, u32[]{:S(2)}, u32[]{:S(2)}) collective-permute-start(bf16[8,7168]{1,0:T(8,128)(2,1)} %get-tuple-element.41), channel_id=1, source_target_pairs={{0,12},{1,9},{2,14},{3,11},{4,8},{5,13},{6,10},{7,15},{8,4},{9,1},... | collective-permute-start | bytes 344072 | tf_op jit(solution)/shard_map/ppermute | solution.py:23
  12.1 8.7 %collective-permute-start.7 = (bf16[8,7168]{1,0:T(8,128)(2,1)}, bf16[8,7168]{1,0:T(8,128)(2,1)S(1)}, u32[]{:S(2)}, u32[]{:S(2)}) collective-permute-start(bf16[8,7168]{1,0:T(8,128)(2,1)} %get-tuple-element.42), channel_id=1, source_target_pairs={{0,2},{1,7},{2,0},{3,5},{4,6},{5,3},{6,4},{7,1},{8,10},{9,15},{10,... | collective-permute-start | bytes 344072 | tf_op jit(solution)/shard_map/ppermute | solution.py:23
  13.7 7.0 %collective-permute-start.6 = (bf16[8,7168]{1,0:T(8,128)(2,1)}, bf16[8,7168]{1,0:T(8,128)(2,1)S(1)}, u32[]{:S(2)}, u32[]{:S(2)}) collective-permute-start(bf16[8,7168]{1,0:T(8,128)(2,1)} %get-tuple-element.42), channel_id=1, source_target_pairs={{0,0},{1,5},{2,2},{3,7},{4,4},{5,1},{6,6},{7,3},{8,8},{9,13},{10,1... | collective-permute-start | bytes 344072 | tf_op jit(solution)/shard_map/ppermute | solution.py:23
  15.3 0.8 %copy-start.3 = (f32[2,32,16]{2,1,0:T(8,128)S(1)}, f32[2,32,16]{2,1,0:T(8,128)}, u32[]{:S(2)}) copy-start(f32[2,32,16]{2,1,0:T(8,128)} %get-tuple-element.37.place_ref._) | copy-start | bytes 12292
  16.0 6.5 %copy-start = (bf16[2,4,64,576]{3,2,1,0:T(8,128)(2,1)S(1)}, bf16[2,4,64,576]{3,2,1,0:T(8,128)(2,1)}, u32[]{:S(2)}) copy-start(bf16[2,4,64,576]{3,2,1,0:T(8,128)(2,1)} %query_ref.1) | copy-start | bytes 1769476
  16.0 6.5 %copy-start.1 = (bf16[4,64,576]{2,1,0:T(8,128)(2,1)S(1)}, bf16[4,64,576]{2,1,0:T(8,128)(2,1)}, u32[]{:S(2)}) copy-start(bf16[4,64,576]{2,1,0:T(8,128)(2,1)} %cache_ref.1) | copy-start | bytes 884740
  16.0 6.5 %copy-start.5 = (bf16[2,4,576]{2,1,0:T(4,128)(2,1)S(1)}, bf16[2,4,576]{2,1,0:T(4,128)(2,1)}, u32[]{:S(2)}) copy-start(bf16[2,4,576]{2,1,0:T(4,128)(2,1)} %fresh_ref.1) | copy-start | bytes 27652
  16.0 6.5 %copy-start.7 = (s32[4]{0:T(128)S(1)}, s32[4]{0:T(128)}, u32[]{:S(2)}) copy-start(s32[4]{0:T(128)} %lengths_ref.1) | copy-start | bytes 52
  16.0 9.5 %copy-start.2 = (bf16[16,7168]{1,0:T(8,128)(2,1)S(1)}, bf16[16,7168]{1,0:T(8,128)(2,1)}, u32[]{:S(2)}) copy-start(bf16[16,7168]{1,0:T(8,128)(2,1)} %get-tuple-element.36.normed_ref) | copy-start | bytes 688132
  16.0 9.5 %copy-start.4 = (bf16[7168,6]{0,1:T(8,128)(2,1)S(1)}, bf16[7168,6]{0,1:T(8,128)(2,1)}, u32[]{:S(2)}) copy-start(bf16[7168,6]{0,1:T(8,128)(2,1)} %param.15) | copy-start | bytes 258052
  16.0 9.5 %copy-start.6 = (f32[2,6,16]{2,1,0:T(8,128)S(1)}, f32[2,6,16]{2,1,0:T(8,128)}, u32[]{:S(2)}) copy-start(f32[2,6,16]{2,1,0:T(8,128)} %get-tuple-element.38.choose_ref) | copy-start | bytes 2308
  20.8 5.0 %collective-permute-start.8 = (bf16[32,7168]{1,0:T(8,128)(2,1)S(1)}, bf16[32,7168]{1,0:T(8,128)(2,1)S(1)}, u32[]{:S(2)}, u32[]{:S(2)}) collective-permute-start(bf16[32,7168]{1,0:T(8,128)(2,1)S(1)} %join.3.refs_0_), channel_id=1, source_target_pairs={{0,1},{1,0},{2,3},{3,2},{4,5},{5,4},{6,7},{7,6},{8,9},{9,8},{10,11... | collective-permute-start | bytes 1376264 | tf_op jit(solution)/shard_map/ppermute | solution.py:23
  21.3 10.1 %collective-permute-start.10 = (bf16[24,7168]{1,0:T(8,128)(2,1)S(1)}, bf16[24,7168]{1,0:T(8,128)(2,1)S(1)}, u32[]{:S(2)}, u32[]{:S(2)}) collective-permute-start(bf16[24,7168]{1,0:T(8,128)(2,1)S(1)} %join.4), channel_id=1, source_target_pairs={{0,2},{1,3},{2,0},{3,1},{4,6},{5,7},{6,4},{7,5},{8,10},{9,11},{10,... | collective-permute-start | bytes 1032200 | tf_op jit(solution)/shard_map/ppermute | solution.py:23
  31.5 1.9 %collective-permute-start.11 = (bf16[32,7168]{1,0:T(8,128)(2,1)S(1)}, bf16[32,7168]{1,0:T(8,128)(2,1)S(1)}, u32[]{:S(2)}, u32[]{:S(2)}) collective-permute-start(bf16[32,7168]{1,0:T(8,128)(2,1)S(1)} %join.5.refs_0_), channel_id=1, source_target_pairs={{0,1},{1,0},{2,3},{3,2},{4,5},{5,4},{6,7},{7,6},{8,9},{9,8},{10,11... | collective-permute-start | bytes 1376264 | tf_op jit(solution)/shard_map/ppermute | solution.py:23
  35.5 1.6 %collective-permute-start.12 = (bf16[16,7168]{1,0:T(8,128)(2,1)S(1)}, bf16[16,7168]{1,0:T(8,128)(2,1)S(1)}, u32[]{:S(2)}, u32[]{:S(2)}) collective-permute-start(bf16[16,7168]{1,0:T(8,128)(2,1)S(1)} %get-tuple-element.53), channel_id=1, source_target_pairs={{0,1},{1,0},{2,3},{3,2},{4,5},{5,4},{6,7},{7,6},{8,9},{9,8},{10,11... | collective-permute-start | bytes 688136 | tf_op jit(solution)/shard_map/ppermute | solution.py:23
  35.7 3.5 %collective-permute-start.18 = (bf16[16,7168]{1,0:T(8,128)(2,1)S(1)}, bf16[16,7168]{1,0:T(8,128)(2,1)S(1)}, u32[]{:S(2)}, u32[]{:S(2)}) collective-permute-start(bf16[16,7168]{1,0:T(8,128)(2,1)S(1)} %get-tuple-element.62), channel_id=1, source_target_pairs={{0,1},{1,0},{2,3},{3,2},{4,5},{5,4},{6,7},{7,6},{8,9},{9,8},{10,11... | collective-permute-start | bytes 688136 | tf_op jit(solution)/shard_map/ppermute | solution.py:23
  36.1 4.8 %collective-permute-start.17 = (bf16[16,7168]{1,0:T(8,128)(2,1)S(1)}, bf16[16,7168]{1,0:T(8,128)(2,1)S(1)}, u32[]{:S(2)}, u32[]{:S(2)}) collective-permute-start(bf16[16,7168]{1,0:T(8,128)(2,1)S(1)} %get-tuple-element.59), channel_id=1, source_target_pairs={{0,1},{1,0},{2,3},{3,2},{4,5},{5,4},{6,7},{7,6},{8,9},{9,8},{10,11... | collective-permute-start | bytes 688136 | tf_op jit(solution)/shard_map/ppermute | solution.py:23
  36.2 5.4 %collective-permute-start.9 = (bf16[16,7168]{1,0:T(8,128)(2,1)S(1)}, bf16[16,7168]{1,0:T(8,128)(2,1)S(1)}, u32[]{:S(2)}, u32[]{:S(2)}) collective-permute-start(bf16[16,7168]{1,0:T(8,128)(2,1)S(1)} %get-tuple-element.48), channel_id=1, source_target_pairs={{0,1},{1,0},{2,3},{3,2},{4,5},{5,4},{6,7},{7,6},{8,9},{9,8},{10,11... | collective-permute-start | bytes 688136 | tf_op jit(solution)/shard_map/ppermute | solution.py:23
  37.1 6.1 %collective-permute-start.13 = (bf16[8,7168]{1,0:T(8,128)(2,1)S(1)}, bf16[8,7168]{1,0:T(8,128)(2,1)S(1)}, u32[]{:S(2)}, u32[]{:S(2)}) collective-permute-start(bf16[8,7168]{1,0:T(8,128)(2,1)S(1)} %get-tuple-element.54), channel_id=1, source_target_pairs={{0,2},{1,3},{2,0},{3,1},{4,6},{5,7},{6,4},{7,5},{8,10},{9,11},{10,... | collective-permute-start | bytes 344072 | tf_op jit(solution)/shard_map/ppermute | solution.py:23
  38.7 8.8 %collective-permute-start.15 = (bf16[8,7168]{1,0:T(8,128)(2,1)S(1)}, bf16[8,7168]{1,0:T(8,128)(2,1)S(1)}, u32[]{:S(2)}, u32[]{:S(2)}) collective-permute-start(bf16[8,7168]{1,0:T(8,128)(2,1)S(1)} %get-tuple-element.57), channel_id=1, source_target_pairs={{0,2},{1,3},{2,0},{3,1},{4,6},{5,7},{6,4},{7,5},{8,10},{9,11},{10,... | collective-permute-start | bytes 344072 | tf_op jit(solution)/shard_map/ppermute | solution.py:23
  39.3 8.8 %collective-permute-start.19 = (bf16[8,7168]{1,0:T(8,128)(2,1)S(1)}, bf16[8,7168]{1,0:T(8,128)(2,1)S(1)}, u32[]{:S(2)}, u32[]{:S(2)}) collective-permute-start(bf16[8,7168]{1,0:T(8,128)(2,1)S(1)} %get-tuple-element.63), channel_id=1, source_target_pairs={{0,2},{1,3},{2,0},{3,1},{4,6},{5,7},{6,4},{7,5},{8,10},{9,11},{10,... | collective-permute-start | bytes 344072 | tf_op jit(solution)/shard_map/ppermute | solution.py:23
  40.9 16.3 %collective-permute-start.21 = (bf16[8,7168]{1,0:T(8,128)(2,1)S(1)}, bf16[8,7168]{1,0:T(8,128)(2,1)S(1)}, u32[]{:S(2)}, u32[]{:S(2)}) collective-permute-start(bf16[8,7168]{1,0:T(8,128)(2,1)S(1)} %convert_element_type.3), channel_id=1, source_target_pairs={{0,0},{1,5},{2,2},{3,7},{4,4},{5,1},{6,6},{7,3},{8,8},{9,13},{10,1... | collective-permute-start | bytes 344072 | tf_op jit(solution)/shard_map/ppermute | solution.py:23
  41.7 15.6 %collective-permute-start.22 = (bf16[8,7168]{1,0:T(8,128)(2,1)S(1)}, bf16[8,7168]{1,0:T(8,128)(2,1)S(1)}, u32[]{:S(2)}, u32[]{:S(2)}) collective-permute-start(bf16[8,7168]{1,0:T(8,128)(2,1)S(1)} %get-tuple-element.65), channel_id=1, source_target_pairs={{0,2},{1,7},{2,0},{3,5},{4,6},{5,3},{6,4},{7,1},{8,10},{9,15},{10,... | collective-permute-start | bytes 344072 | tf_op jit(solution)/shard_map/ppermute | solution.py:23
  43.2 8.8 %collective-permute-start.14 = (bf16[8,7168]{1,0:T(8,128)(2,1)S(1)}, bf16[8,7168]{1,0:T(8,128)(2,1)S(1)}, u32[]{:S(2)}, u32[]{:S(2)}) collective-permute-start(bf16[8,7168]{1,0:T(8,128)(2,1)S(1)} %add.9.refs_2_), channel_id=1, source_target_pairs={{0,28},{1,25},{2,30},{3,27},{4,24},{5,29},{6,26},{7,31},{8,20},{9,... | collective-permute-start | bytes 344072 | tf_op jit(solution)/shard_map/ppermute | solution.py:23
  47.5 9.3 %collective-permute-start.16 = (bf16[8,7168]{1,0:T(8,128)(2,1)S(1)}, bf16[8,7168]{1,0:T(8,128)(2,1)S(1)}, u32[]{:S(2)}, u32[]{:S(2)}) collective-permute-start(bf16[8,7168]{1,0:T(8,128)(2,1)S(1)} %add.10.refs_2_), channel_id=1, source_target_pairs={{0,16},{1,21},{2,18},{3,23},{4,20},{5,17},{6,22},{7,19},{8,24},{9,... | collective-permute-start | bytes 344072 | tf_op jit(solution)/shard_map/ppermute | solution.py:23
  48.1 9.1 %collective-permute-start.20 = (bf16[8,7168]{1,0:T(8,128)(2,1)S(1)}, bf16[8,7168]{1,0:T(8,128)(2,1)S(1)}, u32[]{:S(2)}, u32[]{:S(2)}) collective-permute-start(bf16[8,7168]{1,0:T(8,128)(2,1)S(1)} %add.13), channel_id=1, source_target_pairs={{0,12},{1,9},{2,14},{3,11},{4,8},{5,13},{6,10},{7,15},{8,4},{9,1},... | collective-permute-start | bytes 344072 | tf_op jit(solution)/shard_map/ppermute | solution.py:23
  57.6 1.4 %collective-permute-start.23 = (bf16[8,7168]{1,0:T(8,128)(2,1)S(1)}, bf16[8,7168]{1,0:T(8,128)(2,1)S(1)}, u32[]{:S(2)}, u32[]{:S(2)}) collective-permute-start(bf16[8,7168]{1,0:T(8,128)(2,1)S(1)} %get-tuple-element.67), channel_id=1, source_target_pairs={{0,1},{1,0},{2,3},{3,2},{4,5},{5,4},{6,7},{7,6},{8,9},{9,8},{10,11... | collective-permute-start | bytes 344072 | tf_op jit(solution)/shard_map/ppermute | solution.py:23

commit v7 on v6

--- a/solution.py
+++ b/solution.py
@@ -306,7 +306,7 @@
         out_specs=[vmem] * (3 + messages),
         scratch_shapes=[pltpu.VMEM((columns, depth), jnp.float32)],
         compiler_params=pltpu.CompilerParams(
-            vmem_limit_bytes=62 << 20
+            vmem_limit_bytes=(64 << 20) - (64 << 10)
         ),
         name="pack",
     )(copy_table, *own_choice, *other_choice, hidden, other, gain)
@@ -474,7 +474,7 @@
         *add([near_out[1], swapped(near_out[3])], half, [], jnp.float32),
     ]
     returned_near = to_near(near_sums[-1].astype(jnp.bfloat16))
-    far = join([far, far_last], [mark, weights, attended_mark])
+    far = join([far, far_last], [mark, weights, attended_mark, near_sums[0]])
     far_out, mark = experts([far, swapped(far)], held, mark, half * size)
     far_sums = [
         *add([far_out[0], swapped(far_out[2])], half, []),

time: 59.9 us -> 59.4 us (level)
  local copies, waits for them, and re-layouts: 1.43 us -> 0.79 us
    unnamed x22 -> x16, local copies, waits for them, and re-layouts: 1.43 us -> 0.79 us
  transfers between devices with their start and end apart: 24 -> 24, of which waited for: 11 -> 12; matrix products, arithmetic and copies ran while one was open for 0% -> 0% of each run, Pallas kernels for 17% -> 17%
where the time goes in v7:
time: 59.4 us; the launch traced here: 59.1 us
  starting transfers between devices  25.5 us (43%)
  waiting for transfers between devices  16.3 us (27%)
  Pallas kernels  15.8 us (27%)
  between operations  0.84 us (1%)
  local copies, waits for them, and re-layouts  0.79 us (1%)
    ppermute x24, starting transfers between devices, flipped(): return lax.ppermute(value, 'ep', pairs)  25.5 us
    ppermute x24, waiting for transfers between devices, flipped(): return lax.ppermute(value, 'ep', pairs)  16.3 us
    pallas_call x2, Pallas kernels, experts(): pl.pallas_call(functools.partial(expert_kernel, count), out_shape=[jax.Sh...  4.26 us
    pallas_call x1, Pallas kernels, load(): pl.pallas_call(load_kernel, out_shape=[jax.ShapeDtypeStruct(w.shape, w.dt...  4.23 us
    pallas_call x1, Pallas kernels, attend(): pl.pallas_call(attend_kernel, out_shape=[jax.ShapeDtypeStruct((steps, tok...  2.97 us
    pallas_call x1, Pallas kernels, pack(): pl.pallas_call(functools.partial(pack_kernel, slots, deltas), out_shape=[...  2.26 us
  transfers between devices with their start and end apart: 24, of which 12 were waited for; matrix products, arithmetic and copies ran while one was open for 0% of the time, Pallas kernels for 17%

profile of v7, /device:TPU:0, one launch (start us, length us, event | category | flops | bytes accessed | tf_op | source)
XLA Modules:
  0.0 59.1 jit_solution(13763483138072384213)
XLA Ops:
  0.6 0.5 collective-permute-start.2
  1.1 0.1 collective-permute-start
  1.2 0.4 collective-permute-start.1
  1.7 1.0 %collective-permute-done.other_ids_ref = s32[2,2,4]{2,1,0:T(2,128)} collective-permute-done((s32[2,2,4]{2,1,0:T(2,128)}, s32[2,2,4]{2,1,0:T(2,128)}, u32[]{:S(2)}, u32[]{:S(2)}) %collective-permute-start) | collective-permute-done | bytes 96 | tf_op jit(solution)/shard_map/ppermute | solution.py:23
  2.6 0.2 collective-permute-done.1.other_replica_ref
  2.8 0.0 collective-permute-done.2.other_ref
  2.8 2.3 %pack.1 = (bf16[16,7168]{1,0:T(8,128)(2,1)}, f32[2,32,16]{2,1,0:T(8,128)}, f32[2,6,16]{2,1,0:T(8,128)}, bf16[8,7168]{1,0:T(8,128)(2,1)}, bf16[8,7168]{1,0:T(8,12...) custom-call(s32[2,6]{1,0:T(2,128)} %bitcast.11, s32[2,2,4]{2,1,0:T(2,128)} %bitcast.8, s32[2,2,4]{2,1,0:T(2,128)} %bitcast.10, ...), custom_call_target="tpu_custom_call" | custom-call | tf_op jit(solution)/shard_map/pack/pallas_call | solution.py:297
  5.1 5.9 %collective-permute-start.3 = (bf16[8,7168]{1,0:T(8,128)(2,1)}, bf16[8,7168]{1,0:T(8,128)(2,1)S(1)}, u32[]{:S(2)}, u32[]{:S(2)}) collective-permute-start(bf16[8,7168]{1,0:T(8,128)(2,1)} %get-tuple-element.39), channel_id=1, source_target_pairs={{0,28},{1,25},{2,30},{3,27},{4,24},{5,29},{6,26},{7,31},{8,20},{9,... | collective-permute-start | bytes 344072 | tf_op jit(solution)/shard_map/ppermute | solution.py:23
  11.0 0.0 collective-permute-start.4
  11.0 0.6 %collective-permute-start.5 = (bf16[8,7168]{1,0:T(8,128)(2,1)}, bf16[8,7168]{1,0:T(8,128)(2,1)S(1)}, u32[]{:S(2)}, u32[]{:S(2)}) collective-permute-start(bf16[8,7168]{1,0:T(8,128)(2,1)} %get-tuple-element.41), channel_id=1, source_target_pairs={{0,12},{1,9},{2,14},{3,11},{4,8},{5,13},{6,10},{7,15},{8,4},{9,1},... | collective-permute-start | bytes 344072 | tf_op jit(solution)/shard_map/ppermute | solution.py:23
  11.6 1.6 %collective-permute-start.7 = (bf16[8,7168]{1,0:T(8,128)(2,1)}, bf16[8,7168]{1,0:T(8,128)(2,1)S(1)}, u32[]{:S(2)}, u32[]{:S(2)}) collective-permute-start(bf16[8,7168]{1,0:T(8,128)(2,1)} %get-tuple-element.42), channel_id=1, source_target_pairs={{0,2},{1,7},{2,0},{3,5},{4,6},{5,3},{6,4},{7,1},{8,10},{9,15},{10,... | collective-permute-start | bytes 344072 | tf_op jit(solution)/shard_map/ppermute | solution.py:23
  13.2 1.5 %collective-permute-start.6 = (bf16[8,7168]{1,0:T(8,128)(2,1)}, bf16[8,7168]{1,0:T(8,128)(2,1)S(1)}, u32[]{:S(2)}, u32[]{:S(2)}) collective-permute-start(bf16[8,7168]{1,0:T(8,128)(2,1)} %get-tuple-element.42), channel_id=1, source_target_pairs={{0,0},{1,5},{2,2},{3,7},{4,4},{5,1},{6,6},{7,3},{8,8},{9,13},{10,1... | collective-permute-start | bytes 344072 | tf_op jit(solution)/shard_map/ppermute | solution.py:23
  14.7 0.8 %copy-done.3 = f32[2,32,16]{2,1,0:T(8,128)S(1)} copy-done((f32[2,32,16]{2,1,0:T(8,128)S(1)}, f32[2,32,16]{2,1,0:T(8,128)}, u32[]{:S(2)}) %copy-start.3) | copy-done | bytes 4120
  15.5 4.2 %load.1 = (bf16[7168,256]{1,0:T(8,128)(2,1)S(1)}, bf16[7168,256]{1,0:T(8,128)(2,1)S(1)}, bf16[256,7168]{1,0:T(8,128)(2,1)S(1)}, f32[8,128]{1,0:T(8,128)S(1)}) custom-call(bf16[7168,256]{1,0:T(8,128)(2,1)} %gate_ref.1, bf16[7168,256]{1,0:T(8,128)(2,1)} %up_ref.1, bf16[256,7168]{1,0:T(8,128)(2,1)} %down_ref.1, f32[2,32,16]{2,1,0:T(8,128)S(1)} %copy-done.3), custom_call_target="tpu_custom_call" | custom-call | tf_op jit(solution)/shard_map/load/pallas_call | solution.py:108
  19.7 0.0 collective-permute-done.3.refs_0_
  19.7 0.5 collective-permute-done.4.refs_1_
  20.2 0.0 collective-permute-done.5.refs_2_
  20.2 0.0 collective-permute-done.7.refs_5_.refs_4_.refs_1_
  20.2 0.0 collective-permute-done.6.refs_3_
  20.3 0.4 collective-permute-start.8
  20.7 1.3 %collective-permute-start.10 = (bf16[24,7168]{1,0:T(8,128)(2,1)S(1)}, bf16[24,7168]{1,0:T(8,128)(2,1)S(1)}, u32[]{:S(2)}, u32[]{:S(2)}) collective-permute-start(bf16[24,7168]{1,0:T(8,128)(2,1)S(1)} %join.4), channel_id=1, source_target_pairs={{0,2},{1,3},{2,0},{3,1},{4,6},{5,7},{6,4},{7,5},{8,10},{9,11},{10,... | collective-permute-start | bytes 1032200 | tf_op jit(solution)/shard_map/ppermute | solution.py:23
  22.0 0.2 collective-permute-done.8.refs_1_
  22.2 0.0 copy-start.2
  22.2 0.0 copy-start.4
  22.2 2.1 %experts.2 = (bf16[16,7168]{1,0:T(8,128)(2,1)S(1)}, bf16[16,7168]{1,0:T(8,128)(2,1)S(1)}, bf16[16,7168]{1,0:T(8,128)(2,1)S(1)}, bf16[16,7168]{1,0:T(8,128)(2,1)S(1)}, f32[8,128]{1,0:T(8,128)S(1)}) custom-call(bf16[32,7168]{1,0:T(8,128)(2,1)S(1)} %join.3.refs_0_, bf16[32,7168]{1,0:T(8,128)(2,1)S(1)} %collective-permute-done.8.refs_1_, ...), custom_call_target="tpu_custom_call" | custom-call | tf_op jit(solution)/shard_map/experts/pallas_call | solution.py:148
  24.4 0.4 collective-permute-start.9
  24.7 0.0 copy-done.5
  24.7 3.0 %attention.1 = (bf16[2,4,64,512]{3,2,1,0:T(8,128)(2,1)}, f32[8,128]{1,0:T(8,128)S(1)}) custom-call(s32[4]{0:T(128)S(1)} %copy-done.7, bf16[2,4,64,576]{3,2,1,0:T(8,128)(2,1)S(1)} %copy-done, bf16[4,64,576]{2,1,0:T(8,128)(2,1)S(1)} %copy-done.1, bf16[2,4,576]{2,1,0:T(4,128)(2,1)S(1)} %copy-done.5), custom_call_target="tpu_custom_call" | custom-call | flops 150994944 | bytes 1474560 | tf_op jit(solution)/shard_map/attention/pallas_call | solution.py:76
  27.7 0.2 weigh.1.refs_3_.weigh_ref
  27.9 0.0 collective-permute-done.9.refs_1_
  28.0 0.1 add.7
  28.0 2.9 %collective-permute-done.10.refs_0_ = bf16[24,7168]{1,0:T(8,128)(2,1)S(1)} collective-permute-done((bf16[24,7168]{1,0:T(8,128)(2,1)S(1)}, bf16[24,7168]{1,0:T(8,128)(2,1)S(1)}, u32[]{:S(2)}, u32[]{:S(2)}) %collective-permute-start.10) | collective-permute-done | bytes 344096 | tf_op jit(solution)/shard_map/ppermute | solution.py:23
  31.0 0.1 collective-permute-start.11
  31.0 1.8 %collective-permute-done.11.refs_1_ = bf16[32,7168]{1,0:T(8,128)(2,1)S(1)} collective-permute-done((bf16[32,7168]{1,0:T(8,128)(2,1)S(1)}, bf16[32,7168]{1,0:T(8,128)(2,1)S(1)}, u32[]{:S(2)}, u32[]{:S(2)}) %collective-permute-start.11) | collective-permute-done | bytes 458784 | tf_op jit(solution)/shard_map/ppermute | solution.py:23
  32.8 2.1 %experts.3 = (bf16[16,7168]{1,0:T(8,128)(2,1)S(1)}, bf16[16,7168]{1,0:T(8,128)(2,1)S(1)}, bf16[16,7168]{1,0:T(8,128)(2,1)S(1)}, bf16[16,7168]{1,0:T(8,128)(2,1)S(1)}, f32[8,128]{1,0:T(8,128)S(1)}) custom-call(bf16[32,7168]{1,0:T(8,128)(2,1)S(1)} %join.5.refs_0_, bf16[32,7168]{1,0:T(8,128)(2,1)S(1)} %collective-permute-done.11.refs_1_, ...), custom_call_target="tpu_custom_call" | custom-call | tf_op jit(solution)/shard_map/experts/pallas_call | solution.py:148
  35.0 0.2 collective-permute-start.12
  35.2 0.4 collective-permute-start.18
  35.6 0.1 collective-permute-start.17
  35.7 0.8 %collective-permute-done.12.refs_1_ = bf16[16,7168]{1,0:T(8,128)(2,1)S(1)} collective-permute-done((bf16[16,7168]{1,0:T(8,128)(2,1)S(1)}, bf16[16,7168]{1,0:T(8,128)(2,1)S(1)}, u32[]{:S(2)}, u32[]{:S(2)}) %collective-permute-start.12) | collective-permute-done | bytes 229408 | tf_op jit(solution)/shard_map/ppermute | solution.py:23
  36.5 0.1 add.8
  36.6 1.5 %collective-permute-start.13 = (bf16[8,7168]{1,0:T(8,128)(2,1)S(1)}, bf16[8,7168]{1,0:T(8,128)(2,1)S(1)}, u32[]{:S(2)}, u32[]{:S(2)}) collective-permute-start(bf16[8,7168]{1,0:T(8,128)(2,1)S(1)} %get-tuple-element.54), channel_id=1, source_target_pairs={{0,2},{1,3},{2,0},{3,1},{4,6},{5,7},{6,4},{7,5},{8,10},{9,11},{10,... | collective-permute-start | bytes 344072 | tf_op jit(solution)/shard_map/ppermute | solution.py:23
  38.1 0.5 collective-permute-start.15
  38.7 0.0 collective-permute-done.18.refs_1_
  38.7 0.1 add.12
  38.7 1.5 %collective-permute-start.19 = (bf16[8,7168]{1,0:T(8,128)(2,1)S(1)}, bf16[8,7168]{1,0:T(8,128)(2,1)S(1)}, u32[]{:S(2)}, u32[]{:S(2)}) collective-permute-start(bf16[8,7168]{1,0:T(8,128)(2,1)S(1)} %get-tuple-element.63), channel_id=1, source_target_pairs={{0,2},{1,3},{2,0},{3,1},{4,6},{5,7},{6,4},{7,5},{8,10},{9,11},{10,... | collective-permute-start | bytes 344072 | tf_op jit(solution)/shard_map/ppermute | solution.py:23
  40.3 0.0 collective-permute-done.17.refs_1_
  40.4 0.7 %collective-permute-start.21 = (bf16[8,7168]{1,0:T(8,128)(2,1)S(1)}, bf16[8,7168]{1,0:T(8,128)(2,1)S(1)}, u32[]{:S(2)}, u32[]{:S(2)}) collective-permute-start(bf16[8,7168]{1,0:T(8,128)(2,1)S(1)} %convert_element_type.3), channel_id=1, source_target_pairs={{0,0},{1,5},{2,2},{3,7},{4,4},{5,1},{6,6},{7,3},{8,8},{9,13},{10,1... | collective-permute-start | bytes 344072 | tf_op jit(solution)/shard_map/ppermute | solution.py:23
  41.0 0.6 %collective-permute-start.22 = (bf16[8,7168]{1,0:T(8,128)(2,1)S(1)}, bf16[8,7168]{1,0:T(8,128)(2,1)S(1)}, u32[]{:S(2)}, u32[]{:S(2)}) collective-permute-start(bf16[8,7168]{1,0:T(8,128)(2,1)S(1)} %get-tuple-element.65), channel_id=1, source_target_pairs={{0,2},{1,7},{2,0},{3,5},{4,6},{5,3},{6,4},{7,1},{8,10},{9,15},{10,... | collective-permute-start | bytes 344072 | tf_op jit(solution)/shard_map/ppermute | solution.py:23
  41.7 1.0 %collective-permute-done.13.refs_1_ = bf16[8,7168]{1,0:T(8,128)(2,1)S(1)} collective-permute-done((bf16[8,7168]{1,0:T(8,128)(2,1)S(1)}, bf16[8,7168]{1,0:T(8,128)(2,1)S(1)}, u32[]{:S(2)}, u32[]{:S(2)}) %collective-permute-start.13) | collective-permute-done | bytes 114720 | tf_op jit(solution)/shard_map/ppermute | solution.py:23
  42.7 4.2 %collective-permute-start.14 = (bf16[8,7168]{1,0:T(8,128)(2,1)S(1)}, bf16[8,7168]{1,0:T(8,128)(2,1)S(1)}, u32[]{:S(2)}, u32[]{:S(2)}) collective-permute-start(bf16[8,7168]{1,0:T(8,128)(2,1)S(1)} %add.9.refs_2_), channel_id=1, source_target_pairs={{0,28},{1,25},{2,30},{3,27},{4,24},{5,29},{6,26},{7,31},{8,20},{9,... | collective-permute-start | bytes 344072 | tf_op jit(solution)/shard_map/ppermute | solution.py:23
  46.8 0.0 collective-permute-done.15.refs_1_
  46.9 0.5 collective-permute-start.16
  47.3 0.2 collective-permute-done.19.refs_1_
  47.6 2.4 %collective-permute-start.20 = (bf16[8,7168]{1,0:T(8,128)(2,1)S(1)}, bf16[8,7168]{1,0:T(8,128)(2,1)S(1)}, u32[]{:S(2)}, u32[]{:S(2)}) collective-permute-start(bf16[8,7168]{1,0:T(8,128)(2,1)S(1)} %add.13), channel_id=1, source_target_pairs={{0,12},{1,9},{2,14},{3,11},{4,8},{5,13},{6,10},{7,15},{8,4},{9,1},... | collective-permute-start | bytes 344072 | tf_op jit(solution)/shard_map/ppermute | solution.py:23
  49.9 1.5 %collective-permute-done.14.refs_0_ = bf16[8,7168]{1,0:T(8,128)(2,1)S(1)} collective-permute-done((bf16[8,7168]{1,0:T(8,128)(2,1)S(1)}, bf16[8,7168]{1,0:T(8,128)(2,1)S(1)}, u32[]{:S(2)}, u32[]{:S(2)}) %collective-permute-start.14) | collective-permute-done | bytes 114720 | tf_op jit(solution)/shard_map/ppermute | solution.py:23
  51.5 4.8 %collective-permute-done.16.refs_1_ = bf16[8,7168]{1,0:T(8,128)(2,1)S(1)} collective-permute-done((bf16[8,7168]{1,0:T(8,128)(2,1)S(1)}, bf16[8,7168]{1,0:T(8,128)(2,1)S(1)}, u32[]{:S(2)}, u32[]{:S(2)}) %collective-permute-start.16) | collective-permute-done | bytes 114720 | tf_op jit(solution)/shard_map/ppermute | solution.py:23
  56.3 0.4 combine.2.first_ref
  56.6 0.0 collective-permute-done.21.refs_1_
  56.7 0.0 collective-permute-done.22.refs_2_
  56.7 0.0 collective-permute-done.20.refs_0_
  56.7 0.4 combine.3
  57.1 0.1 collective-permute-start.23
  57.1 1.3 %collective-permute-done.23.received_ref = bf16[8,7168]{1,0:T(8,128)(2,1)S(1)} collective-permute-done((bf16[8,7168]{1,0:T(8,128)(2,1)S(1)}, bf16[8,7168]{1,0:T(8,128)(2,1)S(1)}, u32[]{:S(2)}, u32[]{:S(2)}) %collective-permute-start.23) | collective-permute-done | bytes 114720 | tf_op jit(solution)/shard_map/ppermute | solution.py:23
  58.5 0.7 %finish.1 = bf16[2,4,7168]{2,1,0:T(4,128)(2,1)} custom-call(f32[8,7168]{1,0:T(8,128)S(1)} %get-tuple-element.66.own_ref, bf16[8,7168]{1,0:T(8,128)(2,1)S(1)} %collective-permute-done.23.received_ref), custom_call_target="tpu_custom_call" | custom-call | tf_op jit(solution)/shard_map/finish/pallas_call | solution.py:415
  (20 shorter events, 0.3 us)
Async XLA Ops:
  0.6 2.2 %collective-permute-start.2 = (bf16[2,4,7168]{2,1,0:T(4,128)(2,1)}, bf16[2,4,7168]{2,1,0:T(4,128)(2,1)}, u32[]{:S(2)}, u32[]{:S(2)}) collective-permute-start(bf16[2,4,7168]{2,1,0:T(4,128)(2,1)} %raw_ref.1), channel_id=1, source_target_pairs={{0,1},{1,0},{2,3},{3,2},{4,5},{5,4},{6,7},{7,6},{8,9},{9,8},{10,11... | collective-permute-start | bytes 344072 | tf_op jit(solution)/shard_map/ppermute | solution.py:23
  1.1 1.5 %collective-permute-start = (s32[2,2,4]{2,1,0:T(2,128)}, s32[2,2,4]{2,1,0:T(2,128)}, u32[]{:S(2)}, u32[]{:S(2)}) collective-permute-start(s32[2,2,4]{2,1,0:T(2,128)} %bitcast.7), channel_id=1, source_target_pairs={{0,1},{1,0},{2,3},{3,2},{4,5},{5,4},{6,7},{7,6},{8,9},{9,8},{10,11... | collective-permute-start | bytes 200 | tf_op jit(solution)/shard_map/ppermute | solution.py:23
  1.2 1.6 %collective-permute-start.1 = (s32[2,2,4]{2,1,0:T(2,128)}, s32[2,2,4]{2,1,0:T(2,128)}, u32[]{:S(2)}, u32[]{:S(2)}) collective-permute-start(s32[2,2,4]{2,1,0:T(2,128)} %bitcast.9), channel_id=1, source_target_pairs={{0,1},{1,0},{2,3},{3,2},{4,5},{5,4},{6,7},{7,6},{8,9},{9,8},{10,11... | collective-permute-start | bytes 200 | tf_op jit(solution)/shard_map/ppermute | solution.py:23
  5.1 14.6 %collective-permute-start.3 = (bf16[8,7168]{1,0:T(8,128)(2,1)}, bf16[8,7168]{1,0:T(8,128)(2,1)S(1)}, u32[]{:S(2)}, u32[]{:S(2)}) collective-permute-start(bf16[8,7168]{1,0:T(8,128)(2,1)} %get-tuple-element.39), channel_id=1, source_target_pairs={{0,28},{1,25},{2,30},{3,27},{4,24},{5,29},{6,26},{7,31},{8,20},{9,... | collective-permute-start | bytes 344072 | tf_op jit(solution)/shard_map/ppermute | solution.py:23
  11.0 9.3 %collective-permute-start.4 = (bf16[8,7168]{1,0:T(8,128)(2,1)}, bf16[8,7168]{1,0:T(8,128)(2,1)S(1)}, u32[]{:S(2)}, u32[]{:S(2)}) collective-permute-start(bf16[8,7168]{1,0:T(8,128)(2,1)} %get-tuple-element.40), channel_id=1, source_target_pairs={{0,16},{1,21},{2,18},{3,23},{4,20},{5,17},{6,22},{7,19},{8,24},{9,... | collective-permute-start | bytes 344072 | tf_op jit(solution)/shard_map/ppermute | solution.py:23
  11.0 9.3 %collective-permute-start.5 = (bf16[8,7168]{1,0:T(8,128)(2,1)}, bf16[8,7168]{1,0:T(8,128)(2,1)S(1)}, u32[]{:S(2)}, u32[]{:S(2)}) collective-permute-start(bf16[8,7168]{1,0:T(8,128)(2,1)} %get-tuple-element.41), channel_id=1, source_target_pairs={{0,12},{1,9},{2,14},{3,11},{4,8},{5,13},{6,10},{7,15},{8,4},{9,1},... | collective-permute-start | bytes 344072 | tf_op jit(solution)/shard_map/ppermute | solution.py:23
  11.6 8.7 %collective-permute-start.7 = (bf16[8,7168]{1,0:T(8,128)(2,1)}, bf16[8,7168]{1,0:T(8,128)(2,1)S(1)}, u32[]{:S(2)}, u32[]{:S(2)}) collective-permute-start(bf16[8,7168]{1,0:T(8,128)(2,1)} %get-tuple-element.42), channel_id=1, source_target_pairs={{0,2},{1,7},{2,0},{3,5},{4,6},{5,3},{6,4},{7,1},{8,10},{9,15},{10,... | collective-permute-start | bytes 344072 | tf_op jit(solution)/shard_map/ppermute | solution.py:23
  13.2 7.1 %collective-permute-start.6 = (bf16[8,7168]{1,0:T(8,128)(2,1)}, bf16[8,7168]{1,0:T(8,128)(2,1)S(1)}, u32[]{:S(2)}, u32[]{:S(2)}) collective-permute-start(bf16[8,7168]{1,0:T(8,128)(2,1)} %get-tuple-element.42), channel_id=1, source_target_pairs={{0,0},{1,5},{2,2},{3,7},{4,4},{5,1},{6,6},{7,3},{8,8},{9,13},{10,1... | collective-permute-start | bytes 344072 | tf_op jit(solution)/shard_map/ppermute | solution.py:23
  14.7 0.8 %copy-start.3 = (f32[2,32,16]{2,1,0:T(8,128)S(1)}, f32[2,32,16]{2,1,0:T(8,128)}, u32[]{:S(2)}) copy-start(f32[2,32,16]{2,1,0:T(8,128)} %get-tuple-element.37.place_ref._) | copy-start | bytes 12292
  20.3 1.9 %collective-permute-start.8 = (bf16[32,7168]{1,0:T(8,128)(2,1)S(1)}, bf16[32,7168]{1,0:T(8,128)(2,1)S(1)}, u32[]{:S(2)}, u32[]{:S(2)}) collective-permute-start(bf16[32,7168]{1,0:T(8,128)(2,1)S(1)} %join.3.refs_0_), channel_id=1, source_target_pairs={{0,1},{1,0},{2,3},{3,2},{4,5},{5,4},{6,7},{7,6},{8,9},{9,8},{10,11... | collective-permute-start | bytes 1376264 | tf_op jit(solution)/shard_map/ppermute | solution.py:23
  20.7 10.3 %collective-permute-start.10 = (bf16[24,7168]{1,0:T(8,128)(2,1)S(1)}, bf16[24,7168]{1,0:T(8,128)(2,1)S(1)}, u32[]{:S(2)}, u32[]{:S(2)}) collective-permute-start(bf16[24,7168]{1,0:T(8,128)(2,1)S(1)} %join.4), channel_id=1, source_target_pairs={{0,2},{1,3},{2,0},{3,1},{4,6},{5,7},{6,4},{7,5},{8,10},{9,11},{10,... | collective-permute-start | bytes 1032200 | tf_op jit(solution)/shard_map/ppermute | solution.py:23
  22.2 2.5 %copy-start = (bf16[2,4,64,576]{3,2,1,0:T(8,128)(2,1)S(1)}, bf16[2,4,64,576]{3,2,1,0:T(8,128)(2,1)}, u32[]{:S(2)}) copy-start(bf16[2,4,64,576]{3,2,1,0:T(8,128)(2,1)} %query_ref.1) | copy-start | bytes 1769476
  22.2 2.5 %copy-start.1 = (bf16[4,64,576]{2,1,0:T(8,128)(2,1)S(1)}, bf16[4,64,576]{2,1,0:T(8,128)(2,1)}, u32[]{:S(2)}) copy-start(bf16[4,64,576]{2,1,0:T(8,128)(2,1)} %cache_ref.1) | copy-start | bytes 884740
  22.2 2.5 %copy-start.5 = (bf16[2,4,576]{2,1,0:T(4,128)(2,1)S(1)}, bf16[2,4,576]{2,1,0:T(4,128)(2,1)}, u32[]{:S(2)}) copy-start(bf16[2,4,576]{2,1,0:T(4,128)(2,1)} %fresh_ref.1) | copy-start | bytes 27652
  22.2 2.5 %copy-start.7 = (s32[4]{0:T(128)S(1)}, s32[4]{0:T(128)}, u32[]{:S(2)}) copy-start(s32[4]{0:T(128)} %lengths_ref.1) | copy-start | bytes 52
  22.2 5.5 %copy-start.2 = (bf16[16,7168]{1,0:T(8,128)(2,1)S(1)}, bf16[16,7168]{1,0:T(8,128)(2,1)}, u32[]{:S(2)}) copy-start(bf16[16,7168]{1,0:T(8,128)(2,1)} %get-tuple-element.36.normed_ref) | copy-start | bytes 688132
  22.2 5.5 %copy-start.4 = (bf16[7168,6]{0,1:T(8,128)(2,1)S(1)}, bf16[7168,6]{0,1:T(8,128)(2,1)}, u32[]{:S(2)}) copy-start(bf16[7168,6]{0,1:T(8,128)(2,1)} %param.15) | copy-start | bytes 258052
  22.2 5.5 %copy-start.6 = (f32[2,6,16]{2,1,0:T(8,128)S(1)}, f32[2,6,16]{2,1,0:T(8,128)}, u32[]{:S(2)}) copy-start(f32[2,6,16]{2,1,0:T(8,128)} %get-tuple-element.38.choose_ref) | copy-start | bytes 2308
  24.4 3.6 %collective-permute-start.9 = (bf16[16,7168]{1,0:T(8,128)(2,1)S(1)}, bf16[16,7168]{1,0:T(8,128)(2,1)S(1)}, u32[]{:S(2)}, u32[]{:S(2)}) collective-permute-start(bf16[16,7168]{1,0:T(8,128)(2,1)S(1)} %get-tuple-element.48), channel_id=1, source_target_pairs={{0,1},{1,0},{2,3},{3,2},{4,5},{5,4},{6,7},{7,6},{8,9},{9,8},{10,11... | collective-permute-start | bytes 688136 | tf_op jit(solution)/shard_map/ppermute | solution.py:23
  31.0 1.9 %collective-permute-start.11 = (bf16[32,7168]{1,0:T(8,128)(2,1)S(1)}, bf16[32,7168]{1,0:T(8,128)(2,1)S(1)}, u32[]{:S(2)}, u32[]{:S(2)}) collective-permute-start(bf16[32,7168]{1,0:T(8,128)(2,1)S(1)} %join.5.refs_0_), channel_id=1, source_target_pairs={{0,1},{1,0},{2,3},{3,2},{4,5},{5,4},{6,7},{7,6},{8,9},{9,8},{10,11... | collective-permute-start | bytes 1376264 | tf_op jit(solution)/shard_map/ppermute | solution.py:23
  35.0 1.6 %collective-permute-start.12 = (bf16[16,7168]{1,0:T(8,128)(2,1)S(1)}, bf16[16,7168]{1,0:T(8,128)(2,1)S(1)}, u32[]{:S(2)}, u32[]{:S(2)}) collective-permute-start(bf16[16,7168]{1,0:T(8,128)(2,1)S(1)} %get-tuple-element.53), channel_id=1, source_target_pairs={{0,1},{1,0},{2,3},{3,2},{4,5},{5,4},{6,7},{7,6},{8,9},{9,8},{10,11... | collective-permute-start | bytes 688136 | tf_op jit(solution)/shard_map/ppermute | solution.py:23
  35.2 3.5 %collective-permute-start.18 = (bf16[16,7168]{1,0:T(8,128)(2,1)S(1)}, bf16[16,7168]{1,0:T(8,128)(2,1)S(1)}, u32[]{:S(2)}, u32[]{:S(2)}) collective-permute-start(bf16[16,7168]{1,0:T(8,128)(2,1)S(1)} %get-tuple-element.62), channel_id=1, source_target_pairs={{0,1},{1,0},{2,3},{3,2},{4,5},{5,4},{6,7},{7,6},{8,9},{9,8},{10,11... | collective-permute-start | bytes 688136 | tf_op jit(solution)/shard_map/ppermute | solution.py:23
  35.6 4.7 %collective-permute-start.17 = (bf16[16,7168]{1,0:T(8,128)(2,1)S(1)}, bf16[16,7168]{1,0:T(8,128)(2,1)S(1)}, u32[]{:S(2)}, u32[]{:S(2)}) collective-permute-start(bf16[16,7168]{1,0:T(8,128)(2,1)S(1)} %get-tuple-element.59), channel_id=1, source_target_pairs={{0,1},{1,0},{2,3},{3,2},{4,5},{5,4},{6,7},{7,6},{8,9},{9,8},{10,11... | collective-permute-start | bytes 688136 | tf_op jit(solution)/shard_map/ppermute | solution.py:23
  36.6 6.1 %collective-permute-start.13 = (bf16[8,7168]{1,0:T(8,128)(2,1)S(1)}, bf16[8,7168]{1,0:T(8,128)(2,1)S(1)}, u32[]{:S(2)}, u32[]{:S(2)}) collective-permute-start(bf16[8,7168]{1,0:T(8,128)(2,1)S(1)} %get-tuple-element.54), channel_id=1, source_target_pairs={{0,2},{1,3},{2,0},{3,1},{4,6},{5,7},{6,4},{7,5},{8,10},{9,11},{10,... | collective-permute-start | bytes 344072 | tf_op jit(solution)/shard_map/ppermute | solution.py:23
  38.1 8.7 %collective-permute-start.15 = (bf16[8,7168]{1,0:T(8,128)(2,1)S(1)}, bf16[8,7168]{1,0:T(8,128)(2,1)S(1)}, u32[]{:S(2)}, u32[]{:S(2)}) collective-permute-start(bf16[8,7168]{1,0:T(8,128)(2,1)S(1)} %get-tuple-element.57), channel_id=1, source_target_pairs={{0,2},{1,3},{2,0},{3,1},{4,6},{5,7},{6,4},{7,5},{8,10},{9,11},{10,... | collective-permute-start | bytes 344072 | tf_op jit(solution)/shard_map/ppermute | solution.py:23
  38.7 8.8 %collective-permute-start.19 = (bf16[8,7168]{1,0:T(8,128)(2,1)S(1)}, bf16[8,7168]{1,0:T(8,128)(2,1)S(1)}, u32[]{:S(2)}, u32[]{:S(2)}) collective-permute-start(bf16[8,7168]{1,0:T(8,128)(2,1)S(1)} %get-tuple-element.63), channel_id=1, source_target_pairs={{0,2},{1,3},{2,0},{3,1},{4,6},{5,7},{6,4},{7,5},{8,10},{9,11},{10,... | collective-permute-start | bytes 344072 | tf_op jit(solution)/shard_map/ppermute | solution.py:23
  40.4 16.3 %collective-permute-start.21 = (bf16[8,7168]{1,0:T(8,128)(2,1)S(1)}, bf16[8,7168]{1,0:T(8,128)(2,1)S(1)}, u32[]{:S(2)}, u32[]{:S(2)}) collective-permute-start(bf16[8,7168]{1,0:T(8,128)(2,1)S(1)} %convert_element_type.3), channel_id=1, source_target_pairs={{0,0},{1,5},{2,2},{3,7},{4,4},{5,1},{6,6},{7,3},{8,8},{9,13},{10,1... | collective-permute-start | bytes 344072 | tf_op jit(solution)/shard_map/ppermute | solution.py:23
  41.0 15.6 %collective-permute-start.22 = (bf16[8,7168]{1,0:T(8,128)(2,1)S(1)}, bf16[8,7168]{1,0:T(8,128)(2,1)S(1)}, u32[]{:S(2)}, u32[]{:S(2)}) collective-permute-start(bf16[8,7168]{1,0:T(8,128)(2,1)S(1)} %get-tuple-element.65), channel_id=1, source_target_pairs={{0,2},{1,7},{2,0},{3,5},{4,6},{5,3},{6,4},{7,1},{8,10},{9,15},{10,... | collective-permute-start | bytes 344072 | tf_op jit(solution)/shard_map/ppermute | solution.py:23
  42.7 8.8 %collective-permute-start.14 = (bf16[8,7168]{1,0:T(8,128)(2,1)S(1)}, bf16[8,7168]{1,0:T(8,128)(2,1)S(1)}, u32[]{:S(2)}, u32[]{:S(2)}) collective-permute-start(bf16[8,7168]{1,0:T(8,128)(2,1)S(1)} %add.9.refs_2_), channel_id=1, source_target_pairs={{0,28},{1,25},{2,30},{3,27},{4,24},{5,29},{6,26},{7,31},{8,20},{9,... | collective-permute-start | bytes 344072 | tf_op jit(solution)/shard_map/ppermute | solution.py:23
  46.9 9.4 %collective-permute-start.16 = (bf16[8,7168]{1,0:T(8,128)(2,1)S(1)}, bf16[8,7168]{1,0:T(8,128)(2,1)S(1)}, u32[]{:S(2)}, u32[]{:S(2)}) collective-permute-start(bf16[8,7168]{1,0:T(8,128)(2,1)S(1)} %add.10.refs_2_), channel_id=1, source_target_pairs={{0,16},{1,21},{2,18},{3,23},{4,20},{5,17},{6,22},{7,19},{8,24},{9,... | collective-permute-start | bytes 344072 | tf_op jit(solution)/shard_map/ppermute | solution.py:23
  47.6 9.1 %collective-permute-start.20 = (bf16[8,7168]{1,0:T(8,128)(2,1)S(1)}, bf16[8,7168]{1,0:T(8,128)(2,1)S(1)}, u32[]{:S(2)}, u32[]{:S(2)}) collective-permute-start(bf16[8,7168]{1,0:T(8,128)(2,1)S(1)} %add.13), channel_id=1, source_target_pairs={{0,12},{1,9},{2,14},{3,11},{4,8},{5,13},{6,10},{7,15},{8,4},{9,1},... | collective-permute-start | bytes 344072 | tf_op jit(solution)/shard_map/ppermute | solution.py:23
  57.1 1.4 %collective-permute-start.23 = (bf16[8,7168]{1,0:T(8,128)(2,1)S(1)}, bf16[8,7168]{1,0:T(8,128)(2,1)S(1)}, u32[]{:S(2)}, u32[]{:S(2)}) collective-permute-start(bf16[8,7168]{1,0:T(8,128)(2,1)S(1)} %get-tuple-element.67), channel_id=1, source_target_pairs={{0,1},{1,0},{2,3},{3,2},{4,5},{5,4},{6,7},{7,6},{8,9},{9,8},{10,11... | collective-permute-start | bytes 344072 | tf_op jit(solution)/shard_map/ppermute | solution.py:23

commit v8 on v7

--- a/solution.py
+++ b/solution.py
@@ -119,17 +119,15 @@
 
 def expert_kernel(count, *refs):
     part_refs, refs = refs[:count], refs[count:]
-    gate_ref, up_ref, down_ref, _, *out_refs, mark_ref, rows_v = refs
+    gate_ref, up_ref, down_ref, _, *out_refs, mark_ref = refs
     size = out_refs[0].shape[0]
-    step = rows_v.shape[1] // EXPERT_PARTS
-    rows = part_refs[0].shape[0]
-    for i, ref in enumerate(part_refs):
-        rows_v[i * rows : (i + 1) * rows, :] = ref[...]
+    step = gate_ref.shape[0] // EXPERT_PARTS
     mark_ref[...] = jnp.zeros(mark_ref.shape, mark_ref.dtype)
     gate, upper = 0.0, 0.0
     for i in range(EXPERT_PARTS):
         ds = pl.ds(i * step, step)
-        x = rows_v[:, ds]
+        x = jnp.concatenate([ref[:, ds].astype(jnp.float32) for ref in part_refs], axis=0)
+        x = x.astype(jnp.bfloat16)
         gate = gate + jnp.dot(x, gate_ref[ds, :], preferred_element_type=jnp.float32)
         upper = upper + jnp.dot(x, up_ref[ds, :], preferred_element_type=jnp.float32)
     inner = (gate / (1.0 + jnp.exp(-gate)) * upper).astype(jnp.bfloat16)
@@ -141,18 +139,18 @@
 
 
 def experts(parts, weights, earlier, size):
-    rows, depth = parts[0].shape
+    depth = parts[0].shape[1]
     count = len(parts)
-    outs = count * rows // size
+    rows = sum(part.shape[0] for part in parts)
+    outs = rows // size
     vmem = pl.BlockSpec(memory_space=pltpu.VMEM)
     out = pl.pallas_call(
         functools.partial(expert_kernel, count),
         out_shape=[jax.ShapeDtypeStruct((size, depth), jnp.bfloat16)] * outs + [MARK],
         in_specs=[vmem] * (count + 3) + [pl.BlockSpec(memory_space=pl.ANY)],
         out_specs=[vmem] * (outs + 1),
-        scratch_shapes=[pltpu.VMEM((count * rows, depth), jnp.bfloat16)],
         compiler_params=pltpu.CompilerParams(
-            vmem_limit_bytes=(16 << 20) + count * rows * depth * 8
+            vmem_limit_bytes=(16 << 20) + rows * depth * 8
         ),
         name="experts",
     )(*parts, *weights, earlier)
@@ -474,8 +472,9 @@
         *add([near_out[1], swapped(near_out[3])], half, [], jnp.float32),
     ]
     returned_near = to_near(near_sums[-1].astype(jnp.bfloat16))
-    far = join([far, far_last], [mark, weights, attended_mark, near_sums[0]])
-    far_out, mark = experts([far, swapped(far)], held, mark, half * size)
+    far = join([far], [mark, weights, attended_mark, near_sums[0]])
+    far_parts = [far, far_last, swapped(far), swapped(far_last)]
+    far_out, mark = experts(far_parts, held, mark, half * size)
     far_sums = [
         *add([far_out[0], swapped(far_out[2])], half, []),
         *add([far_out[1], swapped(far_out[3])], half, []),

time: 59.4 us -> 59.4 us (level)
    ppermute x24 -> x25, waiting for transfers between devices: 16.3 us -> 15.8 us  [flipped(): return lax.ppermute(value, 'ep', pairs)]
    ppermute x24 -> x25, starting transfers between devices: 25.5 us -> 25.9 us  [flipped(): return lax.ppermute(value, 'ep', pairs)]
  transfers between devices with their start and end apart: 24 -> 25, of which waited for: 12 -> 12; matrix products, arithmetic and copies ran while one was open for 0% -> 0% of each run, Pallas kernels for 17% -> 17%
where the time goes in v8:
time: 59.4 us; the launch traced here: 59.1 us
  starting transfers between devices  25.9 us (44%)
  waiting for transfers between devices  15.8 us (27%)
  Pallas kernels  15.7 us (26%)
  between operations  0.85 us (1%)
  local copies, waits for them, and re-layouts  0.79 us (1%)
    ppermute x25, starting transfers between devices, flipped(): return lax.ppermute(value, 'ep', pairs)  25.9 us
    ppermute x25, waiting for transfers between devices, flipped(): return lax.ppermute(value, 'ep', pairs)  15.8 us
    pallas_call x2, Pallas kernels, experts(): pl.pallas_call(functools.partial(expert_kernel, count), out_shape=[jax.Sh...  4.28 us
    pallas_call x1, Pallas kernels, load(): pl.pallas_call(load_kernel, out_shape=[jax.ShapeDtypeStruct(w.shape, w.dt...  4.23 us
    pallas_call x1, Pallas kernels, attend(): pl.pallas_call(attend_kernel, out_shape=[jax.ShapeDtypeStruct((steps, tok...  2.97 us
    pallas_call x1, Pallas kernels, pack(): pl.pallas_call(functools.partial(pack_kernel, slots, deltas), out_shape=[...  2.25 us
  transfers between devices with their start and end apart: 25, of which 12 were waited for; matrix products, arithmetic and copies ran while one was open for 0% of the time, Pallas kernels for 17%

profile of v8, /device:TPU:0, one launch (start us, length us, event | category | flops | bytes accessed | tf_op | source)
XLA Modules:
  0.0 59.1 jit_solution(1258613710963176867)
XLA Ops:
  0.6 0.5 collective-permute-start.2
  1.1 0.1 collective-permute-start
  1.2 0.4 collective-permute-start.1
  1.7 1.0 %collective-permute-done.other_ids_ref = s32[2,2,4]{2,1,0:T(2,128)} collective-permute-done((s32[2,2,4]{2,1,0:T(2,128)}, s32[2,2,4]{2,1,0:T(2,128)}, u32[]{:S(2)}, u32[]{:S(2)}) %collective-permute-start) | collective-permute-done | bytes 96 | tf_op jit(solution)/shard_map/ppermute | solution.py:23
  2.6 0.2 collective-permute-done.1.other_replica_ref
  2.8 0.0 collective-permute-done.2.other_ref
  2.8 2.3 %pack.1 = (bf16[16,7168]{1,0:T(8,128)(2,1)}, f32[2,32,16]{2,1,0:T(8,128)}, f32[2,6,16]{2,1,0:T(8,128)}, bf16[8,7168]{1,0:T(8,128)(2,1)}, bf16[8,7168]{1,0:T(8,12...) custom-call(s32[2,6]{1,0:T(2,128)} %bitcast.11, s32[2,2,4]{2,1,0:T(2,128)} %bitcast.8, s32[2,2,4]{2,1,0:T(2,128)} %bitcast.10, ...), custom_call_target="tpu_custom_call" | custom-call | tf_op jit(solution)/shard_map/pack/pallas_call | solution.py:295
  5.1 5.9 %collective-permute-start.3 = (bf16[8,7168]{1,0:T(8,128)(2,1)}, bf16[8,7168]{1,0:T(8,128)(2,1)S(1)}, u32[]{:S(2)}, u32[]{:S(2)}) collective-permute-start(bf16[8,7168]{1,0:T(8,128)(2,1)} %get-tuple-element.39), channel_id=1, source_target_pairs={{0,28},{1,25},{2,30},{3,27},{4,24},{5,29},{6,26},{7,31},{8,20},{9,... | collective-permute-start | bytes 344072 | tf_op jit(solution)/shard_map/ppermute | solution.py:23
  11.0 0.0 collective-permute-start.4
  11.0 0.6 %collective-permute-start.5 = (bf16[8,7168]{1,0:T(8,128)(2,1)}, bf16[8,7168]{1,0:T(8,128)(2,1)S(1)}, u32[]{:S(2)}, u32[]{:S(2)}) collective-permute-start(bf16[8,7168]{1,0:T(8,128)(2,1)} %get-tuple-element.41), channel_id=1, source_target_pairs={{0,12},{1,9},{2,14},{3,11},{4,8},{5,13},{6,10},{7,15},{8,4},{9,1},... | collective-permute-start | bytes 344072 | tf_op jit(solution)/shard_map/ppermute | solution.py:23
  11.6 1.6 %collective-permute-start.7 = (bf16[8,7168]{1,0:T(8,128)(2,1)}, bf16[8,7168]{1,0:T(8,128)(2,1)S(1)}, u32[]{:S(2)}, u32[]{:S(2)}) collective-permute-start(bf16[8,7168]{1,0:T(8,128)(2,1)} %get-tuple-element.42), channel_id=1, source_target_pairs={{0,2},{1,7},{2,0},{3,5},{4,6},{5,3},{6,4},{7,1},{8,10},{9,15},{10,... | collective-permute-start | bytes 344072 | tf_op jit(solution)/shard_map/ppermute | solution.py:23
  13.2 1.5 %collective-permute-start.6 = (bf16[8,7168]{1,0:T(8,128)(2,1)}, bf16[8,7168]{1,0:T(8,128)(2,1)S(1)}, u32[]{:S(2)}, u32[]{:S(2)}) collective-permute-start(bf16[8,7168]{1,0:T(8,128)(2,1)} %get-tuple-element.42), channel_id=1, source_target_pairs={{0,0},{1,5},{2,2},{3,7},{4,4},{5,1},{6,6},{7,3},{8,8},{9,13},{10,1... | collective-permute-start | bytes 344072 | tf_op jit(solution)/shard_map/ppermute | solution.py:23
  14.7 0.8 %copy-done.3 = f32[2,32,16]{2,1,0:T(8,128)S(1)} copy-done((f32[2,32,16]{2,1,0:T(8,128)S(1)}, f32[2,32,16]{2,1,0:T(8,128)}, u32[]{:S(2)}) %copy-start.3) | copy-done | bytes 4120
  15.5 4.2 %load.1 = (bf16[7168,256]{1,0:T(8,128)(2,1)S(1)}, bf16[7168,256]{1,0:T(8,128)(2,1)S(1)}, bf16[256,7168]{1,0:T(8,128)(2,1)S(1)}, f32[8,128]{1,0:T(8,128)S(1)}) custom-call(bf16[7168,256]{1,0:T(8,128)(2,1)} %gate_ref.1, bf16[7168,256]{1,0:T(8,128)(2,1)} %up_ref.1, bf16[256,7168]{1,0:T(8,128)(2,1)} %down_ref.1, f32[2,32,16]{2,1,0:T(8,128)S(1)} %copy-done.3), custom_call_target="tpu_custom_call" | custom-call | tf_op jit(solution)/shard_map/load/pallas_call | solution.py:108
  19.7 0.0 collective-permute-done.3.refs_0_
  19.7 0.5 collective-permute-done.4.refs_1_
  20.2 0.0 collective-permute-done.5.refs_2_
  20.2 0.0 collective-permute-done.7.refs_5_.refs_4_.refs_1_
  20.2 0.0 collective-permute-done.6.refs_3_
  20.3 0.4 collective-permute-start.8
  20.7 1.3 %collective-permute-start.10 = (bf16[24,7168]{1,0:T(8,128)(2,1)S(1)}, bf16[24,7168]{1,0:T(8,128)(2,1)S(1)}, u32[]{:S(2)}, u32[]{:S(2)}) collective-permute-start(bf16[24,7168]{1,0:T(8,128)(2,1)S(1)} %join.4), channel_id=1, source_target_pairs={{0,2},{1,3},{2,0},{3,1},{4,6},{5,7},{6,4},{7,5},{8,10},{9,11},{10,... | collective-permute-start | bytes 1032200 | tf_op jit(solution)/shard_map/ppermute | solution.py:23
  22.0 0.2 collective-permute-done.8.refs_1_
  22.2 0.0 copy-start.4
  22.2 2.1 %experts.2 = (bf16[16,7168]{1,0:T(8,128)(2,1)S(1)}, bf16[16,7168]{1,0:T(8,128)(2,1)S(1)}, bf16[16,7168]{1,0:T(8,128)(2,1)S(1)}, bf16[16,7168]{1,0:T(8,128)(2,1)S(1)}, f32[8,128]{1,0:T(8,128)S(1)}) custom-call(bf16[32,7168]{1,0:T(8,128)(2,1)S(1)} %join.3.refs_0_, bf16[32,7168]{1,0:T(8,128)(2,1)S(1)} %collective-permute-done.8.refs_1_, ...), custom_call_target="tpu_custom_call" | custom-call | tf_op jit(solution)/shard_map/experts/pallas_call | solution.py:147
  24.4 0.4 collective-permute-start.9
  24.7 0.0 copy-done
  24.7 3.0 %attention.1 = (bf16[2,4,64,512]{3,2,1,0:T(8,128)(2,1)}, f32[8,128]{1,0:T(8,128)S(1)}) custom-call(s32[4]{0:T(128)S(1)} %copy-done.7, bf16[2,4,64,576]{3,2,1,0:T(8,128)(2,1)S(1)} %copy-done, bf16[4,64,576]{2,1,0:T(8,128)(2,1)S(1)} %copy-done.1, bf16[2,4,576]{2,1,0:T(4,128)(2,1)S(1)} %copy-done.5), custom_call_target="tpu_custom_call" | custom-call | flops 150994944 | bytes 1474560 | tf_op jit(solution)/shard_map/attention/pallas_call | solution.py:76
  27.7 0.2 weigh.1.refs_2_.weigh_ref
  27.9 0.0 collective-permute-done.9.refs_1_
  28.0 2.9 %collective-permute-done.10.refs_0_ = bf16[24,7168]{1,0:T(8,128)(2,1)S(1)} collective-permute-done((bf16[24,7168]{1,0:T(8,128)(2,1)S(1)}, bf16[24,7168]{1,0:T(8,128)(2,1)S(1)}, u32[]{:S(2)}, u32[]{:S(2)}) %collective-permute-start.10) | collective-permute-done | bytes 344096 | tf_op jit(solution)/shard_map/ppermute | solution.py:23
  30.9 0.1 collective-permute-start.11
  31.0 0.5 collective-permute-start.12
  31.5 1.3 %collective-permute-done.12.refs_3_ = bf16[8,7168]{1,0:T(8,128)(2,1)S(1)} collective-permute-done((bf16[8,7168]{1,0:T(8,128)(2,1)S(1)}, bf16[8,7168]{1,0:T(8,128)(2,1)S(1)}, u32[]{:S(2)}, u32[]{:S(2)}) %collective-permute-start.12) | collective-permute-done | bytes 114720 | tf_op jit(solution)/shard_map/ppermute | solution.py:23
  32.8 0.0 collective-permute-done.11.refs_2_
  32.8 2.1 %experts.3 = (bf16[16,7168]{1,0:T(8,128)(2,1)S(1)}, bf16[16,7168]{1,0:T(8,128)(2,1)S(1)}, bf16[16,7168]{1,0:T(8,128)(2,1)S(1)}, bf16[16,7168]{1,0:T(8,128)(2,1)S(1)}, f32[8,128]{1,0:T(8,128)S(1)}) custom-call(bf16[24,7168]{1,0:T(8,128)(2,1)S(1)} %join.5.refs_0_, bf16[8,7168]{1,0:T(8,128)(2,1)S(1)} %collective-permute-done.7.refs_5_.refs_4_.refs_1_, ...), custom_call_target="tpu_custom_call" | custom-call | tf_op jit(solution)/shard_map/experts/pallas_call | solution.py:147
  35.0 0.2 collective-permute-start.13
  35.2 0.4 collective-permute-start.19
  35.6 0.1 collective-permute-start.18
  35.7 0.8 %collective-permute-done.13.refs_1_ = bf16[16,7168]{1,0:T(8,128)(2,1)S(1)} collective-permute-done((bf16[16,7168]{1,0:T(8,128)(2,1)S(1)}, bf16[16,7168]{1,0:T(8,128)(2,1)S(1)}, u32[]{:S(2)}, u32[]{:S(2)}) %collective-permute-start.13) | collective-permute-done | bytes 229408 | tf_op jit(solution)/shard_map/ppermute | solution.py:23
  36.5 0.1 add.8
  36.6 1.5 %collective-permute-start.14 = (bf16[8,7168]{1,0:T(8,128)(2,1)S(1)}, bf16[8,7168]{1,0:T(8,128)(2,1)S(1)}, u32[]{:S(2)}, u32[]{:S(2)}) collective-permute-start(bf16[8,7168]{1,0:T(8,128)(2,1)S(1)} %get-tuple-element.54), channel_id=1, source_target_pairs={{0,2},{1,3},{2,0},{3,1},{4,6},{5,7},{6,4},{7,5},{8,10},{9,11},{10,... | collective-permute-start | bytes 344072 | tf_op jit(solution)/shard_map/ppermute | solution.py:23
  38.2 0.5 collective-permute-start.16
  38.7 0.0 collective-permute-done.19.refs_1_
  38.7 0.1 add.12
  38.8 1.5 %collective-permute-start.20 = (bf16[8,7168]{1,0:T(8,128)(2,1)S(1)}, bf16[8,7168]{1,0:T(8,128)(2,1)S(1)}, u32[]{:S(2)}, u32[]{:S(2)}) collective-permute-start(bf16[8,7168]{1,0:T(8,128)(2,1)S(1)} %get-tuple-element.63), channel_id=1, source_target_pairs={{0,2},{1,3},{2,0},{3,1},{4,6},{5,7},{6,4},{7,5},{8,10},{9,11},{10,... | collective-permute-start | bytes 344072 | tf_op jit(solution)/shard_map/ppermute | solution.py:23
  40.3 0.0 collective-permute-done.18.refs_1_
  40.4 0.7 %collective-permute-start.22 = (bf16[8,7168]{1,0:T(8,128)(2,1)S(1)}, bf16[8,7168]{1,0:T(8,128)(2,1)S(1)}, u32[]{:S(2)}, u32[]{:S(2)}) collective-permute-start(bf16[8,7168]{1,0:T(8,128)(2,1)S(1)} %convert_element_type.3), channel_id=1, source_target_pairs={{0,0},{1,5},{2,2},{3,7},{4,4},{5,1},{6,6},{7,3},{8,8},{9,13},{10,1... | collective-permute-start | bytes 344072 | tf_op jit(solution)/shard_map/ppermute | solution.py:23
  41.1 0.6 %collective-permute-start.23 = (bf16[8,7168]{1,0:T(8,128)(2,1)S(1)}, bf16[8,7168]{1,0:T(8,128)(2,1)S(1)}, u32[]{:S(2)}, u32[]{:S(2)}) collective-permute-start(bf16[8,7168]{1,0:T(8,128)(2,1)S(1)} %get-tuple-element.65), channel_id=1, source_target_pairs={{0,2},{1,7},{2,0},{3,5},{4,6},{5,3},{6,4},{7,1},{8,10},{9,15},{10,... | collective-permute-start | bytes 344072 | tf_op jit(solution)/shard_map/ppermute | solution.py:23
  41.7 1.0 %collective-permute-done.14.refs_1_ = bf16[8,7168]{1,0:T(8,128)(2,1)S(1)} collective-permute-done((bf16[8,7168]{1,0:T(8,128)(2,1)S(1)}, bf16[8,7168]{1,0:T(8,128)(2,1)S(1)}, u32[]{:S(2)}, u32[]{:S(2)}) %collective-permute-start.14) | collective-permute-done | bytes 114720 | tf_op jit(solution)/shard_map/ppermute | solution.py:23
  42.7 4.2 %collective-permute-start.15 = (bf16[8,7168]{1,0:T(8,128)(2,1)S(1)}, bf16[8,7168]{1,0:T(8,128)(2,1)S(1)}, u32[]{:S(2)}, u32[]{:S(2)}) collective-permute-start(bf16[8,7168]{1,0:T(8,128)(2,1)S(1)} %add.9.refs_2_), channel_id=1, source_target_pairs={{0,28},{1,25},{2,30},{3,27},{4,24},{5,29},{6,26},{7,31},{8,20},{9,... | collective-permute-start | bytes 344072 | tf_op jit(solution)/shard_map/ppermute | solution.py:23
  46.8 0.0 collective-permute-done.16.refs_1_
  46.9 0.5 collective-permute-start.17
  47.3 0.2 collective-permute-done.20.refs_1_
  47.6 2.4 %collective-permute-start.21 = (bf16[8,7168]{1,0:T(8,128)(2,1)S(1)}, bf16[8,7168]{1,0:T(8,128)(2,1)S(1)}, u32[]{:S(2)}, u32[]{:S(2)}) collective-permute-start(bf16[8,7168]{1,0:T(8,128)(2,1)S(1)} %add.13), channel_id=1, source_target_pairs={{0,12},{1,9},{2,14},{3,11},{4,8},{5,13},{6,10},{7,15},{8,4},{9,1},... | collective-permute-start | bytes 344072 | tf_op jit(solution)/shard_map/ppermute | solution.py:23
  50.0 1.5 %collective-permute-done.15.refs_0_ = bf16[8,7168]{1,0:T(8,128)(2,1)S(1)} collective-permute-done((bf16[8,7168]{1,0:T(8,128)(2,1)S(1)}, bf16[8,7168]{1,0:T(8,128)(2,1)S(1)}, u32[]{:S(2)}, u32[]{:S(2)}) %collective-permute-start.15) | collective-permute-done | bytes 114720 | tf_op jit(solution)/shard_map/ppermute | solution.py:23
  51.5 4.8 %collective-permute-done.17.refs_1_ = bf16[8,7168]{1,0:T(8,128)(2,1)S(1)} collective-permute-done((bf16[8,7168]{1,0:T(8,128)(2,1)S(1)}, bf16[8,7168]{1,0:T(8,128)(2,1)S(1)}, u32[]{:S(2)}, u32[]{:S(2)}) %collective-permute-start.17) | collective-permute-done | bytes 114720 | tf_op jit(solution)/shard_map/ppermute | solution.py:23
  56.3 0.4 combine.2.first_ref
  56.6 0.0 collective-permute-done.22.refs_1_
  56.7 0.0 collective-permute-done.23.refs_2_
  56.7 0.0 collective-permute-done.21.refs_0_
  56.7 0.4 combine.3
  57.1 0.1 collective-permute-start.24
  57.1 1.3 %collective-permute-done.24.received_ref = bf16[8,7168]{1,0:T(8,128)(2,1)S(1)} collective-permute-done((bf16[8,7168]{1,0:T(8,128)(2,1)S(1)}, bf16[8,7168]{1,0:T(8,128)(2,1)S(1)}, u32[]{:S(2)}, u32[]{:S(2)}) %collective-permute-start.24) | collective-permute-done | bytes 114720 | tf_op jit(solution)/shard_map/ppermute | solution.py:23
  58.5 0.7 %finish.1 = bf16[2,4,7168]{2,1,0:T(4,128)(2,1)} custom-call(f32[8,7168]{1,0:T(8,128)S(1)} %get-tuple-element.66.own_ref, bf16[8,7168]{1,0:T(8,128)(2,1)S(1)} %collective-permute-done.24.received_ref), custom_call_target="tpu_custom_call" | custom-call | tf_op jit(solution)/shard_map/finish/pallas_call | solution.py:413
  (22 shorter events, 0.3 us)
Async XLA Ops:
  0.6 2.2 %collective-permute-start.2 = (bf16[2,4,7168]{2,1,0:T(4,128)(2,1)}, bf16[2,4,7168]{2,1,0:T(4,128)(2,1)}, u32[]{:S(2)}, u32[]{:S(2)}) collective-permute-start(bf16[2,4,7168]{2,1,0:T(4,128)(2,1)} %raw_ref.1), channel_id=1, source_target_pairs={{0,1},{1,0},{2,3},{3,2},{4,5},{5,4},{6,7},{7,6},{8,9},{9,8},{10,11... | collective-permute-start | bytes 344072 | tf_op jit(solution)/shard_map/ppermute | solution.py:23
  1.1 1.5 %collective-permute-start = (s32[2,2,4]{2,1,0:T(2,128)}, s32[2,2,4]{2,1,0:T(2,128)}, u32[]{:S(2)}, u32[]{:S(2)}) collective-permute-start(s32[2,2,4]{2,1,0:T(2,128)} %bitcast.7), channel_id=1, source_target_pairs={{0,1},{1,0},{2,3},{3,2},{4,5},{5,4},{6,7},{7,6},{8,9},{9,8},{10,11... | collective-permute-start | bytes 200 | tf_op jit(solution)/shard_map/ppermute | solution.py:23
  1.2 1.6 %collective-permute-start.1 = (s32[2,2,4]{2,1,0:T(2,128)}, s32[2,2,4]{2,1,0:T(2,128)}, u32[]{:S(2)}, u32[]{:S(2)}) collective-permute-start(s32[2,2,4]{2,1,0:T(2,128)} %bitcast.9), channel_id=1, source_target_pairs={{0,1},{1,0},{2,3},{3,2},{4,5},{5,4},{6,7},{7,6},{8,9},{9,8},{10,11... | collective-permute-start | bytes 200 | tf_op jit(solution)/shard_map/ppermute | solution.py:23
  5.1 14.6 %collective-permute-start.3 = (bf16[8,7168]{1,0:T(8,128)(2,1)}, bf16[8,7168]{1,0:T(8,128)(2,1)S(1)}, u32[]{:S(2)}, u32[]{:S(2)}) collective-permute-start(bf16[8,7168]{1,0:T(8,128)(2,1)} %get-tuple-element.39), channel_id=1, source_target_pairs={{0,28},{1,25},{2,30},{3,27},{4,24},{5,29},{6,26},{7,31},{8,20},{9,... | collective-permute-start | bytes 344072 | tf_op jit(solution)/shard_map/ppermute | solution.py:23
  11.0 9.3 %collective-permute-start.4 = (bf16[8,7168]{1,0:T(8,128)(2,1)}, bf16[8,7168]{1,0:T(8,128)(2,1)S(1)}, u32[]{:S(2)}, u32[]{:S(2)}) collective-permute-start(bf16[8,7168]{1,0:T(8,128)(2,1)} %get-tuple-element.40), channel_id=1, source_target_pairs={{0,16},{1,21},{2,18},{3,23},{4,20},{5,17},{6,22},{7,19},{8,24},{9,... | collective-permute-start | bytes 344072 | tf_op jit(solution)/shard_map/ppermute | solution.py:23
  11.0 9.3 %collective-permute-start.5 = (bf16[8,7168]{1,0:T(8,128)(2,1)}, bf16[8,7168]{1,0:T(8,128)(2,1)S(1)}, u32[]{:S(2)}, u32[]{:S(2)}) collective-permute-start(bf16[8,7168]{1,0:T(8,128)(2,1)} %get-tuple-element.41), channel_id=1, source_target_pairs={{0,12},{1,9},{2,14},{3,11},{4,8},{5,13},{6,10},{7,15},{8,4},{9,1},... | collective-permute-start | bytes 344072 | tf_op jit(solution)/shard_map/ppermute | solution.py:23
  11.6 8.7 %collective-permute-start.7 = (bf16[8,7168]{1,0:T(8,128)(2,1)}, bf16[8,7168]{1,0:T(8,128)(2,1)S(1)}, u32[]{:S(2)}, u32[]{:S(2)}) collective-permute-start(bf16[8,7168]{1,0:T(8,128)(2,1)} %get-tuple-element.42), channel_id=1, source_target_pairs={{0,2},{1,7},{2,0},{3,5},{4,6},{5,3},{6,4},{7,1},{8,10},{9,15},{10,... | collective-permute-start | bytes 344072 | tf_op jit(solution)/shard_map/ppermute | solution.py:23
  13.2 7.1 %collective-permute-start.6 = (bf16[8,7168]{1,0:T(8,128)(2,1)}, bf16[8,7168]{1,0:T(8,128)(2,1)S(1)}, u32[]{:S(2)}, u32[]{:S(2)}) collective-permute-start(bf16[8,7168]{1,0:T(8,128)(2,1)} %get-tuple-element.42), channel_id=1, source_target_pairs={{0,0},{1,5},{2,2},{3,7},{4,4},{5,1},{6,6},{7,3},{8,8},{9,13},{10,1... | collective-permute-start | bytes 344072 | tf_op jit(solution)/shard_map/ppermute | solution.py:23
  14.7 0.8 %copy-start.3 = (f32[2,32,16]{2,1,0:T(8,128)S(1)}, f32[2,32,16]{2,1,0:T(8,128)}, u32[]{:S(2)}) copy-start(f32[2,32,16]{2,1,0:T(8,128)} %get-tuple-element.37.place_ref._) | copy-start | bytes 12292
  20.3 1.9 %collective-permute-start.8 = (bf16[32,7168]{1,0:T(8,128)(2,1)S(1)}, bf16[32,7168]{1,0:T(8,128)(2,1)S(1)}, u32[]{:S(2)}, u32[]{:S(2)}) collective-permute-start(bf16[32,7168]{1,0:T(8,128)(2,1)S(1)} %join.3.refs_0_), channel_id=1, source_target_pairs={{0,1},{1,0},{2,3},{3,2},{4,5},{5,4},{6,7},{7,6},{8,9},{9,8},{10,11... | collective-permute-start | bytes 1376264 | tf_op jit(solution)/shard_map/ppermute | solution.py:23
  20.7 10.3 %collective-permute-start.10 = (bf16[24,7168]{1,0:T(8,128)(2,1)S(1)}, bf16[24,7168]{1,0:T(8,128)(2,1)S(1)}, u32[]{:S(2)}, u32[]{:S(2)}) collective-permute-start(bf16[24,7168]{1,0:T(8,128)(2,1)S(1)} %join.4), channel_id=1, source_target_pairs={{0,2},{1,3},{2,0},{3,1},{4,6},{5,7},{6,4},{7,5},{8,10},{9,11},{10,... | collective-permute-start | bytes 1032200 | tf_op jit(solution)/shard_map/ppermute | solution.py:23
  22.2 2.5 %copy-start = (bf16[2,4,64,576]{3,2,1,0:T(8,128)(2,1)S(1)}, bf16[2,4,64,576]{3,2,1,0:T(8,128)(2,1)}, u32[]{:S(2)}) copy-start(bf16[2,4,64,576]{3,2,1,0:T(8,128)(2,1)} %query_ref.1) | copy-start | bytes 1769476
  22.2 2.5 %copy-start.1 = (bf16[4,64,576]{2,1,0:T(8,128)(2,1)S(1)}, bf16[4,64,576]{2,1,0:T(8,128)(2,1)}, u32[]{:S(2)}) copy-start(bf16[4,64,576]{2,1,0:T(8,128)(2,1)} %cache_ref.1) | copy-start | bytes 884740
  22.2 2.5 %copy-start.5 = (bf16[2,4,576]{2,1,0:T(4,128)(2,1)S(1)}, bf16[2,4,576]{2,1,0:T(4,128)(2,1)}, u32[]{:S(2)}) copy-start(bf16[2,4,576]{2,1,0:T(4,128)(2,1)} %fresh_ref.1) | copy-start | bytes 27652
  22.2 2.5 %copy-start.7 = (s32[4]{0:T(128)S(1)}, s32[4]{0:T(128)}, u32[]{:S(2)}) copy-start(s32[4]{0:T(128)} %lengths_ref.1) | copy-start | bytes 52
  22.2 5.5 %copy-start.2 = (bf16[16,7168]{1,0:T(8,128)(2,1)S(1)}, bf16[16,7168]{1,0:T(8,128)(2,1)}, u32[]{:S(2)}) copy-start(bf16[16,7168]{1,0:T(8,128)(2,1)} %get-tuple-element.36.normed_ref) | copy-start | bytes 688132
  22.2 5.5 %copy-start.4 = (bf16[7168,6]{0,1:T(8,128)(2,1)S(1)}, bf16[7168,6]{0,1:T(8,128)(2,1)}, u32[]{:S(2)}) copy-start(bf16[7168,6]{0,1:T(8,128)(2,1)} %param.15) | copy-start | bytes 258052
  22.2 5.5 %copy-start.6 = (f32[2,6,16]{2,1,0:T(8,128)S(1)}, f32[2,6,16]{2,1,0:T(8,128)}, u32[]{:S(2)}) copy-start(f32[2,6,16]{2,1,0:T(8,128)} %get-tuple-element.38.choose_ref) | copy-start | bytes 2308
  24.4 3.6 %collective-permute-start.9 = (bf16[16,7168]{1,0:T(8,128)(2,1)S(1)}, bf16[16,7168]{1,0:T(8,128)(2,1)S(1)}, u32[]{:S(2)}, u32[]{:S(2)}) collective-permute-start(bf16[16,7168]{1,0:T(8,128)(2,1)S(1)} %get-tuple-element.48), channel_id=1, source_target_pairs={{0,1},{1,0},{2,3},{3,2},{4,5},{5,4},{6,7},{7,6},{8,9},{9,8},{10,11... | collective-permute-start | bytes 688136 | tf_op jit(solution)/shard_map/ppermute | solution.py:23
  30.9 1.9 %collective-permute-start.11 = (bf16[24,7168]{1,0:T(8,128)(2,1)S(1)}, bf16[24,7168]{1,0:T(8,128)(2,1)S(1)}, u32[]{:S(2)}, u32[]{:S(2)}) collective-permute-start(bf16[24,7168]{1,0:T(8,128)(2,1)S(1)} %join.5.refs_0_), channel_id=1, source_target_pairs={{0,1},{1,0},{2,3},{3,2},{4,5},{5,4},{6,7},{7,6},{8,9},{9,8},{10,11... | collective-permute-start | bytes 1032200 | tf_op jit(solution)/shard_map/ppermute | solution.py:23
  31.0 1.8 %collective-permute-start.12 = (bf16[8,7168]{1,0:T(8,128)(2,1)S(1)}, bf16[8,7168]{1,0:T(8,128)(2,1)S(1)}, u32[]{:S(2)}, u32[]{:S(2)}) collective-permute-start(bf16[8,7168]{1,0:T(8,128)(2,1)S(1)} %collective-permute-done.7.refs_5_.refs_4_.refs_1_), channel_id=1, source_target_pairs={{0,1},{1,0},{2,3},{3,2},{4,5},{5,4},{6,7},{7,6},{8,9},{9,8},{10,11... | collective-permute-start | bytes 344072 | tf_op jit(solution)/shard_map/ppermute | solution.py:23
  35.0 1.6 %collective-permute-start.13 = (bf16[16,7168]{1,0:T(8,128)(2,1)S(1)}, bf16[16,7168]{1,0:T(8,128)(2,1)S(1)}, u32[]{:S(2)}, u32[]{:S(2)}) collective-permute-start(bf16[16,7168]{1,0:T(8,128)(2,1)S(1)} %get-tuple-element.53), channel_id=1, source_target_pairs={{0,1},{1,0},{2,3},{3,2},{4,5},{5,4},{6,7},{7,6},{8,9},{9,8},{10,11... | collective-permute-start | bytes 688136 | tf_op jit(solution)/shard_map/ppermute | solution.py:23
  35.2 3.5 %collective-permute-start.19 = (bf16[16,7168]{1,0:T(8,128)(2,1)S(1)}, bf16[16,7168]{1,0:T(8,128)(2,1)S(1)}, u32[]{:S(2)}, u32[]{:S(2)}) collective-permute-start(bf16[16,7168]{1,0:T(8,128)(2,1)S(1)} %get-tuple-element.62), channel_id=1, source_target_pairs={{0,1},{1,0},{2,3},{3,2},{4,5},{5,4},{6,7},{7,6},{8,9},{9,8},{10,11... | collective-permute-start | bytes 688136 | tf_op jit(solution)/shard_map/ppermute | solution.py:23
  35.6 4.7 %collective-permute-start.18 = (bf16[16,7168]{1,0:T(8,128)(2,1)S(1)}, bf16[16,7168]{1,0:T(8,128)(2,1)S(1)}, u32[]{:S(2)}, u32[]{:S(2)}) collective-permute-start(bf16[16,7168]{1,0:T(8,128)(2,1)S(1)} %get-tuple-element.59), channel_id=1, source_target_pairs={{0,1},{1,0},{2,3},{3,2},{4,5},{5,4},{6,7},{7,6},{8,9},{9,8},{10,11... | collective-permute-start | bytes 688136 | tf_op jit(solution)/shard_map/ppermute | solution.py:23
  36.6 6.1 %collective-permute-start.14 = (bf16[8,7168]{1,0:T(8,128)(2,1)S(1)}, bf16[8,7168]{1,0:T(8,128)(2,1)S(1)}, u32[]{:S(2)}, u32[]{:S(2)}) collective-permute-start(bf16[8,7168]{1,0:T(8,128)(2,1)S(1)} %get-tuple-element.54), channel_id=1, source_target_pairs={{0,2},{1,3},{2,0},{3,1},{4,6},{5,7},{6,4},{7,5},{8,10},{9,11},{10,... | collective-permute-start | bytes 344072 | tf_op jit(solution)/shard_map/ppermute | solution.py:23
  38.2 8.7 %collective-permute-start.16 = (bf16[8,7168]{1,0:T(8,128)(2,1)S(1)}, bf16[8,7168]{1,0:T(8,128)(2,1)S(1)}, u32[]{:S(2)}, u32[]{:S(2)}) collective-permute-start(bf16[8,7168]{1,0:T(8,128)(2,1)S(1)} %get-tuple-element.57), channel_id=1, source_target_pairs={{0,2},{1,3},{2,0},{3,1},{4,6},{5,7},{6,4},{7,5},{8,10},{9,11},{10,... | collective-permute-start | bytes 344072 | tf_op jit(solution)/shard_map/ppermute | solution.py:23
  38.8 8.8 %collective-permute-start.20 = (bf16[8,7168]{1,0:T(8,128)(2,1)S(1)}, bf16[8,7168]{1,0:T(8,128)(2,1)S(1)}, u32[]{:S(2)}, u32[]{:S(2)}) collective-permute-start(bf16[8,7168]{1,0:T(8,128)(2,1)S(1)} %get-tuple-element.63), channel_id=1, source_target_pairs={{0,2},{1,3},{2,0},{3,1},{4,6},{5,7},{6,4},{7,5},{8,10},{9,11},{10,... | collective-permute-start | bytes 344072 | tf_op jit(solution)/shard_map/ppermute | solution.py:23
  40.4 16.3 %collective-permute-start.22 = (bf16[8,7168]{1,0:T(8,128)(2,1)S(1)}, bf16[8,7168]{1,0:T(8,128)(2,1)S(1)}, u32[]{:S(2)}, u32[]{:S(2)}) collective-permute-start(bf16[8,7168]{1,0:T(8,128)(2,1)S(1)} %convert_element_type.3), channel_id=1, source_target_pairs={{0,0},{1,5},{2,2},{3,7},{4,4},{5,1},{6,6},{7,3},{8,8},{9,13},{10,1... | collective-permute-start | bytes 344072 | tf_op jit(solution)/shard_map/ppermute | solution.py:23
  41.1 15.6 %collective-permute-start.23 = (bf16[8,7168]{1,0:T(8,128)(2,1)S(1)}, bf16[8,7168]{1,0:T(8,128)(2,1)S(1)}, u32[]{:S(2)}, u32[]{:S(2)}) collective-permute-start(bf16[8,7168]{1,0:T(8,128)(2,1)S(1)} %get-tuple-element.65), channel_id=1, source_target_pairs={{0,2},{1,7},{2,0},{3,5},{4,6},{5,3},{6,4},{7,1},{8,10},{9,15},{10,... | collective-permute-start | bytes 344072 | tf_op jit(solution)/shard_map/ppermute | solution.py:23
  42.7 8.8 %collective-permute-start.15 = (bf16[8,7168]{1,0:T(8,128)(2,1)S(1)}, bf16[8,7168]{1,0:T(8,128)(2,1)S(1)}, u32[]{:S(2)}, u32[]{:S(2)}) collective-permute-start(bf16[8,7168]{1,0:T(8,128)(2,1)S(1)} %add.9.refs_2_), channel_id=1, source_target_pairs={{0,28},{1,25},{2,30},{3,27},{4,24},{5,29},{6,26},{7,31},{8,20},{9,... | collective-permute-start | bytes 344072 | tf_op jit(solution)/shard_map/ppermute | solution.py:23
  46.9 9.4 %collective-permute-start.17 = (bf16[8,7168]{1,0:T(8,128)(2,1)S(1)}, bf16[8,7168]{1,0:T(8,128)(2,1)S(1)}, u32[]{:S(2)}, u32[]{:S(2)}) collective-permute-start(bf16[8,7168]{1,0:T(8,128)(2,1)S(1)} %add.10.refs_2_), channel_id=1, source_target_pairs={{0,16},{1,21},{2,18},{3,23},{4,20},{5,17},{6,22},{7,19},{8,24},{9,... | collective-permute-start | bytes 344072 | tf_op jit(solution)/shard_map/ppermute | solution.py:23
  47.6 9.1 %collective-permute-start.21 = (bf16[8,7168]{1,0:T(8,128)(2,1)S(1)}, bf16[8,7168]{1,0:T(8,128)(2,1)S(1)}, u32[]{:S(2)}, u32[]{:S(2)}) collective-permute-start(bf16[8,7168]{1,0:T(8,128)(2,1)S(1)} %add.13), channel_id=1, source_target_pairs={{0,12},{1,9},{2,14},{3,11},{4,8},{5,13},{6,10},{7,15},{8,4},{9,1},... | collective-permute-start | bytes 344072 | tf_op jit(solution)/shard_map/ppermute | solution.py:23
  57.1 1.4 %collective-permute-start.24 = (bf16[8,7168]{1,0:T(8,128)(2,1)S(1)}, bf16[8,7168]{1,0:T(8,128)(2,1)S(1)}, u32[]{:S(2)}, u32[]{:S(2)}) collective-permute-start(bf16[8,7168]{1,0:T(8,128)(2,1)S(1)} %get-tuple-element.67), channel_id=1, source_target_pairs={{0,1},{1,0},{2,3},{3,2},{4,5},{5,4},{6,7},{7,6},{8,9},{9,8},{10,11... | collective-permute-start | bytes 344072 | tf_op jit(solution)/shard_map/ppermute | solution.py:23

commit v9 on v8

--- a/solution.py
+++ b/solution.py
@@ -346,16 +346,14 @@
 
 def weighted(weights, part_refs):
     high = weights.astype(jnp.bfloat16)
-    left = weights - high.astype(jnp.float32)
-    middle = left.astype(jnp.bfloat16)
-    low = (left - middle.astype(jnp.float32)).astype(jnp.bfloat16)
+    low = (weights - high.astype(jnp.float32)).astype(jnp.bfloat16)
     rows = jnp.concatenate([ref[...].astype(jnp.float32) for ref in part_refs], axis=0)
     rows = rows.astype(jnp.bfloat16)
     pieces = [
         lax.dot_general(w, rows, (((0,), (0,)), ((), ())), preferred_element_type=jnp.float32)
-        for w in (high, middle, low)
+        for w in (high, low)
     ]
-    return pieces[0] + (pieces[1] + pieces[2])
+    return pieces[0] + pieces[1]
 
 
 def first_half_kernel(weigh_ref, *refs):

time: 59.4 us -> 59.3 us (level)
  no operation moved by 1% of the time
where the time goes in v9:
time: 59.3 us; the launch traced here: 59 us
  starting transfers between devices  25.9 us (44%)
  waiting for transfers between devices  15.8 us (27%)
  Pallas kernels  15.6 us (26%)
  between operations  0.85 us (1%)
  local copies, waits for them, and re-layouts  0.79 us (1%)
    ppermute x25, starting transfers between devices, flipped(): return lax.ppermute(value, 'ep', pairs)  25.9 us
    ppermute x25, waiting for transfers between devices, flipped(): return lax.ppermute(value, 'ep', pairs)  15.8 us
    pallas_call x2, Pallas kernels, experts(): pl.pallas_call(functools.partial(expert_kernel, count), out_shape=[jax.Sh...  4.28 us
    pallas_call x1, Pallas kernels, load(): pl.pallas_call(load_kernel, out_shape=[jax.ShapeDtypeStruct(w.shape, w.dt...  4.23 us
    pallas_call x1, Pallas kernels, attend(): pl.pallas_call(attend_kernel, out_shape=[jax.ShapeDtypeStruct((steps, tok...  2.97 us
    pallas_call x1, Pallas kernels, pack(): pl.pallas_call(functools.partial(pack_kernel, slots, deltas), out_shape=[...  2.25 us
  transfers between devices with their start and end apart: 25, of which 12 were waited for; matrix products, arithmetic and copies ran while one was open for 0% of the time, Pallas kernels for 17%

profile of v9, /device:TPU:0, one launch (start us, length us, event | category | flops | bytes accessed | tf_op | source)
XLA Modules:
  0.0 59.0 jit_solution(3127522274699195653)
XLA Ops:
  0.6 0.5 collective-permute-start.2
  1.1 0.1 collective-permute-start
  1.2 0.4 collective-permute-start.1
  1.7 1.0 %collective-permute-done.other_ids_ref = s32[2,2,4]{2,1,0:T(2,128)} collective-permute-done((s32[2,2,4]{2,1,0:T(2,128)}, s32[2,2,4]{2,1,0:T(2,128)}, u32[]{:S(2)}, u32[]{:S(2)}) %collective-permute-start) | collective-permute-done | bytes 96 | tf_op jit(solution)/shard_map/ppermute | solution.py:23
  2.6 0.2 collective-permute-done.1.other_replica_ref
  2.8 0.0 collective-permute-done.2.other_ref
  2.8 2.3 %pack.1 = (bf16[16,7168]{1,0:T(8,128)(2,1)}, f32[2,32,16]{2,1,0:T(8,128)}, f32[2,6,16]{2,1,0:T(8,128)}, bf16[8,7168]{1,0:T(8,128)(2,1)}, bf16[8,7168]{1,0:T(8,12...) custom-call(s32[2,6]{1,0:T(2,128)} %bitcast.11, s32[2,2,4]{2,1,0:T(2,128)} %bitcast.8, s32[2,2,4]{2,1,0:T(2,128)} %bitcast.10, ...), custom_call_target="tpu_custom_call" | custom-call | tf_op jit(solution)/shard_map/pack/pallas_call | solution.py:295
  5.1 5.9 %collective-permute-start.3 = (bf16[8,7168]{1,0:T(8,128)(2,1)}, bf16[8,7168]{1,0:T(8,128)(2,1)S(1)}, u32[]{:S(2)}, u32[]{:S(2)}) collective-permute-start(bf16[8,7168]{1,0:T(8,128)(2,1)} %get-tuple-element.39), channel_id=1, source_target_pairs={{0,28},{1,25},{2,30},{3,27},{4,24},{5,29},{6,26},{7,31},{8,20},{9,... | collective-permute-start | bytes 344072 | tf_op jit(solution)/shard_map/ppermute | solution.py:23
  11.0 0.0 collective-permute-start.4
  11.0 0.6 %collective-permute-start.5 = (bf16[8,7168]{1,0:T(8,128)(2,1)}, bf16[8,7168]{1,0:T(8,128)(2,1)S(1)}, u32[]{:S(2)}, u32[]{:S(2)}) collective-permute-start(bf16[8,7168]{1,0:T(8,128)(2,1)} %get-tuple-element.41), channel_id=1, source_target_pairs={{0,12},{1,9},{2,14},{3,11},{4,8},{5,13},{6,10},{7,15},{8,4},{9,1},... | collective-permute-start | bytes 344072 | tf_op jit(solution)/shard_map/ppermute | solution.py:23
  11.6 1.6 %collective-permute-start.7 = (bf16[8,7168]{1,0:T(8,128)(2,1)}, bf16[8,7168]{1,0:T(8,128)(2,1)S(1)}, u32[]{:S(2)}, u32[]{:S(2)}) collective-permute-start(bf16[8,7168]{1,0:T(8,128)(2,1)} %get-tuple-element.42), channel_id=1, source_target_pairs={{0,2},{1,7},{2,0},{3,5},{4,6},{5,3},{6,4},{7,1},{8,10},{9,15},{10,... | collective-permute-start | bytes 344072 | tf_op jit(solution)/shard_map/ppermute | solution.py:23
  13.2 1.5 %collective-permute-start.6 = (bf16[8,7168]{1,0:T(8,128)(2,1)}, bf16[8,7168]{1,0:T(8,128)(2,1)S(1)}, u32[]{:S(2)}, u32[]{:S(2)}) collective-permute-start(bf16[8,7168]{1,0:T(8,128)(2,1)} %get-tuple-element.42), channel_id=1, source_target_pairs={{0,0},{1,5},{2,2},{3,7},{4,4},{5,1},{6,6},{7,3},{8,8},{9,13},{10,1... | collective-permute-start | bytes 344072 | tf_op jit(solution)/shard_map/ppermute | solution.py:23
  14.7 0.8 %copy-done.3 = f32[2,32,16]{2,1,0:T(8,128)S(1)} copy-done((f32[2,32,16]{2,1,0:T(8,128)S(1)}, f32[2,32,16]{2,1,0:T(8,128)}, u32[]{:S(2)}) %copy-start.3) | copy-done | bytes 4120
  15.5 4.2 %load.1 = (bf16[7168,256]{1,0:T(8,128)(2,1)S(1)}, bf16[7168,256]{1,0:T(8,128)(2,1)S(1)}, bf16[256,7168]{1,0:T(8,128)(2,1)S(1)}, f32[8,128]{1,0:T(8,128)S(1)}) custom-call(bf16[7168,256]{1,0:T(8,128)(2,1)} %gate_ref.1, bf16[7168,256]{1,0:T(8,128)(2,1)} %up_ref.1, bf16[256,7168]{1,0:T(8,128)(2,1)} %down_ref.1, f32[2,32,16]{2,1,0:T(8,128)S(1)} %copy-done.3), custom_call_target="tpu_custom_call" | custom-call | tf_op jit(solution)/shard_map/load/pallas_call | solution.py:108
  19.7 0.0 collective-permute-done.3.refs_0_
  19.7 0.5 collective-permute-done.4.refs_1_
  20.2 0.0 collective-permute-done.5.refs_2_
  20.2 0.0 collective-permute-done.7.refs_5_.refs_4_.refs_1_
  20.2 0.0 collective-permute-done.6.refs_3_
  20.3 0.4 collective-permute-start.8
  20.7 1.3 %collective-permute-start.10 = (bf16[24,7168]{1,0:T(8,128)(2,1)S(1)}, bf16[24,7168]{1,0:T(8,128)(2,1)S(1)}, u32[]{:S(2)}, u32[]{:S(2)}) collective-permute-start(bf16[24,7168]{1,0:T(8,128)(2,1)S(1)} %join.4), channel_id=1, source_target_pairs={{0,2},{1,3},{2,0},{3,1},{4,6},{5,7},{6,4},{7,5},{8,10},{9,11},{10,... | collective-permute-start | bytes 1032200 | tf_op jit(solution)/shard_map/ppermute | solution.py:23
  22.0 0.2 collective-permute-done.8.refs_1_
  22.2 0.0 copy-start.2
  22.2 0.0 copy-start.4
  22.2 2.1 %experts.2 = (bf16[16,7168]{1,0:T(8,128)(2,1)S(1)}, bf16[16,7168]{1,0:T(8,128)(2,1)S(1)}, bf16[16,7168]{1,0:T(8,128)(2,1)S(1)}, bf16[16,7168]{1,0:T(8,128)(2,1)S(1)}, f32[8,128]{1,0:T(8,128)S(1)}) custom-call(bf16[32,7168]{1,0:T(8,128)(2,1)S(1)} %join.3.refs_0_, bf16[32,7168]{1,0:T(8,128)(2,1)S(1)} %collective-permute-done.8.refs_1_, ...), custom_call_target="tpu_custom_call" | custom-call | tf_op jit(solution)/shard_map/experts/pallas_call | solution.py:147
  24.4 0.4 collective-permute-start.9
  24.7 3.0 %attention.1 = (bf16[2,4,64,512]{3,2,1,0:T(8,128)(2,1)}, f32[8,128]{1,0:T(8,128)S(1)}) custom-call(s32[4]{0:T(128)S(1)} %copy-done.7, bf16[2,4,64,576]{3,2,1,0:T(8,128)(2,1)S(1)} %copy-done, bf16[4,64,576]{2,1,0:T(8,128)(2,1)S(1)} %copy-done.1, bf16[2,4,576]{2,1,0:T(4,128)(2,1)S(1)} %copy-done.5), custom_call_target="tpu_custom_call" | custom-call | flops 150994944 | bytes 1474560 | tf_op jit(solution)/shard_map/attention/pallas_call | solution.py:76
  27.7 0.2 weigh.1.refs_2_.weigh_ref
  27.9 0.0 collective-permute-done.9.refs_1_
  28.0 2.9 %collective-permute-done.10.refs_0_ = bf16[24,7168]{1,0:T(8,128)(2,1)S(1)} collective-permute-done((bf16[24,7168]{1,0:T(8,128)(2,1)S(1)}, bf16[24,7168]{1,0:T(8,128)(2,1)S(1)}, u32[]{:S(2)}, u32[]{:S(2)}) %collective-permute-start.10) | collective-permute-done | bytes 344096 | tf_op jit(solution)/shard_map/ppermute | solution.py:23
  30.9 0.1 collective-permute-start.11
  31.0 0.5 collective-permute-start.12
  31.5 1.3 %collective-permute-done.12.refs_3_ = bf16[8,7168]{1,0:T(8,128)(2,1)S(1)} collective-permute-done((bf16[8,7168]{1,0:T(8,128)(2,1)S(1)}, bf16[8,7168]{1,0:T(8,128)(2,1)S(1)}, u32[]{:S(2)}, u32[]{:S(2)}) %collective-permute-start.12) | collective-permute-done | bytes 114720 | tf_op jit(solution)/shard_map/ppermute | solution.py:23
  32.8 0.0 collective-permute-done.11.refs_2_
  32.8 2.1 %experts.3 = (bf16[16,7168]{1,0:T(8,128)(2,1)S(1)}, bf16[16,7168]{1,0:T(8,128)(2,1)S(1)}, bf16[16,7168]{1,0:T(8,128)(2,1)S(1)}, bf16[16,7168]{1,0:T(8,128)(2,1)S(1)}, f32[8,128]{1,0:T(8,128)S(1)}) custom-call(bf16[24,7168]{1,0:T(8,128)(2,1)S(1)} %join.5.refs_0_, bf16[8,7168]{1,0:T(8,128)(2,1)S(1)} %collective-permute-done.7.refs_5_.refs_4_.refs_1_, ...), custom_call_target="tpu_custom_call" | custom-call | tf_op jit(solution)/shard_map/experts/pallas_call | solution.py:147
  35.0 0.2 collective-permute-start.13
  35.2 0.4 collective-permute-start.19
  35.6 0.1 collective-permute-start.18
  35.7 0.8 %collective-permute-done.13.refs_1_ = bf16[16,7168]{1,0:T(8,128)(2,1)S(1)} collective-permute-done((bf16[16,7168]{1,0:T(8,128)(2,1)S(1)}, bf16[16,7168]{1,0:T(8,128)(2,1)S(1)}, u32[]{:S(2)}, u32[]{:S(2)}) %collective-permute-start.13) | collective-permute-done | bytes 229408 | tf_op jit(solution)/shard_map/ppermute | solution.py:23
  36.5 0.1 add.8
  36.6 1.5 %collective-permute-start.14 = (bf16[8,7168]{1,0:T(8,128)(2,1)S(1)}, bf16[8,7168]{1,0:T(8,128)(2,1)S(1)}, u32[]{:S(2)}, u32[]{:S(2)}) collective-permute-start(bf16[8,7168]{1,0:T(8,128)(2,1)S(1)} %get-tuple-element.54), channel_id=1, source_target_pairs={{0,2},{1,3},{2,0},{3,1},{4,6},{5,7},{6,4},{7,5},{8,10},{9,11},{10,... | collective-permute-start | bytes 344072 | tf_op jit(solution)/shard_map/ppermute | solution.py:23
  38.2 0.5 collective-permute-start.16
  38.7 0.0 collective-permute-done.19.refs_1_
  38.7 0.1 add.12
  38.8 1.5 %collective-permute-start.20 = (bf16[8,7168]{1,0:T(8,128)(2,1)S(1)}, bf16[8,7168]{1,0:T(8,128)(2,1)S(1)}, u32[]{:S(2)}, u32[]{:S(2)}) collective-permute-start(bf16[8,7168]{1,0:T(8,128)(2,1)S(1)} %get-tuple-element.63), channel_id=1, source_target_pairs={{0,2},{1,3},{2,0},{3,1},{4,6},{5,7},{6,4},{7,5},{8,10},{9,11},{10,... | collective-permute-start | bytes 344072 | tf_op jit(solution)/shard_map/ppermute | solution.py:23
  40.3 0.0 collective-permute-done.18.refs_1_
  40.4 0.7 %collective-permute-start.22 = (bf16[8,7168]{1,0:T(8,128)(2,1)S(1)}, bf16[8,7168]{1,0:T(8,128)(2,1)S(1)}, u32[]{:S(2)}, u32[]{:S(2)}) collective-permute-start(bf16[8,7168]{1,0:T(8,128)(2,1)S(1)} %convert_element_type.3), channel_id=1, source_target_pairs={{0,0},{1,5},{2,2},{3,7},{4,4},{5,1},{6,6},{7,3},{8,8},{9,13},{10,1... | collective-permute-start | bytes 344072 | tf_op jit(solution)/shard_map/ppermute | solution.py:23
  41.1 0.6 %collective-permute-start.23 = (bf16[8,7168]{1,0:T(8,128)(2,1)S(1)}, bf16[8,7168]{1,0:T(8,128)(2,1)S(1)}, u32[]{:S(2)}, u32[]{:S(2)}) collective-permute-start(bf16[8,7168]{1,0:T(8,128)(2,1)S(1)} %get-tuple-element.65), channel_id=1, source_target_pairs={{0,2},{1,7},{2,0},{3,5},{4,6},{5,3},{6,4},{7,1},{8,10},{9,15},{10,... | collective-permute-start | bytes 344072 | tf_op jit(solution)/shard_map/ppermute | solution.py:23
  41.7 1.0 %collective-permute-done.14.refs_1_ = bf16[8,7168]{1,0:T(8,128)(2,1)S(1)} collective-permute-done((bf16[8,7168]{1,0:T(8,128)(2,1)S(1)}, bf16[8,7168]{1,0:T(8,128)(2,1)S(1)}, u32[]{:S(2)}, u32[]{:S(2)}) %collective-permute-start.14) | collective-permute-done | bytes 114720 | tf_op jit(solution)/shard_map/ppermute | solution.py:23
  42.7 4.2 %collective-permute-start.15 = (bf16[8,7168]{1,0:T(8,128)(2,1)S(1)}, bf16[8,7168]{1,0:T(8,128)(2,1)S(1)}, u32[]{:S(2)}, u32[]{:S(2)}) collective-permute-start(bf16[8,7168]{1,0:T(8,128)(2,1)S(1)} %add.9.refs_2_), channel_id=1, source_target_pairs={{0,28},{1,25},{2,30},{3,27},{4,24},{5,29},{6,26},{7,31},{8,20},{9,... | collective-permute-start | bytes 344072 | tf_op jit(solution)/shard_map/ppermute | solution.py:23
  46.8 0.0 collective-permute-done.16.refs_1_
  46.9 0.5 collective-permute-start.17
  47.3 0.2 collective-permute-done.20.refs_1_
  47.6 2.4 %collective-permute-start.21 = (bf16[8,7168]{1,0:T(8,128)(2,1)S(1)}, bf16[8,7168]{1,0:T(8,128)(2,1)S(1)}, u32[]{:S(2)}, u32[]{:S(2)}) collective-permute-start(bf16[8,7168]{1,0:T(8,128)(2,1)S(1)} %add.13), channel_id=1, source_target_pairs={{0,12},{1,9},{2,14},{3,11},{4,8},{5,13},{6,10},{7,15},{8,4},{9,1},... | collective-permute-start | bytes 344072 | tf_op jit(solution)/shard_map/ppermute | solution.py:23
  50.0 1.5 %collective-permute-done.15.refs_0_ = bf16[8,7168]{1,0:T(8,128)(2,1)S(1)} collective-permute-done((bf16[8,7168]{1,0:T(8,128)(2,1)S(1)}, bf16[8,7168]{1,0:T(8,128)(2,1)S(1)}, u32[]{:S(2)}, u32[]{:S(2)}) %collective-permute-start.15) | collective-permute-done | bytes 114720 | tf_op jit(solution)/shard_map/ppermute | solution.py:23
  51.5 4.8 %collective-permute-done.17.refs_1_ = bf16[8,7168]{1,0:T(8,128)(2,1)S(1)} collective-permute-done((bf16[8,7168]{1,0:T(8,128)(2,1)S(1)}, bf16[8,7168]{1,0:T(8,128)(2,1)S(1)}, u32[]{:S(2)}, u32[]{:S(2)}) %collective-permute-start.17) | collective-permute-done | bytes 114720 | tf_op jit(solution)/shard_map/ppermute | solution.py:23
  56.3 0.3 combine.2.first_ref
  56.6 0.0 collective-permute-done.22.refs_1_
  56.6 0.0 collective-permute-done.23.refs_2_
  56.6 0.0 collective-permute-done.21.refs_0_
  56.6 0.3 combine.3
  56.9 0.1 collective-permute-start.24
  57.0 1.3 %collective-permute-done.24.received_ref = bf16[8,7168]{1,0:T(8,128)(2,1)S(1)} collective-permute-done((bf16[8,7168]{1,0:T(8,128)(2,1)S(1)}, bf16[8,7168]{1,0:T(8,128)(2,1)S(1)}, u32[]{:S(2)}, u32[]{:S(2)}) %collective-permute-start.24) | collective-permute-done | bytes 114720 | tf_op jit(solution)/shard_map/ppermute | solution.py:23
  58.3 0.7 %finish.1 = bf16[2,4,7168]{2,1,0:T(4,128)(2,1)} custom-call(f32[8,7168]{1,0:T(8,128)S(1)} %get-tuple-element.66.own_ref, bf16[8,7168]{1,0:T(8,128)(2,1)S(1)} %collective-permute-done.24.received_ref), custom_call_target="tpu_custom_call" | custom-call | tf_op jit(solution)/shard_map/finish/pallas_call | solution.py:411
  (22 shorter events, 0.3 us)
Async XLA Ops:
  0.6 2.2 %collective-permute-start.2 = (bf16[2,4,7168]{2,1,0:T(4,128)(2,1)}, bf16[2,4,7168]{2,1,0:T(4,128)(2,1)}, u32[]{:S(2)}, u32[]{:S(2)}) collective-permute-start(bf16[2,4,7168]{2,1,0:T(4,128)(2,1)} %raw_ref.1), channel_id=1, source_target_pairs={{0,1},{1,0},{2,3},{3,2},{4,5},{5,4},{6,7},{7,6},{8,9},{9,8},{10,11... | collective-permute-start | bytes 344072 | tf_op jit(solution)/shard_map/ppermute | solution.py:23
  1.1 1.5 %collective-permute-start = (s32[2,2,4]{2,1,0:T(2,128)}, s32[2,2,4]{2,1,0:T(2,128)}, u32[]{:S(2)}, u32[]{:S(2)}) collective-permute-start(s32[2,2,4]{2,1,0:T(2,128)} %bitcast.7), channel_id=1, source_target_pairs={{0,1},{1,0},{2,3},{3,2},{4,5},{5,4},{6,7},{7,6},{8,9},{9,8},{10,11... | collective-permute-start | bytes 200 | tf_op jit(solution)/shard_map/ppermute | solution.py:23
  1.2 1.6 %collective-permute-start.1 = (s32[2,2,4]{2,1,0:T(2,128)}, s32[2,2,4]{2,1,0:T(2,128)}, u32[]{:S(2)}, u32[]{:S(2)}) collective-permute-start(s32[2,2,4]{2,1,0:T(2,128)} %bitcast.9), channel_id=1, source_target_pairs={{0,1},{1,0},{2,3},{3,2},{4,5},{5,4},{6,7},{7,6},{8,9},{9,8},{10,11... | collective-permute-start | bytes 200 | tf_op jit(solution)/shard_map/ppermute | solution.py:23
  5.1 14.6 %collective-permute-start.3 = (bf16[8,7168]{1,0:T(8,128)(2,1)}, bf16[8,7168]{1,0:T(8,128)(2,1)S(1)}, u32[]{:S(2)}, u32[]{:S(2)}) collective-permute-start(bf16[8,7168]{1,0:T(8,128)(2,1)} %get-tuple-element.39), channel_id=1, source_target_pairs={{0,28},{1,25},{2,30},{3,27},{4,24},{5,29},{6,26},{7,31},{8,20},{9,... | collective-permute-start | bytes 344072 | tf_op jit(solution)/shard_map/ppermute | solution.py:23
  11.0 9.3 %collective-permute-start.4 = (bf16[8,7168]{1,0:T(8,128)(2,1)}, bf16[8,7168]{1,0:T(8,128)(2,1)S(1)}, u32[]{:S(2)}, u32[]{:S(2)}) collective-permute-start(bf16[8,7168]{1,0:T(8,128)(2,1)} %get-tuple-element.40), channel_id=1, source_target_pairs={{0,16},{1,21},{2,18},{3,23},{4,20},{5,17},{6,22},{7,19},{8,24},{9,... | collective-permute-start | bytes 344072 | tf_op jit(solution)/shard_map/ppermute | solution.py:23
  11.0 9.3 %collective-permute-start.5 = (bf16[8,7168]{1,0:T(8,128)(2,1)}, bf16[8,7168]{1,0:T(8,128)(2,1)S(1)}, u32[]{:S(2)}, u32[]{:S(2)}) collective-permute-start(bf16[8,7168]{1,0:T(8,128)(2,1)} %get-tuple-element.41), channel_id=1, source_target_pairs={{0,12},{1,9},{2,14},{3,11},{4,8},{5,13},{6,10},{7,15},{8,4},{9,1},... | collective-permute-start | bytes 344072 | tf_op jit(solution)/shard_map/ppermute | solution.py:23
  11.6 8.7 %collective-permute-start.7 = (bf16[8,7168]{1,0:T(8,128)(2,1)}, bf16[8,7168]{1,0:T(8,128)(2,1)S(1)}, u32[]{:S(2)}, u32[]{:S(2)}) collective-permute-start(bf16[8,7168]{1,0:T(8,128)(2,1)} %get-tuple-element.42), channel_id=1, source_target_pairs={{0,2},{1,7},{2,0},{3,5},{4,6},{5,3},{6,4},{7,1},{8,10},{9,15},{10,... | collective-permute-start | bytes 344072 | tf_op jit(solution)/shard_map/ppermute | solution.py:23
  13.2 7.1 %collective-permute-start.6 = (bf16[8,7168]{1,0:T(8,128)(2,1)}, bf16[8,7168]{1,0:T(8,128)(2,1)S(1)}, u32[]{:S(2)}, u32[]{:S(2)}) collective-permute-start(bf16[8,7168]{1,0:T(8,128)(2,1)} %get-tuple-element.42), channel_id=1, source_target_pairs={{0,0},{1,5},{2,2},{3,7},{4,4},{5,1},{6,6},{7,3},{8,8},{9,13},{10,1... | collective-permute-start | bytes 344072 | tf_op jit(solution)/shard_map/ppermute | solution.py:23
  14.7 0.8 %copy-start.3 = (f32[2,32,16]{2,1,0:T(8,128)S(1)}, f32[2,32,16]{2,1,0:T(8,128)}, u32[]{:S(2)}) copy-start(f32[2,32,16]{2,1,0:T(8,128)} %get-tuple-element.37.place_ref._) | copy-start | bytes 12292
  20.3 1.9 %collective-permute-start.8 = (bf16[32,7168]{1,0:T(8,128)(2,1)S(1)}, bf16[32,7168]{1,0:T(8,128)(2,1)S(1)}, u32[]{:S(2)}, u32[]{:S(2)}) collective-permute-start(bf16[32,7168]{1,0:T(8,128)(2,1)S(1)} %join.3.refs_0_), channel_id=1, source_target_pairs={{0,1},{1,0},{2,3},{3,2},{4,5},{5,4},{6,7},{7,6},{8,9},{9,8},{10,11... | collective-permute-start | bytes 1376264 | tf_op jit(solution)/shard_map/ppermute | solution.py:23
  20.7 10.3 %collective-permute-start.10 = (bf16[24,7168]{1,0:T(8,128)(2,1)S(1)}, bf16[24,7168]{1,0:T(8,128)(2,1)S(1)}, u32[]{:S(2)}, u32[]{:S(2)}) collective-permute-start(bf16[24,7168]{1,0:T(8,128)(2,1)S(1)} %join.4), channel_id=1, source_target_pairs={{0,2},{1,3},{2,0},{3,1},{4,6},{5,7},{6,4},{7,5},{8,10},{9,11},{10,... | collective-permute-start | bytes 1032200 | tf_op jit(solution)/shard_map/ppermute | solution.py:23
  22.2 2.5 %copy-start = (bf16[2,4,64,576]{3,2,1,0:T(8,128)(2,1)S(1)}, bf16[2,4,64,576]{3,2,1,0:T(8,128)(2,1)}, u32[]{:S(2)}) copy-start(bf16[2,4,64,576]{3,2,1,0:T(8,128)(2,1)} %query_ref.1) | copy-start | bytes 1769476
  22.2 2.5 %copy-start.1 = (bf16[4,64,576]{2,1,0:T(8,128)(2,1)S(1)}, bf16[4,64,576]{2,1,0:T(8,128)(2,1)}, u32[]{:S(2)}) copy-start(bf16[4,64,576]{2,1,0:T(8,128)(2,1)} %cache_ref.1) | copy-start | bytes 884740
  22.2 2.5 %copy-start.5 = (bf16[2,4,576]{2,1,0:T(4,128)(2,1)S(1)}, bf16[2,4,576]{2,1,0:T(4,128)(2,1)}, u32[]{:S(2)}) copy-start(bf16[2,4,576]{2,1,0:T(4,128)(2,1)} %fresh_ref.1) | copy-start | bytes 27652
  22.2 2.5 %copy-start.7 = (s32[4]{0:T(128)S(1)}, s32[4]{0:T(128)}, u32[]{:S(2)}) copy-start(s32[4]{0:T(128)} %lengths_ref.1) | copy-start | bytes 52
  22.2 5.5 %copy-start.2 = (bf16[16,7168]{1,0:T(8,128)(2,1)S(1)}, bf16[16,7168]{1,0:T(8,128)(2,1)}, u32[]{:S(2)}) copy-start(bf16[16,7168]{1,0:T(8,128)(2,1)} %get-tuple-element.36.normed_ref) | copy-start | bytes 688132
  22.2 5.5 %copy-start.4 = (bf16[7168,6]{0,1:T(8,128)(2,1)S(1)}, bf16[7168,6]{0,1:T(8,128)(2,1)}, u32[]{:S(2)}) copy-start(bf16[7168,6]{0,1:T(8,128)(2,1)} %param.15) | copy-start | bytes 258052
  22.2 5.5 %copy-start.6 = (f32[2,6,16]{2,1,0:T(8,128)S(1)}, f32[2,6,16]{2,1,0:T(8,128)}, u32[]{:S(2)}) copy-start(f32[2,6,16]{2,1,0:T(8,128)} %get-tuple-element.38.choose_ref) | copy-start | bytes 2308
  24.4 3.6 %collective-permute-start.9 = (bf16[16,7168]{1,0:T(8,128)(2,1)S(1)}, bf16[16,7168]{1,0:T(8,128)(2,1)S(1)}, u32[]{:S(2)}, u32[]{:S(2)}) collective-permute-start(bf16[16,7168]{1,0:T(8,128)(2,1)S(1)} %get-tuple-element.48), channel_id=1, source_target_pairs={{0,1},{1,0},{2,3},{3,2},{4,5},{5,4},{6,7},{7,6},{8,9},{9,8},{10,11... | collective-permute-start | bytes 688136 | tf_op jit(solution)/shard_map/ppermute | solution.py:23
  30.9 1.9 %collective-permute-start.11 = (bf16[24,7168]{1,0:T(8,128)(2,1)S(1)}, bf16[24,7168]{1,0:T(8,128)(2,1)S(1)}, u32[]{:S(2)}, u32[]{:S(2)}) collective-permute-start(bf16[24,7168]{1,0:T(8,128)(2,1)S(1)} %join.5.refs_0_), channel_id=1, source_target_pairs={{0,1},{1,0},{2,3},{3,2},{4,5},{5,4},{6,7},{7,6},{8,9},{9,8},{10,11... | collective-permute-start | bytes 1032200 | tf_op jit(solution)/shard_map/ppermute | solution.py:23
  31.0 1.8 %collective-permute-start.12 = (bf16[8,7168]{1,0:T(8,128)(2,1)S(1)}, bf16[8,7168]{1,0:T(8,128)(2,1)S(1)}, u32[]{:S(2)}, u32[]{:S(2)}) collective-permute-start(bf16[8,7168]{1,0:T(8,128)(2,1)S(1)} %collective-permute-done.7.refs_5_.refs_4_.refs_1_), channel_id=1, source_target_pairs={{0,1},{1,0},{2,3},{3,2},{4,5},{5,4},{6,7},{7,6},{8,9},{9,8},{10,11... | collective-permute-start | bytes 344072 | tf_op jit(solution)/shard_map/ppermute | solution.py:23
  35.0 1.6 %collective-permute-start.13 = (bf16[16,7168]{1,0:T(8,128)(2,1)S(1)}, bf16[16,7168]{1,0:T(8,128)(2,1)S(1)}, u32[]{:S(2)}, u32[]{:S(2)}) collective-permute-start(bf16[16,7168]{1,0:T(8,128)(2,1)S(1)} %get-tuple-element.53), channel_id=1, source_target_pairs={{0,1},{1,0},{2,3},{3,2},{4,5},{5,4},{6,7},{7,6},{8,9},{9,8},{10,11... | collective-permute-start | bytes 688136 | tf_op jit(solution)/shard_map/ppermute | solution.py:23
  35.2 3.5 %collective-permute-start.19 = (bf16[16,7168]{1,0:T(8,128)(2,1)S(1)}, bf16[16,7168]{1,0:T(8,128)(2,1)S(1)}, u32[]{:S(2)}, u32[]{:S(2)}) collective-permute-start(bf16[16,7168]{1,0:T(8,128)(2,1)S(1)} %get-tuple-element.62), channel_id=1, source_target_pairs={{0,1},{1,0},{2,3},{3,2},{4,5},{5,4},{6,7},{7,6},{8,9},{9,8},{10,11... | collective-permute-start | bytes 688136 | tf_op jit(solution)/shard_map/ppermute | solution.py:23
  35.6 4.7 %collective-permute-start.18 = (bf16[16,7168]{1,0:T(8,128)(2,1)S(1)}, bf16[16,7168]{1,0:T(8,128)(2,1)S(1)}, u32[]{:S(2)}, u32[]{:S(2)}) collective-permute-start(bf16[16,7168]{1,0:T(8,128)(2,1)S(1)} %get-tuple-element.59), channel_id=1, source_target_pairs={{0,1},{1,0},{2,3},{3,2},{4,5},{5,4},{6,7},{7,6},{8,9},{9,8},{10,11... | collective-permute-start | bytes 688136 | tf_op jit(solution)/shard_map/ppermute | solution.py:23
  36.6 6.1 %collective-permute-start.14 = (bf16[8,7168]{1,0:T(8,128)(2,1)S(1)}, bf16[8,7168]{1,0:T(8,128)(2,1)S(1)}, u32[]{:S(2)}, u32[]{:S(2)}) collective-permute-start(bf16[8,7168]{1,0:T(8,128)(2,1)S(1)} %get-tuple-element.54), channel_id=1, source_target_pairs={{0,2},{1,3},{2,0},{3,1},{4,6},{5,7},{6,4},{7,5},{8,10},{9,11},{10,... | collective-permute-start | bytes 344072 | tf_op jit(solution)/shard_map/ppermute | solution.py:23
  38.2 8.7 %collective-permute-start.16 = (bf16[8,7168]{1,0:T(8,128)(2,1)S(1)}, bf16[8,7168]{1,0:T(8,128)(2,1)S(1)}, u32[]{:S(2)}, u32[]{:S(2)}) collective-permute-start(bf16[8,7168]{1,0:T(8,128)(2,1)S(1)} %get-tuple-element.57), channel_id=1, source_target_pairs={{0,2},{1,3},{2,0},{3,1},{4,6},{5,7},{6,4},{7,5},{8,10},{9,11},{10,... | collective-permute-start | bytes 344072 | tf_op jit(solution)/shard_map/ppermute | solution.py:23
  38.8 8.8 %collective-permute-start.20 = (bf16[8,7168]{1,0:T(8,128)(2,1)S(1)}, bf16[8,7168]{1,0:T(8,128)(2,1)S(1)}, u32[]{:S(2)}, u32[]{:S(2)}) collective-permute-start(bf16[8,7168]{1,0:T(8,128)(2,1)S(1)} %get-tuple-element.63), channel_id=1, source_target_pairs={{0,2},{1,3},{2,0},{3,1},{4,6},{5,7},{6,4},{7,5},{8,10},{9,11},{10,... | collective-permute-start | bytes 344072 | tf_op jit(solution)/shard_map/ppermute | solution.py:23
  40.4 16.2 %collective-permute-start.22 = (bf16[8,7168]{1,0:T(8,128)(2,1)S(1)}, bf16[8,7168]{1,0:T(8,128)(2,1)S(1)}, u32[]{:S(2)}, u32[]{:S(2)}) collective-permute-start(bf16[8,7168]{1,0:T(8,128)(2,1)S(1)} %convert_element_type.3), channel_id=1, source_target_pairs={{0,0},{1,5},{2,2},{3,7},{4,4},{5,1},{6,6},{7,3},{8,8},{9,13},{10,1... | collective-permute-start | bytes 344072 | tf_op jit(solution)/shard_map/ppermute | solution.py:23
  41.1 15.5 %collective-permute-start.23 = (bf16[8,7168]{1,0:T(8,128)(2,1)S(1)}, bf16[8,7168]{1,0:T(8,128)(2,1)S(1)}, u32[]{:S(2)}, u32[]{:S(2)}) collective-permute-start(bf16[8,7168]{1,0:T(8,128)(2,1)S(1)} %get-tuple-element.65), channel_id=1, source_target_pairs={{0,2},{1,7},{2,0},{3,5},{4,6},{5,3},{6,4},{7,1},{8,10},{9,15},{10,... | collective-permute-start | bytes 344072 | tf_op jit(solution)/shard_map/ppermute | solution.py:23
  42.7 8.8 %collective-permute-start.15 = (bf16[8,7168]{1,0:T(8,128)(2,1)S(1)}, bf16[8,7168]{1,0:T(8,128)(2,1)S(1)}, u32[]{:S(2)}, u32[]{:S(2)}) collective-permute-start(bf16[8,7168]{1,0:T(8,128)(2,1)S(1)} %add.9.refs_2_), channel_id=1, source_target_pairs={{0,28},{1,25},{2,30},{3,27},{4,24},{5,29},{6,26},{7,31},{8,20},{9,... | collective-permute-start | bytes 344072 | tf_op jit(solution)/shard_map/ppermute | solution.py:23
  46.9 9.4 %collective-permute-start.17 = (bf16[8,7168]{1,0:T(8,128)(2,1)S(1)}, bf16[8,7168]{1,0:T(8,128)(2,1)S(1)}, u32[]{:S(2)}, u32[]{:S(2)}) collective-permute-start(bf16[8,7168]{1,0:T(8,128)(2,1)S(1)} %add.10.refs_2_), channel_id=1, source_target_pairs={{0,16},{1,21},{2,18},{3,23},{4,20},{5,17},{6,22},{7,19},{8,24},{9,... | collective-permute-start | bytes 344072 | tf_op jit(solution)/shard_map/ppermute | solution.py:23
  47.6 9.0 %collective-permute-start.21 = (bf16[8,7168]{1,0:T(8,128)(2,1)S(1)}, bf16[8,7168]{1,0:T(8,128)(2,1)S(1)}, u32[]{:S(2)}, u32[]{:S(2)}) collective-permute-start(bf16[8,7168]{1,0:T(8,128)(2,1)S(1)} %add.13), channel_id=1, source_target_pairs={{0,12},{1,9},{2,14},{3,11},{4,8},{5,13},{6,10},{7,15},{8,4},{9,1},... | collective-permute-start | bytes 344072 | tf_op jit(solution)/shard_map/ppermute | solution.py:23
  56.9 1.4 %collective-permute-start.24 = (bf16[8,7168]{1,0:T(8,128)(2,1)S(1)}, bf16[8,7168]{1,0:T(8,128)(2,1)S(1)}, u32[]{:S(2)}, u32[]{:S(2)}) collective-permute-start(bf16[8,7168]{1,0:T(8,128)(2,1)S(1)} %get-tuple-element.67), channel_id=1, source_target_pairs={{0,1},{1,0},{2,3},{3,2},{4,5},{5,4},{6,7},{7,6},{8,9},{9,8},{10,11... | collective-permute-start | bytes 344072 | tf_op jit(solution)/shard_map/ppermute | solution.py:23

commit v10 on v8

--- a/solution.py
+++ b/solution.py
@@ -14,7 +14,7 @@
 routed_scale = 2.5
 norm_eps = 1e-06
 masked_score = -1e30
-EXPERT_PARTS = 7
+EXPERT_PARTS = 4
 MARK = jax.ShapeDtypeStruct((8, 128), jnp.float32)
 
 

time: 59.4 us -> 59.4 us (level)
  no operation moved by 1% of the time
where the time goes in v10:
time: 59.4 us; the launch traced here: 59.1 us
  starting transfers between devices  25.9 us (44%)
  waiting for transfers between devices  15.8 us (27%)
  Pallas kernels  15.7 us (26%)
  between operations  0.85 us (1%)
  local copies, waits for them, and re-layouts  0.79 us (1%)
    ppermute x25, starting transfers between devices, flipped(): return lax.ppermute(value, 'ep', pairs)  25.9 us
    ppermute x25, waiting for transfers between devices, flipped(): return lax.ppermute(value, 'ep', pairs)  15.8 us
    pallas_call x2, Pallas kernels, experts(): pl.pallas_call(functools.partial(expert_kernel, count), out_shape=[jax.Sh...  4.28 us
    pallas_call x1, Pallas kernels, load(): pl.pallas_call(load_kernel, out_shape=[jax.ShapeDtypeStruct(w.shape, w.dt...  4.23 us
    pallas_call x1, Pallas kernels, attend(): pl.pallas_call(attend_kernel, out_shape=[jax.ShapeDtypeStruct((steps, tok...  2.97 us
    pallas_call x1, Pallas kernels, pack(): pl.pallas_call(functools.partial(pack_kernel, slots, deltas), out_shape=[...  2.25 us
  transfers between devices with their start and end apart: 25, of which 12 were waited for; matrix products, arithmetic and copies ran while one was open for 0% of the time, Pallas kernels for 17%

profile of v10, /device:TPU:0, one launch (start us, length us, event | category | flops | bytes accessed | tf_op | source)
XLA Modules:
  0.0 59.1 jit_solution(2046194702030981250)
XLA Ops:
  0.6 0.5 collective-permute-start.2
  1.1 0.1 collective-permute-start
  1.2 0.4 collective-permute-start.1
  1.7 1.0 %collective-permute-done.other_ids_ref = s32[2,2,4]{2,1,0:T(2,128)} collective-permute-done((s32[2,2,4]{2,1,0:T(2,128)}, s32[2,2,4]{2,1,0:T(2,128)}, u32[]{:S(2)}, u32[]{:S(2)}) %collective-permute-start) | collective-permute-done | bytes 96 | tf_op jit(solution)/shard_map/ppermute | solution.py:23
  2.6 0.2 collective-permute-done.1.other_replica_ref
  2.8 0.0 collective-permute-done.2.other_ref
  2.8 2.3 %pack.1 = (bf16[16,7168]{1,0:T(8,128)(2,1)}, f32[2,32,16]{2,1,0:T(8,128)}, f32[2,6,16]{2,1,0:T(8,128)}, bf16[8,7168]{1,0:T(8,128)(2,1)}, bf16[8,7168]{1,0:T(8,12...) custom-call(s32[2,6]{1,0:T(2,128)} %bitcast.11, s32[2,2,4]{2,1,0:T(2,128)} %bitcast.8, s32[2,2,4]{2,1,0:T(2,128)} %bitcast.10, ...), custom_call_target="tpu_custom_call" | custom-call | tf_op jit(solution)/shard_map/pack/pallas_call | solution.py:295
  5.1 5.9 %collective-permute-start.3 = (bf16[8,7168]{1,0:T(8,128)(2,1)}, bf16[8,7168]{1,0:T(8,128)(2,1)S(1)}, u32[]{:S(2)}, u32[]{:S(2)}) collective-permute-start(bf16[8,7168]{1,0:T(8,128)(2,1)} %get-tuple-element.39), channel_id=1, source_target_pairs={{0,28},{1,25},{2,30},{3,27},{4,24},{5,29},{6,26},{7,31},{8,20},{9,... | collective-permute-start | bytes 344072 | tf_op jit(solution)/shard_map/ppermute | solution.py:23
  11.0 0.0 collective-permute-start.4
  11.0 0.6 %collective-permute-start.5 = (bf16[8,7168]{1,0:T(8,128)(2,1)}, bf16[8,7168]{1,0:T(8,128)(2,1)S(1)}, u32[]{:S(2)}, u32[]{:S(2)}) collective-permute-start(bf16[8,7168]{1,0:T(8,128)(2,1)} %get-tuple-element.41), channel_id=1, source_target_pairs={{0,12},{1,9},{2,14},{3,11},{4,8},{5,13},{6,10},{7,15},{8,4},{9,1},... | collective-permute-start | bytes 344072 | tf_op jit(solution)/shard_map/ppermute | solution.py:23
  11.6 1.6 %collective-permute-start.7 = (bf16[8,7168]{1,0:T(8,128)(2,1)}, bf16[8,7168]{1,0:T(8,128)(2,1)S(1)}, u32[]{:S(2)}, u32[]{:S(2)}) collective-permute-start(bf16[8,7168]{1,0:T(8,128)(2,1)} %get-tuple-element.42), channel_id=1, source_target_pairs={{0,2},{1,7},{2,0},{3,5},{4,6},{5,3},{6,4},{7,1},{8,10},{9,15},{10,... | collective-permute-start | bytes 344072 | tf_op jit(solution)/shard_map/ppermute | solution.py:23
  13.2 1.5 %collective-permute-start.6 = (bf16[8,7168]{1,0:T(8,128)(2,1)}, bf16[8,7168]{1,0:T(8,128)(2,1)S(1)}, u32[]{:S(2)}, u32[]{:S(2)}) collective-permute-start(bf16[8,7168]{1,0:T(8,128)(2,1)} %get-tuple-element.42), channel_id=1, source_target_pairs={{0,0},{1,5},{2,2},{3,7},{4,4},{5,1},{6,6},{7,3},{8,8},{9,13},{10,1... | collective-permute-start | bytes 344072 | tf_op jit(solution)/shard_map/ppermute | solution.py:23
  14.7 0.8 %copy-done.3 = f32[2,32,16]{2,1,0:T(8,128)S(1)} copy-done((f32[2,32,16]{2,1,0:T(8,128)S(1)}, f32[2,32,16]{2,1,0:T(8,128)}, u32[]{:S(2)}) %copy-start.3) | copy-done | bytes 4120
  15.5 4.2 %load.1 = (bf16[7168,256]{1,0:T(8,128)(2,1)S(1)}, bf16[7168,256]{1,0:T(8,128)(2,1)S(1)}, bf16[256,7168]{1,0:T(8,128)(2,1)S(1)}, f32[8,128]{1,0:T(8,128)S(1)}) custom-call(bf16[7168,256]{1,0:T(8,128)(2,1)} %gate_ref.1, bf16[7168,256]{1,0:T(8,128)(2,1)} %up_ref.1, bf16[256,7168]{1,0:T(8,128)(2,1)} %down_ref.1, f32[2,32,16]{2,1,0:T(8,128)S(1)} %copy-done.3), custom_call_target="tpu_custom_call" | custom-call | tf_op jit(solution)/shard_map/load/pallas_call | solution.py:108
  19.7 0.0 collective-permute-done.3.refs_0_
  19.7 0.5 collective-permute-done.4.refs_1_
  20.2 0.0 collective-permute-done.5.refs_2_
  20.2 0.0 collective-permute-done.7.refs_5_.refs_4_.refs_1_
  20.2 0.0 collective-permute-done.6.refs_3_
  20.3 0.4 collective-permute-start.8
  20.7 1.3 %collective-permute-start.10 = (bf16[24,7168]{1,0:T(8,128)(2,1)S(1)}, bf16[24,7168]{1,0:T(8,128)(2,1)S(1)}, u32[]{:S(2)}, u32[]{:S(2)}) collective-permute-start(bf16[24,7168]{1,0:T(8,128)(2,1)S(1)} %join.4), channel_id=1, source_target_pairs={{0,2},{1,3},{2,0},{3,1},{4,6},{5,7},{6,4},{7,5},{8,10},{9,11},{10,... | collective-permute-start | bytes 1032200 | tf_op jit(solution)/shard_map/ppermute | solution.py:23
  22.0 0.2 collective-permute-done.8.refs_1_
  22.2 0.0 copy-start.2
  22.2 0.0 copy-start.4
  22.2 2.1 %experts.2 = (bf16[16,7168]{1,0:T(8,128)(2,1)S(1)}, bf16[16,7168]{1,0:T(8,128)(2,1)S(1)}, bf16[16,7168]{1,0:T(8,128)(2,1)S(1)}, bf16[16,7168]{1,0:T(8,128)(2,1)S(1)}, f32[8,128]{1,0:T(8,128)S(1)}) custom-call(bf16[32,7168]{1,0:T(8,128)(2,1)S(1)} %join.3.refs_0_, bf16[32,7168]{1,0:T(8,128)(2,1)S(1)} %collective-permute-done.8.refs_1_, ...), custom_call_target="tpu_custom_call" | custom-call | tf_op jit(solution)/shard_map/experts/pallas_call | solution.py:147
  24.4 0.4 collective-permute-start.9
  24.7 3.0 %attention.1 = (bf16[2,4,64,512]{3,2,1,0:T(8,128)(2,1)}, f32[8,128]{1,0:T(8,128)S(1)}) custom-call(s32[4]{0:T(128)S(1)} %copy-done.7, bf16[2,4,64,576]{3,2,1,0:T(8,128)(2,1)S(1)} %copy-done, bf16[4,64,576]{2,1,0:T(8,128)(2,1)S(1)} %copy-done.1, bf16[2,4,576]{2,1,0:T(4,128)(2,1)S(1)} %copy-done.5), custom_call_target="tpu_custom_call" | custom-call | flops 150994944 | bytes 1474560 | tf_op jit(solution)/shard_map/attention/pallas_call | solution.py:76
  27.7 0.2 weigh.1.refs_2_.weigh_ref
  27.9 0.0 collective-permute-done.9.refs_1_
  28.0 2.9 %collective-permute-done.10.refs_0_ = bf16[24,7168]{1,0:T(8,128)(2,1)S(1)} collective-permute-done((bf16[24,7168]{1,0:T(8,128)(2,1)S(1)}, bf16[24,7168]{1,0:T(8,128)(2,1)S(1)}, u32[]{:S(2)}, u32[]{:S(2)}) %collective-permute-start.10) | collective-permute-done | bytes 344096 | tf_op jit(solution)/shard_map/ppermute | solution.py:23
  30.9 0.1 collective-permute-start.11
  31.0 0.5 collective-permute-start.12
  31.5 1.3 %collective-permute-done.12.refs_3_ = bf16[8,7168]{1,0:T(8,128)(2,1)S(1)} collective-permute-done((bf16[8,7168]{1,0:T(8,128)(2,1)S(1)}, bf16[8,7168]{1,0:T(8,128)(2,1)S(1)}, u32[]{:S(2)}, u32[]{:S(2)}) %collective-permute-start.12) | collective-permute-done | bytes 114720 | tf_op jit(solution)/shard_map/ppermute | solution.py:23
  32.8 0.0 collective-permute-done.11.refs_2_
  32.8 2.1 %experts.3 = (bf16[16,7168]{1,0:T(8,128)(2,1)S(1)}, bf16[16,7168]{1,0:T(8,128)(2,1)S(1)}, bf16[16,7168]{1,0:T(8,128)(2,1)S(1)}, bf16[16,7168]{1,0:T(8,128)(2,1)S(1)}, f32[8,128]{1,0:T(8,128)S(1)}) custom-call(bf16[24,7168]{1,0:T(8,128)(2,1)S(1)} %join.5.refs_0_, bf16[8,7168]{1,0:T(8,128)(2,1)S(1)} %collective-permute-done.7.refs_5_.refs_4_.refs_1_, ...), custom_call_target="tpu_custom_call" | custom-call | tf_op jit(solution)/shard_map/experts/pallas_call | solution.py:147
  35.0 0.2 collective-permute-start.13
  35.2 0.4 collective-permute-start.19
  35.6 0.1 collective-permute-start.18
  35.7 0.8 %collective-permute-done.13.refs_1_ = bf16[16,7168]{1,0:T(8,128)(2,1)S(1)} collective-permute-done((bf16[16,7168]{1,0:T(8,128)(2,1)S(1)}, bf16[16,7168]{1,0:T(8,128)(2,1)S(1)}, u32[]{:S(2)}, u32[]{:S(2)}) %collective-permute-start.13) | collective-permute-done | bytes 229408 | tf_op jit(solution)/shard_map/ppermute | solution.py:23
  36.5 0.1 add.8
  36.6 1.5 %collective-permute-start.14 = (bf16[8,7168]{1,0:T(8,128)(2,1)S(1)}, bf16[8,7168]{1,0:T(8,128)(2,1)S(1)}, u32[]{:S(2)}, u32[]{:S(2)}) collective-permute-start(bf16[8,7168]{1,0:T(8,128)(2,1)S(1)} %get-tuple-element.54), channel_id=1, source_target_pairs={{0,2},{1,3},{2,0},{3,1},{4,6},{5,7},{6,4},{7,5},{8,10},{9,11},{10,... | collective-permute-start | bytes 344072 | tf_op jit(solution)/shard_map/ppermute | solution.py:23
  38.2 0.5 collective-permute-start.16
  38.7 0.0 collective-permute-done.19.refs_1_
  38.7 0.1 add.12
  38.8 1.5 %collective-permute-start.20 = (bf16[8,7168]{1,0:T(8,128)(2,1)S(1)}, bf16[8,7168]{1,0:T(8,128)(2,1)S(1)}, u32[]{:S(2)}, u32[]{:S(2)}) collective-permute-start(bf16[8,7168]{1,0:T(8,128)(2,1)S(1)} %get-tuple-element.63), channel_id=1, source_target_pairs={{0,2},{1,3},{2,0},{3,1},{4,6},{5,7},{6,4},{7,5},{8,10},{9,11},{10,... | collective-permute-start | bytes 344072 | tf_op jit(solution)/shard_map/ppermute | solution.py:23
  40.3 0.0 collective-permute-done.18.refs_1_
  40.4 0.7 %collective-permute-start.22 = (bf16[8,7168]{1,0:T(8,128)(2,1)S(1)}, bf16[8,7168]{1,0:T(8,128)(2,1)S(1)}, u32[]{:S(2)}, u32[]{:S(2)}) collective-permute-start(bf16[8,7168]{1,0:T(8,128)(2,1)S(1)} %convert_element_type.3), channel_id=1, source_target_pairs={{0,0},{1,5},{2,2},{3,7},{4,4},{5,1},{6,6},{7,3},{8,8},{9,13},{10,1... | collective-permute-start | bytes 344072 | tf_op jit(solution)/shard_map/ppermute | solution.py:23
  41.1 0.6 %collective-permute-start.23 = (bf16[8,7168]{1,0:T(8,128)(2,1)S(1)}, bf16[8,7168]{1,0:T(8,128)(2,1)S(1)}, u32[]{:S(2)}, u32[]{:S(2)}) collective-permute-start(bf16[8,7168]{1,0:T(8,128)(2,1)S(1)} %get-tuple-element.65), channel_id=1, source_target_pairs={{0,2},{1,7},{2,0},{3,5},{4,6},{5,3},{6,4},{7,1},{8,10},{9,15},{10,... | collective-permute-start | bytes 344072 | tf_op jit(solution)/shard_map/ppermute | solution.py:23
  41.7 1.0 %collective-permute-done.14.refs_1_ = bf16[8,7168]{1,0:T(8,128)(2,1)S(1)} collective-permute-done((bf16[8,7168]{1,0:T(8,128)(2,1)S(1)}, bf16[8,7168]{1,0:T(8,128)(2,1)S(1)}, u32[]{:S(2)}, u32[]{:S(2)}) %collective-permute-start.14) | collective-permute-done | bytes 114720 | tf_op jit(solution)/shard_map/ppermute | solution.py:23
  42.7 4.2 %collective-permute-start.15 = (bf16[8,7168]{1,0:T(8,128)(2,1)S(1)}, bf16[8,7168]{1,0:T(8,128)(2,1)S(1)}, u32[]{:S(2)}, u32[]{:S(2)}) collective-permute-start(bf16[8,7168]{1,0:T(8,128)(2,1)S(1)} %add.9.refs_2_), channel_id=1, source_target_pairs={{0,28},{1,25},{2,30},{3,27},{4,24},{5,29},{6,26},{7,31},{8,20},{9,... | collective-permute-start | bytes 344072 | tf_op jit(solution)/shard_map/ppermute | solution.py:23
  46.8 0.0 collective-permute-done.16.refs_1_
  46.9 0.5 collective-permute-start.17
  47.3 0.2 collective-permute-done.20.refs_1_
  47.6 2.4 %collective-permute-start.21 = (bf16[8,7168]{1,0:T(8,128)(2,1)S(1)}, bf16[8,7168]{1,0:T(8,128)(2,1)S(1)}, u32[]{:S(2)}, u32[]{:S(2)}) collective-permute-start(bf16[8,7168]{1,0:T(8,128)(2,1)S(1)} %add.13), channel_id=1, source_target_pairs={{0,12},{1,9},{2,14},{3,11},{4,8},{5,13},{6,10},{7,15},{8,4},{9,1},... | collective-permute-start | bytes 344072 | tf_op jit(solution)/shard_map/ppermute | solution.py:23
  50.0 1.5 %collective-permute-done.15.refs_0_ = bf16[8,7168]{1,0:T(8,128)(2,1)S(1)} collective-permute-done((bf16[8,7168]{1,0:T(8,128)(2,1)S(1)}, bf16[8,7168]{1,0:T(8,128)(2,1)S(1)}, u32[]{:S(2)}, u32[]{:S(2)}) %collective-permute-start.15) | collective-permute-done | bytes 114720 | tf_op jit(solution)/shard_map/ppermute | solution.py:23
  51.5 4.8 %collective-permute-done.17.refs_1_ = bf16[8,7168]{1,0:T(8,128)(2,1)S(1)} collective-permute-done((bf16[8,7168]{1,0:T(8,128)(2,1)S(1)}, bf16[8,7168]{1,0:T(8,128)(2,1)S(1)}, u32[]{:S(2)}, u32[]{:S(2)}) %collective-permute-start.17) | collective-permute-done | bytes 114720 | tf_op jit(solution)/shard_map/ppermute | solution.py:23
  56.3 0.4 combine.2.first_ref
  56.6 0.0 collective-permute-done.22.refs_1_
  56.7 0.0 collective-permute-done.23.refs_2_
  56.7 0.0 collective-permute-done.21.refs_0_
  56.7 0.4 combine.3
  57.1 0.1 collective-permute-start.24
  57.1 1.3 %collective-permute-done.24.received_ref = bf16[8,7168]{1,0:T(8,128)(2,1)S(1)} collective-permute-done((bf16[8,7168]{1,0:T(8,128)(2,1)S(1)}, bf16[8,7168]{1,0:T(8,128)(2,1)S(1)}, u32[]{:S(2)}, u32[]{:S(2)}) %collective-permute-start.24) | collective-permute-done | bytes 114720 | tf_op jit(solution)/shard_map/ppermute | solution.py:23
  58.5 0.7 %finish.1 = bf16[2,4,7168]{2,1,0:T(4,128)(2,1)} custom-call(f32[8,7168]{1,0:T(8,128)S(1)} %get-tuple-element.66.own_ref, bf16[8,7168]{1,0:T(8,128)(2,1)S(1)} %collective-permute-done.24.received_ref), custom_call_target="tpu_custom_call" | custom-call | tf_op jit(solution)/shard_map/finish/pallas_call | solution.py:413
  (22 shorter events, 0.3 us)
Async XLA Ops:
  0.6 2.2 %collective-permute-start.2 = (bf16[2,4,7168]{2,1,0:T(4,128)(2,1)}, bf16[2,4,7168]{2,1,0:T(4,128)(2,1)}, u32[]{:S(2)}, u32[]{:S(2)}) collective-permute-start(bf16[2,4,7168]{2,1,0:T(4,128)(2,1)} %raw_ref.1), channel_id=1, source_target_pairs={{0,1},{1,0},{2,3},{3,2},{4,5},{5,4},{6,7},{7,6},{8,9},{9,8},{10,11... | collective-permute-start | bytes 344072 | tf_op jit(solution)/shard_map/ppermute | solution.py:23
  1.1 1.5 %collective-permute-start = (s32[2,2,4]{2,1,0:T(2,128)}, s32[2,2,4]{2,1,0:T(2,128)}, u32[]{:S(2)}, u32[]{:S(2)}) collective-permute-start(s32[2,2,4]{2,1,0:T(2,128)} %bitcast.7), channel_id=1, source_target_pairs={{0,1},{1,0},{2,3},{3,2},{4,5},{5,4},{6,7},{7,6},{8,9},{9,8},{10,11... | collective-permute-start | bytes 200 | tf_op jit(solution)/shard_map/ppermute | solution.py:23
  1.2 1.6 %collective-permute-start.1 = (s32[2,2,4]{2,1,0:T(2,128)}, s32[2,2,4]{2,1,0:T(2,128)}, u32[]{:S(2)}, u32[]{:S(2)}) collective-permute-start(s32[2,2,4]{2,1,0:T(2,128)} %bitcast.9), channel_id=1, source_target_pairs={{0,1},{1,0},{2,3},{3,2},{4,5},{5,4},{6,7},{7,6},{8,9},{9,8},{10,11... | collective-permute-start | bytes 200 | tf_op jit(solution)/shard_map/ppermute | solution.py:23
  5.1 14.6 %collective-permute-start.3 = (bf16[8,7168]{1,0:T(8,128)(2,1)}, bf16[8,7168]{1,0:T(8,128)(2,1)S(1)}, u32[]{:S(2)}, u32[]{:S(2)}) collective-permute-start(bf16[8,7168]{1,0:T(8,128)(2,1)} %get-tuple-element.39), channel_id=1, source_target_pairs={{0,28},{1,25},{2,30},{3,27},{4,24},{5,29},{6,26},{7,31},{8,20},{9,... | collective-permute-start | bytes 344072 | tf_op jit(solution)/shard_map/ppermute | solution.py:23
  11.0 9.3 %collective-permute-start.4 = (bf16[8,7168]{1,0:T(8,128)(2,1)}, bf16[8,7168]{1,0:T(8,128)(2,1)S(1)}, u32[]{:S(2)}, u32[]{:S(2)}) collective-permute-start(bf16[8,7168]{1,0:T(8,128)(2,1)} %get-tuple-element.40), channel_id=1, source_target_pairs={{0,16},{1,21},{2,18},{3,23},{4,20},{5,17},{6,22},{7,19},{8,24},{9,... | collective-permute-start | bytes 344072 | tf_op jit(solution)/shard_map/ppermute | solution.py:23
  11.0 9.3 %collective-permute-start.5 = (bf16[8,7168]{1,0:T(8,128)(2,1)}, bf16[8,7168]{1,0:T(8,128)(2,1)S(1)}, u32[]{:S(2)}, u32[]{:S(2)}) collective-permute-start(bf16[8,7168]{1,0:T(8,128)(2,1)} %get-tuple-element.41), channel_id=1, source_target_pairs={{0,12},{1,9},{2,14},{3,11},{4,8},{5,13},{6,10},{7,15},{8,4},{9,1},... | collective-permute-start | bytes 344072 | tf_op jit(solution)/shard_map/ppermute | solution.py:23
  11.6 8.7 %collective-permute-start.7 = (bf16[8,7168]{1,0:T(8,128)(2,1)}, bf16[8,7168]{1,0:T(8,128)(2,1)S(1)}, u32[]{:S(2)}, u32[]{:S(2)}) collective-permute-start(bf16[8,7168]{1,0:T(8,128)(2,1)} %get-tuple-element.42), channel_id=1, source_target_pairs={{0,2},{1,7},{2,0},{3,5},{4,6},{5,3},{6,4},{7,1},{8,10},{9,15},{10,... | collective-permute-start | bytes 344072 | tf_op jit(solution)/shard_map/ppermute | solution.py:23
  13.2 7.1 %collective-permute-start.6 = (bf16[8,7168]{1,0:T(8,128)(2,1)}, bf16[8,7168]{1,0:T(8,128)(2,1)S(1)}, u32[]{:S(2)}, u32[]{:S(2)}) collective-permute-start(bf16[8,7168]{1,0:T(8,128)(2,1)} %get-tuple-element.42), channel_id=1, source_target_pairs={{0,0},{1,5},{2,2},{3,7},{4,4},{5,1},{6,6},{7,3},{8,8},{9,13},{10,1... | collective-permute-start | bytes 344072 | tf_op jit(solution)/shard_map/ppermute | solution.py:23
  14.7 0.8 %copy-start.3 = (f32[2,32,16]{2,1,0:T(8,128)S(1)}, f32[2,32,16]{2,1,0:T(8,128)}, u32[]{:S(2)}) copy-start(f32[2,32,16]{2,1,0:T(8,128)} %get-tuple-element.37.place_ref._) | copy-start | bytes 12292
  20.3 1.9 %collective-permute-start.8 = (bf16[32,7168]{1,0:T(8,128)(2,1)S(1)}, bf16[32,7168]{1,0:T(8,128)(2,1)S(1)}, u32[]{:S(2)}, u32[]{:S(2)}) collective-permute-start(bf16[32,7168]{1,0:T(8,128)(2,1)S(1)} %join.3.refs_0_), channel_id=1, source_target_pairs={{0,1},{1,0},{2,3},{3,2},{4,5},{5,4},{6,7},{7,6},{8,9},{9,8},{10,11... | collective-permute-start | bytes 1376264 | tf_op jit(solution)/shard_map/ppermute | solution.py:23
  20.7 10.3 %collective-permute-start.10 = (bf16[24,7168]{1,0:T(8,128)(2,1)S(1)}, bf16[24,7168]{1,0:T(8,128)(2,1)S(1)}, u32[]{:S(2)}, u32[]{:S(2)}) collective-permute-start(bf16[24,7168]{1,0:T(8,128)(2,1)S(1)} %join.4), channel_id=1, source_target_pairs={{0,2},{1,3},{2,0},{3,1},{4,6},{5,7},{6,4},{7,5},{8,10},{9,11},{10,... | collective-permute-start | bytes 1032200 | tf_op jit(solution)/shard_map/ppermute | solution.py:23
  22.2 2.5 %copy-start = (bf16[2,4,64,576]{3,2,1,0:T(8,128)(2,1)S(1)}, bf16[2,4,64,576]{3,2,1,0:T(8,128)(2,1)}, u32[]{:S(2)}) copy-start(bf16[2,4,64,576]{3,2,1,0:T(8,128)(2,1)} %query_ref.1) | copy-start | bytes 1769476
  22.2 2.5 %copy-start.1 = (bf16[4,64,576]{2,1,0:T(8,128)(2,1)S(1)}, bf16[4,64,576]{2,1,0:T(8,128)(2,1)}, u32[]{:S(2)}) copy-start(bf16[4,64,576]{2,1,0:T(8,128)(2,1)} %cache_ref.1) | copy-start | bytes 884740
  22.2 2.5 %copy-start.5 = (bf16[2,4,576]{2,1,0:T(4,128)(2,1)S(1)}, bf16[2,4,576]{2,1,0:T(4,128)(2,1)}, u32[]{:S(2)}) copy-start(bf16[2,4,576]{2,1,0:T(4,128)(2,1)} %fresh_ref.1) | copy-start | bytes 27652
  22.2 2.5 %copy-start.7 = (s32[4]{0:T(128)S(1)}, s32[4]{0:T(128)}, u32[]{:S(2)}) copy-start(s32[4]{0:T(128)} %lengths_ref.1) | copy-start | bytes 52
  22.2 5.5 %copy-start.2 = (bf16[16,7168]{1,0:T(8,128)(2,1)S(1)}, bf16[16,7168]{1,0:T(8,128)(2,1)}, u32[]{:S(2)}) copy-start(bf16[16,7168]{1,0:T(8,128)(2,1)} %get-tuple-element.36.normed_ref) | copy-start | bytes 688132
  22.2 5.5 %copy-start.4 = (bf16[7168,6]{0,1:T(8,128)(2,1)S(1)}, bf16[7168,6]{0,1:T(8,128)(2,1)}, u32[]{:S(2)}) copy-start(bf16[7168,6]{0,1:T(8,128)(2,1)} %param.15) | copy-start | bytes 258052
  22.2 5.5 %copy-start.6 = (f32[2,6,16]{2,1,0:T(8,128)S(1)}, f32[2,6,16]{2,1,0:T(8,128)}, u32[]{:S(2)}) copy-start(f32[2,6,16]{2,1,0:T(8,128)} %get-tuple-element.38.choose_ref) | copy-start | bytes 2308
  24.4 3.6 %collective-permute-start.9 = (bf16[16,7168]{1,0:T(8,128)(2,1)S(1)}, bf16[16,7168]{1,0:T(8,128)(2,1)S(1)}, u32[]{:S(2)}, u32[]{:S(2)}) collective-permute-start(bf16[16,7168]{1,0:T(8,128)(2,1)S(1)} %get-tuple-element.48), channel_id=1, source_target_pairs={{0,1},{1,0},{2,3},{3,2},{4,5},{5,4},{6,7},{7,6},{8,9},{9,8},{10,11... | collective-permute-start | bytes 688136 | tf_op jit(solution)/shard_map/ppermute | solution.py:23
  30.9 1.9 %collective-permute-start.11 = (bf16[24,7168]{1,0:T(8,128)(2,1)S(1)}, bf16[24,7168]{1,0:T(8,128)(2,1)S(1)}, u32[]{:S(2)}, u32[]{:S(2)}) collective-permute-start(bf16[24,7168]{1,0:T(8,128)(2,1)S(1)} %join.5.refs_0_), channel_id=1, source_target_pairs={{0,1},{1,0},{2,3},{3,2},{4,5},{5,4},{6,7},{7,6},{8,9},{9,8},{10,11... | collective-permute-start | bytes 1032200 | tf_op jit(solution)/shard_map/ppermute | solution.py:23
  31.0 1.8 %collective-permute-start.12 = (bf16[8,7168]{1,0:T(8,128)(2,1)S(1)}, bf16[8,7168]{1,0:T(8,128)(2,1)S(1)}, u32[]{:S(2)}, u32[]{:S(2)}) collective-permute-start(bf16[8,7168]{1,0:T(8,128)(2,1)S(1)} %collective-permute-done.7.refs_5_.refs_4_.refs_1_), channel_id=1, source_target_pairs={{0,1},{1,0},{2,3},{3,2},{4,5},{5,4},{6,7},{7,6},{8,9},{9,8},{10,11... | collective-permute-start | bytes 344072 | tf_op jit(solution)/shard_map/ppermute | solution.py:23
  35.0 1.6 %collective-permute-start.13 = (bf16[16,7168]{1,0:T(8,128)(2,1)S(1)}, bf16[16,7168]{1,0:T(8,128)(2,1)S(1)}, u32[]{:S(2)}, u32[]{:S(2)}) collective-permute-start(bf16[16,7168]{1,0:T(8,128)(2,1)S(1)} %get-tuple-element.53), channel_id=1, source_target_pairs={{0,1},{1,0},{2,3},{3,2},{4,5},{5,4},{6,7},{7,6},{8,9},{9,8},{10,11... | collective-permute-start | bytes 688136 | tf_op jit(solution)/shard_map/ppermute | solution.py:23
  35.2 3.5 %collective-permute-start.19 = (bf16[16,7168]{1,0:T(8,128)(2,1)S(1)}, bf16[16,7168]{1,0:T(8,128)(2,1)S(1)}, u32[]{:S(2)}, u32[]{:S(2)}) collective-permute-start(bf16[16,7168]{1,0:T(8,128)(2,1)S(1)} %get-tuple-element.62), channel_id=1, source_target_pairs={{0,1},{1,0},{2,3},{3,2},{4,5},{5,4},{6,7},{7,6},{8,9},{9,8},{10,11... | collective-permute-start | bytes 688136 | tf_op jit(solution)/shard_map/ppermute | solution.py:23
  35.6 4.7 %collective-permute-start.18 = (bf16[16,7168]{1,0:T(8,128)(2,1)S(1)}, bf16[16,7168]{1,0:T(8,128)(2,1)S(1)}, u32[]{:S(2)}, u32[]{:S(2)}) collective-permute-start(bf16[16,7168]{1,0:T(8,128)(2,1)S(1)} %get-tuple-element.59), channel_id=1, source_target_pairs={{0,1},{1,0},{2,3},{3,2},{4,5},{5,4},{6,7},{7,6},{8,9},{9,8},{10,11... | collective-permute-start | bytes 688136 | tf_op jit(solution)/shard_map/ppermute | solution.py:23
  36.6 6.1 %collective-permute-start.14 = (bf16[8,7168]{1,0:T(8,128)(2,1)S(1)}, bf16[8,7168]{1,0:T(8,128)(2,1)S(1)}, u32[]{:S(2)}, u32[]{:S(2)}) collective-permute-start(bf16[8,7168]{1,0:T(8,128)(2,1)S(1)} %get-tuple-element.54), channel_id=1, source_target_pairs={{0,2},{1,3},{2,0},{3,1},{4,6},{5,7},{6,4},{7,5},{8,10},{9,11},{10,... | collective-permute-start | bytes 344072 | tf_op jit(solution)/shard_map/ppermute | solution.py:23
  38.2 8.7 %collective-permute-start.16 = (bf16[8,7168]{1,0:T(8,128)(2,1)S(1)}, bf16[8,7168]{1,0:T(8,128)(2,1)S(1)}, u32[]{:S(2)}, u32[]{:S(2)}) collective-permute-start(bf16[8,7168]{1,0:T(8,128)(2,1)S(1)} %get-tuple-element.57), channel_id=1, source_target_pairs={{0,2},{1,3},{2,0},{3,1},{4,6},{5,7},{6,4},{7,5},{8,10},{9,11},{10,... | collective-permute-start | bytes 344072 | tf_op jit(solution)/shard_map/ppermute | solution.py:23
  38.8 8.8 %collective-permute-start.20 = (bf16[8,7168]{1,0:T(8,128)(2,1)S(1)}, bf16[8,7168]{1,0:T(8,128)(2,1)S(1)}, u32[]{:S(2)}, u32[]{:S(2)}) collective-permute-start(bf16[8,7168]{1,0:T(8,128)(2,1)S(1)} %get-tuple-element.63), channel_id=1, source_target_pairs={{0,2},{1,3},{2,0},{3,1},{4,6},{5,7},{6,4},{7,5},{8,10},{9,11},{10,... | collective-permute-start | bytes 344072 | tf_op jit(solution)/shard_map/ppermute | solution.py:23
  40.4 16.3 %collective-permute-start.22 = (bf16[8,7168]{1,0:T(8,128)(2,1)S(1)}, bf16[8,7168]{1,0:T(8,128)(2,1)S(1)}, u32[]{:S(2)}, u32[]{:S(2)}) collective-permute-start(bf16[8,7168]{1,0:T(8,128)(2,1)S(1)} %convert_element_type.3), channel_id=1, source_target_pairs={{0,0},{1,5},{2,2},{3,7},{4,4},{5,1},{6,6},{7,3},{8,8},{9,13},{10,1... | collective-permute-start | bytes 344072 | tf_op jit(solution)/shard_map/ppermute | solution.py:23
  41.1 15.6 %collective-permute-start.23 = (bf16[8,7168]{1,0:T(8,128)(2,1)S(1)}, bf16[8,7168]{1,0:T(8,128)(2,1)S(1)}, u32[]{:S(2)}, u32[]{:S(2)}) collective-permute-start(bf16[8,7168]{1,0:T(8,128)(2,1)S(1)} %get-tuple-element.65), channel_id=1, source_target_pairs={{0,2},{1,7},{2,0},{3,5},{4,6},{5,3},{6,4},{7,1},{8,10},{9,15},{10,... | collective-permute-start | bytes 344072 | tf_op jit(solution)/shard_map/ppermute | solution.py:23
  42.7 8.8 %collective-permute-start.15 = (bf16[8,7168]{1,0:T(8,128)(2,1)S(1)}, bf16[8,7168]{1,0:T(8,128)(2,1)S(1)}, u32[]{:S(2)}, u32[]{:S(2)}) collective-permute-start(bf16[8,7168]{1,0:T(8,128)(2,1)S(1)} %add.9.refs_2_), channel_id=1, source_target_pairs={{0,28},{1,25},{2,30},{3,27},{4,24},{5,29},{6,26},{7,31},{8,20},{9,... | collective-permute-start | bytes 344072 | tf_op jit(solution)/shard_map/ppermute | solution.py:23
  46.9 9.4 %collective-permute-start.17 = (bf16[8,7168]{1,0:T(8,128)(2,1)S(1)}, bf16[8,7168]{1,0:T(8,128)(2,1)S(1)}, u32[]{:S(2)}, u32[]{:S(2)}) collective-permute-start(bf16[8,7168]{1,0:T(8,128)(2,1)S(1)} %add.10.refs_2_), channel_id=1, source_target_pairs={{0,16},{1,21},{2,18},{3,23},{4,20},{5,17},{6,22},{7,19},{8,24},{9,... | collective-permute-start | bytes 344072 | tf_op jit(solution)/shard_map/ppermute | solution.py:23
  47.6 9.1 %collective-permute-start.21 = (bf16[8,7168]{1,0:T(8,128)(2,1)S(1)}, bf16[8,7168]{1,0:T(8,128)(2,1)S(1)}, u32[]{:S(2)}, u32[]{:S(2)}) collective-permute-start(bf16[8,7168]{1,0:T(8,128)(2,1)S(1)} %add.13), channel_id=1, source_target_pairs={{0,12},{1,9},{2,14},{3,11},{4,8},{5,13},{6,10},{7,15},{8,4},{9,1},... | collective-permute-start | bytes 344072 | tf_op jit(solution)/shard_map/ppermute | solution.py:23
  57.1 1.4 %collective-permute-start.24 = (bf16[8,7168]{1,0:T(8,128)(2,1)S(1)}, bf16[8,7168]{1,0:T(8,128)(2,1)S(1)}, u32[]{:S(2)}, u32[]{:S(2)}) collective-permute-start(bf16[8,7168]{1,0:T(8,128)(2,1)S(1)} %get-tuple-element.67), channel_id=1, source_target_pairs={{0,1},{1,0},{2,3},{3,2},{4,5},{5,4},{6,7},{7,6},{8,9},{9,8},{10,11... | collective-permute-start | bytes 344072 | tf_op jit(solution)/shard_map/ppermute | solution.py:23
